TPU v7x, 32 devices: a whole 2x2x4 slice. The times are simulated.
32 devices in a mesh: dp: 8 (over y, x, core), tp: 4 (over z).
Axes of the slice: x: 2, y: 2, z: 4, core: 2. Of those that a mesh axis runs over, the one named last changes fastest.
Arguments:
- residual: bfloat16 [128, 7168], P(('dp', 'tp')), may hold values from -6 to 6
- queries: bfloat16 [128, 73728], P(('dp', 'tp')), may hold values from -240 to 240
- paged_latent_cache: bfloat16 [458752, 576], P(('dp', 'tp')), may hold values from -6 to 6
- lengths: int32 [128], replicated, may hold values from 1 to 14144, as said below
- w_uv: bfloat16 [128, 512, 128], P(('dp', 'tp')), may hold values from -1.5 to 1.5
- w_o: bfloat16 [16384, 7168], P('dp', 'tp'), may hold values from -0.046875 to 0.046875
- norm_gain: bfloat16 [7168], replicated, may hold values from 0.099609375 to 1.8984375
- w_gate: bfloat16 [7168, 18432], P('tp', 'dp'), may hold values from -0.0625 to 0.0625
- w_up: bfloat16 [7168, 18432], P('tp', 'dp'), may hold values from -0.0625 to 0.0625
- w_down: bfloat16 [18432, 7168], P('dp', 'tp'), may hold values from -0.125 to 0.125
Outputs:
- layer_out: bfloat16 [128, 7168], P(('dp', 'tp'))
Inputs may be any that keep to these rules, and one draw needn't show every extreme that they name: `lengths`: requests are owned 4 after one another by the ranks in rank order. On every rank, the sum over its requests of ceil(length / 64) is at most 224, and it is exactly 224 on at least one rank. One request has exactly the largest length.
All inputs are finite; a program needn't handle non-finite values.
Results may differ from a plain program's by a relative error of at most 0.018.
Values may be sent and summed in bfloat16 or wider, within the bound.
No kernel may reach another device: no remote copies, remote signals or barrier semaphores. Data moves between devices by JAX's collectives and lax.ppermute only.
A program may use at most 192 MiB of HBM per device.

v0:
```python
import jax
import jax.numpy as jnp
from jax import lax
from jax.sharding import PartitionSpec as P

C = 512
BLOCK_TOKENS = 64


score_scale = 192.0 ** (-0.5)
negative = -1e30
blocks_each_step = 8


def block_table(lens, count_blocks, width):
    nreq = lens.shape[0]
    need = (lens + width - 1) // width
    ends = jnp.cumsum(need)
    starts = ends - need
    index = jnp.arange(count_blocks, dtype=jnp.int32)[:, None]
    inside = (index >= starts[None, :]) & (index < ends[None, :])
    owners = jnp.arange(nreq, dtype=jnp.int32)[None, :]
    which = jnp.where(jnp.any(inside, 1), jnp.sum(jnp.where(inside, owners, 0), 1), -1)
    filled = jnp.clip(lens[None, :] - width * (index - starts[None, :]), 0, width)
    valid = jnp.sum(jnp.where(inside, filled, 0), 1)
    return (which, valid, ends[-1])


def attend(query_matrix, cache_blocks, which, valid, count):
    nreq = query_matrix.shape[0]
    width = cache_blocks.shape[1]
    row_length = cache_blocks.shape[2]
    query_heads = query_matrix.shape[1] // row_length
    init = (
        jnp.full((nreq, query_heads), negative, jnp.float32),
        jnp.zeros((nreq, query_heads), jnp.float32),
        jnp.zeros((nreq, query_heads, C), jnp.float32),
    )

    def step(i, carry):
        best, total, acc = carry
        start = (i * blocks_each_step).astype(jnp.int32)
        part = lax.dynamic_slice_in_dim(cache_blocks, start, blocks_each_step, 0)
        owner = lax.dynamic_slice_in_dim(which, start, blocks_each_step, 0)
        filled = lax.dynamic_slice_in_dim(valid, start, blocks_each_step, 0)
        onehot = owner[:, None] == jnp.arange(nreq, dtype=jnp.int32)[None, :]
        selected_blocks = jnp.dot(
            onehot.astype(jnp.bfloat16), query_matrix, preferred_element_type=jnp.float32
        )
        selected_blocks = selected_blocks.astype(jnp.bfloat16).reshape(
            blocks_each_step, query_heads, row_length
        )
        scores = (
            jnp.einsum("ghc,gtc->ght", selected_blocks, part, preferred_element_type=jnp.float32)
            * score_scale
        )
        live = jnp.arange(width, dtype=jnp.int32)[None, :] < filled[:, None]
        scores = jnp.where(live[:, None, :], scores, negative)
        peak = jnp.max(scores, 2)
        weights = jnp.exp(scores - peak[..., None])
        mass = jnp.sum(weights, 2)
        values = jnp.einsum(
            "ght,gtc->ghc",
            weights.astype(jnp.bfloat16),
            part[:, :, :C],
            preferred_element_type=jnp.float32,
        )
        mine = onehot[:, :, None]
        newbest = jnp.maximum(best, jnp.max(jnp.where(mine, peak[:, None, :], negative), 0))
        factor = jnp.where(mine, jnp.exp(peak[:, None, :] - newbest[None]), 0.0)
        keep = jnp.exp(best - newbest)
        total = total * keep + jnp.sum(factor * mass[:, None, :], 0)
        acc = acc * keep[..., None] + jnp.einsum(
            "grh,ghc->rhc", factor, values, precision=lax.Precision.HIGHEST
        )
        return (newbest, total, acc)

    steps = (count + blocks_each_step - 1) // blocks_each_step
    return lax.fori_loop(0, steps, step, init)


def finish(total, acc):
    return (acc / total[..., None]).astype(jnp.bfloat16)


def local(
    residual, queries, paged_latent_cache, lengths, w_uv, w_o, norm_gain, w_gate, w_up, w_down
):
    ranks_dp = lax.axis_size("dp")
    ranks_tp = lax.axis_size("tp")
    per_rank = residual.shape[0]
    row_length = paged_latent_cache.shape[1]
    block_capacity = paged_latent_cache.shape[0] // BLOCK_TOKENS
    rank_all = lax.axis_index("dp") * ranks_tp + lax.axis_index("tp")
    block_store = paged_latent_cache.reshape(block_capacity, BLOCK_TOKENS, row_length)
    own_lens = lax.dynamic_slice_in_dim(lengths, rank_all * per_rank, per_rank, 0)
    which, valid, used = block_table(own_lens, block_capacity, BLOCK_TOKENS)
    best, total, acc = attend(queries, block_store, which, valid, used)
    latent_out = finish(total, acc)
    heads_all = latent_out.shape[1]
    heads_here = heads_all // (ranks_dp * ranks_tp)
    local_heads = lax.all_to_all(latent_out, ("dp", "tp"), split_axis=1, concat_axis=0, tiled=True)
    head_values = jnp.einsum("rhc,hcv->rhv", local_heads, w_uv, preferred_element_type=jnp.float32)
    head_values = head_values.astype(jnp.bfloat16)
    flat_values = head_values.reshape(head_values.shape[0], heads_here * w_uv.shape[2])
    group_values = lax.all_gather(flat_values, "tp", axis=1, tiled=True)
    attn_part = lax.psum_scatter(
        jnp.dot(group_values, w_o, preferred_element_type=jnp.float32),
        "dp",
        scatter_dimension=0,
        tiled=True,
    )
    attn = lax.all_to_all(attn_part, "tp", split_axis=0, concat_axis=1, tiled=True)
    hidden = (residual.astype(jnp.float32) + attn).astype(jnp.bfloat16)
    hidden_f = hidden.astype(jnp.float32)
    normed = (
        hidden_f
        * lax.rsqrt(jnp.mean(hidden_f * hidden_f, 1, keepdims=True) + 1e-06)
        * norm_gain.astype(jnp.float32)
    )
    normed = normed.astype(jnp.bfloat16)
    normed_slice = lax.all_to_all(normed, "tp", split_axis=1, concat_axis=0, tiled=True)
    units_here = w_gate.shape[1]
    piece = lax.all_gather(normed_slice, "dp", axis=0, tiled=True)
    gate_part = jnp.dot(piece, w_gate, preferred_element_type=jnp.float32)
    up_part = jnp.dot(piece, w_up, preferred_element_type=jnp.float32)
    both = jnp.concatenate([gate_part, up_part], 1)
    gate = both[:, :units_here]
    up = both[:, units_here:]
    gate, up = (
        lax.psum(gate.astype(jnp.bfloat16), "tp").astype(jnp.float32),
        lax.psum(up.astype(jnp.bfloat16), "tp").astype(jnp.float32),
    )
    inner = (jax.nn.silu(gate) * up).astype(jnp.bfloat16)
    ffn_part = lax.psum_scatter(
        jnp.dot(inner, w_down, preferred_element_type=jnp.float32).astype(jnp.bfloat16),
        "dp",
        scatter_dimension=0,
        tiled=True,
    ).astype(jnp.float32)
    ffn = lax.all_to_all(
        ffn_part.astype(jnp.bfloat16), "tp", split_axis=0, concat_axis=1, tiled=True
    ).astype(ffn_part.dtype)
    return (hidden_f + ffn).astype(jnp.bfloat16)


def solution(mesh):
    placed = (
        P(("dp", "tp"), None),
        P(("dp", "tp"), None),
        P(("dp", "tp"), None),
        P(),
        P(("dp", "tp"), None, None),
        P("dp", "tp"),
        P(),
        P("tp", "dp"),
        P("tp", "dp"),
        P("dp", "tp"),
    )
    return jax.shard_map(
        local, mesh=mesh, in_specs=placed, out_specs=P(("dp", "tp"), None), check_vma=False
    )
```

profile of v0, /device:TPU:0, one launch (start us, length us, event | category | flops | bytes accessed | tf_op | source)
XLA Modules:
  0.0 630.8 jit_solution(3920443333269046042)
XLA Ops:
  9.0 23.6 %copy.40 = bf16[14336,576]{1,0:T(8,128)(2,1)} copy(bf16[14336,576]{0,1:T(8,128)(2,1)} %param.14) | data formatting | bytes 33030144 | tf_op args[2]
  33.7 131.8 %while.14 = (s32[]{:T(128)}, f32[4,128]{0,1:T(8,128)S(1)}, f32[4,128]{0,1:T(8,128)S(1)}, f32[4,128,512]{2,0,1:T(4,128)}, s32[]{:T(128)}, /*index=5*/s32[224]{0:T...) while((s32[]{:T(128)}, f32[4,128]{0,1:T(8,128)S(1)}, ...), condition=%wide.region_9.10_spmd, body=%wide.region_4.9_spmd.sunk | while | flops 174095936 | bytes 16008731 | solution.py:79
  41.5 5.4 fusion.67
  54.6 5.4 fusion.67
  67.8 5.4 fusion.67
  81.0 5.4 fusion.67
  94.2 5.4 fusion.67
  107.4 5.4 fusion.67
  120.5 5.4 fusion.67
  133.7 5.4 fusion.67
  146.9 5.4 fusion.67
  160.1 5.4 fusion.67
  167.0 254.7 %all_to_all.69 = bf16[4,128,512]{2,0,1:T(4,128)(2,1)S(1)} all-to-all(bf16[4,128,512]{2,0,1:T(4,128)(2,1)S(1)} %divide_convert_fusion), channel_id=1, replica_groups=mesh['dp'=8,'tp'=4] {'dp','tp'}, dimensions={1} | all-to-all | bytes 1048576 | tf_op jit(solution)/shard_map/all_to_all | solution.py:102
  422.4 16.0 %all_gather.6 = bf16[128,2048]{0,1:T(8,128)(2,1)S(1)} all-gather(bf16[128,512]{0,1:T(8,128)(2,1)S(1)} %bitcast.46), channel_id=1, replica_groups=mesh['dp'=8,'tp'=4] {'tp'}, dimensions={1}, use_global_device_ids=true | all-gather | bytes 655360 | tf_op jit(solution)/shard_map/all_gather | solution.py:106
  443.7 34.0 %reduce-scatter.3.cloned.1.call-done = f32[16,1792]{1,0:T(8,128)} async-done(((f32[128,1792]{1,0:T(8,128)}), f32[16,1792]{1,0:T(8,128)}) %reduce-scatter.3.cloned.1.call-update) | async-done | bytes 114704 | tf_op jit(solution)/shard_map/reduce_scatter | solution.py:107
  483.9 5.9 all-to-all-done.1
  490.1 8.1 %all_to_all.70 = bf16[4,4,1792]{2,0,1:T(4,128)(2,1)S(1)} all-to-all(bf16[4,4,1792]{2,0,1:T(4,128)(2,1)S(1)} %bitcast.49), channel_id=1, replica_groups=mesh['dp'=8,'tp'=4] {'tp'}, dimensions={1} | all-to-all | bytes 114688 | tf_op jit(solution)/shard_map/all_to_all | solution.py:122
  498.2 9.8 %all_gather.7 = bf16[128,1792]{1,0:T(8,128)(2,1)S(1)} all-gather(bf16[16,1792]{1,0:T(8,128)(2,1)S(1)} %all_to_all.62), channel_id=1, replica_groups=mesh['dp'=8,'tp'=4] {'dp'}, dimensions={0}, use_global_device_ids=true | all-gather | bytes 516096 | tf_op jit(solution)/shard_map/all_gather | solution.py:124
  508.0 5.5 convolution_convert_fusion.1
  513.5 5.5 convolution_convert_fusion.2
  519.0 54.0 %all-reduce.3.cloned.1.call-done = (bf16[128,2304]{1,0:T(8,128)(2,1)}, bf16[128,2304]{1,0:T(8,128)(2,1)}) async-done(((bf16[128,2304]{1,0:T(8,128)(2,1)}, bf16[128,2304]{1,0:T(8,128)(2,1)}), (bf16[128,2304]{1,0:T(8,128)(2,1)}, bf16[128,2304]{1,0:T(8,128)(2,1)})) %all-reduce.3.cloned.1.call-update) | async-done | bytes 1179664 | tf_op jit(solution)/shard_map/psum | solution.py:132
  573.0 5.9 convolution_convert_fusion.3
  578.9 33.7 %reduce-scatter.5.cloned.1.call-done = bf16[16,1792]{1,0:T(8,128)(2,1)} async-done(((bf16[128,1792]{1,0:T(8,128)(2,1)}), bf16[16,1792]{1,0:T(8,128)(2,1)}) %reduce-scatter.5.cloned.1.call-update) | async-done | bytes 57360 | tf_op jit(solution)/shard_map/reduce_scatter | solution.py:135
  613.5 10.1 %all_to_all.71 = bf16[4,4,1792]{2,1,0:T(4,128)(2,1)S(1)} all-to-all(bf16[4,4,1792]{2,1,0:T(4,128)(2,1)S(1)} %all_to_all.63), channel_id=1, replica_groups=mesh['dp'=8,'tp'=4] {'tp'}, dimensions={0} | all-to-all | bytes 114688 | tf_op jit(solution)/shard_map/all_to_all | solution.py:141
  (207 shorter events, 94.9 us)
Async XLA Ops:
  6.5 415.5 %copy-start = (bf16[4,512,128]{2,1,0:T(8,128)(2,1)S(1)}, bf16[4,512,128]{2,1,0:T(8,128)(2,1)}, u32[]{:S(2)}) copy-start(bf16[4,512,128]{2,1,0:T(8,128)(2,1)} %param.16) | copy-start | bytes 1572868
  6.5 471.2 %reduce-scatter.3.cloned.1.call-start = ((), (), s32[]{:S(2)}) async-start(), calls=%async_computation.6 | async-start | bytes 1032192 | tf_op jit(solution)/shard_map/reduce_scatter | solution.py:107
  438.5 45.4 %copy-start.2 = (bf16[7168]{0:T(1024)(128)(2,1)S(1)}, bf16[7168]{0:T(1024)(128)(2,1)}, u32[]{:S(2)}) copy-start(bf16[7168]{0:T(1024)(128)(2,1)} %param.18) | copy-start | bytes 43012
  438.5 51.3 %copy-start.1 = (bf16[4,7168]{1,0:T(4,128)(2,1)S(1)}, bf16[4,7168]{1,0:T(4,128)(2,1)}, u32[]{:S(2)}) copy-start(bf16[4,7168]{1,0:T(4,128)(2,1)} %param.12) | copy-start | bytes 172036
  479.3 10.5 %all-to-all-start.1 = ((f32[4,4,1792]{2,1,0:T(4,128)}), f32[4,4,1792]{2,1,0:T(4,128)S(1)}, u32[]{:S(2)}, u32[]{:S(2)}) async-start(f32[4,4,1792]{2,1,0:T(4,128)} %all_to_all.55), calls=%async_computation.2 | async-start | bytes 229376 | tf_op jit(solution)/shard_map/all_to_all | solution.py:113
  483.9 89.1 %all-reduce.3.cloned.1.call-start = ((), (), s32[]{:S(2)}) async-start(), calls=%async_computation.8 | async-start | bytes 2359296 | tf_op jit(solution)/shard_map/psum | solution.py:132
  519.0 93.7 %reduce-scatter.5.cloned.1.call-start = ((), (), s32[]{:S(2)}) async-start(), calls=%async_computation.7 | async-start | bytes 516096 | tf_op jit(solution)/shard_map/reduce_scatter | solution.py:135
Sparse Core Ops, SparseCore 0:
  443.8 33.8 reduce-scatter.2
  519.1 53.8 all-reduce.2
  579.1 33.5 reduce-scatter.4
where the time goes:
time: 638 us; the launch traced here: 631 us
  blocking collectives  299 us (47%)
  waiting for transfers between devices  128 us (20%)
  matrix products  126 us (20%)
  local copies, waits for them, and re-layouts  48.1 us (8%)
  between operations  13.8 us (2%)
  other arithmetic  11.2 us (2%)
    all_to_all x1, blocking collectives, local(): lax.all_to_all(latent_out, ('dp', 'tp'), split_axis=1, concat_axis=0, til...  255 us
    dot_general x10, matrix products, step(): jnp.einsum('grh,ghc->rhc', factor, values, precision=lax.Precision.HIGHEST)  54.5 us
    psum x1, waiting for transfers between devices, local(): lax.psum(up.astype(jnp.bfloat16), 'tp').astype(jnp.float32)  54 us
    reduce_scatter x1, waiting for transfers between devices, local(): lax.psum_scatter(jnp.dot(group_values, w_o, preferred_element_type=jnp.fl...  34 us
    reduce_scatter x1, waiting for transfers between devices, local(): lax.psum_scatter(jnp.dot(inner, w_down, preferred_element_type=jnp.float3...  33.7 us
    unnamed x7, local copies, waits for them, and re-layouts  23.6 us
    dot_general x10, matrix products, step(): jnp.einsum('ghc,gtc->ght', selected_blocks, part, preferred_element_type=...  17.4 us
    dot_general x10, matrix products, step(): jnp.dot(onehot.astype(jnp.bfloat16), query_matrix, preferred_element_type...  16.2 us
  transfers between devices with their start and end apart: 4, of which 4 were waited for; matrix products, arithmetic and copies ran while one was open for 0% of the time, Pallas kernels for 0%

commit v1 on v0

v1 whole, which is shorter than its diff:
```python
import functools

import jax
import jax.numpy as jnp
from jax import lax
from jax.experimental import pallas as pl
from jax.experimental.pallas import tpu as pltpu
from jax.sharding import PartitionSpec as P

C = 512
BLOCK_TOKENS = 64
TILE = 1024
VMEM_BYTES = 48 * 1024 * 1024

score_scale = 192.0 ** (-0.5)
log2_e = 1.4426950408889634
negative = -1e30


def attention_kernel(
    lens_ref, q_ref, cache_ref, out_ref, held, score0, score1, acc, best, mass, lo, hi, first, last, sems
):
    nreq = q_ref.shape[0]
    tiles = held.shape[0]
    tile = held.shape[2]
    heads = q_ref.shape[1]

    begin = jnp.int32(0)
    pairs = jnp.int32(0)
    for r in range(nreq):
        length = lens_ref[r]
        lo[r] = begin
        hi[r] = begin + length
        first[r] = begin // tile
        last[r] = (begin + length - 1) // tile
        pairs = pairs + (last[r] - first[r] + 1)
        begin = begin + ((length + BLOCK_TOKENS - 1) // BLOCK_TOKENS) * BLOCK_TOKENS
    used = last[nreq - 1] + 1

    def copy(i):
        return pltpu.make_async_copy(
            cache_ref.at[:, pl.ds(pl.multiple_of(i * tile, tile), tile)], held.at[i], sems.at[i]
        )

    @pl.loop(0, used)
    def _(i):
        copy(i).start()

    def reset():
        acc[...] = jnp.zeros_like(acc)
        best[...] = jnp.full_like(best, negative)
        mass[...] = jnp.zeros_like(mass)

    def scores(r, i, live, target):
        begin_at = jnp.where(live, lo[r], 0)
        end_at = jnp.where(live, hi[r], 0)
        s = jnp.dot(q_ref[r], held[i], preferred_element_type=jnp.float32)
        token = i * tile + lax.broadcasted_iota(jnp.int32, (1, tile), 1)
        s = jnp.where((token >= begin_at) & (token < end_at), s, negative)
        target[...] = s

    def advance(p, r, i):
        ends = i == last[r]
        live = p + 1 < pairs
        nr = jnp.where(ends & live, r + 1, r)
        ni = jnp.where(ends, jnp.where(live, first[nr], i), i + 1)
        return nr, ni, live

    def fetch(i, r, live):
        fresh = live & ((r == 0) | (i > last[jnp.maximum(r - 1, 0)]))

        @pl.when(fresh)
        def _():
            copy(i).wait()

    def absorb(r, i, live, source):
        factor = score_scale * log2_e
        s = source[...]
        old = best[...]
        new = jnp.maximum(old, jnp.max(s, axis=1, keepdims=True))
        weight = jnp.exp2((s - new[:, :1]) * factor)
        keep = jnp.exp2((old - new) * factor)
        part = weight[:, :128]
        for at in range(128, tile, 128):
            part = part + weight[:, at : at + 128]
        mass[...] = mass[...] * keep + part
        best[...] = new
        values = lax.dot_general(
            weight.astype(jnp.bfloat16),
            held[i, :C, :],
            (((1,), (1,)), ((), ())),
            preferred_element_type=jnp.float32,
        )
        acc[...] = acc[...] * keep[:, :1] + values

    def close(r, i, live):
        @pl.when(live & (i == last[r]))
        def _():
            total = jnp.sum(mass[...], axis=1, keepdims=True)
            out_ref[r] = (acc[...] / total).astype(out_ref.dtype)
            reset()

    reset()
    fetch(jnp.int32(0), jnp.int32(0), pairs > 0)
    scores(jnp.int32(0), jnp.int32(0), pairs > 0, score0)

    def step(j, carry):
        r, i, live = carry
        p = 2 * j
        for now, later in ((score0, score1), (score1, score0)):
            nr, ni, nlive = advance(p, r, i)
            fetch(ni, nr, nlive)
            scores(nr, ni, nlive, later)
            absorb(r, i, live, now)
            close(r, i, live)
            r, i, live, p = nr, ni, nlive, p + 1
        return r, i, live

    lax.fori_loop(0, (pairs + 1) // 2, step, (jnp.int32(0), jnp.int32(0), pairs > 0))


def attend(own_lens, queries, cache_t):
    nreq, heads, width = queries.shape
    tokens = cache_t.shape[1]
    tile = TILE
    tiles = tokens // tile
    return pl.pallas_call(
        attention_kernel,
        out_shape=jax.ShapeDtypeStruct((nreq, heads, C), jnp.bfloat16),
        in_specs=[
            pl.BlockSpec(memory_space=pltpu.SMEM),
            pl.BlockSpec(memory_space=pltpu.VMEM),
            pl.BlockSpec(memory_space=pl.ANY),
        ],
        out_specs=pl.BlockSpec(memory_space=pltpu.VMEM),
        scratch_shapes=[
            pltpu.VMEM((tiles, width, tile), jnp.bfloat16),
            pltpu.VMEM((heads, tile), jnp.float32),
            pltpu.VMEM((heads, tile), jnp.float32),
            pltpu.VMEM((heads, C), jnp.float32),
            pltpu.VMEM((heads, 128), jnp.float32),
            pltpu.VMEM((heads, 128), jnp.float32),
            pltpu.SMEM((nreq,), jnp.int32),
            pltpu.SMEM((nreq,), jnp.int32),
            pltpu.SMEM((nreq,), jnp.int32),
            pltpu.SMEM((nreq,), jnp.int32),
            pltpu.SemaphoreType.DMA((tiles,)),
        ],
        compiler_params=pltpu.CompilerParams(vmem_limit_bytes=VMEM_BYTES),
        cost_estimate=pl.CostEstimate(
            flops=2 * heads * tokens * (width + C),
            bytes_accessed=2 * tokens * width,
            transcendentals=heads * tokens,
        ),
        name="attention",
    )(own_lens, queries, cache_t)


def exchange_columns(rows, axis):
    size = lax.axis_size(axis)
    me = lax.axis_index(axis)
    width = rows.shape[1] // size
    slices = rows.reshape(rows.shape[0], size, width)
    out = jnp.zeros((size, rows.shape[0], width), rows.dtype)
    own = lax.dynamic_index_in_dim(slices, me, 1, keepdims=False)
    out = lax.dynamic_update_index_in_dim(out, own, me, 0)
    for shift in range(1, size):
        piece = lax.dynamic_index_in_dim(slices, (me + shift) % size, 1, keepdims=False)
        got = lax.ppermute(piece, axis, [(k, (k + shift) % size) for k in range(size)])
        out = lax.dynamic_update_index_in_dim(out, got, (me - shift) % size, 0)
    return out


def scatter_sum(part, axis):
    size = lax.axis_size(axis)
    pieces = part.reshape(size, part.shape[0] // size, part.shape[1])
    pieces = lax.all_to_all(pieces, axis, split_axis=0, concat_axis=0, tiled=True)
    return jnp.sum(pieces.astype(jnp.float32), 0)


def local(
    residual, queries, paged_latent_cache, lengths, w_uv, w_o, norm_gain, w_gate, w_up, w_down
):
    ranks_dp = lax.axis_size("dp")
    ranks_tp = lax.axis_size("tp")
    me_dp = lax.axis_index("dp")
    me_tp = lax.axis_index("tp")
    per_rank, model = residual.shape
    row_length = paged_latent_cache.shape[1]
    heads_all = queries.shape[1] // row_length
    heads_here = w_uv.shape[0]
    units = w_gate.shape[1]
    width = w_o.shape[1]
    rank = me_dp * ranks_tp + me_tp

    residual_slice = exchange_columns(residual, "tp").reshape(ranks_tp * per_rank, width)
    gain_slice = lax.dynamic_slice_in_dim(norm_gain, me_tp * width, width, 0)

    own_lens = lax.dynamic_slice_in_dim(lengths, rank * per_rank, per_rank, 0)
    query = queries.reshape(per_rank, heads_all, row_length)
    latent_out = attend(own_lens, query, paged_latent_cache.T)

    local_heads = lax.all_to_all(latent_out, ("dp", "tp"), split_axis=1, concat_axis=0, tiled=True)
    head_values = jnp.einsum("rhc,hcv->rhv", local_heads, w_uv, preferred_element_type=jnp.float32)
    head_values = head_values.astype(jnp.bfloat16)
    flat_values = head_values.reshape(head_values.shape[0], heads_here * w_uv.shape[2])
    group_values = lax.all_gather(flat_values, "tp", axis=1, tiled=True)
    attn_part = jnp.dot(group_values, w_o, preferred_element_type=jnp.float32).astype(jnp.bfloat16)
    attn = scatter_sum(attn_part, "dp")

    hidden = (residual_slice.astype(jnp.float32) + attn).astype(jnp.bfloat16)
    piece = lax.all_gather(hidden, "dp", axis=0, tiled=True).astype(jnp.float32)
    square = jnp.sum(piece * piece, 1, keepdims=True)
    scaled = (piece * gain_slice.astype(jnp.float32)).astype(jnp.bfloat16)
    gate_part = jnp.dot(scaled, w_gate, preferred_element_type=jnp.float32).astype(jnp.bfloat16)
    up_part = jnp.dot(scaled, w_up, preferred_element_type=jnp.float32).astype(jnp.bfloat16)
    top = square.astype(jnp.bfloat16)
    rest = square - top.astype(jnp.float32)
    middle = rest.astype(jnp.bfloat16)
    low = (rest - middle.astype(jnp.float32)).astype(jnp.bfloat16)
    extra = jnp.concatenate(
        [top, middle, low, jnp.zeros((top.shape[0], 125), jnp.bfloat16)], 1
    )
    both = scatter_sum(jnp.concatenate([gate_part, up_part, extra], 1), "tp")
    mean = jnp.sum(both[:, 2 * units :], 1, keepdims=True) / model
    factor = lax.rsqrt(mean + 1e-06)
    gate = both[:, :units] * factor
    up = both[:, units : 2 * units] * factor
    inner = (jax.nn.silu(gate) * up).astype(jnp.bfloat16)
    inner = lax.all_gather(inner, "tp", axis=0, tiled=True)
    ffn_part = jnp.dot(inner, w_down, preferred_element_type=jnp.float32).astype(jnp.bfloat16)
    ffn = scatter_sum(ffn_part, "dp")
    layer = (hidden.astype(jnp.float32) + ffn).astype(jnp.bfloat16)
    return lax.all_to_all(layer, "tp", split_axis=0, concat_axis=1, tiled=True)


def solution(mesh):
    placed = (
        P(("dp", "tp"), None),
        P(("dp", "tp"), None),
        P(("dp", "tp"), None),
        P(),
        P(("dp", "tp"), None, None),
        P("dp", "tp"),
        P(),
        P("tp", "dp"),
        P("tp", "dp"),
        P("dp", "tp"),
    )
    return jax.shard_map(
        local, mesh=mesh, in_specs=placed, out_specs=P(("dp", "tp"), None), check_vma=False
    )
```

time: 638 us -> 175 us (0.27); the launches traced: 631 us -> 175 us
  blocking collectives: 299 us -> 81.6 us
  matrix products: 126 us -> 20 us
  waiting for transfers between devices: 128 us -> 30.7 us
  local copies, waits for them, and re-layouts: 48.1 us -> 7.79 us
  starting transfers between devices: 4.63 us -> 23 us
  between operations: 13.8 us -> 0.2 us
  Pallas kernels: 0 us -> 10.3 us
  other arithmetic: 11.2 us -> 1.61 us
    all_to_all x3 -> x2, blocking collectives: 273 us -> 41 us  [the longest x1 32.5 us: scatter_sum(): lax.all_to_all(pieces, axis, split_axis=0, concat_axis=0, tiled=True)]
    dot_general x42 -> x2, matrix products: 114 us -> 9.19 us  [the longest x1 4.6 us: local(): jnp.dot(scaled, w_up, preferred_element_type=jnp.float32)]
    reduce_scatter x2 -> x0, waiting for transfers between devices: 67.7 us -> none  [the longest x1 34 us: local(): lax.psum_scatter(jnp.dot(group_values, w_o, preferred_element_type=jnp.fl...]
    psum x1 -> x0, waiting for transfers between devices: 54 us -> none  [local(): lax.psum(up.astype(jnp.bfloat16), 'tp').astype(jnp.float32)]
    all_to_all x1 -> x3, waiting for transfers between devices: 5.86 us -> 30.7 us  [the longest x2 17.9 us: scatter_sum(): lax.all_to_all(pieces, axis, split_axis=0, concat_axis=0, tiled=True)]
    unnamed x7 -> x3, local copies, waits for them, and re-layouts: 23.6 us -> 0.63 us
    all_gather x1 -> x2, blocking collectives: 9.85 us -> 24.6 us  [the longest x1 15.8 us: local(): inner = lax.all_gather(inner, 'tp', axis=0, tiled=True)]
    all_to_all x1 -> x3, starting transfers between devices: 4.58 us -> 16.9 us  [the longest x1 9.81 us: local(): lax.all_to_all(latent_out, ('dp', 'tp'), split_axis=1, concat_axis=0, til...]
  transfers between devices with their start and end apart: 4 -> 6, of which waited for: 4 -> 3; matrix products, arithmetic and copies ran while one was open for 0% -> 6% of each run, Pallas kernels for 0% -> 6%
where the time goes in v1:
time: 175 us
  blocking collectives  81.6 us (47%)
  waiting for transfers between devices  30.7 us (18%)
  starting transfers between devices  23 us (13%)
  matrix products  20 us (11%)
  Pallas kernels  10.3 us (6%)
  local copies, waits for them, and re-layouts  7.79 us (4%)
    all_to_all x1, blocking collectives, scatter_sum(): lax.all_to_all(pieces, axis, split_axis=0, concat_axis=0, tiled=True)  32.5 us
    all_to_all x2, waiting for transfers between devices, scatter_sum(): lax.all_to_all(pieces, axis, split_axis=0, concat_axis=0, tiled=True)  17.9 us
    all_gather x1, blocking collectives, local(): group_values = lax.all_gather(flat_values, 'tp', axis=1, tiled=True)  16 us
    all_gather x1, blocking collectives, local(): inner = lax.all_gather(inner, 'tp', axis=0, tiled=True)  15.8 us
    all_to_all x1, waiting for transfers between devices, local(): lax.all_to_all(latent_out, ('dp', 'tp'), split_axis=1, concat_axis=0, til...  12.8 us
    pallas_call x1, Pallas kernels, attend(): pl.pallas_call(attention_kernel, out_shape=jax.ShapeDtypeStruct((nreq, he...  10.3 us
    all_to_all x1, starting transfers between devices, local(): lax.all_to_all(latent_out, ('dp', 'tp'), split_axis=1, concat_axis=0, til...  9.81 us
    all_gather x1, blocking collectives, local(): piece = lax.all_gather(hidden, 'dp', axis=0, tiled=True).astype(jnp.float32)  8.78 us
  transfers between devices with their start and end apart: 6, of which 3 were waited for; matrix products, arithmetic and copies ran while one was open for 6% of the time, Pallas kernels for 6%

profile of v1, /device:TPU:0, one launch (start us, length us, event | category | flops | bytes accessed | tf_op | source)
XLA Modules:
  0.0 175.2 jit_solution(3005989309786342792)
XLA Ops:
  0.0 0.8 dynamic-slice_bitcast_fusion
  0.8 5.1 %collective-permute-start.2 = (bf16[4,1792]{1,0:T(4,128)(2,1)S(1)}, bf16[4,1792]{1,0:T(4,128)(2,1)S(1)}, u32[]{:S(2)}, u32[]{:S(2)}) collective-permute-start(bf16[4,1792]{1,0:T(4,128)(2,1)S(1)} %get-tuple-element.5), channel_id=1, source_target_pairs={{0,3},{1,0},{2,1},{3,2},{4,7},{5,4},{6,5},{7,6},{8,11},{9,8},{10,9... | collective-permute-start | bytes 43016 | tf_op jit(solution)/shard_map/ppermute | solution.py:169
  5.9 1.0 collective-permute-start
  6.9 1.7 reshape.96.q_ref
  8.7 0.7 dynamic_slice.23.lens_ref
  9.4 10.3 %attention.1 = bf16[4,128,512]{2,1,0:T(8,128)(2,1)S(1)} custom-call(s32[4]{0:T(128)S(1)} %dynamic_slice.23.lens_ref, bf16[4,128,576]{2,1,0:T(8,128)(2,1)S(1)} %reshape.96.q_ref, bf16[576,14336]{1,0:T(8,128)(2,1)} %bitcast.43), custom_call_target="tpu_custom_call" | custom-call | flops 3992977408 | bytes 16515072 | tf_op jit(solution)/shard_map/attention/pallas_call | solution.py:127
  19.8 1.2 copy.39
  21.0 9.8 %all-to-all-start = ((bf16[4,128,512]{2,0,1:T(4,128)(2,1)}), bf16[4,128,512]{2,0,1:T(4,128)(2,1)S(1)}, u32[]{:S(2)}, u32[]{:S(2)}) async-start(bf16[4,128,512]{2,0,1:T(4,128)(2,1)} %copy.39), calls=%async_computation | async-start | bytes 1048576 | tf_op jit(solution)/shard_map/all_to_all | solution.py:203
  31.5 0.8 dynamic-slice_convert_fusion
  32.4 12.8 %all-to-all-done = bf16[4,128,512]{2,0,1:T(4,128)(2,1)S(1)} async-done(((bf16[4,128,512]{2,0,1:T(4,128)(2,1)}), bf16[4,128,512]{2,0,1:T(4,128)(2,1)S(1)}, u32[]{:S(2)}, u32[]{:S(2)}) %all-to-all-start) | async-done | bytes 524320 | tf_op jit(solution)/shard_map/all_to_all | solution.py:203
  45.8 16.0 %all_gather.9 = bf16[128,2048]{0,1:T(8,128)(2,1)S(1)} all-gather(bf16[128,512]{0,1:T(8,128)(2,1)S(1)} %bitcast.48), channel_id=1, replica_groups=mesh['dp'=8,'tp'=4] {'tp'}, dimensions={1}, use_global_device_ids=true | all-gather | bytes 655360 | tf_op jit(solution)/shard_map/all_gather | solution.py:207
  61.9 5.0 %convolution_convert_fusion.3 = bf16[128,1792]{1,0:T(8,128)(2,1)} fusion(bf16[128,2048]{0,1:T(8,128)(2,1)S(1)} %all_gather.9, bf16[2048,1792]{1,0:T(8,128)(2,1)} %param.15), kind=kOutput, calls=%fused_computation.4 | convolution fusion | flops 939753472 | bytes 8323072 | tf_op jit(solution)/shard_map/dot_general | solution.py:208
  66.9 3.6 %all-to-all-start.1 = ((bf16[8,16,1792]{2,1,0:T(8,128)(2,1)}), bf16[8,16,1792]{2,1,0:T(8,128)(2,1)S(1)}, u32[]{:S(2)}, u32[]{:S(2)}) async-start(bf16[8,16,1792]{2,1,0:T(8,128)(2,1)} %bitcast.16), calls=%async_computation.1 | async-start | bytes 917504 | tf_op jit(solution)/shard_map/all_to_all | solution.py:177
  70.5 9.0 %all-to-all-done.1 = bf16[8,16,1792]{2,1,0:T(8,128)(2,1)S(1)} async-done(((bf16[8,16,1792]{2,1,0:T(8,128)(2,1)}), bf16[8,16,1792]{2,1,0:T(8,128)(2,1)S(1)}, u32[]{:S(2)}, u32[]{:S(2)}) %all-to-all-start.1) | async-done | bytes 458784 | tf_op jit(solution)/shard_map/all_to_all | solution.py:177
  79.6 8.8 %all_gather.10 = bf16[128,1792]{1,0:T(8,128)(2,1)S(1)} all-gather(bf16[16,1792]{1,0:T(8,128)(2,1)S(1)} %add_convert_fusion.1), channel_id=1, replica_groups=mesh['dp'=8,'tp'=4] {'dp'}, dimensions={0}, use_global_device_ids=true | all-gather | bytes 516096 | tf_op jit(solution)/shard_map/all_gather | solution.py:212
  89.0 4.6 %convolution_convert_fusion = bf16[128,2304]{1,0:T(8,128)(2,1)S(1)} fusion(bf16[1792,2304]{1,0:T(8,128)(2,1)} %param.18, bf16[128,1792]{1,0:T(8,128)(2,1)S(1)} %all_gather.10, f32[1792]{0:T(1024)S(1)} %dynamic-slice_convert_fusion), kind=kOutput, calls=%fused_computation | convolution fusion | flops 1057947648 | bytes 9313280 | tf_op jit(solution)/shard_map/dot_general | solution.py:216
  93.7 4.6 %convolution_convert_fusion.1 = bf16[128,2304]{1,0:T(8,128)(2,1)S(1)} fusion(bf16[1792,2304]{1,0:T(8,128)(2,1)} %param.17, bf16[128,1792]{1,0:T(8,128)(2,1)S(1)} %all_gather.10, f32[1792]{0:T(1024)S(1)} %dynamic-slice_convert_fusion), kind=kOutput, calls=%fused_computation.1 | convolution fusion | flops 1057947648 | bytes 9313280 | tf_op jit(solution)/shard_map/dot_general | solution.py:215
  98.3 1.0 concatenate.10
  99.3 32.5 %all_to_all.49 = bf16[4,32,4736]{2,1,0:T(8,128)(2,1)S(1)} all-to-all(bf16[4,32,4736]{2,1,0:T(8,128)(2,1)S(1)} %concatenate.10), channel_id=1, replica_groups=mesh['dp'=8,'tp'=4] {'tp'}, dimensions={0} | all-to-all | bytes 2424832 | tf_op jit(solution)/shard_map/all_to_all | solution.py:177
  132.3 15.8 %all_gather.11 = bf16[128,2304]{1,0:T(8,128)(2,1)S(1)} all-gather(bf16[32,2304]{1,0:T(8,128)(2,1)S(1)} %fusion.5), channel_id=1, replica_groups=mesh['dp'=8,'tp'=4] {'tp'}, dimensions={0}, use_global_device_ids=true | all-gather | bytes 737280 | tf_op jit(solution)/shard_map/all_gather | solution.py:230
  148.1 5.4 %convolution_convert_fusion.2 = bf16[128,1792]{1,0:T(8,128)(2,1)} fusion(bf16[128,2304]{1,0:T(8,128)(2,1)S(1)} %all_gather.11, bf16[2304,1792]{1,0:T(8,128)(2,1)} %param.19), kind=kOutput, calls=%fused_computation.3 | convolution fusion | flops 1057193984 | bytes 9306112 | tf_op jit(solution)/shard_map/dot_general | solution.py:231
  153.5 3.5 %all-to-all-start.3 = ((bf16[8,16,1792]{2,1,0:T(8,128)(2,1)}), bf16[8,16,1792]{2,1,0:T(8,128)(2,1)S(1)}, u32[]{:S(2)}, u32[]{:S(2)}) async-start(bf16[8,16,1792]{2,1,0:T(8,128)(2,1)} %bitcast.19), calls=%async_computation.3 | async-start | bytes 917504 | tf_op jit(solution)/shard_map/all_to_all | solution.py:177
  157.0 8.9 %all-to-all-done.3 = bf16[8,16,1792]{2,1,0:T(8,128)(2,1)S(1)} async-done(((bf16[8,16,1792]{2,1,0:T(8,128)(2,1)}), bf16[8,16,1792]{2,1,0:T(8,128)(2,1)S(1)}, u32[]{:S(2)}, u32[]{:S(2)}) %all-to-all-start.3) | async-done | bytes 458784 | tf_op jit(solution)/shard_map/all_to_all | solution.py:177
  166.1 8.5 %all_to_all.50 = bf16[4,4,1792]{2,1,0:T(4,128)(2,1)S(1)} all-to-all(bf16[4,4,1792]{2,1,0:T(4,128)(2,1)S(1)} %add_convert_fusion), channel_id=1, replica_groups=mesh['dp'=8,'tp'=4] {'tp'}, dimensions={0} | all-to-all | bytes 114688 | tf_op jit(solution)/shard_map/all_to_all | solution.py:234
  (33 shorter events, 3.5 us)
Async XLA Ops:
  0.0 45.5 %copy-start = (bf16[4,512,128]{2,1,0:T(8,128)(2,1)S(1)}, bf16[4,512,128]{2,1,0:T(8,128)(2,1)}, u32[]{:S(2)}) copy-start(bf16[4,512,128]{2,1,0:T(8,128)(2,1)} %param.14) | copy-start | bytes 1572868
  0.8 69.7 %collective-permute-start.2 = (bf16[4,1792]{1,0:T(4,128)(2,1)S(1)}, bf16[4,1792]{1,0:T(4,128)(2,1)S(1)}, u32[]{:S(2)}, u32[]{:S(2)}) collective-permute-start(bf16[4,1792]{1,0:T(4,128)(2,1)S(1)} %get-tuple-element.5), channel_id=1, source_target_pairs={{0,3},{1,0},{2,1},{3,2},{4,7},{5,4},{6,5},{7,6},{8,11},{9,8},{10,9... | collective-permute-start | bytes 43016 | tf_op jit(solution)/shard_map/ppermute | solution.py:169
  5.9 26.4 %collective-permute-start.1 = (bf16[4,1792]{1,0:T(4,128)(2,1)S(1)}, bf16[4,1792]{1,0:T(4,128)(2,1)S(1)}, u32[]{:S(2)}, u32[]{:S(2)}) collective-permute-start(bf16[4,1792]{1,0:T(4,128)(2,1)S(1)} %get-tuple-element.6), channel_id=1, source_target_pairs={{0,2},{1,3},{2,0},{3,1},{4,6},{5,7},{6,4},{7,5},{8,10},{9,11},{10,... | collective-permute-start | bytes 43016 | tf_op jit(solution)/shard_map/ppermute | solution.py:169
  5.9 26.4 %collective-permute-start = (bf16[4,1792]{1,0:T(4,128)(2,1)S(1)}, bf16[4,1792]{1,0:T(4,128)(2,1)S(1)}, u32[]{:S(2)}, u32[]{:S(2)}) collective-permute-start(bf16[4,1792]{1,0:T(4,128)(2,1)S(1)} %get-tuple-element.7), channel_id=1, source_target_pairs={{0,1},{1,2},{2,3},{3,0},{4,5},{5,6},{6,7},{7,4},{8,9},{9,10},{10,1... | collective-permute-start | bytes 43016 | tf_op jit(solution)/shard_map/ppermute | solution.py:169
  21.0 24.2 %all-to-all-start = ((bf16[4,128,512]{2,0,1:T(4,128)(2,1)}), bf16[4,128,512]{2,0,1:T(4,128)(2,1)S(1)}, u32[]{:S(2)}, u32[]{:S(2)}) async-start(bf16[4,128,512]{2,0,1:T(4,128)(2,1)} %copy.39), calls=%async_computation | async-start | bytes 1048576 | tf_op jit(solution)/shard_map/all_to_all | solution.py:203
  66.9 12.7 %all-to-all-start.1 = ((bf16[8,16,1792]{2,1,0:T(8,128)(2,1)}), bf16[8,16,1792]{2,1,0:T(8,128)(2,1)S(1)}, u32[]{:S(2)}, u32[]{:S(2)}) async-start(bf16[8,16,1792]{2,1,0:T(8,128)(2,1)} %bitcast.16), calls=%async_computation.1 | async-start | bytes 917504 | tf_op jit(solution)/shard_map/all_to_all | solution.py:177
  153.5 12.5 %all-to-all-start.3 = ((bf16[8,16,1792]{2,1,0:T(8,128)(2,1)}), bf16[8,16,1792]{2,1,0:T(8,128)(2,1)S(1)}, u32[]{:S(2)}, u32[]{:S(2)}) async-start(bf16[8,16,1792]{2,1,0:T(8,128)(2,1)} %bitcast.19), calls=%async_computation.3 | async-start | bytes 917504 | tf_op jit(solution)/shard_map/all_to_all | solution.py:177

commit v2 on v1

--- a/solution.py
+++ b/solution.py
@@ -1,5 +1,3 @@
-import functools
-
 import jax
 import jax.numpy as jnp
 from jax import lax
@@ -10,6 +8,7 @@
 C = 512
 BLOCK_TOKENS = 64
 TILE = 1024
+CHUNKS = 2
 VMEM_BYTES = 48 * 1024 * 1024
 
 score_scale = 192.0 ** (-0.5)
@@ -25,10 +24,11 @@
     tile = held.shape[2]
     heads = q_ref.shape[1]
 
+    rank = lax.axis_index("dp") * lax.axis_size("tp") + lax.axis_index("tp")
     begin = jnp.int32(0)
     pairs = jnp.int32(0)
     for r in range(nreq):
-        length = lens_ref[r]
+        length = lens_ref[rank * nreq + r]
         lo[r] = begin
         hi[r] = begin + length
         first[r] = begin // tile
@@ -119,7 +119,7 @@
     lax.fori_loop(0, (pairs + 1) // 2, step, (jnp.int32(0), jnp.int32(0), pairs > 0))
 
 
-def attend(own_lens, queries, cache_t):
+def attend(lengths, queries, cache_t):
     nreq, heads, width = queries.shape
     tokens = cache_t.shape[1]
     tile = TILE
@@ -153,22 +153,38 @@
             transcendentals=heads * tokens,
         ),
         name="attention",
-    )(own_lens, queries, cache_t)
-
-
-def exchange_columns(rows, axis):
+    )(lengths, queries, cache_t)
+
+
+def dynamic_piece(pieces, at):
+    return lax.dynamic_index_in_dim(pieces, at, 0, keepdims=False)
+
+
+def exchange(pieces, axis):
     size = lax.axis_size(axis)
     me = lax.axis_index(axis)
-    width = rows.shape[1] // size
-    slices = rows.reshape(rows.shape[0], size, width)
-    out = jnp.zeros((size, rows.shape[0], width), rows.dtype)
-    own = lax.dynamic_index_in_dim(slices, me, 1, keepdims=False)
-    out = lax.dynamic_update_index_in_dim(out, own, me, 0)
+    got = [dynamic_piece(pieces, me)]
     for shift in range(1, size):
-        piece = lax.dynamic_index_in_dim(slices, (me + shift) % size, 1, keepdims=False)
-        got = lax.ppermute(piece, axis, [(k, (k + shift) % size) for k in range(size)])
-        out = lax.dynamic_update_index_in_dim(out, got, (me - shift) % size, 0)
+        piece = dynamic_piece(pieces, (me + shift) % size)
+        got.append(lax.ppermute(piece, axis, [(k, (k + shift) % size) for k in range(size)]))
+    return got
+
+
+def ordered(got, axis):
+    size = lax.axis_size(axis)
+    me = lax.axis_index(axis)
+    out = jnp.zeros((size,) + got[0].shape, got[0].dtype)
+    for shift, piece in enumerate(got):
+        out = lax.dynamic_update_index_in_dim(out, piece, (me - shift) % size, 0)
     return out
+
+
+def gather(piece, axis):
+    size = lax.axis_size(axis)
+    return [piece] + [
+        lax.ppermute(piece, axis, [(k, (k + shift) % size) for k in range(size)])
+        for shift in range(1, size)
+    ]
 
 
 def scatter_sum(part, axis):
@@ -183,7 +199,6 @@
 ):
     ranks_dp = lax.axis_size("dp")
     ranks_tp = lax.axis_size("tp")
-    me_dp = lax.axis_index("dp")
     me_tp = lax.axis_index("tp")
     per_rank, model = residual.shape
     row_length = paged_latent_cache.shape[1]
@@ -191,47 +206,70 @@
     heads_here = w_uv.shape[0]
     units = w_gate.shape[1]
     width = w_o.shape[1]
-    rank = me_dp * ranks_tp + me_tp
-
-    residual_slice = exchange_columns(residual, "tp").reshape(ranks_tp * per_rank, width)
-    gain_slice = lax.dynamic_slice_in_dim(norm_gain, me_tp * width, width, 0)
-
-    own_lens = lax.dynamic_slice_in_dim(lengths, rank * per_rank, per_rank, 0)
+
     query = queries.reshape(per_rank, heads_all, row_length)
-    latent_out = attend(own_lens, query, paged_latent_cache.T)
+    latent_out = attend(lengths, query, paged_latent_cache.T)
 
     local_heads = lax.all_to_all(latent_out, ("dp", "tp"), split_axis=1, concat_axis=0, tiled=True)
+    local_heads, residual = lax.optimization_barrier((local_heads, residual))
     head_values = jnp.einsum("rhc,hcv->rhv", local_heads, w_uv, preferred_element_type=jnp.float32)
     head_values = head_values.astype(jnp.bfloat16)
     flat_values = head_values.reshape(head_values.shape[0], heads_here * w_uv.shape[2])
-    group_values = lax.all_gather(flat_values, "tp", axis=1, tiled=True)
-    attn_part = jnp.dot(group_values, w_o, preferred_element_type=jnp.float32).astype(jnp.bfloat16)
-    attn = scatter_sum(attn_part, "dp")
+    depth = flat_values.shape[1]
+    attn_part = None
+    for shift, values in enumerate(gather(flat_values, "tp")):
+        rows = lax.dynamic_slice_in_dim(w_o, ((me_tp - shift) % ranks_tp) * depth, depth, 0)
+        term = jnp.dot(values, rows, preferred_element_type=jnp.float32)
+        attn_part = term if attn_part is None else attn_part + term
+    residual_pieces = residual.reshape(per_rank, ranks_tp, width).transpose(1, 0, 2)
+    residual_slice = ordered(exchange(residual_pieces, "tp"), "tp").reshape(-1, width)
+    attn = scatter_sum(attn_part.astype(jnp.bfloat16), "dp")
 
     hidden = (residual_slice.astype(jnp.float32) + attn).astype(jnp.bfloat16)
+    hidden_got = exchange(hidden.reshape(ranks_tp, per_rank, width), "tp")
+    gain_slice = lax.dynamic_slice_in_dim(norm_gain, me_tp * width, width, 0)
     piece = lax.all_gather(hidden, "dp", axis=0, tiled=True).astype(jnp.float32)
     square = jnp.sum(piece * piece, 1, keepdims=True)
     scaled = (piece * gain_slice.astype(jnp.float32)).astype(jnp.bfloat16)
-    gate_part = jnp.dot(scaled, w_gate, preferred_element_type=jnp.float32).astype(jnp.bfloat16)
-    up_part = jnp.dot(scaled, w_up, preferred_element_type=jnp.float32).astype(jnp.bfloat16)
     top = square.astype(jnp.bfloat16)
     rest = square - top.astype(jnp.float32)
     middle = rest.astype(jnp.bfloat16)
     low = (rest - middle.astype(jnp.float32)).astype(jnp.bfloat16)
-    extra = jnp.concatenate(
-        [top, middle, low, jnp.zeros((top.shape[0], 125), jnp.bfloat16)], 1
+    extra = jnp.concatenate([top, middle, low, jnp.zeros((top.shape[0], 125), jnp.bfloat16)], 1)
+
+    chunk = units // CHUNKS
+    factor = None
+    sums = []
+    for c in range(CHUNKS):
+        columns = slice(c * chunk, (c + 1) * chunk)
+        parts = [
+            jnp.dot(scaled, w[:, columns], preferred_element_type=jnp.float32).astype(jnp.bfloat16)
+            for w in (w_gate, w_up)
+        ]
+        if c == 0:
+            parts.append(extra)
+        both = jnp.concatenate(parts, 1).reshape(ranks_tp, -1, 2 * chunk + 128 * (c == 0))
+        sums.append(sum(got.astype(jnp.float32) for got in exchange(both, "tp")))
+    ffn_part = None
+    for c, both in enumerate(sums):
+        if c == 0:
+            mean = jnp.sum(both[:, 2 * chunk :], 1, keepdims=True) / model
+            factor = lax.rsqrt(mean + 1e-06)
+        gate = both[:, :chunk] * factor
+        up = both[:, chunk : 2 * chunk] * factor
+        inner = (jax.nn.silu(gate) * up).astype(jnp.bfloat16)
+        inner = ordered(gather(inner, "tp"), "tp").reshape(-1, chunk)
+        term = jnp.dot(
+            inner, w_down[c * chunk : (c + 1) * chunk], preferred_element_type=jnp.float32
+        )
+        ffn_part = term if ffn_part is None else ffn_part + term
+    ffn_pieces = ffn_part.astype(jnp.bfloat16).reshape(ranks_dp * ranks_tp, per_rank, width)
+    ffn_pieces = lax.all_to_all(
+        ffn_pieces, ("dp", "tp"), split_axis=0, concat_axis=0, tiled=True
     )
-    both = scatter_sum(jnp.concatenate([gate_part, up_part, extra], 1), "tp")
-    mean = jnp.sum(both[:, 2 * units :], 1, keepdims=True) / model
-    factor = lax.rsqrt(mean + 1e-06)
-    gate = both[:, :units] * factor
-    up = both[:, units : 2 * units] * factor
-    inner = (jax.nn.silu(gate) * up).astype(jnp.bfloat16)
-    inner = lax.all_gather(inner, "tp", axis=0, tiled=True)
-    ffn_part = jnp.dot(inner, w_down, preferred_element_type=jnp.float32).astype(jnp.bfloat16)
-    ffn = scatter_sum(ffn_part, "dp")
-    layer = (hidden.astype(jnp.float32) + ffn).astype(jnp.bfloat16)
-    return lax.all_to_all(layer, "tp", split_axis=0, concat_axis=1, tiled=True)
+    ffn = jnp.sum(ffn_pieces.astype(jnp.float32).reshape(ranks_dp, ranks_tp, per_rank, width), 0)
+    layer = ordered(hidden_got, "tp").astype(jnp.float32) + ffn
+    return layer.astype(jnp.bfloat16).transpose(1, 0, 2).reshape(per_rank, model)
 
 
 def solution(mesh):

time: 175 us -> 169 us (0.966)
  blocking collectives: 81.6 us -> 8.76 us
  waiting for transfers between devices: 30.7 us -> 63.9 us
  starting transfers between devices: 23 us -> 55.5 us
  matrix products: 20 us -> 21.8 us
    all_to_all x2 -> x0, blocking collectives: 41 us -> none  [the longest x1 32.5 us: scatter_sum(): lax.all_to_all(pieces, axis, split_axis=0, concat_axis=0, tiled=True)]
    all_gather x2 -> x0, blocking collectives: 31.8 us -> none  [the longest x1 16 us: local(): group_values = lax.all_gather(flat_values, 'tp', axis=1, tiled=True)]
    ppermute x3 -> x21, starting transfers between devices: 6.11 us -> 35.1 us  [the longest x12 24.5 us: exchange(): lax.ppermute(piece, axis, [(k, (k + shift) % size) for k in range(size)])]
    ppermute x3 -> x21, waiting for transfers between devices: 0.01 us -> 28.5 us  [the longest x12 18 us: exchange(): lax.ppermute(piece, axis, [(k, (k + shift) % size) for k in range(size)])]
    all_to_all x0 -> x1, waiting for transfers between devices: none -> 13 us  [local(): lax.all_to_all(ffn_pieces, ('dp', 'tp'), split_axis=0, concat_axis=0, til...]
    all_to_all x2 -> x1, waiting for transfers between devices: 17.9 us -> 8.92 us  [scatter_sum(): lax.all_to_all(pieces, axis, split_axis=0, concat_axis=0, tiled=True)]
    all_to_all x0 -> x1, starting transfers between devices: none -> 3.79 us  [local(): lax.all_to_all(ffn_pieces, ('dp', 'tp'), split_axis=0, concat_axis=0, til...]
    all_to_all x2 -> x1, starting transfers between devices: 7.08 us -> 3.47 us  [scatter_sum(): lax.all_to_all(pieces, axis, split_axis=0, concat_axis=0, tiled=True)]
  transfers between devices with their start and end apart: 6 -> 24, of which waited for: 3 -> 14; matrix products, arithmetic and copies ran while one was open for 6% -> 9% of each run, Pallas kernels for 6% -> 0%
where the time goes in v2:
time: 169 us; the launch traced here: 168 us
  waiting for transfers between devices  63.9 us (38%)
  starting transfers between devices  55.5 us (33%)
  matrix products  21.8 us (13%)
  Pallas kernels  9.04 us (5%)
  blocking collectives  8.76 us (5%)
  local copies, waits for them, and re-layouts  6.14 us (4%)
  other arithmetic  2.53 us (1%)
    ppermute x12, starting transfers between devices, exchange(): lax.ppermute(piece, axis, [(k, (k + shift) % size) for k in range(size)])  24.5 us
    ppermute x12, waiting for transfers between devices, exchange(): lax.ppermute(piece, axis, [(k, (k + shift) % size) for k in range(size)])  18 us
    all_to_all x1, waiting for transfers between devices, local(): lax.all_to_all(latent_out, ('dp', 'tp'), split_axis=1, concat_axis=0, til...  13.5 us
    all_to_all x1, starting transfers between devices, local(): lax.all_to_all(latent_out, ('dp', 'tp'), split_axis=1, concat_axis=0, til...  13.2 us
    all_to_all x1, waiting for transfers between devices, local(): lax.all_to_all(ffn_pieces, ('dp', 'tp'), split_axis=0, concat_axis=0, til...  13 us
    ppermute x9, starting transfers between devices, gather(): lax.ppermute(piece, axis, [(k, (k + shift) % size) for k in range(size)])  10.6 us
    ppermute x9, waiting for transfers between devices, gather(): lax.ppermute(piece, axis, [(k, (k + shift) % size) for k in range(size)])  10.5 us
    dot_general x4, matrix products, local(): jnp.dot(scaled, w[:, columns], preferred_element_type=jnp.float32)  9.93 us
  transfers between devices with their start and end apart: 24, of which 14 were waited for; matrix products, arithmetic and copies ran while one was open for 9% of the time, Pallas kernels for 0%

profile of v2, /device:TPU:0, one launch (start us, length us, event | category | flops | bytes accessed | tf_op | source)
XLA Modules:
  0.0 168.2 jit_solution(9286549582925405539)
XLA Ops:
  2.5 9.0 %attention.1 = bf16[4,128,512]{2,1,0:T(8,128)(2,1)S(1)} custom-call(s32[128]{0:T(128)S(1)} %copy-done.2, bf16[4,128,576]{2,1,0:T(8,128)(2,1)S(1)} %reshape.120.q_ref, bf16[576,14336]{1,0:T(8,128)(2,1)} %bitcast.92), custom_call_target="tpu_custom_call" | custom-call | flops 3992977408 | bytes 16515072 | tf_op jit(solution)/shard_map/attention/pallas_call | solution.py:127
  12.7 13.2 %all-to-all-start = ((bf16[4,128,512]{2,0,1:T(4,128)(2,1)}), bf16[4,128,512]{2,0,1:T(4,128)(2,1)S(1)}, u32[]{:S(2)}, u32[]{:S(2)}) async-start(bf16[4,128,512]{2,0,1:T(4,128)(2,1)} %copy.25), calls=%async_computation | async-start | bytes 1048576 | tf_op jit(solution)/shard_map/all_to_all | solution.py:213
  26.8 13.5 %all-to-all-done = bf16[4,128,512]{2,0,1:T(4,128)(2,1)S(1)} async-done(((bf16[4,128,512]{2,0,1:T(4,128)(2,1)}), bf16[4,128,512]{2,0,1:T(4,128)(2,1)S(1)}, u32[]{:S(2)}, u32[]{:S(2)}) %all-to-all-start) | async-done | bytes 524320 | tf_op jit(solution)/shard_map/all_to_all | solution.py:213
  41.0 2.6 %collective-permute-start.3 = (bf16[128,512]{0,1:T(8,128)(2,1)S(1)}, bf16[128,512]{0,1:T(8,128)(2,1)S(1)}, u32[]{:S(2)}, u32[]{:S(2)}) collective-permute-start(bf16[128,512]{0,1:T(8,128)(2,1)S(1)} %bitcast.97), channel_id=1, source_target_pairs={{0,1},{1,2},{2,3},{3,0},{4,5},{5,6},{6,7},{7,4},{8,9},{9,10},{10,1... | collective-permute-start | bytes 393224 | tf_op jit(solution)/shard_map/ppermute | solution.py:185
  50.6 4.5 %collective-permute-done = bf16[4,1792]{1,0:T(4,128)(2,1)S(1)} collective-permute-done((bf16[4,1792]{1,0:T(4,128)(2,1)S(1)}, bf16[4,1792]{1,0:T(4,128)(2,1)S(1)}, u32[]{:S(2)}, u32[]{:S(2)}) %collective-permute-start) | collective-permute-done | bytes 14368 | tf_op jit(solution)/shard_map/ppermute | solution.py:169
  55.1 2.8 %collective-permute-done.1 = bf16[4,1792]{1,0:T(4,128)(2,1)S(1)} collective-permute-done((bf16[4,1792]{1,0:T(4,128)(2,1)S(1)}, bf16[4,1792]{1,0:T(4,128)(2,1)S(1)}, u32[]{:S(2)}, u32[]{:S(2)}) %collective-permute-start.1) | collective-permute-done | bytes 14368 | tf_op jit(solution)/shard_map/ppermute | solution.py:169
  61.5 3.5 %all-to-all-start.1 = ((bf16[8,16,1792]{2,1,0:T(8,128)(2,1)}), bf16[8,16,1792]{2,1,0:T(8,128)(2,1)S(1)}, u32[]{:S(2)}, u32[]{:S(2)}) async-start(bf16[8,16,1792]{2,1,0:T(8,128)(2,1)} %bitcast.17), calls=%async_computation.1 | async-start | bytes 917504 | tf_op jit(solution)/shard_map/all_to_all | solution.py:193
  65.1 8.9 %all-to-all-done.1 = bf16[8,16,1792]{2,1,0:T(8,128)(2,1)S(1)} async-done(((bf16[8,16,1792]{2,1,0:T(8,128)(2,1)}), bf16[8,16,1792]{2,1,0:T(8,128)(2,1)S(1)}, u32[]{:S(2)}, u32[]{:S(2)}) %all-to-all-start.1) | async-done | bytes 458784 | tf_op jit(solution)/shard_map/all_to_all | solution.py:193
  74.1 8.8 %all_gather.3 = bf16[128,1792]{1,0:T(8,128)(2,1)S(1)} all-gather(bf16[16,1792]{1,0:T(8,128)(2,1)S(1)} %add_convert_fusion.1), channel_id=1, replica_groups=mesh['dp'=8,'tp'=4] {'dp'}, dimensions={0}, use_global_device_ids=true | all-gather | bytes 516096 | tf_op jit(solution)/shard_map/all_gather | solution.py:231
  83.1 3.1 %fusion.17 = bf16[128,1152]{1,0:T(8,128)(2,1)S(1)} fusion(bf16[1792,2304]{1,0:T(8,128)(2,1)} %param.17, bf16[128,1792]{1,0:T(8,128)(2,1)S(1)} %all_gather.3, f32[1792]{0:T(1024)S(1)} %dynamic-slice_convert_fusion), kind=kOutput, calls=%fused_computation.17 | convolution fusion | flops 529317888 | bytes 4889600 | tf_op jit(solution)/shard_map/dot_general | solution.py:246
  86.2 3.1 %fusion.23 = bf16[128,1152]{1,0:T(8,128)(2,1)S(1)} fusion(bf16[1792,2304]{1,0:T(8,128)(2,1)} %param.17, bf16[128,1792]{1,0:T(8,128)(2,1)S(1)} %all_gather.3, f32[1792]{0:T(1024)S(1)} %dynamic-slice_convert_fusion), kind=kOutput, calls=%fused_computation.19 | convolution fusion | flops 529317888 | bytes 4889600 | tf_op jit(solution)/shard_map/dot_general | solution.py:246
  89.3 3.0 %fusion.20 = bf16[128,1152]{1,0:T(8,128)(2,1)S(1)} fusion(bf16[1792,2304]{1,0:T(8,128)(2,1)} %param.18, bf16[128,1792]{1,0:T(8,128)(2,1)S(1)} %all_gather.3, f32[1792]{0:T(1024)S(1)} %dynamic-slice_convert_fusion), kind=kOutput, calls=%fused_computation.18 | convolution fusion | flops 529317888 | bytes 4889600 | tf_op jit(solution)/shard_map/dot_general | solution.py:246
  100.1 2.8 %collective-permute-start.17 = (bf16[32,2304]{1,0:T(8,128)(2,1)S(1)}, bf16[32,2304]{1,0:T(8,128)(2,1)S(1)}, u32[]{:S(2)}, u32[]{:S(2)}) collective-permute-start(bf16[32,2304]{1,0:T(8,128)(2,1)S(1)} %get-tuple-element.17), channel_id=1, source_target_pairs={{0,3},{1,0},{2,1},{3,2},{4,7},{5,4},{6,5},{7,6},{8,11},{9,8},{10,9... | collective-permute-start | bytes 442376 | tf_op jit(solution)/shard_map/ppermute | solution.py:169
  103.0 3.7 %collective-permute-done.15 = bf16[32,2304]{1,0:T(8,128)(2,1)S(1)} collective-permute-done((bf16[32,2304]{1,0:T(8,128)(2,1)S(1)}, bf16[32,2304]{1,0:T(8,128)(2,1)S(1)}, u32[]{:S(2)}, u32[]{:S(2)}) %collective-permute-start.15) | collective-permute-done | bytes 147488 | tf_op jit(solution)/shard_map/ppermute | solution.py:169
  106.7 8.0 %collective-permute-start.10 = (bf16[32,2432]{1,0:T(8,128)(2,1)S(1)}, bf16[32,2432]{1,0:T(8,128)(2,1)S(1)}, u32[]{:S(2)}, u32[]{:S(2)}) collective-permute-start(bf16[32,2432]{1,0:T(8,128)(2,1)S(1)} %get-tuple-element.15), channel_id=1, source_target_pairs={{0,2},{1,3},{2,0},{3,1},{4,6},{5,7},{6,4},{7,5},{8,10},{9,11},{10,... | collective-permute-start | bytes 466952 | tf_op jit(solution)/shard_map/ppermute | solution.py:169
  114.7 4.1 %collective-permute-start.11 = (bf16[32,2432]{1,0:T(8,128)(2,1)S(1)}, bf16[32,2432]{1,0:T(8,128)(2,1)S(1)}, u32[]{:S(2)}, u32[]{:S(2)}) collective-permute-start(bf16[32,2432]{1,0:T(8,128)(2,1)S(1)} %get-tuple-element.14), channel_id=1, source_target_pairs={{0,3},{1,0},{2,1},{3,2},{4,7},{5,4},{6,5},{7,6},{8,11},{9,8},{10,9... | collective-permute-start | bytes 466952 | tf_op jit(solution)/shard_map/ppermute | solution.py:169
  118.9 4.5 %collective-permute-done.10 = bf16[32,2432]{1,0:T(8,128)(2,1)S(1)} collective-permute-done((bf16[32,2432]{1,0:T(8,128)(2,1)S(1)}, bf16[32,2432]{1,0:T(8,128)(2,1)S(1)}, u32[]{:S(2)}, u32[]{:S(2)}) %collective-permute-start.10) | collective-permute-done | bytes 155680 | tf_op jit(solution)/shard_map/ppermute | solution.py:169
  123.5 2.5 %collective-permute-done.9 = bf16[32,2432]{1,0:T(8,128)(2,1)S(1)} collective-permute-done((bf16[32,2432]{1,0:T(8,128)(2,1)S(1)}, bf16[32,2432]{1,0:T(8,128)(2,1)S(1)}, u32[]{:S(2)}, u32[]{:S(2)}) %collective-permute-start.9) | collective-permute-done | bytes 155680 | tf_op jit(solution)/shard_map/ppermute | solution.py:169
  128.6 2.8 %collective-permute-start.14 = (bf16[32,1152]{1,0:T(8,128)(2,1)S(1)}, bf16[32,1152]{1,0:T(8,128)(2,1)S(1)}, u32[]{:S(2)}, u32[]{:S(2)}) collective-permute-start(bf16[32,1152]{1,0:T(8,128)(2,1)S(1)} %get-tuple-element.10), channel_id=1, source_target_pairs={{0,3},{1,0},{2,1},{3,2},{4,7},{5,4},{6,5},{7,6},{8,11},{9,8},{10,9... | collective-permute-start | bytes 221192 | tf_op jit(solution)/shard_map/ppermute | solution.py:185
  133.3 3.8 %collective-permute-done.13 = bf16[32,1152]{1,0:T(8,128)(2,1)S(1)} collective-permute-done((bf16[32,1152]{1,0:T(8,128)(2,1)S(1)}, bf16[32,1152]{1,0:T(8,128)(2,1)S(1)}, u32[]{:S(2)}, u32[]{:S(2)}) %collective-permute-start.13) | collective-permute-done | bytes 73760 | tf_op jit(solution)/shard_map/ppermute | solution.py:185
  143.5 3.0 %fusion = f32[128,1792]{1,0:T(8,128)S(1)} fusion(bf16[128,1152]{1,0:T(8,128)(2,1)S(1)} %bitcast.101, bf16[2304,1792]{1,0:T(8,128)(2,1)} %param.19), kind=kOutput, calls=%fused_computation | convolution fusion | flops 528482304 | bytes 5341184 | tf_op jit(solution)/shard_map/dot_general | solution.py:262
  146.6 2.9 %fusion.29 = bf16[128,1792]{1,0:T(8,128)(2,1)S(1)} fusion(f32[128,1792]{1,0:T(8,128)S(1)} %fusion, bf16[128,1152]{1,0:T(8,128)(2,1)S(1)} %bitcast.102, bf16[2304,1792]{1,0:T(8,128)(2,1)} %param.19), kind=kOutput, calls=%fused_computation.21 | convolution fusion | flops 528941056 | bytes 5799936 | tf_op jit(solution)/shard_map/dot_general | solution.py:262
  150.4 3.8 %all-to-all-start.2 = ((bf16[32,4,1792]{2,1,0:T(4,128)(2,1)}), bf16[32,4,1792]{2,1,0:T(4,128)(2,1)S(1)}, u32[]{:S(2)}, u32[]{:S(2)}) async-start(bf16[32,4,1792]{2,1,0:T(4,128)(2,1)} %reshape.127), calls=%async_computation.2 | async-start | bytes 917504 | tf_op jit(solution)/shard_map/all_to_all | solution.py:267
  154.3 13.0 %all-to-all-done.2 = bf16[32,4,1792]{2,1,0:T(4,128)(2,1)S(1)} async-done(((bf16[32,4,1792]{2,1,0:T(4,128)(2,1)}), bf16[32,4,1792]{2,1,0:T(4,128)(2,1)S(1)}, u32[]{:S(2)}, u32[]{:S(2)}) %all-to-all-start.2) | async-done | bytes 458784 | tf_op jit(solution)/shard_map/all_to_all | solution.py:267
  (101 shorter events, 36.8 us)
Async XLA Ops:
  12.7 27.5 %all-to-all-start = ((bf16[4,128,512]{2,0,1:T(4,128)(2,1)}), bf16[4,128,512]{2,0,1:T(4,128)(2,1)S(1)}, u32[]{:S(2)}, u32[]{:S(2)}) async-start(bf16[4,128,512]{2,0,1:T(4,128)(2,1)} %copy.25), calls=%async_computation | async-start | bytes 1048576 | tf_op jit(solution)/shard_map/all_to_all | solution.py:213
  41.0 16.9 %collective-permute-start.3 = (bf16[128,512]{0,1:T(8,128)(2,1)S(1)}, bf16[128,512]{0,1:T(8,128)(2,1)S(1)}, u32[]{:S(2)}, u32[]{:S(2)}) collective-permute-start(bf16[128,512]{0,1:T(8,128)(2,1)S(1)} %bitcast.97), channel_id=1, source_target_pairs={{0,1},{1,2},{2,3},{3,0},{4,5},{5,6},{6,7},{7,4},{8,9},{9,10},{10,1... | collective-permute-start | bytes 393224 | tf_op jit(solution)/shard_map/ppermute | solution.py:185
  43.6 16.3 %collective-permute-start.5 = (bf16[128,512]{0,1:T(8,128)(2,1)S(1)}, bf16[128,512]{0,1:T(8,128)(2,1)S(1)}, u32[]{:S(2)}, u32[]{:S(2)}) collective-permute-start(bf16[128,512]{0,1:T(8,128)(2,1)S(1)} %bitcast.98), channel_id=1, source_target_pairs={{0,3},{1,0},{2,1},{3,2},{4,7},{5,4},{6,5},{7,6},{8,11},{9,8},{10,9... | collective-permute-start | bytes 393224 | tf_op jit(solution)/shard_map/ppermute | solution.py:185
  44.8 15.5 %collective-permute-start.4 = (bf16[128,512]{0,1:T(8,128)(2,1)S(1)}, bf16[128,512]{0,1:T(8,128)(2,1)S(1)}, u32[]{:S(2)}, u32[]{:S(2)}) collective-permute-start(bf16[128,512]{0,1:T(8,128)(2,1)S(1)} %bitcast.99), channel_id=1, source_target_pairs={{0,2},{1,3},{2,0},{3,1},{4,6},{5,7},{6,4},{7,5},{8,10},{9,11},{10,... | collective-permute-start | bytes 393224 | tf_op jit(solution)/shard_map/ppermute | solution.py:185
  45.1 9.9 %collective-permute-start = (bf16[4,1792]{1,0:T(4,128)(2,1)S(1)}, bf16[4,1792]{1,0:T(4,128)(2,1)S(1)}, u32[]{:S(2)}, u32[]{:S(2)}) collective-permute-start(bf16[4,1792]{1,0:T(4,128)(2,1)S(1)} %get-tuple-element.25), channel_id=1, source_target_pairs={{0,1},{1,2},{2,3},{3,0},{4,5},{5,6},{6,7},{7,4},{8,9},{9,10},{10,1... | collective-permute-start | bytes 43016 | tf_op jit(solution)/shard_map/ppermute | solution.py:169
  46.5 11.4 %collective-permute-start.1 = (bf16[4,1792]{1,0:T(4,128)(2,1)S(1)}, bf16[4,1792]{1,0:T(4,128)(2,1)S(1)}, u32[]{:S(2)}, u32[]{:S(2)}) collective-permute-start(bf16[4,1792]{1,0:T(4,128)(2,1)S(1)} %get-tuple-element.24), channel_id=1, source_target_pairs={{0,2},{1,3},{2,0},{3,1},{4,6},{5,7},{6,4},{7,5},{8,10},{9,11},{10,... | collective-permute-start | bytes 43016 | tf_op jit(solution)/shard_map/ppermute | solution.py:169
  55.1 10.0 %collective-permute-start.2 = (bf16[4,1792]{1,0:T(4,128)(2,1)S(1)}, bf16[4,1792]{1,0:T(4,128)(2,1)S(1)}, u32[]{:S(2)}, u32[]{:S(2)}) collective-permute-start(bf16[4,1792]{1,0:T(4,128)(2,1)S(1)} %get-tuple-element.23), channel_id=1, source_target_pairs={{0,3},{1,0},{2,1},{3,2},{4,7},{5,4},{6,5},{7,6},{8,11},{9,8},{10,9... | collective-permute-start | bytes 43016 | tf_op jit(solution)/shard_map/ppermute | solution.py:169
  61.5 12.5 %all-to-all-start.1 = ((bf16[8,16,1792]{2,1,0:T(8,128)(2,1)}), bf16[8,16,1792]{2,1,0:T(8,128)(2,1)S(1)}, u32[]{:S(2)}, u32[]{:S(2)}) async-start(bf16[8,16,1792]{2,1,0:T(8,128)(2,1)} %bitcast.17), calls=%async_computation.1 | async-start | bytes 917504 | tf_op jit(solution)/shard_map/all_to_all | solution.py:193
  93.2 7.0 %collective-permute-start.6 = (bf16[4,1792]{1,0:T(4,128)(2,1)S(1)}, bf16[4,1792]{1,0:T(4,128)(2,1)S(1)}, u32[]{:S(2)}, u32[]{:S(2)}) collective-permute-start(bf16[4,1792]{1,0:T(4,128)(2,1)S(1)} %get-tuple-element.21), channel_id=1, source_target_pairs={{0,1},{1,2},{2,3},{3,0},{4,5},{5,6},{6,7},{7,4},{8,9},{9,10},{10,1... | collective-permute-start | bytes 43016 | tf_op jit(solution)/shard_map/ppermute | solution.py:169
  93.2 61.0 %collective-permute-start.7 = (bf16[4,1792]{1,0:T(4,128)(2,1)S(1)}, bf16[4,1792]{1,0:T(4,128)(2,1)S(1)}, u32[]{:S(2)}, u32[]{:S(2)}) collective-permute-start(bf16[4,1792]{1,0:T(4,128)(2,1)S(1)} %get-tuple-element.20), channel_id=1, source_target_pairs={{0,2},{1,3},{2,0},{3,1},{4,6},{5,7},{6,4},{7,5},{8,10},{9,11},{10,... | collective-permute-start | bytes 43016 | tf_op jit(solution)/shard_map/ppermute | solution.py:169
  95.4 58.8 %collective-permute-start.8 = (bf16[4,1792]{1,0:T(4,128)(2,1)S(1)}, bf16[4,1792]{1,0:T(4,128)(2,1)S(1)}, u32[]{:S(2)}, u32[]{:S(2)}) collective-permute-start(bf16[4,1792]{1,0:T(4,128)(2,1)S(1)} %get-tuple-element.19), channel_id=1, source_target_pairs={{0,3},{1,0},{2,1},{3,2},{4,7},{5,4},{6,5},{7,6},{8,11},{9,8},{10,9... | collective-permute-start | bytes 43016 | tf_op jit(solution)/shard_map/ppermute | solution.py:169
  98.0 8.7 %collective-permute-start.15 = (bf16[32,2304]{1,0:T(8,128)(2,1)S(1)}, bf16[32,2304]{1,0:T(8,128)(2,1)S(1)}, u32[]{:S(2)}, u32[]{:S(2)}) collective-permute-start(bf16[32,2304]{1,0:T(8,128)(2,1)S(1)} %get-tuple-element.16), channel_id=1, source_target_pairs={{0,1},{1,2},{2,3},{3,0},{4,5},{5,6},{6,7},{7,4},{8,9},{9,10},{10,1... | collective-permute-start | bytes 442376 | tf_op jit(solution)/shard_map/ppermute | solution.py:169
  98.6 16.1 %collective-permute-start.16 = (bf16[32,2304]{1,0:T(8,128)(2,1)S(1)}, bf16[32,2304]{1,0:T(8,128)(2,1)S(1)}, u32[]{:S(2)}, u32[]{:S(2)}) collective-permute-start(bf16[32,2304]{1,0:T(8,128)(2,1)S(1)} %get-tuple-element.18), channel_id=1, source_target_pairs={{0,2},{1,3},{2,0},{3,1},{4,6},{5,7},{6,4},{7,5},{8,10},{9,11},{10,... | collective-permute-start | bytes 442376 | tf_op jit(solution)/shard_map/ppermute | solution.py:169
  100.1 18.6 %collective-permute-start.17 = (bf16[32,2304]{1,0:T(8,128)(2,1)S(1)}, bf16[32,2304]{1,0:T(8,128)(2,1)S(1)}, u32[]{:S(2)}, u32[]{:S(2)}) collective-permute-start(bf16[32,2304]{1,0:T(8,128)(2,1)S(1)} %get-tuple-element.17), channel_id=1, source_target_pairs={{0,3},{1,0},{2,1},{3,2},{4,7},{5,4},{6,5},{7,6},{8,11},{9,8},{10,9... | collective-permute-start | bytes 442376 | tf_op jit(solution)/shard_map/ppermute | solution.py:169
  106.7 16.7 %collective-permute-start.10 = (bf16[32,2432]{1,0:T(8,128)(2,1)S(1)}, bf16[32,2432]{1,0:T(8,128)(2,1)S(1)}, u32[]{:S(2)}, u32[]{:S(2)}) collective-permute-start(bf16[32,2432]{1,0:T(8,128)(2,1)S(1)} %get-tuple-element.15), channel_id=1, source_target_pairs={{0,2},{1,3},{2,0},{3,1},{4,6},{5,7},{6,4},{7,5},{8,10},{9,11},{10,... | collective-permute-start | bytes 466952 | tf_op jit(solution)/shard_map/ppermute | solution.py:169
  114.7 8.7 %collective-permute-start.11 = (bf16[32,2432]{1,0:T(8,128)(2,1)S(1)}, bf16[32,2432]{1,0:T(8,128)(2,1)S(1)}, u32[]{:S(2)}, u32[]{:S(2)}) collective-permute-start(bf16[32,2432]{1,0:T(8,128)(2,1)S(1)} %get-tuple-element.14), channel_id=1, source_target_pairs={{0,3},{1,0},{2,1},{3,2},{4,7},{5,4},{6,5},{7,6},{8,11},{9,8},{10,9... | collective-permute-start | bytes 466952 | tf_op jit(solution)/shard_map/ppermute | solution.py:169
  118.8 7.1 %collective-permute-start.9 = (bf16[32,2432]{1,0:T(8,128)(2,1)S(1)}, bf16[32,2432]{1,0:T(8,128)(2,1)S(1)}, u32[]{:S(2)}, u32[]{:S(2)}) collective-permute-start(bf16[32,2432]{1,0:T(8,128)(2,1)S(1)} %get-tuple-element.13), channel_id=1, source_target_pairs={{0,1},{1,2},{2,3},{3,0},{4,5},{5,6},{6,7},{7,4},{8,9},{9,10},{10,1... | collective-permute-start | bytes 466952 | tf_op jit(solution)/shard_map/ppermute | solution.py:169
  126.3 6.5 %collective-permute-start.12 = (bf16[32,1152]{1,0:T(8,128)(2,1)S(1)}, bf16[32,1152]{1,0:T(8,128)(2,1)S(1)}, u32[]{:S(2)}, u32[]{:S(2)}) collective-permute-start(bf16[32,1152]{1,0:T(8,128)(2,1)S(1)} %get-tuple-element.10), channel_id=1, source_target_pairs={{0,1},{1,2},{2,3},{3,0},{4,5},{5,6},{6,7},{7,4},{8,9},{9,10},{10,1... | collective-permute-start | bytes 221192 | tf_op jit(solution)/shard_map/ppermute | solution.py:185
  128.6 8.4 %collective-permute-start.13 = (bf16[32,1152]{1,0:T(8,128)(2,1)S(1)}, bf16[32,1152]{1,0:T(8,128)(2,1)S(1)}, u32[]{:S(2)}, u32[]{:S(2)}) collective-permute-start(bf16[32,1152]{1,0:T(8,128)(2,1)S(1)} %get-tuple-element.10), channel_id=1, source_target_pairs={{0,2},{1,3},{2,0},{3,1},{4,6},{5,7},{6,4},{7,5},{8,10},{9,11},{10,... | collective-permute-start | bytes 221192 | tf_op jit(solution)/shard_map/ppermute | solution.py:185
  128.6 17.9 %collective-permute-start.14 = (bf16[32,1152]{1,0:T(8,128)(2,1)S(1)}, bf16[32,1152]{1,0:T(8,128)(2,1)S(1)}, u32[]{:S(2)}, u32[]{:S(2)}) collective-permute-start(bf16[32,1152]{1,0:T(8,128)(2,1)S(1)} %get-tuple-element.10), channel_id=1, source_target_pairs={{0,3},{1,0},{2,1},{3,2},{4,7},{5,4},{6,5},{7,6},{8,11},{9,8},{10,9... | collective-permute-start | bytes 221192 | tf_op jit(solution)/shard_map/ppermute | solution.py:185
  132.8 6.3 %collective-permute-start.18 = (bf16[32,1152]{1,0:T(8,128)(2,1)S(1)}, bf16[32,1152]{1,0:T(8,128)(2,1)S(1)}, u32[]{:S(2)}, u32[]{:S(2)}) collective-permute-start(bf16[32,1152]{1,0:T(8,128)(2,1)S(1)} %get-tuple-element.12), channel_id=1, source_target_pairs={{0,1},{1,2},{2,3},{3,0},{4,5},{5,6},{6,7},{7,4},{8,9},{9,10},{10,1... | collective-permute-start | bytes 221192 | tf_op jit(solution)/shard_map/ppermute | solution.py:185
  137.0 5.3 %collective-permute-start.19 = (bf16[32,1152]{1,0:T(8,128)(2,1)S(1)}, bf16[32,1152]{1,0:T(8,128)(2,1)S(1)}, u32[]{:S(2)}, u32[]{:S(2)}) collective-permute-start(bf16[32,1152]{1,0:T(8,128)(2,1)S(1)} %get-tuple-element.12), channel_id=1, source_target_pairs={{0,2},{1,3},{2,0},{3,1},{4,6},{5,7},{6,4},{7,5},{8,10},{9,11},{10,... | collective-permute-start | bytes 221192 | tf_op jit(solution)/shard_map/ppermute | solution.py:185
  139.2 4.4 %collective-permute-start.20 = (bf16[32,1152]{1,0:T(8,128)(2,1)S(1)}, bf16[32,1152]{1,0:T(8,128)(2,1)S(1)}, u32[]{:S(2)}, u32[]{:S(2)}) collective-permute-start(bf16[32,1152]{1,0:T(8,128)(2,1)S(1)} %get-tuple-element.12), channel_id=1, source_target_pairs={{0,3},{1,0},{2,1},{3,2},{4,7},{5,4},{6,5},{7,6},{8,11},{9,8},{10,9... | collective-permute-start | bytes 221192 | tf_op jit(solution)/shard_map/ppermute | solution.py:185
  150.4 16.9 %all-to-all-start.2 = ((bf16[32,4,1792]{2,1,0:T(4,128)(2,1)}), bf16[32,4,1792]{2,1,0:T(4,128)(2,1)S(1)}, u32[]{:S(2)}, u32[]{:S(2)}) async-start(bf16[32,4,1792]{2,1,0:T(4,128)(2,1)} %reshape.127), calls=%async_computation.2 | async-start | bytes 917504 | tf_op jit(solution)/shard_map/all_to_all | solution.py:267
  (7 other events, 143.1 us)

commit v3 on v2

--- a/solution.py
+++ b/solution.py
@@ -9,7 +9,7 @@
 BLOCK_TOKENS = 64
 TILE = 1024
 CHUNKS = 2
-VMEM_BYTES = 48 * 1024 * 1024
+VMEM_BYTES = 24 * 1024 * 1024
 
 score_scale = 192.0 ** (-0.5)
 log2_e = 1.4426950408889634
@@ -17,8 +17,14 @@
 
 
 def attention_kernel(
-    lens_ref, q_ref, cache_ref, out_ref, held, score0, score1, acc, best, mass, lo, hi, first, last, sems
+    lens_ref,
+    q_ref,
+    cache_ref,
+    *refs,
 ):
+    weights = (len(refs) - 12) // 2
+    sources, (out_ref, *staged) = refs[:weights], refs[weights : 2 * weights + 1]
+    held, score0, score1, acc, best, mass, lo, hi, first, last, sems = refs[2 * weights + 1 :]
     nreq = q_ref.shape[0]
     tiles = held.shape[0]
     tile = held.shape[2]
@@ -45,6 +51,13 @@
     @pl.loop(0, used)
     def _(i):
         copy(i).start()
+
+    copies = [
+        pltpu.make_async_copy(source, target, sems.at[tiles + k])
+        for k, (source, target) in enumerate(zip(sources, staged))
+    ]
+    for each in copies:
+        each.start()
 
     def reset():
         acc[...] = jnp.zeros_like(acc)
@@ -86,18 +99,18 @@
         mass[...] = mass[...] * keep + part
         best[...] = new
         values = lax.dot_general(
+            held[i, :C, :],
             weight.astype(jnp.bfloat16),
-            held[i, :C, :],
             (((1,), (1,)), ((), ())),
             preferred_element_type=jnp.float32,
         )
-        acc[...] = acc[...] * keep[:, :1] + values
+        acc[...] = acc[...] * keep.T[:1, :] + values
 
     def close(r, i, live):
         @pl.when(live & (i == last[r]))
         def _():
             total = jnp.sum(mass[...], axis=1, keepdims=True)
-            out_ref[r] = (acc[...] / total).astype(out_ref.dtype)
+            out_ref[r] = (acc[...].T / total).astype(out_ref.dtype)
             reset()
 
     reset()
@@ -117,43 +130,46 @@
         return r, i, live
 
     lax.fori_loop(0, (pairs + 1) // 2, step, (jnp.int32(0), jnp.int32(0), pairs > 0))
-
-
-def attend(lengths, queries, cache_t):
+    for each in copies:
+        each.wait()
+
+
+def attend(lengths, queries, cache_t, *weights):
     nreq, heads, width = queries.shape
     tokens = cache_t.shape[1]
     tile = TILE
     tiles = tokens // tile
     return pl.pallas_call(
         attention_kernel,
-        out_shape=jax.ShapeDtypeStruct((nreq, heads, C), jnp.bfloat16),
+        out_shape=[jax.ShapeDtypeStruct((nreq, heads, C), jnp.bfloat16)]
+        + [pltpu.VMEM(w.shape, w.dtype) for w in weights],
         in_specs=[
             pl.BlockSpec(memory_space=pltpu.SMEM),
             pl.BlockSpec(memory_space=pltpu.VMEM),
-            pl.BlockSpec(memory_space=pl.ANY),
-        ],
-        out_specs=pl.BlockSpec(memory_space=pltpu.VMEM),
+        ]
+        + [pl.BlockSpec(memory_space=pl.ANY)] * (1 + len(weights)),
+        out_specs=[pl.BlockSpec(memory_space=pltpu.VMEM)] * (1 + len(weights)),
         scratch_shapes=[
             pltpu.VMEM((tiles, width, tile), jnp.bfloat16),
             pltpu.VMEM((heads, tile), jnp.float32),
             pltpu.VMEM((heads, tile), jnp.float32),
-            pltpu.VMEM((heads, C), jnp.float32),
+            pltpu.VMEM((C, heads), jnp.float32),
             pltpu.VMEM((heads, 128), jnp.float32),
             pltpu.VMEM((heads, 128), jnp.float32),
             pltpu.SMEM((nreq,), jnp.int32),
             pltpu.SMEM((nreq,), jnp.int32),
             pltpu.SMEM((nreq,), jnp.int32),
             pltpu.SMEM((nreq,), jnp.int32),
-            pltpu.SemaphoreType.DMA((tiles,)),
+            pltpu.SemaphoreType.DMA((tiles + len(weights),)),
         ],
         compiler_params=pltpu.CompilerParams(vmem_limit_bytes=VMEM_BYTES),
         cost_estimate=pl.CostEstimate(
             flops=2 * heads * tokens * (width + C),
-            bytes_accessed=2 * tokens * width,
+            bytes_accessed=2 * tokens * width + sum(2 * w.size for w in weights),
             transcendentals=heads * tokens,
         ),
         name="attention",
-    )(lengths, queries, cache_t)
+    )(lengths, queries, cache_t, *weights)
 
 
 def dynamic_piece(pieces, at):
@@ -208,7 +224,9 @@
     width = w_o.shape[1]
 
     query = queries.reshape(per_rank, heads_all, row_length)
-    latent_out = attend(lengths, query, paged_latent_cache.T)
+    latent_out, w_o, w_gate, w_up, w_down = attend(
+        lengths, query, paged_latent_cache.T, w_o, w_gate, w_up, w_down
+    )
 
     local_heads = lax.all_to_all(latent_out, ("dp", "tp"), split_axis=1, concat_axis=0, tiled=True)
     local_heads, residual = lax.optimization_barrier((local_heads, residual))
@@ -248,8 +266,7 @@
         ]
         if c == 0:
             parts.append(extra)
-        both = jnp.concatenate(parts, 1).reshape(ranks_tp, -1, 2 * chunk + 128 * (c == 0))
-        sums.append(sum(got.astype(jnp.float32) for got in exchange(both, "tp")))
+        sums.append(scatter_sum(jnp.concatenate(parts, 1), "tp"))
     ffn_part = None
     for c, both in enumerate(sums):
         if c == 0:

time: 169 us -> 188 us (1.11)
  starting transfers between devices: 55.5 us -> 38.9 us
  local copies, waits for them, and re-layouts: 6.14 us -> 20.5 us
  waiting for transfers between devices: 63.9 us -> 76.4 us
  Pallas kernels: 9.04 us -> 14.4 us
  matrix products: 21.8 us -> 23.7 us
    ppermute x12 -> x6, starting transfers between devices: 24.5 us -> 9.34 us  [exchange(): lax.ppermute(piece, axis, [(k, (k + shift) % size) for k in range(size)])]
    unnamed x14 -> x16, local copies, waits for them, and re-layouts: 0.68 us -> 12.5 us
    all_to_all x1 -> x3, waiting for transfers between devices: 8.92 us -> 20.7 us  [scatter_sum(): lax.all_to_all(pieces, axis, split_axis=0, concat_axis=0, tiled=True)]
    all_to_all x1 -> x3, starting transfers between devices: 3.47 us -> 10.4 us  [scatter_sum(): lax.all_to_all(pieces, axis, split_axis=0, concat_axis=0, tiled=True)]
    pallas_call x1, Pallas kernels: 9.04 us -> 14.4 us  [attend(): pl.pallas_call(attention_kernel, out_shape=[jax.ShapeDtypeStruct((nreq, h...]
    all_to_all x1, starting transfers between devices: 13.2 us -> 8.01 us  [local(): lax.all_to_all(latent_out, ('dp', 'tp'), split_axis=1, concat_axis=0, til...]
    ppermute x9, starting transfers between devices: 10.6 us -> 8 us  [gather(): lax.ppermute(piece, axis, [(k, (k + shift) % size) for k in range(size)])]
    ppermute x9, waiting for transfers between devices: 10.5 us -> 13.1 us  [gather(): lax.ppermute(piece, axis, [(k, (k + shift) % size) for k in range(size)])]
  transfers between devices with their start and end apart: 24 -> 20, of which waited for: 14 -> 13; matrix products, arithmetic and copies ran while one was open for 9% -> 12% of each run, Pallas kernels for 0% -> 0%
where the time goes in v3:
time: 188 us; the launch traced here: 187 us
  waiting for transfers between devices  76.4 us (41%)
  starting transfers between devices  38.9 us (21%)
  matrix products  23.7 us (13%)
  local copies, waits for them, and re-layouts  20.5 us (11%)
  Pallas kernels  14.4 us (8%)
  blocking collectives  8.76 us (5%)
  other arithmetic  3.41 us (2%)
    all_to_all x3, waiting for transfers between devices, scatter_sum(): lax.all_to_all(pieces, axis, split_axis=0, concat_axis=0, tiled=True)  20.7 us
    ppermute x6, waiting for transfers between devices, exchange(): lax.ppermute(piece, axis, [(k, (k + shift) % size) for k in range(size)])  16.1 us
    pallas_call x1, Pallas kernels, attend(): pl.pallas_call(attention_kernel, out_shape=[jax.ShapeDtypeStruct((nreq, h...  14.4 us
    all_to_all x1, waiting for transfers between devices, local(): lax.all_to_all(latent_out, ('dp', 'tp'), split_axis=1, concat_axis=0, til...  13.5 us
    ppermute x9, waiting for transfers between devices, gather(): lax.ppermute(piece, axis, [(k, (k + shift) % size) for k in range(size)])  13.1 us
    all_to_all x1, waiting for transfers between devices, local(): lax.all_to_all(ffn_pieces, ('dp', 'tp'), split_axis=0, concat_axis=0, til...  13 us
    unnamed x16, local copies, waits for them, and re-layouts  12.5 us
    dot_general x4, matrix products, local(): jnp.dot(scaled, w[:, columns], preferred_element_type=jnp.float32)  11.8 us
  transfers between devices with their start and end apart: 20, of which 13 were waited for; matrix products, arithmetic and copies ran while one was open for 12% of the time, Pallas kernels for 0%

profile of v3, /device:TPU:0, one launch (start us, length us, event | category | flops | bytes accessed | tf_op | source)
XLA Modules:
  0.0 186.6 jit_solution(5122594046867405739)
XLA Ops:
  2.7 14.4 %attention.1 = (bf16[4,128,512]{2,1,0:T(8,128)(2,1)}, bf16[2048,1792]{1,0:T(8,128)(2,1)S(1)}, bf16[1792,2304]{1,0:T(8,128)(2,1)S(1)}, bf16[1792,2304]{1,0:T(8,128)(2,1)S(1)}, bf16[2304,1792]{1,0:T(8,128)(2,1)S(1)}) custom-call(s32[128]{0:T(128)} %lens_ref.1, bf16[4,128,576]{2,1,0:T(8,128)(2,1)} %reshape.116.q_ref, bf16[576,14336]{1,0:T(8,128)(2,1)} %bitcast.74, ...), custom_call_target="tpu_custom_call" | custom-call | flops 3992977408 | bytes 48627712 | tf_op jit(solution)/shard_map/attention/pallas_call | solution.py:142
  17.1 3.0 %copy-done.2 = bf16[2048,1792]{1,0:T(8,128)(2,1)} copy-done((bf16[2048,1792]{1,0:T(8,128)(2,1)}, bf16[2048,1792]{1,0:T(8,128)(2,1)S(1)}, u32[]{:S(2)}) %copy-start.2) | copy-done | bytes 7340056
  20.1 3.2 %copy-done.4 = bf16[2304,1792]{1,0:T(8,128)(2,1)} copy-done((bf16[2304,1792]{1,0:T(8,128)(2,1)}, bf16[2304,1792]{1,0:T(8,128)(2,1)S(1)}, u32[]{:S(2)}) %copy-start.4) | copy-done | bytes 8257560
  23.3 3.2 %copy-done.5 = bf16[1792,2304]{1,0:T(8,128)(2,1)} copy-done((bf16[1792,2304]{1,0:T(8,128)(2,1)}, bf16[1792,2304]{1,0:T(8,128)(2,1)S(1)}, u32[]{:S(2)}) %copy-start.5) | copy-done | bytes 8257560
  26.4 3.2 %copy-done.6 = bf16[1792,2304]{1,0:T(8,128)(2,1)} copy-done((bf16[1792,2304]{1,0:T(8,128)(2,1)}, bf16[1792,2304]{1,0:T(8,128)(2,1)S(1)}, u32[]{:S(2)}) %copy-start.6) | copy-done | bytes 8257560
  31.9 8.0 %all-to-all-start = ((bf16[4,128,512]{2,0,1:T(4,128)(2,1)}), bf16[4,128,512]{2,0,1:T(4,128)(2,1)S(1)}, u32[]{:S(2)}, u32[]{:S(2)}) async-start(bf16[4,128,512]{2,0,1:T(4,128)(2,1)} %copy.35), calls=%async_computation | async-start | bytes 1048576 | tf_op jit(solution)/shard_map/all_to_all | solution.py:231
  40.8 13.5 %all-to-all-done = bf16[4,128,512]{2,0,1:T(4,128)(2,1)S(1)} async-done(((bf16[4,128,512]{2,0,1:T(4,128)(2,1)}), bf16[4,128,512]{2,0,1:T(4,128)(2,1)S(1)}, u32[]{:S(2)}, u32[]{:S(2)}) %all-to-all-start) | async-done | bytes 524320 | tf_op jit(solution)/shard_map/all_to_all | solution.py:231
  64.6 4.5 %collective-permute-done = bf16[4,1792]{1,0:T(4,128)(2,1)S(1)} collective-permute-done((bf16[4,1792]{1,0:T(4,128)(2,1)S(1)}, bf16[4,1792]{1,0:T(4,128)(2,1)S(1)}, u32[]{:S(2)}, u32[]{:S(2)}) %collective-permute-start) | collective-permute-done | bytes 14368 | tf_op jit(solution)/shard_map/ppermute | solution.py:185
  75.6 3.5 %all-to-all-start.1 = ((bf16[8,16,1792]{2,1,0:T(8,128)(2,1)}), bf16[8,16,1792]{2,1,0:T(8,128)(2,1)S(1)}, u32[]{:S(2)}, u32[]{:S(2)}) async-start(bf16[8,16,1792]{2,1,0:T(8,128)(2,1)} %bitcast.17), calls=%async_computation.1 | async-start | bytes 917504 | tf_op jit(solution)/shard_map/all_to_all | solution.py:209
  79.1 8.9 %all-to-all-done.1 = bf16[8,16,1792]{2,1,0:T(8,128)(2,1)S(1)} async-done(((bf16[8,16,1792]{2,1,0:T(8,128)(2,1)}), bf16[8,16,1792]{2,1,0:T(8,128)(2,1)S(1)}, u32[]{:S(2)}, u32[]{:S(2)}) %all-to-all-start.1) | async-done | bytes 458784 | tf_op jit(solution)/shard_map/all_to_all | solution.py:209
  88.1 8.8 %all_gather.3 = bf16[128,1792]{1,0:T(8,128)(2,1)S(1)} all-gather(bf16[16,1792]{1,0:T(8,128)(2,1)S(1)} %add_convert_fusion.1), channel_id=1, replica_groups=mesh['dp'=8,'tp'=4] {'dp'}, dimensions={0}, use_global_device_ids=true | all-gather | bytes 516096 | tf_op jit(solution)/shard_map/all_gather | solution.py:249
  97.1 2.9 %fusion.23 = bf16[128,1152]{1,0:T(8,128)(2,1)S(1)} fusion(bf16[1792,2304]{1,0:T(8,128)(2,1)} %copy-done.5, bf16[128,1792]{1,0:T(8,128)(2,1)S(1)} %all_gather.3, f32[1792]{0:T(1024)S(1)} %dynamic-slice_convert_fusion), kind=kOutput, calls=%fused_computation.19 | convolution fusion | flops 529317888 | bytes 4889600 | tf_op jit(solution)/shard_map/dot_general | solution.py:264
  100.1 2.9 %fusion.26 = bf16[128,1152]{1,0:T(8,128)(2,1)S(1)} fusion(bf16[1792,2304]{1,0:T(8,128)(2,1)} %copy-done.6, bf16[128,1792]{1,0:T(8,128)(2,1)S(1)} %all_gather.3, f32[1792]{0:T(1024)S(1)} %dynamic-slice_convert_fusion), kind=kOutput, calls=%fused_computation.20 | convolution fusion | flops 529317888 | bytes 4889600 | tf_op jit(solution)/shard_map/dot_general | solution.py:264
  104.0 3.5 %all-to-all-start.3 = ((bf16[4,32,2304]{2,1,0:T(8,128)(2,1)}), bf16[4,32,2304]{2,1,0:T(8,128)(2,1)S(1)}, u32[]{:S(2)}, u32[]{:S(2)}) async-start(bf16[4,32,2304]{2,1,0:T(8,128)(2,1)} %bitcast.31), calls=%async_computation.3 | async-start | bytes 1179648 | tf_op jit(solution)/shard_map/all_to_all | solution.py:209
  107.9 2.9 %fusion.20 = bf16[128,1152]{1,0:T(8,128)(2,1)S(1)} fusion(bf16[1792,2304]{1,0:T(8,128)(2,1)} %copy-done.6, bf16[128,1792]{1,0:T(8,128)(2,1)S(1)} %all_gather.3, f32[1792]{0:T(1024)S(1)} %dynamic-slice_convert_fusion), kind=kOutput, calls=%fused_computation.18 | convolution fusion | flops 529317888 | bytes 4889600 | tf_op jit(solution)/shard_map/dot_general | solution.py:264
  110.8 2.9 %fusion.17 = bf16[128,1152]{1,0:T(8,128)(2,1)S(1)} fusion(bf16[1792,2304]{1,0:T(8,128)(2,1)} %copy-done.5, bf16[128,1792]{1,0:T(8,128)(2,1)S(1)} %all_gather.3, f32[1792]{0:T(1024)S(1)} %dynamic-slice_convert_fusion), kind=kOutput, calls=%fused_computation.17 | convolution fusion | flops 529317888 | bytes 4889600 | tf_op jit(solution)/shard_map/dot_general | solution.py:264
  114.8 9.3 %all-to-all-done.3 = bf16[4,32,2304]{2,1,0:T(8,128)(2,1)S(1)} async-done(((bf16[4,32,2304]{2,1,0:T(8,128)(2,1)}), bf16[4,32,2304]{2,1,0:T(8,128)(2,1)S(1)}, u32[]{:S(2)}, u32[]{:S(2)}) %all-to-all-start.3) | async-done | bytes 589856 | tf_op jit(solution)/shard_map/all_to_all | solution.py:209
  124.1 3.5 %all-to-all-start.2 = ((bf16[4,32,2432]{2,1,0:T(8,128)(2,1)}), bf16[4,32,2432]{2,1,0:T(8,128)(2,1)S(1)}, u32[]{:S(2)}, u32[]{:S(2)}) async-start(bf16[4,32,2432]{2,1,0:T(8,128)(2,1)} %concatenate.13), calls=%async_computation.2 | async-start | bytes 1245184 | tf_op jit(solution)/shard_map/all_to_all | solution.py:209
  133.6 8.9 %collective-permute-done.6 = bf16[4,1792]{1,0:T(4,128)(2,1)S(1)} collective-permute-done((bf16[4,1792]{1,0:T(4,128)(2,1)S(1)}, bf16[4,1792]{1,0:T(4,128)(2,1)S(1)}, u32[]{:S(2)}, u32[]{:S(2)}) %collective-permute-start.6) | collective-permute-done | bytes 14368 | tf_op jit(solution)/shard_map/ppermute | solution.py:185
  153.4 4.9 %collective-permute-done.12 = bf16[32,1152]{1,0:T(8,128)(2,1)S(1)} collective-permute-done((bf16[32,1152]{1,0:T(8,128)(2,1)S(1)}, bf16[32,1152]{1,0:T(8,128)(2,1)S(1)}, u32[]{:S(2)}, u32[]{:S(2)}) %collective-permute-start.12) | collective-permute-done | bytes 73760 | tf_op jit(solution)/shard_map/ppermute | solution.py:201
  162.6 3.0 %fusion = f32[128,1792]{1,0:T(8,128)S(1)} fusion(bf16[128,1152]{1,0:T(8,128)(2,1)S(1)} %bitcast.81, bf16[2304,1792]{1,0:T(8,128)(2,1)} %copy-done.4), kind=kOutput, calls=%fused_computation | convolution fusion | flops 528482304 | bytes 5341184 | tf_op jit(solution)/shard_map/dot_general | solution.py:279
  165.7 3.0 %fusion.29 = bf16[128,1792]{1,0:T(8,128)(2,1)S(1)} fusion(f32[128,1792]{1,0:T(8,128)S(1)} %fusion, bf16[128,1152]{1,0:T(8,128)(2,1)S(1)} %bitcast.82, bf16[2304,1792]{1,0:T(8,128)(2,1)} %copy-done.4), kind=kOutput, calls=%fused_computation.21 | convolution fusion | flops 528941056 | bytes 5799936 | tf_op jit(solution)/shard_map/dot_general | solution.py:279
  169.6 3.1 %all-to-all-start.4 = ((bf16[32,4,1792]{2,1,0:T(4,128)(2,1)}), bf16[32,4,1792]{2,1,0:T(4,128)(2,1)S(1)}, u32[]{:S(2)}, u32[]{:S(2)}) async-start(bf16[32,4,1792]{2,1,0:T(4,128)(2,1)} %reshape.123), calls=%async_computation.4 | async-start | bytes 917504 | tf_op jit(solution)/shard_map/all_to_all | solution.py:284
  172.7 13.0 %all-to-all-done.4 = bf16[32,4,1792]{2,1,0:T(4,128)(2,1)S(1)} async-done(((bf16[32,4,1792]{2,1,0:T(4,128)(2,1)}), bf16[32,4,1792]{2,1,0:T(4,128)(2,1)S(1)}, u32[]{:S(2)}, u32[]{:S(2)}) %all-to-all-start.4) | async-done | bytes 458784 | tf_op jit(solution)/shard_map/all_to_all | solution.py:284
  (92 shorter events, 48.3 us)
Async XLA Ops:
  0.0 54.6 %copy-start = (bf16[4,512,128]{2,1,0:T(8,128)(2,1)S(1)}, bf16[4,512,128]{2,1,0:T(8,128)(2,1)}, u32[]{:S(2)}) copy-start(bf16[4,512,128]{2,1,0:T(8,128)(2,1)} %param.14) | copy-start | bytes 1572868
  2.7 56.4 %copy-start.7 = (bf16[4,7168]{1,0:T(4,128)(2,1)S(1)}, bf16[4,7168]{1,0:T(4,128)(2,1)}, u32[]{:S(2)}) copy-start(bf16[4,7168]{1,0:T(4,128)(2,1)} %param.10) | copy-start | bytes 172036
  31.9 22.4 %all-to-all-start = ((bf16[4,128,512]{2,0,1:T(4,128)(2,1)}), bf16[4,128,512]{2,0,1:T(4,128)(2,1)S(1)}, u32[]{:S(2)}, u32[]{:S(2)}) async-start(bf16[4,128,512]{2,0,1:T(4,128)(2,1)} %copy.35), calls=%async_computation | async-start | bytes 1048576 | tf_op jit(solution)/shard_map/all_to_all | solution.py:231
  54.6 19.3 %copy-start.3 = (bf16[2048,1792]{1,0:T(8,128)(2,1)S(1)}, bf16[2048,1792]{1,0:T(8,128)(2,1)}, u32[]{:S(2)}) copy-start(bf16[2048,1792]{1,0:T(8,128)(2,1)} %copy-done.2) | copy-start | bytes 22020100
  55.0 16.9 %collective-permute-start.3 = (bf16[128,512]{0,1:T(8,128)(2,1)S(1)}, bf16[128,512]{0,1:T(8,128)(2,1)S(1)}, u32[]{:S(2)}, u32[]{:S(2)}) collective-permute-start(bf16[128,512]{0,1:T(8,128)(2,1)S(1)} %bitcast.77), channel_id=1, source_target_pairs={{0,1},{1,2},{2,3},{3,0},{4,5},{5,6},{6,7},{7,4},{8,9},{9,10},{10,1... | collective-permute-start | bytes 393224 | tf_op jit(solution)/shard_map/ppermute | solution.py:201
  57.6 16.3 %collective-permute-start.5 = (bf16[128,512]{0,1:T(8,128)(2,1)S(1)}, bf16[128,512]{0,1:T(8,128)(2,1)S(1)}, u32[]{:S(2)}, u32[]{:S(2)}) collective-permute-start(bf16[128,512]{0,1:T(8,128)(2,1)S(1)} %bitcast.78), channel_id=1, source_target_pairs={{0,3},{1,0},{2,1},{3,2},{4,7},{5,4},{6,5},{7,6},{8,11},{9,8},{10,9... | collective-permute-start | bytes 393224 | tf_op jit(solution)/shard_map/ppermute | solution.py:201
  58.8 15.5 %collective-permute-start.4 = (bf16[128,512]{0,1:T(8,128)(2,1)S(1)}, bf16[128,512]{0,1:T(8,128)(2,1)S(1)}, u32[]{:S(2)}, u32[]{:S(2)}) collective-permute-start(bf16[128,512]{0,1:T(8,128)(2,1)S(1)} %bitcast.79), channel_id=1, source_target_pairs={{0,2},{1,3},{2,0},{3,1},{4,6},{5,7},{6,4},{7,5},{8,10},{9,11},{10,... | collective-permute-start | bytes 393224 | tf_op jit(solution)/shard_map/ppermute | solution.py:201
  59.1 9.9 %collective-permute-start = (bf16[4,1792]{1,0:T(4,128)(2,1)S(1)}, bf16[4,1792]{1,0:T(4,128)(2,1)S(1)}, u32[]{:S(2)}, u32[]{:S(2)}) collective-permute-start(bf16[4,1792]{1,0:T(4,128)(2,1)S(1)} %get-tuple-element.29), channel_id=1, source_target_pairs={{0,1},{1,2},{2,3},{3,0},{4,5},{5,6},{6,7},{7,4},{8,9},{9,10},{10,1... | collective-permute-start | bytes 43016 | tf_op jit(solution)/shard_map/ppermute | solution.py:185
  60.5 11.4 %collective-permute-start.1 = (bf16[4,1792]{1,0:T(4,128)(2,1)S(1)}, bf16[4,1792]{1,0:T(4,128)(2,1)S(1)}, u32[]{:S(2)}, u32[]{:S(2)}) collective-permute-start(bf16[4,1792]{1,0:T(4,128)(2,1)S(1)} %get-tuple-element.28), channel_id=1, source_target_pairs={{0,2},{1,3},{2,0},{3,1},{4,6},{5,7},{6,4},{7,5},{8,10},{9,11},{10,... | collective-permute-start | bytes 43016 | tf_op jit(solution)/shard_map/ppermute | solution.py:185
  69.0 10.0 %collective-permute-start.2 = (bf16[4,1792]{1,0:T(4,128)(2,1)S(1)}, bf16[4,1792]{1,0:T(4,128)(2,1)S(1)}, u32[]{:S(2)}, u32[]{:S(2)}) collective-permute-start(bf16[4,1792]{1,0:T(4,128)(2,1)S(1)} %get-tuple-element.27), channel_id=1, source_target_pairs={{0,3},{1,0},{2,1},{3,2},{4,7},{5,4},{6,5},{7,6},{8,11},{9,8},{10,9... | collective-permute-start | bytes 43016 | tf_op jit(solution)/shard_map/ppermute | solution.py:185
  75.6 12.5 %all-to-all-start.1 = ((bf16[8,16,1792]{2,1,0:T(8,128)(2,1)}), bf16[8,16,1792]{2,1,0:T(8,128)(2,1)S(1)}, u32[]{:S(2)}, u32[]{:S(2)}) async-start(bf16[8,16,1792]{2,1,0:T(8,128)(2,1)} %bitcast.17), calls=%async_computation.1 | async-start | bytes 917504 | tf_op jit(solution)/shard_map/all_to_all | solution.py:209
  104.0 20.1 %all-to-all-start.3 = ((bf16[4,32,2304]{2,1,0:T(8,128)(2,1)}), bf16[4,32,2304]{2,1,0:T(8,128)(2,1)S(1)}, u32[]{:S(2)}, u32[]{:S(2)}) async-start(bf16[4,32,2304]{2,1,0:T(8,128)(2,1)} %bitcast.31), calls=%async_computation.3 | async-start | bytes 1179648 | tf_op jit(solution)/shard_map/all_to_all | solution.py:209
  124.1 21.0 %all-to-all-start.2 = ((bf16[4,32,2432]{2,1,0:T(8,128)(2,1)}), bf16[4,32,2432]{2,1,0:T(8,128)(2,1)S(1)}, u32[]{:S(2)}, u32[]{:S(2)}) async-start(bf16[4,32,2432]{2,1,0:T(8,128)(2,1)} %concatenate.13), calls=%async_computation.2 | async-start | bytes 1245184 | tf_op jit(solution)/shard_map/all_to_all | solution.py:209
  127.7 14.7 %collective-permute-start.6 = (bf16[4,1792]{1,0:T(4,128)(2,1)S(1)}, bf16[4,1792]{1,0:T(4,128)(2,1)S(1)}, u32[]{:S(2)}, u32[]{:S(2)}) collective-permute-start(bf16[4,1792]{1,0:T(4,128)(2,1)S(1)} %get-tuple-element.25), channel_id=1, source_target_pairs={{0,1},{1,2},{2,3},{3,0},{4,5},{5,6},{6,7},{7,4},{8,9},{9,10},{10,1... | collective-permute-start | bytes 43016 | tf_op jit(solution)/shard_map/ppermute | solution.py:185
  129.7 42.9 %collective-permute-start.7 = (bf16[4,1792]{1,0:T(4,128)(2,1)S(1)}, bf16[4,1792]{1,0:T(4,128)(2,1)S(1)}, u32[]{:S(2)}, u32[]{:S(2)}) collective-permute-start(bf16[4,1792]{1,0:T(4,128)(2,1)S(1)} %get-tuple-element.24), channel_id=1, source_target_pairs={{0,2},{1,3},{2,0},{3,1},{4,6},{5,7},{6,4},{7,5},{8,10},{9,11},{10,... | collective-permute-start | bytes 43016 | tf_op jit(solution)/shard_map/ppermute | solution.py:185
  132.1 40.6 %collective-permute-start.8 = (bf16[4,1792]{1,0:T(4,128)(2,1)S(1)}, bf16[4,1792]{1,0:T(4,128)(2,1)S(1)}, u32[]{:S(2)}, u32[]{:S(2)}) collective-permute-start(bf16[4,1792]{1,0:T(4,128)(2,1)S(1)} %get-tuple-element.23), channel_id=1, source_target_pairs={{0,3},{1,0},{2,1},{3,2},{4,7},{5,4},{6,5},{7,6},{8,11},{9,8},{10,9... | collective-permute-start | bytes 43016 | tf_op jit(solution)/shard_map/ppermute | solution.py:185
  145.4 6.5 %collective-permute-start.9 = (bf16[32,1152]{1,0:T(8,128)(2,1)S(1)}, bf16[32,1152]{1,0:T(8,128)(2,1)S(1)}, u32[]{:S(2)}, u32[]{:S(2)}) collective-permute-start(bf16[32,1152]{1,0:T(8,128)(2,1)S(1)} %get-tuple-element.20), channel_id=1, source_target_pairs={{0,1},{1,2},{2,3},{3,0},{4,5},{5,6},{6,7},{7,4},{8,9},{9,10},{10,1... | collective-permute-start | bytes 221192 | tf_op jit(solution)/shard_map/ppermute | solution.py:201
  145.5 7.9 %collective-permute-start.10 = (bf16[32,1152]{1,0:T(8,128)(2,1)S(1)}, bf16[32,1152]{1,0:T(8,128)(2,1)S(1)}, u32[]{:S(2)}, u32[]{:S(2)}) collective-permute-start(bf16[32,1152]{1,0:T(8,128)(2,1)S(1)} %get-tuple-element.20), channel_id=1, source_target_pairs={{0,2},{1,3},{2,0},{3,1},{4,6},{5,7},{6,4},{7,5},{8,10},{9,11},{10,... | collective-permute-start | bytes 221192 | tf_op jit(solution)/shard_map/ppermute | solution.py:201
  147.5 18.1 %collective-permute-start.11 = (bf16[32,1152]{1,0:T(8,128)(2,1)S(1)}, bf16[32,1152]{1,0:T(8,128)(2,1)S(1)}, u32[]{:S(2)}, u32[]{:S(2)}) collective-permute-start(bf16[32,1152]{1,0:T(8,128)(2,1)S(1)} %get-tuple-element.20), channel_id=1, source_target_pairs={{0,3},{1,0},{2,1},{3,2},{4,7},{5,4},{6,5},{7,6},{8,11},{9,8},{10,9... | collective-permute-start | bytes 221192 | tf_op jit(solution)/shard_map/ppermute | solution.py:201
  151.9 6.3 %collective-permute-start.12 = (bf16[32,1152]{1,0:T(8,128)(2,1)S(1)}, bf16[32,1152]{1,0:T(8,128)(2,1)S(1)}, u32[]{:S(2)}, u32[]{:S(2)}) collective-permute-start(bf16[32,1152]{1,0:T(8,128)(2,1)S(1)} %get-tuple-element.22), channel_id=1, source_target_pairs={{0,1},{1,2},{2,3},{3,0},{4,5},{5,6},{6,7},{7,4},{8,9},{9,10},{10,1... | collective-permute-start | bytes 221192 | tf_op jit(solution)/shard_map/ppermute | solution.py:201
  153.4 7.0 %collective-permute-start.13 = (bf16[32,1152]{1,0:T(8,128)(2,1)S(1)}, bf16[32,1152]{1,0:T(8,128)(2,1)S(1)}, u32[]{:S(2)}, u32[]{:S(2)}) collective-permute-start(bf16[32,1152]{1,0:T(8,128)(2,1)S(1)} %get-tuple-element.22), channel_id=1, source_target_pairs={{0,2},{1,3},{2,0},{3,1},{4,6},{5,7},{6,4},{7,5},{8,10},{9,11},{10,... | collective-permute-start | bytes 221192 | tf_op jit(solution)/shard_map/ppermute | solution.py:201
  158.3 4.4 %collective-permute-start.14 = (bf16[32,1152]{1,0:T(8,128)(2,1)S(1)}, bf16[32,1152]{1,0:T(8,128)(2,1)S(1)}, u32[]{:S(2)}, u32[]{:S(2)}) collective-permute-start(bf16[32,1152]{1,0:T(8,128)(2,1)S(1)} %get-tuple-element.22), channel_id=1, source_target_pairs={{0,3},{1,0},{2,1},{3,2},{4,7},{5,4},{6,5},{7,6},{8,11},{9,8},{10,9... | collective-permute-start | bytes 221192 | tf_op jit(solution)/shard_map/ppermute | solution.py:201
  162.6 24.0 %copy-start.1 = (bf16[4,512,128]{2,1,0:T(8,128)(2,1)S(1)}, bf16[4,512,128]{2,1,0:T(8,128)(2,1)}, u32[]{:S(2)}) copy-start(bf16[4,512,128]{2,1,0:T(8,128)(2,1)} %param.14) | copy-start | bytes 1572868
  169.6 16.2 %all-to-all-start.4 = ((bf16[32,4,1792]{2,1,0:T(4,128)(2,1)}), bf16[32,4,1792]{2,1,0:T(4,128)(2,1)S(1)}, u32[]{:S(2)}, u32[]{:S(2)}) async-start(bf16[32,4,1792]{2,1,0:T(4,128)(2,1)} %reshape.123), calls=%async_computation.4 | async-start | bytes 917504 | tf_op jit(solution)/shard_map/all_to_all | solution.py:284
  (4 other events, 12.5 us)

commit v4 on v1

v4 whole, which is shorter than its diff:
```python
import functools

import jax
import jax.numpy as jnp
from jax import lax
from jax.experimental import pallas as pl
from jax.experimental.pallas import tpu as pltpu
from jax.sharding import PartitionSpec as P

C = 512
BLOCK_TOKENS = 64
TILE = 1024

score_scale = 192.0 ** (-0.5)
log2_e = 1.4426950408889634
negative = -1e30


def attention_kernel(
    lens_ref,
    q_ref,
    cache_ref,
    out_ref,
    held,
    score0,
    score1,
    acc,
    done,
    best,
    mass,
    lo,
    hi,
    first,
    last,
    sems,
):
    nreq = q_ref.shape[0]
    tiles = held.shape[0]
    tile = held.shape[2]
    heads = q_ref.shape[1]

    rank = lax.axis_index("dp") * lax.axis_size("tp") + lax.axis_index("tp")
    begin = jnp.int32(0)
    pairs = jnp.int32(0)
    for r in range(nreq):
        length = lens_ref[rank * nreq + r]
        lo[r] = begin
        hi[r] = begin + length
        first[r] = begin // tile
        last[r] = (begin + length - 1) // tile
        pairs = pairs + (last[r] - first[r] + 1)
        begin = begin + ((length + BLOCK_TOKENS - 1) // BLOCK_TOKENS) * BLOCK_TOKENS
    used = last[nreq - 1] + 1

    def copy(i):
        return pltpu.make_async_copy(
            cache_ref.at[:, pl.ds(pl.multiple_of(i * tile, tile), tile)], held.at[i], sems.at[i]
        )

    @pl.loop(0, used)
    def _(i):
        copy(i).start()

    def reset():
        acc[...] = jnp.zeros_like(acc)
        best[...] = jnp.full_like(best, negative)
        mass[...] = jnp.zeros_like(mass)

    def scores(r, i, live, target):
        begin_at = jnp.where(live, lo[r], 0)
        end_at = jnp.where(live, hi[r], 0)
        s = jnp.dot(q_ref[r], held[i], preferred_element_type=jnp.float32)
        token = i * tile + lax.broadcasted_iota(jnp.int32, (1, tile), 1)
        s = jnp.where((token >= begin_at) & (token < end_at), s, negative)
        target[...] = s

    def advance(p, r, i):
        ends = i == last[r]
        live = p + 1 < pairs
        nr = jnp.where(ends & live, r + 1, r)
        ni = jnp.where(ends, jnp.where(live, first[nr], i), i + 1)
        return nr, ni, live

    def fetch(i, r, live):
        fresh = live & ((r == 0) | (i > last[jnp.maximum(r - 1, 0)]))

        @pl.when(fresh)
        def _():
            copy(i).wait()

    def absorb(r, i, live, source):
        factor = score_scale * log2_e
        s = source[...]
        old = best[...]
        new = jnp.maximum(old, jnp.max(s, axis=1, keepdims=True))
        weight = jnp.exp2((s - new[:, :1]) * factor)
        keep = jnp.exp2((old - new) * factor)
        part = weight[:, :128]
        for at in range(128, tile, 128):
            part = part + weight[:, at : at + 128]
        mass[...] = mass[...] * keep + part
        best[...] = new
        values = lax.dot_general(
            held[i, :C, :],
            weight.astype(jnp.bfloat16),
            (((1,), (1,)), ((), ())),
            preferred_element_type=jnp.float32,
        )
        acc[...] = acc[...] * keep.T[:1, :] + values

    def close(r, i, live):
        @pl.when(live & (i == last[r]))
        def _():
            total = jnp.sum(mass[...], axis=1, keepdims=True)
            done[r] = acc[...].T / total
            reset()

    reset()
    fetch(jnp.int32(0), jnp.int32(0), pairs > 0)
    scores(jnp.int32(0), jnp.int32(0), pairs > 0, score0)

    def step(j, carry):
        r, i, live = carry
        p = 2 * j
        for now, later in ((score0, score1), (score1, score0)):
            nr, ni, nlive = advance(p, r, i)
            fetch(ni, nr, nlive)
            scores(nr, ni, nlive, later)
            absorb(r, i, live, now)
            close(r, i, live)
            r, i, live, p = nr, ni, nlive, p + 1
        return r, i, live

    lax.fori_loop(0, (pairs + 1) // 2, step, (jnp.int32(0), jnp.int32(0), pairs > 0))
    share = heads // out_ref.shape[0]
    for d in range(out_ref.shape[0]):
        rows = [done[r, d * share : (d + 1) * share, :] for r in range(nreq)]
        out_ref[d] = jnp.concatenate(rows, 0).astype(out_ref.dtype)


def kernel_params(limit):
    return pltpu.CompilerParams(vmem_limit_bytes=limit * 1024 * 1024)


def in_vmem(count):
    return [pl.BlockSpec(memory_space=pltpu.VMEM)] * count


def in_any(count):
    return [pl.BlockSpec(memory_space=pl.ANY)] * count


def attend(lengths, queries, cache_t, ranks):
    nreq, heads, width = queries.shape
    tokens = cache_t.shape[1]
    tile = TILE
    tiles = tokens // tile
    return pl.pallas_call(
        attention_kernel,
        out_shape=jax.ShapeDtypeStruct((ranks, nreq * heads // ranks, C), jnp.bfloat16),
        in_specs=[pl.BlockSpec(memory_space=pltpu.SMEM)] + in_vmem(1) + in_any(1),
        out_specs=pl.BlockSpec(memory_space=pltpu.VMEM),
        scratch_shapes=[
            pltpu.VMEM((tiles, width, tile), jnp.bfloat16),
            pltpu.VMEM((heads, tile), jnp.float32),
            pltpu.VMEM((heads, tile), jnp.float32),
            pltpu.VMEM((C, heads), jnp.float32),
            pltpu.VMEM((nreq, heads, C), jnp.float32),
            pltpu.VMEM((heads, 128), jnp.float32),
            pltpu.VMEM((heads, 128), jnp.float32),
            pltpu.SMEM((nreq,), jnp.int32),
            pltpu.SMEM((nreq,), jnp.int32),
            pltpu.SMEM((nreq,), jnp.int32),
            pltpu.SMEM((nreq,), jnp.int32),
            pltpu.SemaphoreType.DMA((tiles,)),
        ],
        compiler_params=kernel_params(28),
        cost_estimate=pl.CostEstimate(
            flops=2 * heads * tokens * (width + C),
            bytes_accessed=2 * tokens * width,
            transcendentals=heads * tokens,
        ),
        name="attention",
    )(lengths, queries, cache_t)


def head_values_kernel(latent_ref, w_ref, residual_ref, out_ref, values, slots):
    heads, _, wide = w_ref.shape
    per_rank, model = residual_ref.shape
    requests = latent_ref.shape[0] // heads
    latent = latent_ref[...]
    for h in range(heads):
        values[...] = jnp.dot(latent, w_ref[h], preferred_element_type=jnp.float32)
        picked = values[pl.ds(h, requests, stride=heads), :]
        out_ref[:requests, h * wide : (h + 1) * wide] = picked.astype(out_ref.dtype)
    ranks = lax.axis_size("tp")
    groups = model // ranks // 128
    rows = (out_ref.shape[0] - requests) // ranks
    across = out_ref.shape[1] // 128
    slots[...] = jnp.zeros_like(slots)
    for t in range(ranks):
        for g in range(groups):
            at = (t * groups + g) * 128
            row = t * rows + (g // across) * per_rank
            column = (g % across) * 128
            slots[row : row + per_rank, column : column + 128] = residual_ref[
                :, at : at + 128
            ].astype(jnp.float32)
    out_ref[requests:, :] = slots[...].astype(out_ref.dtype)


def head_values(latent, w_uv, residual, slot_rows):
    heads, _, wide = w_uv.shape
    requests = latent.shape[0] // heads
    return pl.pallas_call(
        head_values_kernel,
        out_shape=jax.ShapeDtypeStruct((requests + slot_rows, heads * wide), jnp.bfloat16),
        in_specs=in_vmem(3),
        out_specs=pl.BlockSpec(memory_space=pltpu.VMEM),
        scratch_shapes=[
            pltpu.VMEM((latent.shape[0], wide), jnp.float32),
            pltpu.VMEM((slot_rows, heads * wide), jnp.float32),
        ],
        compiler_params=kernel_params(12),
        name="head_values",
    )(latent, w_uv, residual)


def stream(sources, target, sems):
    copies = [pltpu.make_async_copy(s, target.at[k], sems.at[k]) for k, s in enumerate(sources)]
    for copy in copies:
        copy.start()
    return copies


def output_kernel(values_ref, w_ref, out_ref, held, total, sems):
    steps, depth, _ = held.shape
    requests = out_ref.shape[0]
    copies = stream([w_ref.at[pl.ds(k * depth, depth), :] for k in range(steps)], held, sems)
    for k in range(steps):
        copies[k].wait()
        term = jnp.dot(values_ref[k, :requests, :], held[k], preferred_element_type=jnp.float32)
        if k == 0:
            total[...] = term
        else:
            total[...] += term
    out_ref[...] = total[...].astype(out_ref.dtype)


def project_out(values, w_o, requests):
    steps, _, depth = values.shape
    width = w_o.shape[1]
    return pl.pallas_call(
        output_kernel,
        out_shape=jax.ShapeDtypeStruct((requests, width), jnp.bfloat16),
        in_specs=in_vmem(1) + in_any(1),
        out_specs=pl.BlockSpec(memory_space=pltpu.VMEM),
        scratch_shapes=[
            pltpu.VMEM((steps, depth, width), w_o.dtype),
            pltpu.VMEM((requests, width), jnp.float32),
            pltpu.SemaphoreType.DMA((steps,)),
        ],
        compiler_params=kernel_params(20),
        name="project_out",
    )(values, w_o)


def hidden_kernel(parts_ref, values_ref, out_ref, slots):
    ranks = values_ref.shape[0]
    width = out_ref.shape[1]
    per_rank = out_ref.shape[0] // ranks
    across = values_ref.shape[2] // 128
    rows = slots.shape[1]
    requests = values_ref.shape[1] - ranks * rows
    start = pl.multiple_of(requests + lax.axis_index("tp") * rows, 16)
    for s in range(ranks):
        slots[s] = values_ref[s, pl.ds(start, rows), :].astype(jnp.float32)
    for g in range(width // 128):
        at = slice(g * 128, (g + 1) * 128)
        row = (g // across) * per_rank
        column = (g % across) * 128
        terms = [
            slots[s, row : row + per_rank, column : column + 128] for s in range(ranks)
        ]
        total = parts_ref[0, :, at].astype(jnp.float32)
        for d in range(1, parts_ref.shape[0]):
            total = total + parts_ref[d, :, at].astype(jnp.float32)
        total = total + jnp.concatenate(terms, 0)
        out_ref[:, at] = total.astype(out_ref.dtype)


def make_hidden(parts, values, slot_rows):
    ranks = values.shape[0]
    return pl.pallas_call(
        hidden_kernel,
        out_shape=jax.ShapeDtypeStruct(parts.shape[1:], jnp.bfloat16),
        in_specs=in_vmem(2),
        out_specs=pl.BlockSpec(memory_space=pltpu.VMEM),
        scratch_shapes=[pltpu.VMEM((ranks, slot_rows // ranks, values.shape[2]), jnp.float32)],
        compiler_params=kernel_params(12),
        name="hidden",
    )(parts, values)


def gate_up_kernel(
    hidden_ref, gain_ref, gate_ref, up_ref, out_ref, held, scaled, gains, own, sems
):
    steps, _, chunk = held.shape
    half = steps // 2
    requests, width = hidden_ref.shape
    units = gate_ref.shape[1]
    ranks = lax.axis_size("tp")
    groups = width // 128
    copies = stream(
        [w.at[:, pl.ds(k * chunk, chunk)] for w in (gate_ref, up_ref) for k in range(half)],
        held,
        sems,
    )
    gains[...] = gain_ref[...].astype(jnp.float32)
    base = lax.axis_index("tp") * groups
    square = jnp.zeros((requests, 128), jnp.float32)
    for g in range(groups):
        at = slice(g * 128, (g + 1) * 128)
        x = hidden_ref[:, at].astype(jnp.float32)
        square = square + x * x
        scaled[:, at] = (x * gains[pl.ds(base + g, 1), :]).astype(scaled.dtype)
    square = jnp.sum(square, 1, keepdims=True)
    top = square.astype(jnp.bfloat16).astype(jnp.float32)
    middle = (square - top).astype(jnp.bfloat16).astype(jnp.float32)
    low = square - top - middle
    lane = lax.broadcasted_iota(jnp.int32, (requests, 128), 1)
    digits = jnp.where(lane == 0, top, jnp.where(lane == 1, middle, jnp.where(lane == 2, low, 0.0)))
    out_ref[:, 2 * units : 2 * units + 128] = digits.astype(out_ref.dtype)

    rows = own.shape[0]
    per_rank = rows // ranks
    start = pl.multiple_of(lax.axis_index("dp") * rows, 16)
    own[...] = hidden_ref[pl.ds(start, rows), :].astype(jnp.float32)
    share = requests // ranks
    high = share // per_rank
    for t in range(ranks):
        for block in range((groups + high - 1) // high):
            pieces = []
            for g in range(block * high, (block + 1) * high):
                g = min(g, groups - 1)
                pieces.append(
                    own[t * per_rank : (t + 1) * per_rank, g * 128 : (g + 1) * 128]
                )
            column = 2 * units + 128 * (1 + block)
            out_ref[t * share : (t + 1) * share, column : column + 128] = jnp.concatenate(
                pieces, 0
            ).astype(out_ref.dtype)

    for k in range(steps):
        copies[k].wait()
        term = jnp.dot(scaled[...], held[k], preferred_element_type=jnp.float32)
        out_ref[:, k * chunk : (k + 1) * chunk] = term.astype(out_ref.dtype)


def gate_up(hidden, gain, w_gate, w_up, own_rows, columns):
    requests, width = hidden.shape
    units = w_gate.shape[1]
    chunk = units // 3
    return pl.pallas_call(
        gate_up_kernel,
        out_shape=jax.ShapeDtypeStruct((requests, columns), jnp.bfloat16),
        in_specs=in_vmem(2) + in_any(2),
        out_specs=pl.BlockSpec(memory_space=pltpu.VMEM),
        scratch_shapes=[
            pltpu.VMEM((6, width, chunk), w_gate.dtype),
            pltpu.VMEM((requests, width), jnp.bfloat16),
            pltpu.VMEM(gain.shape, jnp.float32),
            pltpu.VMEM((own_rows, width), jnp.float32),
            pltpu.SemaphoreType.DMA((6,)),
        ],
        compiler_params=kernel_params(32),
        name="gate_up",
    )(hidden, gain, w_gate, w_up)


def inner_kernel(model, parts_ref, out_ref, slots_ref):
    ranks = parts_ref.shape[0]
    units = out_ref.shape[1]

    def total(at):
        return sum(parts_ref[s, :, at].astype(jnp.float32) for s in range(ranks))

    square = jnp.sum(total(slice(2 * units, 2 * units + 128)), 1, keepdims=True)
    factor = lax.rsqrt(square / model + 1e-06)
    for at in range(0, units, 128):
        gate = total(slice(at, at + 128)) * factor
        up = total(slice(units + at, units + at + 128)) * factor
        out_ref[:, at : at + 128] = (gate / (1.0 + jnp.exp(-gate)) * up).astype(out_ref.dtype)
    slots_ref[...] = parts_ref[:, :, 2 * units + 128 :]


def make_inner(parts, units, model):
    ranks, rows, columns = parts.shape
    return pl.pallas_call(
        functools.partial(inner_kernel, model),
        out_shape=[
            jax.ShapeDtypeStruct((rows, units), jnp.bfloat16),
            jax.ShapeDtypeStruct((ranks, rows, columns - 2 * units - 128), jnp.bfloat16),
        ],
        in_specs=in_vmem(1),
        out_specs=in_vmem(2),
        compiler_params=kernel_params(12),
        name="inner",
    )(parts)


def down_kernel(inner_ref, w_ref, out_ref, held, total, sems):
    steps, depth, width = held.shape
    copies = stream([w_ref.at[pl.ds(k * depth, depth), :] for k in range(steps)], held, sems)
    for k in range(steps):
        copies[k].wait()
        term = jnp.dot(
            inner_ref[:, k * depth : (k + 1) * depth], held[k], preferred_element_type=jnp.float32
        )
        if k == 0:
            total[...] = term
        else:
            total[...] += term
    groups = width // 128
    per_rank = out_ref.shape[1] // groups
    for d in range(out_ref.shape[0]):
        pieces = [
            total[d * per_rank : (d + 1) * per_rank, g * 128 : (g + 1) * 128]
            for g in range(groups)
        ]
        out_ref[d] = jnp.concatenate(pieces, 0).astype(out_ref.dtype)


def project_down(inner, w_down, ranks):
    requests, units = inner.shape
    width = w_down.shape[1]
    return pl.pallas_call(
        down_kernel,
        out_shape=jax.ShapeDtypeStruct(
            (ranks, requests // ranks * (width // 128), 128), jnp.bfloat16
        ),
        in_specs=in_vmem(1) + in_any(1),
        out_specs=pl.BlockSpec(memory_space=pltpu.VMEM),
        scratch_shapes=[
            pltpu.VMEM((3, units // 3, width), w_down.dtype),
            pltpu.VMEM((requests, width), jnp.float32),
            pltpu.SemaphoreType.DMA((3,)),
        ],
        compiler_params=kernel_params(20),
        name="project_down",
    )(inner, w_down)


def layer_kernel(parts_ref, slots_ref, out_ref, total, hidden):
    ranks = slots_ref.shape[0]
    per_rank, model = out_ref.shape
    groups = model // ranks // 128
    high = slots_ref.shape[1] // per_rank
    hidden[...] = slots_ref[...].astype(jnp.float32)
    for t in range(ranks):
        ffn = sum(
            parts_ref[d, :, :].astype(jnp.float32) for d in range(t, parts_ref.shape[0], ranks)
        )
        for g in range(groups):
            row = (g % high) * per_rank
            column = (g // high) * 128
            at = (t * groups + g) * 128
            total[:, at : at + 128] = (
                ffn[g * per_rank : (g + 1) * per_rank, :]
                + hidden[t, row : row + per_rank, column : column + 128]
            )
    out_ref[...] = total[...].astype(out_ref.dtype)


def make_layer(parts, slots, per_rank, model):
    return pl.pallas_call(
        layer_kernel,
        out_shape=jax.ShapeDtypeStruct((per_rank, model), jnp.bfloat16),
        in_specs=in_vmem(2),
        out_specs=pl.BlockSpec(memory_space=pltpu.VMEM),
        scratch_shapes=[
            pltpu.VMEM((per_rank, model), jnp.float32),
            pltpu.VMEM(slots.shape, jnp.float32),
        ],
        compiler_params=kernel_params(12),
        name="layer",
    )(parts, slots)


def round_up(value, step):
    return (value + step - 1) // step * step


def swap(parts, axes):
    return lax.all_to_all(parts, axes, split_axis=0, concat_axis=0, tiled=True)


def local(
    residual, queries, paged_latent_cache, lengths, w_uv, w_o, norm_gain, w_gate, w_up, w_down
):
    ranks_dp = lax.axis_size("dp")
    ranks_tp = lax.axis_size("tp")
    ranks = ranks_dp * ranks_tp
    per_rank, model = residual.shape
    requests = per_rank * ranks
    row_length = paged_latent_cache.shape[1]
    heads_all = queries.shape[1] // row_length
    heads_here = w_uv.shape[0]
    units = w_gate.shape[1]
    width = w_o.shape[1]
    groups = width // 128

    query = queries.reshape(per_rank, heads_all, row_length)
    latent = swap(attend(lengths, query, paged_latent_cache.T, ranks), ("dp", "tp"))

    across = heads_here * w_uv.shape[2] // 128
    slot_rows = ranks_tp * round_up(per_rank * ((groups + across - 1) // across), 16)
    values = head_values(latent.reshape(requests * heads_here, C), w_uv, residual, slot_rows)
    values = lax.all_gather(values, "tp", axis=0)
    attn = project_out(values, w_o, requests)
    attn = swap(attn.reshape(ranks_dp, requests // ranks_dp, width), "dp")
    hidden = make_hidden(attn, values, slot_rows)
    hidden = lax.all_gather(hidden, "dp", axis=0, tiled=True)

    share = requests // ranks_tp
    high = share // per_rank
    columns = 2 * units + 128 + 128 * ((groups + high - 1) // high)
    both = gate_up(
        hidden, norm_gain.reshape(-1, 128), w_gate, w_up, requests // ranks_dp, columns
    )
    both = swap(both.reshape(ranks_tp, share, columns), "tp")
    inner, slots = make_inner(both, units, model)
    inner = lax.all_gather(inner, "tp", axis=0, tiled=True)
    ffn = swap(project_down(inner, w_down, ranks), ("dp", "tp"))
    return make_layer(ffn, slots, per_rank, model)


def solution(mesh):
    placed = (
        P(("dp", "tp"), None),
        P(("dp", "tp"), None),
        P(("dp", "tp"), None),
        P(),
        P(("dp", "tp"), None, None),
        P("dp", "tp"),
        P(),
        P("tp", "dp"),
        P("tp", "dp"),
        P("dp", "tp"),
    )
    return jax.shard_map(
        local, mesh=mesh, in_specs=placed, out_specs=P(("dp", "tp"), None), check_vma=False
    )
```

time: 175 us -> 164 us (0.937)
  blocking collectives: 81.6 us -> 130 us
  waiting for transfers between devices: 30.7 us -> 0 us
  starting transfers between devices: 23 us -> 0 us
  matrix products: 20 us -> 0 us
  Pallas kernels: 10.3 us -> 21.8 us
  local copies, waits for them, and re-layouts: 7.79 us -> 11.2 us
    all_to_all x2 -> x4, blocking collectives: 41 us -> 86.9 us  [swap(): return lax.all_to_all(parts, axes, split_axis=0, concat_axis=0, tiled=True)]
    all_to_all x3 -> x0, waiting for transfers between devices: 30.7 us -> none  [the longest x2 17.9 us: scatter_sum(): lax.all_to_all(pieces, axis, split_axis=0, concat_axis=0, tiled=True)]
    dot_general x5 -> x0, matrix products: 20 us -> none  [the longest x1 5.4 us: local(): jnp.dot(inner, w_down, preferred_element_type=jnp.float32)]
    all_to_all x3 -> x0, starting transfers between devices: 16.9 us -> none  [the longest x1 9.81 us: local(): lax.all_to_all(latent_out, ('dp', 'tp'), split_axis=1, concat_axis=0, til...]
    pallas_call x1 -> x8, Pallas kernels: 10.3 us -> 21.8 us  [the longest x1 10.1 us: attend(): pl.pallas_call(attention_kernel, out_shape=jax.ShapeDtypeStruct((ranks, n...]
    unnamed x3 -> x20, local copies, waits for them, and re-layouts: 0.63 us -> 9.46 us
    ppermute x3 -> x0, starting transfers between devices: 6.11 us -> none  [exchange_columns(): lax.ppermute(piece, axis, [(k, (k + shift) % size) for k in range(size)])]
    all_gather x2, blocking collectives: 24.8 us -> 27.2 us  [the longest x1 18.4 us: local(): values = lax.all_gather(values, 'tp', axis=0)]
  transfers between devices with their start and end apart: 6 -> 0, of which waited for: 3 -> 0; matrix products, arithmetic and copies ran while one was open for 6% -> 0% of each run, Pallas kernels for 6% -> 0%
where the time goes in v4:
time: 164 us; the launch traced here: 163 us
  blocking collectives  130 us (79%)
  Pallas kernels  21.8 us (13%)
  local copies, waits for them, and re-layouts  11.2 us (7%)
    all_to_all x4, blocking collectives, swap(): return lax.all_to_all(parts, axes, split_axis=0, concat_axis=0, tiled=True)  86.9 us
    all_gather x1, blocking collectives, local(): values = lax.all_gather(values, 'tp', axis=0)  18.4 us
    all_gather x1, blocking collectives, local(): inner = lax.all_gather(inner, 'tp', axis=0, tiled=True)  16.3 us
    pallas_call x1, Pallas kernels, attend(): pl.pallas_call(attention_kernel, out_shape=jax.ShapeDtypeStruct((ranks, n...  10.1 us
    unnamed x20, local copies, waits for them, and re-layouts  9.46 us
    all_gather x1, blocking collectives, local(): hidden = lax.all_gather(hidden, 'dp', axis=0, tiled=True)  8.78 us
    pallas_call x1, Pallas kernels, gate_up(): pl.pallas_call(gate_up_kernel, out_shape=jax.ShapeDtypeStruct((requests,...  5.26 us

profile of v4, /device:TPU:0, one launch (start us, length us, event | category | flops | bytes accessed | tf_op | source)
XLA Modules:
  0.0 163.5 jit_solution(485637577684699131)
XLA Ops:
  0.0 1.7 %reshape.15.q_ref = bf16[4,128,576]{2,1,0:T(8,128)(2,1)S(1)} reshape(bf16[4,73728]{1,0:T(4,128)(2,1)} %param.11) | data formatting | bytes 1179648 | tf_op jit(solution)/shard_map/reshape | solution.py:513
  1.7 0.0 copy-start
  1.8 5.7 %copy-done = bf16[14336,576]{0,1:T(8,128)(2,1)S(1)} copy-done((bf16[14336,576]{0,1:T(8,128)(2,1)S(1)}, bf16[14336,576]{0,1:T(8,128)(2,1)}, u32[]{:S(2)}) %copy-start) | copy-done | bytes 16515096
  7.4 0.7 copy-done.7
  8.1 10.1 %attention.1 = bf16[32,16,512]{2,1,0:T(8,128)(2,1)S(1)} custom-call(s32[128]{0:T(128)S(1)} %copy-done.7, bf16[4,128,576]{2,1,0:T(8,128)(2,1)S(1)} %reshape.15.q_ref, bf16[576,14336]{1,0:T(8,128)(2,1)S(1)} %bitcast.6), custom_call_target="tpu_custom_call" | custom-call | flops 3992977408 | bytes 16515072 | tf_op jit(solution)/shard_map/attention/pallas_call | solution.py:158
  18.2 0.0 copy-start.1
  18.2 25.2 %all_to_all.20 = bf16[32,16,512]{2,1,0:T(8,128)(2,1)S(1)} all-to-all(bf16[32,16,512]{2,1,0:T(8,128)(2,1)S(1)} %attention.1), channel_id=1, replica_groups=mesh['dp'=8,'tp'=4] {'dp','tp'}, dimensions={0} | all-to-all | bytes 1048576 | tf_op jit(solution)/shard_map/all_to_all | solution.py:495
  43.4 0.0 copy-done.4
  43.4 0.8 head_values.1
  44.2 18.4 %all-gather = bf16[768,512]{1,0:T(8,128)(2,1)S(1)} all-gather(bf16[192,512]{1,0:T(8,128)(2,1)S(1)} %head_values.1), channel_id=2, replica_groups=mesh['dp'=8,'tp'=4] {'tp'}, dimensions={0}, use_global_device_ids=true | all-gather | bytes 983040 | tf_op jit(solution)/shard_map/all_gather | solution.py:519
  62.6 3.1 %copy-done.3 = bf16[2048,1792]{1,0:T(8,128)(2,1)S(1)} copy-done((bf16[2048,1792]{1,0:T(8,128)(2,1)S(1)}, bf16[2048,1792]{1,0:T(8,128)(2,1)}, u32[]{:S(2)}) %copy-start.3) | copy-done | bytes 7340056
  65.7 2.0 %project_out.1 = bf16[128,1792]{1,0:T(8,128)(2,1)S(1)} custom-call(bf16[4,192,512]{2,1,0:T(8,128)(2,1)S(1)} %bitcast.9, bf16[2048,1792]{1,0:T(8,128)(2,1)S(1)} %copy-done.3), custom_call_target="tpu_custom_call" | custom-call | tf_op jit(solution)/shard_map/project_out/pallas_call | solution.py:253
  67.7 11.8 %all_to_all.21.parts_ref = bf16[8,16,1792]{2,1,0:T(8,128)(2,1)S(1)} all-to-all(bf16[8,16,1792]{2,1,0:T(8,128)(2,1)S(1)} %bitcast.13), channel_id=1, replica_groups=mesh['dp'=8,'tp'=4] {'dp'}, dimensions={0} | all-to-all | bytes 917504 | tf_op jit(solution)/shard_map/all_to_all | solution.py:495
  79.5 0.1 hidden.1
  79.6 8.8 %all_gather.14.hidden_ref = bf16[128,1792]{1,0:T(8,128)(2,1)S(1)} all-gather(bf16[16,1792]{1,0:T(8,128)(2,1)S(1)} %hidden.1), channel_id=1, replica_groups=mesh['dp'=8,'tp'=4] {'dp'}, dimensions={0}, use_global_device_ids=true | all-gather | bytes 516096 | tf_op jit(solution)/shard_map/all_gather | solution.py:523
  88.3 0.0 copy-done.2
  88.4 0.0 slice-start.1
  88.4 5.3 %gate_up.1 = bf16[128,4992]{1,0:T(8,128)(2,1)S(1)} custom-call(bf16[128,1792]{1,0:T(8,128)(2,1)S(1)} %all_gather.14.hidden_ref, bf16[56,128]{1,0:T(8,128)(2,1)S(1)} %bitcast.14, bf16[1792,2304]{1,0:T(8,128)(2,1)S(1)} %copy-done.1, bf16[1792,2304]{1,0:T(8,128)(2,1)S(1)} %copy-done.2), custom_call_target="tpu_custom_call" | custom-call | tf_op jit(solution)/shard_map/gate_up/pallas_call | solution.py:364
  93.6 34.8 %all_to_all.22.parts_ref = bf16[4,32,4992]{2,1,0:T(8,128)(2,1)S(1)} all-to-all(bf16[4,32,4992]{2,1,0:T(8,128)(2,1)S(1)} %bitcast.11), channel_id=1, replica_groups=mesh['dp'=8,'tp'=4] {'tp'}, dimensions={0} | all-to-all | bytes 2555904 | tf_op jit(solution)/shard_map/all_to_all | solution.py:495
  128.5 0.3 inner.1
  128.7 16.3 %all_gather.15.inner_ref = bf16[128,2304]{1,0:T(8,128)(2,1)S(1)} all-gather(bf16[32,2304]{1,0:T(8,128)(2,1)S(1)} %get-tuple-element.7), channel_id=1, replica_groups=mesh['dp'=8,'tp'=4] {'tp'}, dimensions={0}, use_global_device_ids=true | all-gather | bytes 737280 | tf_op jit(solution)/shard_map/all_gather | solution.py:533
  145.0 2.6 %project_down.1 = bf16[32,56,128]{2,1,0:T(8,128)(2,1)S(1)} custom-call(bf16[128,2304]{1,0:T(8,128)(2,1)S(1)} %all_gather.15.inner_ref, bf16[2304,1792]{1,0:T(8,128)(2,1)S(1)} %bitcast.8), custom_call_target="tpu_custom_call" | custom-call | tf_op jit(solution)/shard_map/project_down/pallas_call | solution.py:437
  147.7 15.1 %all_to_all.23.parts_ref = bf16[32,56,128]{2,1,0:T(8,128)(2,1)S(1)} all-to-all(bf16[32,56,128]{2,1,0:T(8,128)(2,1)S(1)} %project_down.1), channel_id=1, replica_groups=mesh['dp'=8,'tp'=4] {'dp','tp'}, dimensions={0} | all-to-all | bytes 917504 | tf_op jit(solution)/shard_map/all_to_all | solution.py:495
  162.7 0.7 layer.1
  (13 shorter events, 0.0 us)
Async XLA Ops:
  1.7 5.7 %copy-start = (bf16[14336,576]{0,1:T(8,128)(2,1)S(1)}, bf16[14336,576]{0,1:T(8,128)(2,1)}, u32[]{:S(2)}) copy-start(bf16[14336,576]{0,1:T(8,128)(2,1)} %param.12) | copy-start | bytes 49545220
  7.4 0.7 copy-start.7
  8.1 35.3 %copy-start.4 = (bf16[4,512,128]{2,1,0:T(8,128)(2,1)S(1)}, bf16[4,512,128]{2,1,0:T(8,128)(2,1)}, u32[]{:S(2)}) copy-start(bf16[4,512,128]{2,1,0:T(8,128)(2,1)} %w_ref.3) | copy-start | bytes 1572868
  8.1 35.3 %copy-start.5 = (bf16[4,7168]{1,0:T(4,128)(2,1)S(1)}, bf16[4,7168]{1,0:T(4,128)(2,1)}, u32[]{:S(2)}) copy-start(bf16[4,7168]{1,0:T(4,128)(2,1)} %residual_ref.1) | copy-start | bytes 172036
  8.1 80.3 %copy-start.2 = (bf16[1792,2304]{1,0:T(8,128)(2,1)S(1)}, bf16[1792,2304]{1,0:T(8,128)(2,1)}, u32[]{:S(2)}) copy-start(bf16[1792,2304]{1,0:T(8,128)(2,1)} %up_ref.1) | copy-start | bytes 24772612
  8.1 80.3 %copy-start.6 = (bf16[7168]{0:T(1024)(128)(2,1)S(1)}, bf16[7168]{0:T(1024)(128)(2,1)}, u32[]{:S(2)}) copy-start(bf16[7168]{0:T(1024)(128)(2,1)} %param.16) | copy-start | bytes 43012
  18.2 70.1 %copy-start.1 = (bf16[1792,2304]{1,0:T(8,128)(2,1)S(1)}, bf16[1792,2304]{1,0:T(8,128)(2,1)}, u32[]{:S(2)}) copy-start(bf16[1792,2304]{1,0:T(8,128)(2,1)} %gate_ref.1) | copy-start | bytes 24772612
  62.6 3.1 %copy-start.3 = (bf16[2048,1792]{1,0:T(8,128)(2,1)S(1)}, bf16[2048,1792]{1,0:T(8,128)(2,1)}, u32[]{:S(2)}) copy-start(bf16[2048,1792]{1,0:T(8,128)(2,1)} %w_ref.4) | copy-start | bytes 22020100
  88.3 56.7 %slice-start = ((s8[8257536]{0:T(1024)(128)(4,1)}), s8[4194304]{0:T(1024)(128)(4,1)S(1)}, s32[]{:S(2)}) async-start(s8[8257536]{0:T(1024)(128)(4,1)} %bitcast.7), calls=%async_computation.4 | async-start | bytes 8388608
  88.4 56.7 %slice-start.1 = ((s8[8257536]{0:T(1024)(128)(4,1)}), s8[4063232]{0:T(1024)(128)(4,1)S(1)}, s32[]{:S(2)}) async-start(s8[8257536]{0:T(1024)(128)(4,1)} %bitcast.7), calls=%async_computation.5 | async-start | bytes 8126464

commit v5 on v4

--- a/solution.py
+++ b/solution.py
@@ -24,6 +24,10 @@
     held,
     score0,
     score1,
+    weight0,
+    weight1,
+    keep0,
+    keep1,
     acc,
     done,
     best,
@@ -34,10 +38,9 @@
     last,
     sems,
 ):
-    nreq = q_ref.shape[0]
-    tiles = held.shape[0]
+    nreq, heads, _ = q_ref.shape
     tile = held.shape[2]
-    heads = q_ref.shape[1]
+    factor = score_scale * log2_e
 
     rank = lax.axis_index("dp") * lax.axis_size("tp") + lax.axis_index("tp")
     begin = jnp.int32(0)
@@ -61,81 +64,85 @@
     def _(i):
         copy(i).start()
 
-    def reset():
-        acc[...] = jnp.zeros_like(acc)
-        best[...] = jnp.full_like(best, negative)
-        mass[...] = jnp.zeros_like(mass)
+    acc[...] = jnp.zeros_like(acc)
+    best[...] = jnp.full_like(best, negative)
+    mass[...] = jnp.zeros_like(mass)
+    weight1[...] = jnp.zeros_like(weight1)
+    keep1[...] = jnp.ones_like(keep1)
+
+    def advance(p, r, i):
+        live = p + 1 < pairs
+        step = (i == last[r]) & live
+        nr = jnp.where(step, r + 1, r)
+        ni = jnp.where(step, first[nr], jnp.where(live, i + 1, i))
+        return nr, ni, live
+
+    def fetch(r, i, live):
+        fresh = live & ((r == 0) | (i > last[jnp.maximum(r - 1, 0)]))
+
+        @pl.when(fresh)
+        def _():
+            copy(i).wait()
 
     def scores(r, i, live, target):
         begin_at = jnp.where(live, lo[r], 0)
         end_at = jnp.where(live, hi[r], 0)
         s = jnp.dot(q_ref[r], held[i], preferred_element_type=jnp.float32)
         token = i * tile + lax.broadcasted_iota(jnp.int32, (1, tile), 1)
-        s = jnp.where((token >= begin_at) & (token < end_at), s, negative)
-        target[...] = s
-
-    def advance(p, r, i):
-        ends = i == last[r]
-        live = p + 1 < pairs
-        nr = jnp.where(ends & live, r + 1, r)
-        ni = jnp.where(ends, jnp.where(live, first[nr], i), i + 1)
-        return nr, ni, live
-
-    def fetch(i, r, live):
-        fresh = live & ((r == 0) | (i > last[jnp.maximum(r - 1, 0)]))
-
-        @pl.when(fresh)
-        def _():
-            copy(i).wait()
-
-    def absorb(r, i, live, source):
-        factor = score_scale * log2_e
+        target[...] = jnp.where((token >= begin_at) & (token < end_at), s, negative)
+
+    def soften(r, source, weights, keeps):
         s = source[...]
-        old = best[...]
+        old = best[r]
         new = jnp.maximum(old, jnp.max(s, axis=1, keepdims=True))
         weight = jnp.exp2((s - new[:, :1]) * factor)
         keep = jnp.exp2((old - new) * factor)
         part = weight[:, :128]
         for at in range(128, tile, 128):
             part = part + weight[:, at : at + 128]
-        mass[...] = mass[...] * keep + part
-        best[...] = new
+        mass[r] = mass[r] * keep + part
+        best[r] = new
+        weights[...] = weight.astype(weights.dtype)
+        keeps[...] = keep.T[:8, :]
+
+    def gather(r, i, weights, keeps):
         values = lax.dot_general(
             held[i, :C, :],
-            weight.astype(jnp.bfloat16),
+            weights[...],
             (((1,), (1,)), ((), ())),
             preferred_element_type=jnp.float32,
         )
-        acc[...] = acc[...] * keep.T[:1, :] + values
-
-    def close(r, i, live):
-        @pl.when(live & (i == last[r]))
-        def _():
-            total = jnp.sum(mass[...], axis=1, keepdims=True)
-            done[r] = acc[...].T / total
-            reset()
-
-    reset()
-    fetch(jnp.int32(0), jnp.int32(0), pairs > 0)
-    scores(jnp.int32(0), jnp.int32(0), pairs > 0, score0)
+        acc[r] = acc[r] * keeps[:1, :] + values
+
+    zero = jnp.int32(0)
+    fetch(zero, zero, pairs > 0)
+    scores(zero, zero, pairs > 0, score0)
 
     def step(j, carry):
-        r, i, live = carry
+        r0, i0, r1, i1 = carry
         p = 2 * j
-        for now, later in ((score0, score1), (score1, score0)):
-            nr, ni, nlive = advance(p, r, i)
-            fetch(ni, nr, nlive)
-            scores(nr, ni, nlive, later)
-            absorb(r, i, live, now)
-            close(r, i, live)
-            r, i, live, p = nr, ni, nlive, p + 1
-        return r, i, live
-
-    lax.fori_loop(0, (pairs + 1) // 2, step, (jnp.int32(0), jnp.int32(0), pairs > 0))
+        r2, i2, live2 = advance(p, r1, i1)
+        r3, i3, live3 = advance(p + 1, r2, i2)
+        fetch(r2, i2, live2)
+        fetch(r3, i3, live3)
+        gather(r0, i0, weight1, keep1)
+        scores(r2, i2, live2, score1)
+        soften(r1, score0, weight0, keep0)
+        gather(r1, i1, weight0, keep0)
+        scores(r3, i3, live3, score0)
+        soften(r2, score1, weight1, keep1)
+        return r2, i2, r3, i3
+
+    r0, i0, _, _ = lax.fori_loop(0, (pairs + 1) // 2, step, (zero, zero, zero, zero))
+    gather(r0, i0, weight1, keep1)
+
     share = heads // out_ref.shape[0]
-    for d in range(out_ref.shape[0]):
-        rows = [done[r, d * share : (d + 1) * share, :] for r in range(nreq)]
-        out_ref[d] = jnp.concatenate(rows, 0).astype(out_ref.dtype)
+    for r in range(nreq):
+        total = jnp.sum(mass[r], axis=1, keepdims=True)
+        score0[:, :C] = acc[r].T / total
+        for d in range(out_ref.shape[0]):
+            done[d, r * share : (r + 1) * share, :] = score0[d * share : (d + 1) * share, :C]
+    out_ref[...] = done[...].astype(out_ref.dtype)
 
 
 def kernel_params(limit):
@@ -146,8 +153,8 @@
     return [pl.BlockSpec(memory_space=pltpu.VMEM)] * count
 
 
-def in_any(count):
-    return [pl.BlockSpec(memory_space=pl.ANY)] * count
+def fetched(weight):
+    return pltpu.with_memory_space_constraint(weight, pltpu.VMEM)
 
 
 def attend(lengths, queries, cache_t, ranks):
@@ -158,30 +165,36 @@
     return pl.pallas_call(
         attention_kernel,
         out_shape=jax.ShapeDtypeStruct((ranks, nreq * heads // ranks, C), jnp.bfloat16),
-        in_specs=[pl.BlockSpec(memory_space=pltpu.SMEM)] + in_vmem(1) + in_any(1),
+        in_specs=[pl.BlockSpec(memory_space=pltpu.SMEM)]
+        + in_vmem(1)
+        + [pl.BlockSpec(memory_space=pltpu.HBM)],
         out_specs=pl.BlockSpec(memory_space=pltpu.VMEM),
         scratch_shapes=[
             pltpu.VMEM((tiles, width, tile), jnp.bfloat16),
             pltpu.VMEM((heads, tile), jnp.float32),
             pltpu.VMEM((heads, tile), jnp.float32),
-            pltpu.VMEM((C, heads), jnp.float32),
-            pltpu.VMEM((nreq, heads, C), jnp.float32),
-            pltpu.VMEM((heads, 128), jnp.float32),
-            pltpu.VMEM((heads, 128), jnp.float32),
+            pltpu.VMEM((heads, tile), jnp.bfloat16),
+            pltpu.VMEM((heads, tile), jnp.bfloat16),
+            pltpu.VMEM((8, heads), jnp.float32),
+            pltpu.VMEM((8, heads), jnp.float32),
+            pltpu.VMEM((nreq, C, heads), jnp.float32),
+            pltpu.VMEM((ranks, nreq * heads // ranks, C), jnp.float32),
+            pltpu.VMEM((nreq, heads, 128), jnp.float32),
+            pltpu.VMEM((nreq, heads, 128), jnp.float32),
             pltpu.SMEM((nreq,), jnp.int32),
             pltpu.SMEM((nreq,), jnp.int32),
             pltpu.SMEM((nreq,), jnp.int32),
             pltpu.SMEM((nreq,), jnp.int32),
             pltpu.SemaphoreType.DMA((tiles,)),
         ],
-        compiler_params=kernel_params(28),
+        compiler_params=kernel_params(26),
         cost_estimate=pl.CostEstimate(
             flops=2 * heads * tokens * (width + C),
             bytes_accessed=2 * tokens * width,
             transcendentals=heads * tokens,
         ),
         name="attention",
-    )(lengths, queries, cache_t)
+    )(lengths, queries, pltpu.with_memory_space_constraint(cache_t, pltpu.HBM))
 
 
 def head_values_kernel(latent_ref, w_ref, residual_ref, out_ref, values, slots):
@@ -226,20 +239,15 @@
     )(latent, w_uv, residual)
 
 
-def stream(sources, target, sems):
-    copies = [pltpu.make_async_copy(s, target.at[k], sems.at[k]) for k, s in enumerate(sources)]
-    for copy in copies:
-        copy.start()
-    return copies
-
-
-def output_kernel(values_ref, w_ref, out_ref, held, total, sems):
-    steps, depth, _ = held.shape
+def output_kernel(values_ref, w_ref, out_ref, total):
+    steps, _, depth = values_ref.shape
     requests = out_ref.shape[0]
-    copies = stream([w_ref.at[pl.ds(k * depth, depth), :] for k in range(steps)], held, sems)
     for k in range(steps):
-        copies[k].wait()
-        term = jnp.dot(values_ref[k, :requests, :], held[k], preferred_element_type=jnp.float32)
+        term = jnp.dot(
+            values_ref[k, :requests, :],
+            w_ref[k * depth : (k + 1) * depth, :],
+            preferred_element_type=jnp.float32,
+        )
         if k == 0:
             total[...] = term
         else:
@@ -248,21 +256,16 @@
 
 
 def project_out(values, w_o, requests):
-    steps, _, depth = values.shape
     width = w_o.shape[1]
     return pl.pallas_call(
         output_kernel,
         out_shape=jax.ShapeDtypeStruct((requests, width), jnp.bfloat16),
-        in_specs=in_vmem(1) + in_any(1),
-        out_specs=pl.BlockSpec(memory_space=pltpu.VMEM),
-        scratch_shapes=[
-            pltpu.VMEM((steps, depth, width), w_o.dtype),
-            pltpu.VMEM((requests, width), jnp.float32),
-            pltpu.SemaphoreType.DMA((steps,)),
-        ],
-        compiler_params=kernel_params(20),
+        in_specs=in_vmem(2),
+        out_specs=pl.BlockSpec(memory_space=pltpu.VMEM),
+        scratch_shapes=[pltpu.VMEM((requests, width), jnp.float32)],
+        compiler_params=kernel_params(12),
         name="project_out",
-    )(values, w_o)
+    )(values, fetched(w_o))
 
 
 def hidden_kernel(parts_ref, values_ref, out_ref, slots):
@@ -303,19 +306,12 @@
 
 
 def gate_up_kernel(
-    hidden_ref, gain_ref, gate_ref, up_ref, out_ref, held, scaled, gains, own, sems
+    hidden_ref, gain_ref, gate_ref, up_ref, out_ref, scaled, gains, own
 ):
-    steps, _, chunk = held.shape
-    half = steps // 2
     requests, width = hidden_ref.shape
     units = gate_ref.shape[1]
     ranks = lax.axis_size("tp")
     groups = width // 128
-    copies = stream(
-        [w.at[:, pl.ds(k * chunk, chunk)] for w in (gate_ref, up_ref) for k in range(half)],
-        held,
-        sems,
-    )
     gains[...] = gain_ref[...].astype(jnp.float32)
     base = lax.axis_index("tp") * groups
     square = jnp.zeros((requests, 128), jnp.float32)
@@ -351,31 +347,30 @@
                 pieces, 0
             ).astype(out_ref.dtype)
 
-    for k in range(steps):
-        copies[k].wait()
-        term = jnp.dot(scaled[...], held[k], preferred_element_type=jnp.float32)
-        out_ref[:, k * chunk : (k + 1) * chunk] = term.astype(out_ref.dtype)
+    chunk = units // 3
+    for k, w_ref in enumerate((gate_ref, up_ref)):
+        for at in range(0, units, chunk):
+            term = jnp.dot(
+                scaled[...], w_ref[:, at : at + chunk], preferred_element_type=jnp.float32
+            )
+            out_ref[:, k * units + at : k * units + at + chunk] = term.astype(out_ref.dtype)
 
 
 def gate_up(hidden, gain, w_gate, w_up, own_rows, columns):
     requests, width = hidden.shape
-    units = w_gate.shape[1]
-    chunk = units // 3
     return pl.pallas_call(
         gate_up_kernel,
         out_shape=jax.ShapeDtypeStruct((requests, columns), jnp.bfloat16),
-        in_specs=in_vmem(2) + in_any(2),
+        in_specs=in_vmem(4),
         out_specs=pl.BlockSpec(memory_space=pltpu.VMEM),
         scratch_shapes=[
-            pltpu.VMEM((6, width, chunk), w_gate.dtype),
             pltpu.VMEM((requests, width), jnp.bfloat16),
             pltpu.VMEM(gain.shape, jnp.float32),
             pltpu.VMEM((own_rows, width), jnp.float32),
-            pltpu.SemaphoreType.DMA((6,)),
         ],
-        compiler_params=kernel_params(32),
+        compiler_params=kernel_params(12),
         name="gate_up",
-    )(hidden, gain, w_gate, w_up)
+    )(hidden, gain, fetched(w_gate), fetched(w_up))
 
 
 def inner_kernel(model, parts_ref, out_ref, slots_ref):
@@ -409,18 +404,9 @@
     )(parts)
 
 
-def down_kernel(inner_ref, w_ref, out_ref, held, total, sems):
-    steps, depth, width = held.shape
-    copies = stream([w_ref.at[pl.ds(k * depth, depth), :] for k in range(steps)], held, sems)
-    for k in range(steps):
-        copies[k].wait()
-        term = jnp.dot(
-            inner_ref[:, k * depth : (k + 1) * depth], held[k], preferred_element_type=jnp.float32
-        )
-        if k == 0:
-            total[...] = term
-        else:
-            total[...] += term
+def down_kernel(inner_ref, w_ref, out_ref, total):
+    width = w_ref.shape[1]
+    total[...] = jnp.dot(inner_ref[...], w_ref[...], preferred_element_type=jnp.float32)
     groups = width // 128
     per_rank = out_ref.shape[1] // groups
     for d in range(out_ref.shape[0]):
@@ -439,16 +425,12 @@
         out_shape=jax.ShapeDtypeStruct(
             (ranks, requests // ranks * (width // 128), 128), jnp.bfloat16
         ),
-        in_specs=in_vmem(1) + in_any(1),
-        out_specs=pl.BlockSpec(memory_space=pltpu.VMEM),
-        scratch_shapes=[
-            pltpu.VMEM((3, units // 3, width), w_down.dtype),
-            pltpu.VMEM((requests, width), jnp.float32),
-            pltpu.SemaphoreType.DMA((3,)),
-        ],
-        compiler_params=kernel_params(20),
+        in_specs=in_vmem(2),
+        out_specs=pl.BlockSpec(memory_space=pltpu.VMEM),
+        scratch_shapes=[pltpu.VMEM((requests, width), jnp.float32)],
+        compiler_params=kernel_params(12),
         name="project_down",
-    )(inner, w_down)
+    )(inner, fetched(w_down))
 
 
 def layer_kernel(parts_ref, slots_ref, out_ref, total, hidden):

time: 164 us -> 151 us (0.921)
  local copies, waits for them, and re-layouts: 11.2 us -> 2.64 us
  Pallas kernels: 21.8 us -> 15.7 us
  blocking collectives: 130 us -> 133 us
    unnamed x20 -> x22, local copies, waits for them, and re-layouts: 9.46 us -> 0.85 us
    pallas_call x1, Pallas kernels: 5.26 us -> 2.31 us  [gate_up(): pl.pallas_call(gate_up_kernel, out_shape=jax.ShapeDtypeStruct((requests,...]
    all_to_all x4, blocking collectives: 86.9 us -> 89.4 us  [swap(): return lax.all_to_all(parts, axes, split_axis=0, concat_axis=0, tiled=True)]
where the time goes in v5:
time: 151 us
  blocking collectives  133 us (88%)
  Pallas kernels  15.7 us (10%)
  local copies, waits for them, and re-layouts  2.64 us (2%)
    all_to_all x4, blocking collectives, swap(): return lax.all_to_all(parts, axes, split_axis=0, concat_axis=0, tiled=True)  89.4 us
    all_gather x1, blocking collectives, local(): values = lax.all_gather(values, 'tp', axis=0)  18.4 us
    all_gather x1, blocking collectives, local(): inner = lax.all_gather(inner, 'tp', axis=0, tiled=True)  16.3 us
    pallas_call x1, Pallas kernels, attend(): pl.pallas_call(attention_kernel, out_shape=jax.ShapeDtypeStruct((ranks, n...  9.03 us
    all_gather x1, blocking collectives, local(): hidden = lax.all_gather(hidden, 'dp', axis=0, tiled=True)  8.78 us

profile of v5, /device:TPU:0, one launch (start us, length us, event | category | flops | bytes accessed | tf_op | source)
XLA Modules:
  0.0 151.3 jit_solution(13135185887344749723)
XLA Ops:
  0.0 1.8 %reshape.15.q_ref = bf16[4,128,576]{2,1,0:T(8,128)(2,1)S(1)} reshape(bf16[4,73728]{1,0:T(4,128)(2,1)} %param.11) | data formatting | bytes 1179648 | tf_op jit(solution)/shard_map/reshape | solution.py:495
  1.8 0.0 copy-start
  1.8 0.0 slice-start
  1.8 0.0 slice-start.2
  1.8 0.0 copy-start.4
  1.9 0.8 copy-done.4
  2.7 9.0 %attention.1 = bf16[32,16,512]{2,1,0:T(8,128)(2,1)S(1)} custom-call(s32[128]{0:T(128)S(1)} %copy-done.4, bf16[4,128,576]{2,1,0:T(8,128)(2,1)S(1)} %reshape.15.q_ref, bf16[576,14336]{1,0:T(8,128)(2,1)} %bitcast.18), custom_call_target="tpu_custom_call" | custom-call | flops 3992977408 | bytes 16515072 | tf_op jit(solution)/shard_map/attention/pallas_call | solution.py:165
  11.7 0.0 copy-start.3
  11.7 27.5 %all_to_all.20 = bf16[32,16,512]{2,1,0:T(8,128)(2,1)S(1)} all-to-all(bf16[32,16,512]{2,1,0:T(8,128)(2,1)S(1)} %attention.1), channel_id=1, replica_groups=mesh['dp'=8,'tp'=4] {'dp','tp'}, dimensions={0} | all-to-all | bytes 1048576 | tf_op jit(solution)/shard_map/all_to_all | solution.py:477
  39.3 0.8 head_values.1
  40.1 18.4 %all-gather = bf16[768,512]{1,0:T(8,128)(2,1)S(1)} all-gather(bf16[192,512]{1,0:T(8,128)(2,1)S(1)} %head_values.1), channel_id=2, replica_groups=mesh['dp'=8,'tp'=4] {'tp'}, dimensions={0}, use_global_device_ids=true | all-gather | bytes 983040 | tf_op jit(solution)/shard_map/all_gather | solution.py:501
  58.4 0.0 copy-done
  58.5 1.1 project_out.1
  59.6 11.8 %all_to_all.21.parts_ref = bf16[8,16,1792]{2,1,0:T(8,128)(2,1)S(1)} all-to-all(bf16[8,16,1792]{2,1,0:T(8,128)(2,1)S(1)} %bitcast.16), channel_id=1, replica_groups=mesh['dp'=8,'tp'=4] {'dp'}, dimensions={0} | all-to-all | bytes 917504 | tf_op jit(solution)/shard_map/all_to_all | solution.py:477
  71.4 0.1 hidden.1
  71.5 8.8 %all_gather.14.hidden_ref = bf16[128,1792]{1,0:T(8,128)(2,1)S(1)} all-gather(bf16[16,1792]{1,0:T(8,128)(2,1)S(1)} %hidden.1), channel_id=1, replica_groups=mesh['dp'=8,'tp'=4] {'dp'}, dimensions={0}, use_global_device_ids=true | all-gather | bytes 516096 | tf_op jit(solution)/shard_map/all_gather | solution.py:505
  80.3 0.0 slice-start.5
  80.3 2.3 %gate_up.1 = bf16[128,4992]{1,0:T(8,128)(2,1)S(1)} custom-call(bf16[128,1792]{1,0:T(8,128)(2,1)S(1)} %all_gather.14.hidden_ref, bf16[56,128]{1,0:T(8,128)(2,1)S(1)} %bitcast.17, bf16[1792,2304]{1,0:T(8,128)(2,1)S(1)} %bitcast.7, bf16[1792,2304]{1,0:T(8,128)(2,1)S(1)} %bitcast.9), custom_call_target="tpu_custom_call" | custom-call | tf_op jit(solution)/shard_map/gate_up/pallas_call | solution.py:361
  82.6 35.0 %all_to_all.22.parts_ref = bf16[4,32,4992]{2,1,0:T(8,128)(2,1)S(1)} all-to-all(bf16[4,32,4992]{2,1,0:T(8,128)(2,1)S(1)} %bitcast.14), channel_id=1, replica_groups=mesh['dp'=8,'tp'=4] {'tp'}, dimensions={0} | all-to-all | bytes 2555904 | tf_op jit(solution)/shard_map/all_to_all | solution.py:477
  117.6 0.3 inner.1
  117.9 16.3 %all_gather.15.inner_ref = bf16[128,2304]{1,0:T(8,128)(2,1)S(1)} all-gather(bf16[32,2304]{1,0:T(8,128)(2,1)S(1)} %get-tuple-element.7), channel_id=1, replica_groups=mesh['dp'=8,'tp'=4] {'tp'}, dimensions={0}, use_global_device_ids=true | all-gather | bytes 737280 | tf_op jit(solution)/shard_map/all_gather | solution.py:515
  134.2 1.3 project_down.1
  135.5 15.1 %all_to_all.23.parts_ref = bf16[32,56,128]{2,1,0:T(8,128)(2,1)S(1)} all-to-all(bf16[32,56,128]{2,1,0:T(8,128)(2,1)S(1)} %project_down.1), channel_id=1, replica_groups=mesh['dp'=8,'tp'=4] {'dp','tp'}, dimensions={0} | all-to-all | bytes 917504 | tf_op jit(solution)/shard_map/all_to_all | solution.py:477
  150.6 0.7 layer.1
  (17 shorter events, 0.0 us)
Async XLA Ops:
  0.0 39.2 %copy-start.1 = (bf16[4,512,128]{2,1,0:T(8,128)(2,1)S(1)}, bf16[4,512,128]{2,1,0:T(8,128)(2,1)}, u32[]{:S(2)}) copy-start(bf16[4,512,128]{2,1,0:T(8,128)(2,1)} %w_ref.3) | copy-start | bytes 1572868
  0.0 39.2 %copy-start.2 = (bf16[4,7168]{1,0:T(4,128)(2,1)S(1)}, bf16[4,7168]{1,0:T(4,128)(2,1)}, u32[]{:S(2)}) copy-start(bf16[4,7168]{1,0:T(4,128)(2,1)} %residual_ref.1) | copy-start | bytes 172036
  1.8 56.6 %copy-start = (bf16[2048,1792]{1,0:T(8,128)(2,1)S(1)}, bf16[2048,1792]{1,0:T(8,128)(2,1)}, u32[]{:S(2)}) copy-start(bf16[2048,1792]{1,0:T(8,128)(2,1)} %w_ref.4) | copy-start | bytes 22020100
  1.8 78.4 %slice-start = ((s8[8257536]{0:T(1024)(128)(4,1)}), s8[4194304]{0:T(1024)(128)(4,1)S(1)}, s32[]{:S(2)}) async-start(s8[8257536]{0:T(1024)(128)(4,1)} %bitcast.6), calls=%async_computation.4 | async-start | bytes 8388608
  1.8 78.4 %slice-start.2 = ((s8[8257536]{0:T(1024)(128)(4,1)}), s8[4194304]{0:T(1024)(128)(4,1)S(1)}, s32[]{:S(2)}) async-start(s8[8257536]{0:T(1024)(128)(4,1)} %bitcast.8), calls=%async_computation.6 | async-start | bytes 8388608
  1.8 0.8 copy-start.4
  2.6 77.6 %slice-start.1 = ((s8[8257536]{0:T(1024)(128)(4,1)}), s8[4063232]{0:T(1024)(128)(4,1)S(1)}, s32[]{:S(2)}) async-start(s8[8257536]{0:T(1024)(128)(4,1)} %bitcast.6), calls=%async_computation.5 | async-start | bytes 8126464
  2.6 77.6 %slice-start.3 = ((s8[8257536]{0:T(1024)(128)(4,1)}), s8[4063232]{0:T(1024)(128)(4,1)S(1)}, s32[]{:S(2)}) async-start(s8[8257536]{0:T(1024)(128)(4,1)} %bitcast.8), calls=%async_computation.7 | async-start | bytes 8126464
  11.7 68.6 %copy-start.3 = (bf16[7168]{0:T(1024)(128)(2,1)S(1)}, bf16[7168]{0:T(1024)(128)(2,1)}, u32[]{:S(2)}) copy-start(bf16[7168]{0:T(1024)(128)(2,1)} %param.16) | copy-start | bytes 43012
  80.3 53.9 %slice-start.4 = ((s8[8257536]{0:T(1024)(128)(4,1)}), s8[4194304]{0:T(1024)(128)(4,1)S(1)}, s32[]{:S(2)}) async-start(s8[8257536]{0:T(1024)(128)(4,1)} %bitcast.10), calls=%async_computation.8 | async-start | bytes 8388608
  80.3 53.9 %slice-start.5 = ((s8[8257536]{0:T(1024)(128)(4,1)}), s8[4063232]{0:T(1024)(128)(4,1)S(1)}, s32[]{:S(2)}) async-start(s8[8257536]{0:T(1024)(128)(4,1)} %bitcast.10), calls=%async_computation.9 | async-start | bytes 8126464

commit v6 on v5

--- a/solution.py
+++ b/solution.py
@@ -197,46 +197,52 @@
     )(lengths, queries, pltpu.with_memory_space_constraint(cache_t, pltpu.HBM))
 
 
-def head_values_kernel(latent_ref, w_ref, residual_ref, out_ref, values, slots):
+def head_values_kernel(latent_ref, w_ref, out_ref, values):
     heads, _, wide = w_ref.shape
-    per_rank, model = residual_ref.shape
-    requests = latent_ref.shape[0] // heads
+    requests = out_ref.shape[0]
     latent = latent_ref[...]
     for h in range(heads):
         values[...] = jnp.dot(latent, w_ref[h], preferred_element_type=jnp.float32)
         picked = values[pl.ds(h, requests, stride=heads), :]
-        out_ref[:requests, h * wide : (h + 1) * wide] = picked.astype(out_ref.dtype)
-    ranks = lax.axis_size("tp")
-    groups = model // ranks // 128
-    rows = (out_ref.shape[0] - requests) // ranks
-    across = out_ref.shape[1] // 128
-    slots[...] = jnp.zeros_like(slots)
-    for t in range(ranks):
-        for g in range(groups):
-            at = (t * groups + g) * 128
-            row = t * rows + (g // across) * per_rank
-            column = (g % across) * 128
-            slots[row : row + per_rank, column : column + 128] = residual_ref[
-                :, at : at + 128
-            ].astype(jnp.float32)
-    out_ref[requests:, :] = slots[...].astype(out_ref.dtype)
-
-
-def head_values(latent, w_uv, residual, slot_rows):
+        out_ref[:, h * wide : (h + 1) * wide] = picked.astype(out_ref.dtype)
+
+
+def head_values(latent, w_uv):
     heads, _, wide = w_uv.shape
     requests = latent.shape[0] // heads
     return pl.pallas_call(
         head_values_kernel,
-        out_shape=jax.ShapeDtypeStruct((requests + slot_rows, heads * wide), jnp.bfloat16),
-        in_specs=in_vmem(3),
-        out_specs=pl.BlockSpec(memory_space=pltpu.VMEM),
-        scratch_shapes=[
-            pltpu.VMEM((latent.shape[0], wide), jnp.float32),
-            pltpu.VMEM((slot_rows, heads * wide), jnp.float32),
-        ],
+        out_shape=jax.ShapeDtypeStruct((requests, heads * wide), jnp.bfloat16),
+        in_specs=in_vmem(2),
+        out_specs=pl.BlockSpec(memory_space=pltpu.VMEM),
+        scratch_shapes=[pltpu.VMEM((latent.shape[0], wide), jnp.float32)],
         compiler_params=kernel_params(12),
         name="head_values",
-    )(latent, w_uv, residual)
+    )(latent, w_uv)
+
+
+def split_kernel(rows_ref, *out_refs):
+    width = out_refs[0].shape[1]
+    me = lax.axis_index("tp")
+    for k, out_ref in enumerate(out_refs):
+        start = pl.multiple_of((me ^ k) * width, 128)
+        out_ref[...] = rows_ref[:, pl.ds(start, width)]
+
+
+def split_columns(rows, ranks):
+    shape = jax.ShapeDtypeStruct((rows.shape[0], rows.shape[1] // ranks), rows.dtype)
+    return pl.pallas_call(
+        split_kernel,
+        out_shape=[shape] * ranks,
+        in_specs=in_vmem(1),
+        out_specs=in_vmem(ranks),
+        compiler_params=kernel_params(8),
+        name="split_columns",
+    )(rows)
+
+
+def across(piece, axis, distance):
+    return lax.ppermute(piece, axis, [(k, k ^ distance) for k in range(lax.axis_size(axis))])
 
 
 def output_kernel(values_ref, w_ref, out_ref, total):
@@ -244,7 +250,7 @@
     requests = out_ref.shape[0]
     for k in range(steps):
         term = jnp.dot(
-            values_ref[k, :requests, :],
+            values_ref[k],
             w_ref[k * depth : (k + 1) * depth, :],
             preferred_element_type=jnp.float32,
         )
@@ -268,140 +274,174 @@
     )(values, fetched(w_o))
 
 
-def hidden_kernel(parts_ref, values_ref, out_ref, slots):
-    ranks = values_ref.shape[0]
+def hidden_kernel(parts_ref, *refs):
+    *slices, out_ref, added = refs
+    per_rank = slices[0].shape[0]
+    me = lax.axis_index("tp")
+    for k, piece in enumerate(slices):
+        added[me ^ k] = piece[...].astype(jnp.float32)
     width = out_ref.shape[1]
-    per_rank = out_ref.shape[0] // ranks
-    across = values_ref.shape[2] // 128
-    rows = slots.shape[1]
-    requests = values_ref.shape[1] - ranks * rows
-    start = pl.multiple_of(requests + lax.axis_index("tp") * rows, 16)
-    for s in range(ranks):
-        slots[s] = values_ref[s, pl.ds(start, rows), :].astype(jnp.float32)
-    for g in range(width // 128):
-        at = slice(g * 128, (g + 1) * 128)
-        row = (g // across) * per_rank
-        column = (g % across) * 128
-        terms = [
-            slots[s, row : row + per_rank, column : column + 128] for s in range(ranks)
-        ]
+    for at in range(0, width, 128):
+        at = slice(at, at + 128)
         total = parts_ref[0, :, at].astype(jnp.float32)
         for d in range(1, parts_ref.shape[0]):
             total = total + parts_ref[d, :, at].astype(jnp.float32)
-        total = total + jnp.concatenate(terms, 0)
-        out_ref[:, at] = total.astype(out_ref.dtype)
-
-
-def make_hidden(parts, values, slot_rows):
-    ranks = values.shape[0]
+        terms = [added[s, :, at] for s in range(len(slices))]
+        out_ref[:, at] = (total + jnp.concatenate(terms, 0)).astype(out_ref.dtype)
+
+
+def make_hidden(parts, slices):
     return pl.pallas_call(
         hidden_kernel,
         out_shape=jax.ShapeDtypeStruct(parts.shape[1:], jnp.bfloat16),
-        in_specs=in_vmem(2),
-        out_specs=pl.BlockSpec(memory_space=pltpu.VMEM),
-        scratch_shapes=[pltpu.VMEM((ranks, slot_rows // ranks, values.shape[2]), jnp.float32)],
+        in_specs=in_vmem(1 + len(slices)),
+        out_specs=pl.BlockSpec(memory_space=pltpu.VMEM),
+        scratch_shapes=[pltpu.VMEM((len(slices),) + slices[0].shape, jnp.float32)],
         compiler_params=kernel_params(12),
         name="hidden",
-    )(parts, values)
-
-
-def gate_up_kernel(
-    hidden_ref, gain_ref, gate_ref, up_ref, out_ref, scaled, gains, own
-):
+    )(parts, *slices)
+
+
+def gate_up_kernel(hidden_ref, gain_ref, gate_ref, up_ref, *refs):
+    ranks = lax.axis_size("tp")
+    *outs, scaled, gains, own = refs
+    gate_outs, up_outs, rows_out = outs[:-ranks][0::2], outs[:-ranks][1::2], outs[-ranks:]
     requests, width = hidden_ref.shape
     units = gate_ref.shape[1]
-    ranks = lax.axis_size("tp")
+    share = requests // ranks
     groups = width // 128
+    me = lax.axis_index("tp")
+    if len(gate_outs) == 1:
+        orders = [[0 * me + t for t in range(ranks)]] * 2
+    else:
+        orders = [[me ^ 3, me ^ 1, me ^ 2, me], [me ^ 3, me ^ 2, me ^ 1, me]]
+
     gains[...] = gain_ref[...].astype(jnp.float32)
-    base = lax.axis_index("tp") * groups
-    square = jnp.zeros((requests, 128), jnp.float32)
-    for g in range(groups):
-        at = slice(g * 128, (g + 1) * 128)
-        x = hidden_ref[:, at].astype(jnp.float32)
-        square = square + x * x
-        scaled[:, at] = (x * gains[pl.ds(base + g, 1), :]).astype(scaled.dtype)
-    square = jnp.sum(square, 1, keepdims=True)
+    squares = []
+    for k, order in enumerate(orders[:1] if len(gate_outs) == 1 else orders):
+        square = [jnp.zeros((share, 128), jnp.float32) for _ in order]
+        for t, block in enumerate(order):
+            start = pl.multiple_of(block * share, 16)
+            for g in range(groups):
+                at = slice(g * 128, (g + 1) * 128)
+                x = hidden_ref[pl.ds(start, share), at].astype(jnp.float32)
+                square[t] = square[t] + x * x
+                gain = gains[pl.ds(me * groups + g, 1), :]
+                scaled[k, t * share : (t + 1) * share, at] = (x * gain).astype(scaled.dtype)
+        squares.append(square)
+    square = jnp.sum(jnp.concatenate(squares[0], 0), 1, keepdims=True)
     top = square.astype(jnp.bfloat16).astype(jnp.float32)
     middle = (square - top).astype(jnp.bfloat16).astype(jnp.float32)
     low = square - top - middle
     lane = lax.broadcasted_iota(jnp.int32, (requests, 128), 1)
     digits = jnp.where(lane == 0, top, jnp.where(lane == 1, middle, jnp.where(lane == 2, low, 0.0)))
-    out_ref[:, 2 * units : 2 * units + 128] = digits.astype(out_ref.dtype)
-
-    rows = own.shape[0]
-    per_rank = rows // ranks
+
+    def store(targets, at, value):
+        rows = requests // len(targets)
+        for n, target in enumerate(targets):
+            block = value[n * rows : (n + 1) * rows].astype(target.dtype)
+            target[:, at : at + value.shape[1]] = block
+
+    store(gate_outs, units, digits)
+    per_rank = own.shape[1]
+    rows = ranks * per_rank
     start = pl.multiple_of(lax.axis_index("dp") * rows, 16)
-    own[...] = hidden_ref[pl.ds(start, rows), :].astype(jnp.float32)
-    share = requests // ranks
-    high = share // per_rank
-    for t in range(ranks):
-        for block in range((groups + high - 1) // high):
-            pieces = []
-            for g in range(block * high, (block + 1) * high):
-                g = min(g, groups - 1)
-                pieces.append(
-                    own[t * per_rank : (t + 1) * per_rank, g * 128 : (g + 1) * 128]
-                )
-            column = 2 * units + 128 * (1 + block)
-            out_ref[t * share : (t + 1) * share, column : column + 128] = jnp.concatenate(
-                pieces, 0
-            ).astype(out_ref.dtype)
+    own[...] = (
+        hidden_ref[pl.ds(start, rows), :].astype(jnp.float32).reshape(ranks, per_rank, width)
+    )
+    for k, target in enumerate(rows_out):
+        target[...] = own[me ^ k].astype(target.dtype)
 
     chunk = units // 3
-    for k, w_ref in enumerate((gate_ref, up_ref)):
+    for w_ref, left, targets in ((gate_ref, 0, gate_outs), (up_ref, scaled.shape[0] - 1, up_outs)):
         for at in range(0, units, chunk):
             term = jnp.dot(
-                scaled[...], w_ref[:, at : at + chunk], preferred_element_type=jnp.float32
+                scaled[left], w_ref[:, at : at + chunk], preferred_element_type=jnp.float32
             )
-            out_ref[:, k * units + at : k * units + at + chunk] = term.astype(out_ref.dtype)
-
-
-def gate_up(hidden, gain, w_gate, w_up, own_rows, columns):
+            store(targets, at, term)
+
+
+def gate_up(hidden, gain, w_gate, w_up, ranks_dp, ranks_tp, halves):
     requests, width = hidden.shape
-    return pl.pallas_call(
+    units = w_gate.shape[1]
+    rows = requests // ranks_dp
+    per_rank = rows // ranks_tp
+    shapes = [
+        jax.ShapeDtypeStruct((requests // halves, columns), jnp.bfloat16)
+        for _ in range(halves)
+        for columns in (units + 128, units)
+    ] + [jax.ShapeDtypeStruct((per_rank, width), jnp.bfloat16)] * ranks_tp
+    outs = pl.pallas_call(
         gate_up_kernel,
-        out_shape=jax.ShapeDtypeStruct((requests, columns), jnp.bfloat16),
+        out_shape=shapes,
         in_specs=in_vmem(4),
-        out_specs=pl.BlockSpec(memory_space=pltpu.VMEM),
+        out_specs=in_vmem(len(shapes)),
         scratch_shapes=[
-            pltpu.VMEM((requests, width), jnp.bfloat16),
+            pltpu.VMEM((halves, requests, width), jnp.bfloat16),
             pltpu.VMEM(gain.shape, jnp.float32),
-            pltpu.VMEM((own_rows, width), jnp.float32),
+            pltpu.VMEM((ranks_tp, per_rank, width), jnp.float32),
         ],
         compiler_params=kernel_params(12),
         name="gate_up",
     )(hidden, gain, fetched(w_gate), fetched(w_up))
-
-
-def inner_kernel(model, parts_ref, out_ref, slots_ref):
-    ranks = parts_ref.shape[0]
+    return outs[: 2 * halves], outs[2 * halves :]
+
+
+def halve_kernel(*refs):
+    count = len(refs) // 4
+    for n in range(count):
+        kept, came, send, keep = refs[n], refs[count + n], refs[2 * count + n], refs[3 * count + n]
+        rows = send.shape[0]
+        for at in range(0, send.shape[1], 128):
+            at = slice(at, at + 128)
+            total = kept[:, at].astype(jnp.float32) + came[:, at].astype(jnp.float32)
+            send[:, at] = total[:rows].astype(send.dtype)
+            keep[:, at] = total[rows:]
+
+
+def halve(kept, came):
+    half = [(k.shape[0] // 2, k.shape[1]) for k in kept]
+    outs = pl.pallas_call(
+        halve_kernel,
+        out_shape=[jax.ShapeDtypeStruct(shape, jnp.bfloat16) for shape in half]
+        + [jax.ShapeDtypeStruct(shape, jnp.float32) for shape in half],
+        in_specs=in_vmem(2 * len(kept)),
+        out_specs=in_vmem(2 * len(kept)),
+        compiler_params=kernel_params(12),
+        name="halve",
+    )(*kept, *came)
+    return outs[: len(kept)], outs[len(kept) :]
+
+
+def inner_kernel(model, *refs):
+    *parts, out_ref = refs
+    gates, ups = parts[0::2], parts[1::2]
     units = out_ref.shape[1]
 
-    def total(at):
-        return sum(parts_ref[s, :, at].astype(jnp.float32) for s in range(ranks))
-
-    square = jnp.sum(total(slice(2 * units, 2 * units + 128)), 1, keepdims=True)
+    def total(parts, at):
+        terms = [
+            part[n, :, at].astype(jnp.float32) for part in parts for n in range(part.shape[0])
+        ]
+        return sum(terms[1:], terms[0])
+
+    square = jnp.sum(total(gates, slice(units, units + 128)), 1, keepdims=True)
     factor = lax.rsqrt(square / model + 1e-06)
     for at in range(0, units, 128):
-        gate = total(slice(at, at + 128)) * factor
-        up = total(slice(units + at, units + at + 128)) * factor
-        out_ref[:, at : at + 128] = (gate / (1.0 + jnp.exp(-gate)) * up).astype(out_ref.dtype)
-    slots_ref[...] = parts_ref[:, :, 2 * units + 128 :]
+        at = slice(at, at + 128)
+        gate = total(gates, at) * factor
+        up = total(ups, at) * factor
+        out_ref[:, at] = (gate / (1.0 + jnp.exp(-gate)) * up).astype(out_ref.dtype)
 
 
 def make_inner(parts, units, model):
-    ranks, rows, columns = parts.shape
     return pl.pallas_call(
         functools.partial(inner_kernel, model),
-        out_shape=[
-            jax.ShapeDtypeStruct((rows, units), jnp.bfloat16),
-            jax.ShapeDtypeStruct((ranks, rows, columns - 2 * units - 128), jnp.bfloat16),
-        ],
-        in_specs=in_vmem(1),
-        out_specs=in_vmem(2),
+        out_shape=jax.ShapeDtypeStruct((parts[0].shape[1], units), jnp.bfloat16),
+        in_specs=in_vmem(len(parts)),
+        out_specs=pl.BlockSpec(memory_space=pltpu.VMEM),
         compiler_params=kernel_params(12),
         name="inner",
-    )(parts)
+    )(*parts)
 
 
 def down_kernel(inner_ref, w_ref, out_ref, total):
@@ -433,44 +473,37 @@
     )(inner, fetched(w_down))
 
 
-def layer_kernel(parts_ref, slots_ref, out_ref, total, hidden):
-    ranks = slots_ref.shape[0]
+def layer_kernel(parts_ref, *refs):
+    *slices, out_ref, total = refs
+    ranks = len(slices)
     per_rank, model = out_ref.shape
-    groups = model // ranks // 128
-    high = slots_ref.shape[1] // per_rank
-    hidden[...] = slots_ref[...].astype(jnp.float32)
+    width = model // ranks
+    groups = width // 128
+    me = lax.axis_index("tp")
     for t in range(ranks):
         ffn = sum(
             parts_ref[d, :, :].astype(jnp.float32) for d in range(t, parts_ref.shape[0], ranks)
         )
         for g in range(groups):
-            row = (g % high) * per_rank
-            column = (g // high) * 128
             at = (t * groups + g) * 128
-            total[:, at : at + 128] = (
-                ffn[g * per_rank : (g + 1) * per_rank, :]
-                + hidden[t, row : row + per_rank, column : column + 128]
-            )
+            total[:, at : at + 128] = ffn[g * per_rank : (g + 1) * per_rank, :]
+    for k, piece in enumerate(slices):
+        at = pl.ds(pl.multiple_of((me ^ k) * width, 128), width)
+        total[:, at] += piece[...].astype(jnp.float32)
     out_ref[...] = total[...].astype(out_ref.dtype)
 
 
-def make_layer(parts, slots, per_rank, model):
+def make_layer(parts, slices, model):
+    per_rank = slices[0].shape[0]
     return pl.pallas_call(
         layer_kernel,
         out_shape=jax.ShapeDtypeStruct((per_rank, model), jnp.bfloat16),
-        in_specs=in_vmem(2),
-        out_specs=pl.BlockSpec(memory_space=pltpu.VMEM),
-        scratch_shapes=[
-            pltpu.VMEM((per_rank, model), jnp.float32),
-            pltpu.VMEM(slots.shape, jnp.float32),
-        ],
+        in_specs=in_vmem(1 + len(slices)),
+        out_specs=pl.BlockSpec(memory_space=pltpu.VMEM),
+        scratch_shapes=[pltpu.VMEM((per_rank, model), jnp.float32)],
         compiler_params=kernel_params(12),
         name="layer",
-    )(parts, slots)
-
-
-def round_up(value, step):
-    return (value + step - 1) // step * step
+    )(parts, *slices)
 
 
 def swap(parts, axes):
@@ -490,31 +523,41 @@
     heads_here = w_uv.shape[0]
     units = w_gate.shape[1]
     width = w_o.shape[1]
-    groups = width // 128
 
     query = queries.reshape(per_rank, heads_all, row_length)
-    latent = swap(attend(lengths, query, paged_latent_cache.T, ranks), ("dp", "tp"))
-
-    across = heads_here * w_uv.shape[2] // 128
-    slot_rows = ranks_tp * round_up(per_rank * ((groups + across - 1) // across), 16)
-    values = head_values(latent.reshape(requests * heads_here, C), w_uv, residual, slot_rows)
+    latent = attend(lengths, query, paged_latent_cache.T, ranks)
+    latent, residual, w_o, w_gate, w_up, w_down = lax.optimization_barrier(
+        (latent, residual, w_o, w_gate, w_up, w_down)
+    )
+    added = split_columns(residual, ranks_tp)
+    added = [added[0]] + [across(added[k], "tp", k) for k in range(1, ranks_tp)]
+    latent = swap(latent, ("dp", "tp"))
+
+    values = head_values(latent.reshape(requests * heads_here, C), w_uv)
     values = lax.all_gather(values, "tp", axis=0)
     attn = project_out(values, w_o, requests)
     attn = swap(attn.reshape(ranks_dp, requests // ranks_dp, width), "dp")
-    hidden = make_hidden(attn, values, slot_rows)
+    hidden = make_hidden(attn, added)
     hidden = lax.all_gather(hidden, "dp", axis=0, tiled=True)
 
-    share = requests // ranks_tp
-    high = share // per_rank
-    columns = 2 * units + 128 + 128 * ((groups + high - 1) // high)
-    both = gate_up(
-        hidden, norm_gain.reshape(-1, 128), w_gate, w_up, requests // ranks_dp, columns
+    halves = 2 if ranks_tp == 4 else 1
+    parts, rows = gate_up(
+        hidden, norm_gain.reshape(-1, 128), w_gate, w_up, ranks_dp, ranks_tp, halves
     )
-    both = swap(both.reshape(ranks_tp, share, columns), "tp")
-    inner, slots = make_inner(both, units, model)
+    if halves == 2:
+        gate_send, up_send, gate_keep, up_keep = parts
+        came = [across(gate_send, "tp", 1), across(up_send, "tp", 2)]
+        rows = [rows[0]] + [across(rows[k], "tp", k) for k in range(1, ranks_tp)]
+        (gate_send, up_send), (gate_keep, up_keep) = halve([gate_keep, up_keep], came)
+        parts = [gate_keep, up_keep, across(gate_send, "tp", 2), across(up_send, "tp", 1)]
+        parts = [part[None] for part in parts]
+    else:
+        rows = [rows[0]] + [across(rows[k], "tp", k) for k in range(1, ranks_tp)]
+        parts = [swap(part.reshape(ranks_tp, -1, part.shape[1]), "tp") for part in parts]
+    inner = make_inner(parts, units, model)
     inner = lax.all_gather(inner, "tp", axis=0, tiled=True)
     ffn = swap(project_down(inner, w_down, ranks), ("dp", "tp"))
-    return make_layer(ffn, slots, per_rank, model)
+    return make_layer(ffn, rows, model)
 
 
 def solution(mesh):

time: 151 us -> 156 us (1.033); the launches traced: 151 us -> 154 us
  blocking collectives: 133 us -> 65.8 us
  waiting for transfers between devices: 0 us -> 34.8 us
  starting transfers between devices: 0 us -> 22.8 us
  local copies, waits for them, and re-layouts: 2.64 us -> 15.3 us
    all_to_all x4 -> x1, blocking collectives: 89.4 us -> 24.9 us  [swap(): return lax.all_to_all(parts, axes, split_axis=0, concat_axis=0, tiled=True)]
    ppermute x0 -> x10, waiting for transfers between devices: none -> 33.7 us  [across(): lax.ppermute(piece, axis, [(k, k ^ distance) for k in range(lax.axis_size...]
    ppermute x0 -> x10, starting transfers between devices: none -> 14.5 us  [across(): lax.ppermute(piece, axis, [(k, k ^ distance) for k in range(lax.axis_size...]
    unnamed x22, local copies, waits for them, and re-layouts: 0.85 us -> 12.6 us
    all_to_all x0 -> x2, starting transfers between devices: none -> 8.27 us  [swap(): return lax.all_to_all(parts, axes, split_axis=0, concat_axis=0, tiled=True)]
    all_gather x1, blocking collectives: 18.4 us -> 16 us  [local(): values = lax.all_gather(values, 'tp', axis=0)]
    pallas_call x1, Pallas kernels: 9.03 us -> 7.37 us  [attend(): pl.pallas_call(attention_kernel, out_shape=jax.ShapeDtypeStruct((ranks, n...]
  transfers between devices with their start and end apart: 0 -> 12, of which waited for: 0 -> 8; matrix products, arithmetic and copies ran while one was open for 0% -> 0% of each run, Pallas kernels for 0% -> 0%
where the time goes in v6:
time: 156 us; the launch traced here: 154 us
  blocking collectives  65.8 us (42%)
  waiting for transfers between devices  34.8 us (22%)
  starting transfers between devices  22.8 us (15%)
  local copies, waits for them, and re-layouts  15.3 us (10%)
  Pallas kernels  14.9 us (10%)
    ppermute x10, waiting for transfers between devices, across(): lax.ppermute(piece, axis, [(k, k ^ distance) for k in range(lax.axis_size...  33.7 us
    all_to_all x1, blocking collectives, swap(): return lax.all_to_all(parts, axes, split_axis=0, concat_axis=0, tiled=True)  24.9 us
    all_gather x1, blocking collectives, local(): values = lax.all_gather(values, 'tp', axis=0)  16 us
    all_gather x1, blocking collectives, local(): inner = lax.all_gather(inner, 'tp', axis=0, tiled=True)  15.9 us
    ppermute x10, starting transfers between devices, across(): lax.ppermute(piece, axis, [(k, k ^ distance) for k in range(lax.axis_size...  14.5 us
    unnamed x22, local copies, waits for them, and re-layouts  12.6 us
    all_gather x1, blocking collectives, local(): hidden = lax.all_gather(hidden, 'dp', axis=0, tiled=True)  9 us
    all_to_all x2, starting transfers between devices, swap(): return lax.all_to_all(parts, axes, split_axis=0, concat_axis=0, tiled=True)  8.27 us
  transfers between devices with their start and end apart: 12, of which 8 were waited for; matrix products, arithmetic and copies ran while one was open for 0% of the time, Pallas kernels for 0%

profile of v6, /device:TPU:0, one launch (start us, length us, event | category | flops | bytes accessed | tf_op | source)
XLA Modules:
  0.0 153.7 jit_solution(18093144677351002039)
XLA Ops:
  0.0 2.7 %reshape.12.q_ref = bf16[4,128,576]{2,1,0:T(8,128)(2,1)} reshape(bf16[4,73728]{1,0:T(4,128)(2,1)} %param.11) | data formatting | bytes 1179648 | tf_op jit(solution)/shard_map/reshape | solution.py:527
  4.5 7.4 %attention.1 = bf16[32,16,512]{2,1,0:T(8,128)(2,1)S(1)} custom-call(s32[128]{0:T(128)S(1)} %copy-done.8, bf16[4,128,576]{2,1,0:T(8,128)(2,1)S(1)} %copy-done.3, bf16[576,14336]{1,0:T(8,128)(2,1)} %bitcast.19), custom_call_target="tpu_custom_call" | custom-call | flops 3992977408 | bytes 16515072 | tf_op jit(solution)/shard_map/attention/pallas_call | solution.py:165
  11.9 24.9 %all_to_all.15 = bf16[32,16,512]{2,1,0:T(8,128)(2,1)S(1)} all-to-all(bf16[32,16,512]{2,1,0:T(8,128)(2,1)S(1)} %attention.1), channel_id=1, replica_groups=mesh['dp'=8,'tp'=4] {'dp','tp'}, dimensions={0} | all-to-all | bytes 1048576 | tf_op jit(solution)/shard_map/all_to_all | solution.py:510
  37.6 16.0 %all-gather = bf16[512,512]{1,0:T(8,128)(2,1)S(1)} all-gather(bf16[128,512]{1,0:T(8,128)(2,1)S(1)} %head_values.1), channel_id=2, replica_groups=mesh['dp'=8,'tp'=4] {'tp'}, dimensions={0}, use_global_device_ids=true | all-gather | bytes 655360 | tf_op jit(solution)/shard_map/all_gather | solution.py:537
  55.5 3.6 %all-to-all-start.1 = ((bf16[8,16,1792]{2,1,0:T(8,128)(2,1)}), bf16[8,16,1792]{2,1,0:T(8,128)(2,1)S(1)}, u32[]{:S(2)}, u32[]{:S(2)}) async-start(bf16[8,16,1792]{2,1,0:T(8,128)(2,1)} %bitcast.13), calls=%async_computation.1 | async-start | bytes 917504 | tf_op jit(solution)/shard_map/all_to_all | solution.py:510
  59.2 2.3 %collective-permute-start.1 = (bf16[4,1792]{1,0:T(4,128)(2,1)S(1)}, bf16[4,1792]{1,0:T(4,128)(2,1)S(1)}, u32[]{:S(2)}, u32[]{:S(2)}) collective-permute-start(bf16[4,1792]{1,0:T(4,128)(2,1)S(1)} %get-tuple-element.32), channel_id=1, source_target_pairs={{0,2},{1,3},{2,0},{3,1},{4,6},{5,7},{6,4},{7,5},{8,10},{9,11},{10,... | collective-permute-start | bytes 43016 | tf_op jit(solution)/shard_map/ppermute | solution.py:245
  61.5 2.1 %collective-permute-start.2 = (bf16[4,1792]{1,0:T(4,128)(2,1)S(1)}, bf16[4,1792]{1,0:T(4,128)(2,1)S(1)}, u32[]{:S(2)}, u32[]{:S(2)}) collective-permute-start(bf16[4,1792]{1,0:T(4,128)(2,1)S(1)} %get-tuple-element.33), channel_id=1, source_target_pairs={{0,3},{1,2},{2,1},{3,0},{4,7},{5,6},{6,5},{7,4},{8,11},{9,10},{10,... | collective-permute-start | bytes 43016 | tf_op jit(solution)/shard_map/ppermute | solution.py:245
  63.9 3.1 %collective-permute-done.2.refs_3_ = bf16[4,1792]{1,0:T(4,128)(2,1)S(1)} collective-permute-done((bf16[4,1792]{1,0:T(4,128)(2,1)S(1)}, bf16[4,1792]{1,0:T(4,128)(2,1)S(1)}, u32[]{:S(2)}, u32[]{:S(2)}) %collective-permute-start.2) | collective-permute-done | bytes 14368 | tf_op jit(solution)/shard_map/ppermute | solution.py:245
  68.2 9.0 %all_gather.14.hidden_ref = bf16[128,1792]{1,0:T(8,128)(2,1)S(1)} all-gather(bf16[16,1792]{1,0:T(8,128)(2,1)S(1)} %hidden.1), channel_id=1, replica_groups=mesh['dp'=8,'tp'=4] {'dp'}, dimensions={0}, use_global_device_ids=true | all-gather | bytes 516096 | tf_op jit(solution)/shard_map/all_gather | solution.py:541
  77.2 3.3 %copy-done = bf16[1792,2304]{1,0:T(8,128)(2,1)S(1)} copy-done((bf16[1792,2304]{1,0:T(8,128)(2,1)S(1)}, bf16[1792,2304]{1,0:T(8,128)(2,1)}, u32[]{:S(2)}) %copy-start) | copy-done | bytes 8257560
  80.6 3.3 %copy-done.1 = bf16[1792,2304]{1,0:T(8,128)(2,1)S(1)} copy-done((bf16[1792,2304]{1,0:T(8,128)(2,1)S(1)}, bf16[1792,2304]{1,0:T(8,128)(2,1)}, u32[]{:S(2)}) %copy-start.1) | copy-done | bytes 8257560
  83.9 2.3 %gate_up.1 = (bf16[64,2432]{1,0:T(8,128)(2,1)S(1)}, bf16[64,2304]{1,0:T(8,128)(2,1)S(1)}, bf16[64,2432]{1,0:T(8,128)(2,1)S(1)}, bf16[64,2304]{1,0:T(8,128)(2,1)S...) custom-call(bf16[128,1792]{1,0:T(8,128)(2,1)S(1)} %all_gather.14.hid, ...), custom_call_target="tpu_custom_call" | custom-call | tf_op jit(solution)/shard_map/gate_up/pallas_call | solution.py:374
  86.3 2.7 %collective-permute-start.4 = (bf16[64,2304]{1,0:T(8,128)(2,1)S(1)}, bf16[64,2304]{1,0:T(8,128)(2,1)S(1)}, u32[]{:S(2)}, u32[]{:S(2)}) collective-permute-start(bf16[64,2304]{1,0:T(8,128)(2,1)S(1)} %get-tuple-element.39), channel_id=1, source_target_pairs={{0,2},{1,3},{2,0},{3,1},{4,6},{5,7},{6,4},{7,5},{8,10},{9,11},{10,... | collective-permute-start | bytes 884744 | tf_op jit(solution)/shard_map/ppermute | solution.py:245
  89.1 13.9 %collective-permute-done.4.refs_3_ = bf16[64,2304]{1,0:T(8,128)(2,1)S(1)} collective-permute-done((bf16[64,2304]{1,0:T(8,128)(2,1)S(1)}, bf16[64,2304]{1,0:T(8,128)(2,1)S(1)}, u32[]{:S(2)}, u32[]{:S(2)}) %collective-permute-start.4) | collective-permute-done | bytes 294944 | tf_op jit(solution)/shard_map/ppermute | solution.py:245
  103.7 2.1 %collective-permute-start.6 = (bf16[32,2304]{1,0:T(8,128)(2,1)S(1)}, bf16[32,2304]{1,0:T(8,128)(2,1)S(1)}, u32[]{:S(2)}, u32[]{:S(2)}) collective-permute-start(bf16[32,2304]{1,0:T(8,128)(2,1)S(1)} %get-tuple-element.43), channel_id=1, source_target_pairs={{0,1},{1,0},{2,3},{3,2},{4,5},{5,4},{6,7},{7,6},{8,9},{9,8},{10,11... | collective-permute-start | bytes 442376 | tf_op jit(solution)/shard_map/ppermute | solution.py:245
  105.9 4.6 %collective-permute-done.6 = bf16[32,2304]{1,0:T(8,128)(2,1)S(1)} collective-permute-done((bf16[32,2304]{1,0:T(8,128)(2,1)S(1)}, bf16[32,2304]{1,0:T(8,128)(2,1)S(1)}, u32[]{:S(2)}, u32[]{:S(2)}) %collective-permute-start.6) | collective-permute-done | bytes 147488 | tf_op jit(solution)/shard_map/ppermute | solution.py:245
  112.2 15.9 %all_gather.15.inner_ref = bf16[128,2304]{1,0:T(8,128)(2,1)S(1)} all-gather(bf16[32,2304]{1,0:T(8,128)(2,1)S(1)} %inner.1), channel_id=1, replica_groups=mesh['dp'=8,'tp'=4] {'tp'}, dimensions={0}, use_global_device_ids=true | all-gather | bytes 737280 | tf_op jit(solution)/shard_map/all_gather | solution.py:558
  128.1 3.3 %copy-done.2 = bf16[2304,1792]{1,0:T(8,128)(2,1)S(1)} copy-done((bf16[2304,1792]{1,0:T(8,128)(2,1)S(1)}, bf16[2304,1792]{1,0:T(8,128)(2,1)}, u32[]{:S(2)}) %copy-start.2) | copy-done | bytes 8257560
  131.5 2.1 %project_down.1 = bf16[32,56,128]{2,1,0:T(8,128)(2,1)} custom-call(bf16[128,2304]{1,0:T(8,128)(2,1)S(1)} %all_gather.15.inner_ref, bf16[2304,1792]{1,0:T(8,128)(2,1)S(1)} %copy-done.2), custom_call_target="tpu_custom_call" | custom-call | tf_op jit(solution)/shard_map/project_down/pallas_call | solution.py:463
  133.6 4.7 %all-to-all-start.2 = ((bf16[32,56,128]{2,1,0:T(8,128)(2,1)}), bf16[32,56,128]{2,1,0:T(8,128)(2,1)S(1)}, u32[]{:S(2)}, u32[]{:S(2)}) async-start(bf16[32,56,128]{2,1,0:T(8,128)(2,1)} %project_down.1), calls=%async_computation.2 | async-start | bytes 917504 | tf_op jit(solution)/shard_map/all_to_all | solution.py:510
  138.3 1.8 %collective-permute-start.7 = (bf16[4,1792]{1,0:T(4,128)(2,1)S(1)}, bf16[4,1792]{1,0:T(4,128)(2,1)S(1)}, u32[]{:S(2)}, u32[]{:S(2)}) collective-permute-start(bf16[4,1792]{1,0:T(4,128)(2,1)S(1)} %get-tuple-element.46), channel_id=1, source_target_pairs={{0,1},{1,0},{2,3},{3,2},{4,5},{5,4},{6,7},{7,6},{8,9},{9,8},{10,11... | collective-permute-start | bytes 43016 | tf_op jit(solution)/shard_map/ppermute | solution.py:245
  140.1 2.4 %collective-permute-start.8 = (bf16[4,1792]{1,0:T(4,128)(2,1)S(1)}, bf16[4,1792]{1,0:T(4,128)(2,1)S(1)}, u32[]{:S(2)}, u32[]{:S(2)}) collective-permute-start(bf16[4,1792]{1,0:T(4,128)(2,1)S(1)} %get-tuple-element.47), channel_id=1, source_target_pairs={{0,2},{1,3},{2,0},{3,1},{4,6},{5,7},{6,4},{7,5},{8,10},{9,11},{10,... | collective-permute-start | bytes 43016 | tf_op jit(solution)/shard_map/ppermute | solution.py:245
  142.8 4.3 %collective-permute-done.7.refs_1_ = bf16[4,1792]{1,0:T(4,128)(2,1)S(1)} collective-permute-done((bf16[4,1792]{1,0:T(4,128)(2,1)S(1)}, bf16[4,1792]{1,0:T(4,128)(2,1)S(1)}, u32[]{:S(2)}, u32[]{:S(2)}) %collective-permute-start.7) | collective-permute-done | bytes 14368 | tf_op jit(solution)/shard_map/ppermute | solution.py:245
  147.0 5.9 %collective-permute-done.8.refs_2_ = bf16[4,1792]{1,0:T(4,128)(2,1)S(1)} collective-permute-done((bf16[4,1792]{1,0:T(4,128)(2,1)S(1)}, bf16[4,1792]{1,0:T(4,128)(2,1)S(1)}, u32[]{:S(2)}, u32[]{:S(2)}) %collective-permute-start.8) | collective-permute-done | bytes 14368 | tf_op jit(solution)/shard_map/ppermute | solution.py:245
  (38 shorter events, 9.6 us)
Async XLA Ops:
  0.0 53.6 %slice-start = ((s8[7340032]{0:T(1024)(128)(4,1)}), s8[3145728]{0:T(1024)(128)(4,1)S(1)}, s32[]{:S(2)}) async-start(s8[7340032]{0:T(1024)(128)(4,1)} %bitcast.9), calls=%async_computation.3 | async-start | bytes 6291456
  2.7 1.1 copy-start.3
  3.8 0.7 copy-start.8
  4.5 32.3 %copy-start.5 = (bf16[4,512,128]{2,1,0:T(8,128)(2,1)S(1)}, bf16[4,512,128]{2,1,0:T(8,128)(2,1)}, u32[]{:S(2)}) copy-start(bf16[4,512,128]{2,1,0:T(8,128)(2,1)} %w_ref.1) | copy-start | bytes 1572868
  4.5 49.1 %slice-start.1 = ((s8[7340032]{0:T(1024)(128)(4,1)}), s8[4194304]{0:T(1024)(128)(4,1)S(1)}, s32[]{:S(2)}) async-start(s8[7340032]{0:T(1024)(128)(4,1)} %bitcast.9), calls=%async_computation.4 | async-start | bytes 8388608
  11.8 47.3 %copy-start.6 = (bf16[4,7168]{1,0:T(4,128)(2,1)S(1)}, bf16[4,7168]{1,0:T(4,128)(2,1)}, u32[]{:S(2)}) copy-start(bf16[4,7168]{1,0:T(4,128)(2,1)} %rows_ref) | copy-start | bytes 172036
  11.9 65.4 %copy-start.7 = (bf16[7168]{0:T(1024)(128)(2,1)S(1)}, bf16[7168]{0:T(1024)(128)(2,1)}, u32[]{:S(2)}) copy-start(bf16[7168]{0:T(1024)(128)(2,1)} %param.16) | copy-start | bytes 43012
  54.7 0.8 copy-start.4
  55.5 12.6 %all-to-all-start.1 = ((bf16[8,16,1792]{2,1,0:T(8,128)(2,1)}), bf16[8,16,1792]{2,1,0:T(8,128)(2,1)S(1)}, u32[]{:S(2)}, u32[]{:S(2)}) async-start(bf16[8,16,1792]{2,1,0:T(8,128)(2,1)} %bitcast.13), calls=%async_computation.1 | async-start | bytes 917504 | tf_op jit(solution)/shard_map/all_to_all | solution.py:510
  59.1 4.5 %collective-permute-start = (bf16[4,1792]{1,0:T(4,128)(2,1)S(1)}, bf16[4,1792]{1,0:T(4,128)(2,1)S(1)}, u32[]{:S(2)}, u32[]{:S(2)}) collective-permute-start(bf16[4,1792]{1,0:T(4,128)(2,1)S(1)} %get-tuple-element.31), channel_id=1, source_target_pairs={{0,1},{1,0},{2,3},{3,2},{4,5},{5,4},{6,7},{7,6},{8,9},{9,8},{10,11... | collective-permute-start | bytes 43016 | tf_op jit(solution)/shard_map/ppermute | solution.py:245
  59.2 4.7 %collective-permute-start.1 = (bf16[4,1792]{1,0:T(4,128)(2,1)S(1)}, bf16[4,1792]{1,0:T(4,128)(2,1)S(1)}, u32[]{:S(2)}, u32[]{:S(2)}) collective-permute-start(bf16[4,1792]{1,0:T(4,128)(2,1)S(1)} %get-tuple-element.32), channel_id=1, source_target_pairs={{0,2},{1,3},{2,0},{3,1},{4,6},{5,7},{6,4},{7,5},{8,10},{9,11},{10,... | collective-permute-start | bytes 43016 | tf_op jit(solution)/shard_map/ppermute | solution.py:245
  61.5 5.5 %collective-permute-start.2 = (bf16[4,1792]{1,0:T(4,128)(2,1)S(1)}, bf16[4,1792]{1,0:T(4,128)(2,1)S(1)}, u32[]{:S(2)}, u32[]{:S(2)}) collective-permute-start(bf16[4,1792]{1,0:T(4,128)(2,1)S(1)} %get-tuple-element.33), channel_id=1, source_target_pairs={{0,3},{1,2},{2,1},{3,0},{4,7},{5,6},{6,5},{7,4},{8,11},{9,10},{10,... | collective-permute-start | bytes 43016 | tf_op jit(solution)/shard_map/ppermute | solution.py:245
  77.2 3.3 %copy-start = (bf16[1792,2304]{1,0:T(8,128)(2,1)S(1)}, bf16[1792,2304]{1,0:T(8,128)(2,1)}, u32[]{:S(2)}) copy-start(bf16[1792,2304]{1,0:T(8,128)(2,1)} %gate_ref) | copy-start | bytes 24772612
  80.6 3.3 %copy-start.1 = (bf16[1792,2304]{1,0:T(8,128)(2,1)S(1)}, bf16[1792,2304]{1,0:T(8,128)(2,1)}, u32[]{:S(2)}) copy-start(bf16[1792,2304]{1,0:T(8,128)(2,1)} %up_ref) | copy-start | bytes 24772612
  86.2 16.7 %collective-permute-start.3 = (bf16[64,2432]{1,0:T(8,128)(2,1)S(1)}, bf16[64,2432]{1,0:T(8,128)(2,1)S(1)}, u32[]{:S(2)}, u32[]{:S(2)}) collective-permute-start(bf16[64,2432]{1,0:T(8,128)(2,1)S(1)} %get-tuple-element.38), channel_id=1, source_target_pairs={{0,1},{1,0},{2,3},{3,2},{4,5},{5,4},{6,7},{7,6},{8,9},{9,8},{10,11... | collective-permute-start | bytes 933896 | tf_op jit(solution)/shard_map/ppermute | solution.py:245
  86.3 16.6 %collective-permute-start.4 = (bf16[64,2304]{1,0:T(8,128)(2,1)S(1)}, bf16[64,2304]{1,0:T(8,128)(2,1)S(1)}, u32[]{:S(2)}, u32[]{:S(2)}) collective-permute-start(bf16[64,2304]{1,0:T(8,128)(2,1)S(1)} %get-tuple-element.39), channel_id=1, source_target_pairs={{0,2},{1,3},{2,0},{3,1},{4,6},{5,7},{6,4},{7,5},{8,10},{9,11},{10,... | collective-permute-start | bytes 884744 | tf_op jit(solution)/shard_map/ppermute | solution.py:245
  103.1 9.0 %collective-permute-start.5 = (bf16[32,2432]{1,0:T(8,128)(2,1)S(1)}, bf16[32,2432]{1,0:T(8,128)(2,1)S(1)}, u32[]{:S(2)}, u32[]{:S(2)}) collective-permute-start(bf16[32,2432]{1,0:T(8,128)(2,1)S(1)} %get-tuple-element.42), channel_id=1, source_target_pairs={{0,2},{1,3},{2,0},{3,1},{4,6},{5,7},{6,4},{7,5},{8,10},{9,11},{10,... | collective-permute-start | bytes 466952 | tf_op jit(solution)/shard_map/ppermute | solution.py:245
  103.7 6.7 %collective-permute-start.6 = (bf16[32,2304]{1,0:T(8,128)(2,1)S(1)}, bf16[32,2304]{1,0:T(8,128)(2,1)S(1)}, u32[]{:S(2)}, u32[]{:S(2)}) collective-permute-start(bf16[32,2304]{1,0:T(8,128)(2,1)S(1)} %get-tuple-element.43), channel_id=1, source_target_pairs={{0,1},{1,0},{2,3},{3,2},{4,5},{5,4},{6,7},{7,6},{8,9},{9,8},{10,11... | collective-permute-start | bytes 442376 | tf_op jit(solution)/shard_map/ppermute | solution.py:245
  128.1 3.3 %copy-start.2 = (bf16[2304,1792]{1,0:T(8,128)(2,1)S(1)}, bf16[2304,1792]{1,0:T(8,128)(2,1)}, u32[]{:S(2)}) copy-start(bf16[2304,1792]{1,0:T(8,128)(2,1)} %w_ref.3) | copy-start | bytes 24772612
  133.6 19.4 %all-to-all-start.2 = ((bf16[32,56,128]{2,1,0:T(8,128)(2,1)}), bf16[32,56,128]{2,1,0:T(8,128)(2,1)S(1)}, u32[]{:S(2)}, u32[]{:S(2)}) async-start(bf16[32,56,128]{2,1,0:T(8,128)(2,1)} %project_down.1), calls=%async_computation.2 | async-start | bytes 917504 | tf_op jit(solution)/shard_map/all_to_all | solution.py:510
  138.3 8.7 %collective-permute-start.7 = (bf16[4,1792]{1,0:T(4,128)(2,1)S(1)}, bf16[4,1792]{1,0:T(4,128)(2,1)S(1)}, u32[]{:S(2)}, u32[]{:S(2)}) collective-permute-start(bf16[4,1792]{1,0:T(4,128)(2,1)S(1)} %get-tuple-element.46), channel_id=1, source_target_pairs={{0,1},{1,0},{2,3},{3,2},{4,5},{5,4},{6,7},{7,6},{8,9},{9,8},{10,11... | collective-permute-start | bytes 43016 | tf_op jit(solution)/shard_map/ppermute | solution.py:245
  140.1 12.8 %collective-permute-start.8 = (bf16[4,1792]{1,0:T(4,128)(2,1)S(1)}, bf16[4,1792]{1,0:T(4,128)(2,1)S(1)}, u32[]{:S(2)}, u32[]{:S(2)}) collective-permute-start(bf16[4,1792]{1,0:T(4,128)(2,1)S(1)} %get-tuple-element.47), channel_id=1, source_target_pairs={{0,2},{1,3},{2,0},{3,1},{4,6},{5,7},{6,4},{7,5},{8,10},{9,11},{10,... | collective-permute-start | bytes 43016 | tf_op jit(solution)/shard_map/ppermute | solution.py:245
  142.5 10.4 %collective-permute-start.9 = (bf16[4,1792]{1,0:T(4,128)(2,1)S(1)}, bf16[4,1792]{1,0:T(4,128)(2,1)S(1)}, u32[]{:S(2)}, u32[]{:S(2)}) collective-permute-start(bf16[4,1792]{1,0:T(4,128)(2,1)S(1)} %get-tuple-element.48), channel_id=1, source_target_pairs={{0,3},{1,2},{2,1},{3,0},{4,7},{5,6},{6,5},{7,4},{8,11},{9,10},{10,... | collective-permute-start | bytes 43016 | tf_op jit(solution)/shard_map/ppermute | solution.py:245

commit v7 on v6

--- a/solution.py
+++ b/solution.py
@@ -103,16 +103,16 @@
         mass[r] = mass[r] * keep + part
         best[r] = new
         weights[...] = weight.astype(weights.dtype)
-        keeps[...] = keep.T[:8, :]
+        keeps[...] = keep
 
     def gather(r, i, weights, keeps):
         values = lax.dot_general(
+            weights[...],
             held[i, :C, :],
-            weights[...],
             (((1,), (1,)), ((), ())),
             preferred_element_type=jnp.float32,
         )
-        acc[r] = acc[r] * keeps[:1, :] + values
+        acc[r] = acc[r] * keeps[:, :1] + values
 
     zero = jnp.int32(0)
     fetch(zero, zero, pairs > 0)
@@ -139,7 +139,7 @@
     share = heads // out_ref.shape[0]
     for r in range(nreq):
         total = jnp.sum(mass[r], axis=1, keepdims=True)
-        score0[:, :C] = acc[r].T / total
+        score0[:, :C] = acc[r] / total
         for d in range(out_ref.shape[0]):
             done[d, r * share : (r + 1) * share, :] = score0[d * share : (d + 1) * share, :C]
     out_ref[...] = done[...].astype(out_ref.dtype)
@@ -175,9 +175,9 @@
             pltpu.VMEM((heads, tile), jnp.float32),
             pltpu.VMEM((heads, tile), jnp.bfloat16),
             pltpu.VMEM((heads, tile), jnp.bfloat16),
-            pltpu.VMEM((8, heads), jnp.float32),
-            pltpu.VMEM((8, heads), jnp.float32),
-            pltpu.VMEM((nreq, C, heads), jnp.float32),
+            pltpu.VMEM((heads, 128), jnp.float32),
+            pltpu.VMEM((heads, 128), jnp.float32),
+            pltpu.VMEM((nreq, heads, C), jnp.float32),
             pltpu.VMEM((ranks, nreq * heads // ranks, C), jnp.float32),
             pltpu.VMEM((nreq, heads, 128), jnp.float32),
             pltpu.VMEM((nreq, heads, 128), jnp.float32),
@@ -194,7 +194,11 @@
             transcendentals=heads * tokens,
         ),
         name="attention",
-    )(lengths, queries, pltpu.with_memory_space_constraint(cache_t, pltpu.HBM))
+    )(
+        pltpu.with_memory_space_constraint(lengths, pltpu.HBM),
+        fetched(queries),
+        pltpu.with_memory_space_constraint(cache_t, pltpu.HBM),
+    )
 
 
 def head_values_kernel(latent_ref, w_ref, out_ref, values):
@@ -526,9 +530,7 @@
 
     query = queries.reshape(per_rank, heads_all, row_length)
     latent = attend(lengths, query, paged_latent_cache.T, ranks)
-    latent, residual, w_o, w_gate, w_up, w_down = lax.optimization_barrier(
-        (latent, residual, w_o, w_gate, w_up, w_down)
-    )
+    latent, residual = lax.optimization_barrier((latent, residual))
     added = split_columns(residual, ranks_tp)
     added = [added[0]] + [across(added[k], "tp", k) for k in range(1, ranks_tp)]
     latent = swap(latent, ("dp", "tp"))
@@ -536,6 +538,7 @@
     values = head_values(latent.reshape(requests * heads_here, C), w_uv)
     values = lax.all_gather(values, "tp", axis=0)
     attn = project_out(values, w_o, requests)
+    attn, added = lax.optimization_barrier((attn, added))
     attn = swap(attn.reshape(ranks_dp, requests // ranks_dp, width), "dp")
     hidden = make_hidden(attn, added)
     hidden = lax.all_gather(hidden, "dp", axis=0, tiled=True)
@@ -555,6 +558,7 @@
         rows = [rows[0]] + [across(rows[k], "tp", k) for k in range(1, ranks_tp)]
         parts = [swap(part.reshape(ranks_tp, -1, part.shape[1]), "tp") for part in parts]
     inner = make_inner(parts, units, model)
+    inner, rows = lax.optimization_barrier((inner, rows))
     inner = lax.all_gather(inner, "tp", axis=0, tiled=True)
     ffn = swap(project_down(inner, w_down, ranks), ("dp", "tp"))
     return make_layer(ffn, rows, model)

time: 156 us -> 154 us (0.987); the launches traced: 154 us -> 154 us
  waiting for transfers between devices: 34.8 us -> 29 us
  blocking collectives: 65.8 us -> 70.1 us
  local copies, waits for them, and re-layouts: 15.3 us -> 11.5 us
  Pallas kernels: 14.9 us -> 18 us
  starting transfers between devices: 22.8 us -> 25.1 us
    ppermute x10, waiting for transfers between devices: 33.7 us -> 18.5 us  [across(): lax.ppermute(piece, axis, [(k, k ^ distance) for k in range(lax.axis_size...]
    all_to_all x2 -> x1, waiting for transfers between devices: 1.12 us -> 10.5 us  [swap(): return lax.all_to_all(parts, axes, split_axis=0, concat_axis=0, tiled=True)]
    all_to_all x1 -> x2, blocking collectives: 24.9 us -> 29 us  [swap(): return lax.all_to_all(parts, axes, split_axis=0, concat_axis=0, tiled=True)]
    all_to_all x2 -> x1, starting transfers between devices: 8.27 us -> 12.2 us  [swap(): return lax.all_to_all(parts, axes, split_axis=0, concat_axis=0, tiled=True)]
    pallas_call x1, Pallas kernels: 7.37 us -> 11.3 us  [attend(): pl.pallas_call(attention_kernel, out_shape=jax.ShapeDtypeStruct((ranks, n...]
    unnamed x22 -> x16, local copies, waits for them, and re-layouts: 12.6 us -> 9.8 us
    ppermute x10, starting transfers between devices: 14.5 us -> 12.9 us  [across(): lax.ppermute(piece, axis, [(k, k ^ distance) for k in range(lax.axis_size...]
  transfers between devices with their start and end apart: 12 -> 11, of which waited for: 8 -> 5; matrix products, arithmetic and copies ran while one was open for 0% -> 0% of each run, Pallas kernels for 0% -> 1%
where the time goes in v7:
time: 154 us
  blocking collectives  70.1 us (46%)
  waiting for transfers between devices  29 us (19%)
  starting transfers between devices  25.1 us (16%)
  Pallas kernels  18 us (12%)
  local copies, waits for them, and re-layouts  11.5 us (7%)
    all_to_all x2, blocking collectives, swap(): return lax.all_to_all(parts, axes, split_axis=0, concat_axis=0, tiled=True)  29 us
    ppermute x10, waiting for transfers between devices, across(): lax.ppermute(piece, axis, [(k, k ^ distance) for k in range(lax.axis_size...  18.5 us
    all_gather x1, blocking collectives, local(): inner = lax.all_gather(inner, 'tp', axis=0, tiled=True)  16.3 us
    all_gather x1, blocking collectives, local(): values = lax.all_gather(values, 'tp', axis=0)  16 us
    ppermute x10, starting transfers between devices, across(): lax.ppermute(piece, axis, [(k, k ^ distance) for k in range(lax.axis_size...  12.9 us
    all_to_all x1, starting transfers between devices, swap(): return lax.all_to_all(parts, axes, split_axis=0, concat_axis=0, tiled=True)  12.2 us
    pallas_call x1, Pallas kernels, attend(): pl.pallas_call(attention_kernel, out_shape=jax.ShapeDtypeStruct((ranks, n...  11.3 us
    all_to_all x1, waiting for transfers between devices, swap(): return lax.all_to_all(parts, axes, split_axis=0, concat_axis=0, tiled=True)  10.5 us
  transfers between devices with their start and end apart: 11, of which 5 were waited for; matrix products, arithmetic and copies ran while one was open for 0% of the time, Pallas kernels for 1%

profile of v7, /device:TPU:0, one launch (start us, length us, event | category | flops | bytes accessed | tf_op | source)
XLA Modules:
  0.0 154.0 jit_solution(7124304042267766637)
XLA Ops:
  0.0 1.7 %reshape.12.q_ref = bf16[4,128,576]{2,1,0:T(8,128)(2,1)S(1)} reshape(bf16[4,73728]{1,0:T(4,128)(2,1)} %param.11) | data formatting | bytes 1179648 | tf_op jit(solution)/shard_map/reshape | solution.py:531
  1.8 11.3 %attention.1 = bf16[32,16,512]{2,1,0:T(8,128)(2,1)} custom-call(s32[128]{0:T(128)} %lens_ref.1, bf16[4,128,576]{2,1,0:T(8,128)(2,1)S(1)} %reshape.12.q_ref, bf16[576,14336]{1,0:T(8,128)(2,1)} %bitcast.19), custom_call_target="tpu_custom_call" | custom-call | flops 3992977408 | bytes 16515072 | tf_op jit(solution)/shard_map/attention/pallas_call | solution.py:165
  13.1 12.2 %all-to-all-start = ((bf16[32,16,512]{2,1,0:T(8,128)(2,1)}), bf16[32,16,512]{2,1,0:T(8,128)(2,1)S(1)}, u32[]{:S(2)}, u32[]{:S(2)}) async-start(bf16[32,16,512]{2,1,0:T(8,128)(2,1)} %attention.1), calls=%async_computation | async-start | bytes 1048576 | tf_op jit(solution)/shard_map/all_to_all | solution.py:514
  25.3 1.8 %collective-permute-start = (bf16[4,1792]{1,0:T(4,128)(2,1)S(1)}, bf16[4,1792]{1,0:T(4,128)(2,1)S(1)}, u32[]{:S(2)}, u32[]{:S(2)}) collective-permute-start(bf16[4,1792]{1,0:T(4,128)(2,1)S(1)} %get-tuple-element.36), channel_id=1, source_target_pairs={{0,1},{1,0},{2,3},{3,2},{4,5},{5,4},{6,7},{7,6},{8,9},{9,8},{10,11... | collective-permute-start | bytes 43016 | tf_op jit(solution)/shard_map/ppermute | solution.py:249
  27.1 2.4 %collective-permute-start.1 = (bf16[4,1792]{1,0:T(4,128)(2,1)S(1)}, bf16[4,1792]{1,0:T(4,128)(2,1)S(1)}, u32[]{:S(2)}, u32[]{:S(2)}) collective-permute-start(bf16[4,1792]{1,0:T(4,128)(2,1)S(1)} %get-tuple-element.37), channel_id=1, source_target_pairs={{0,2},{1,3},{2,0},{3,1},{4,6},{5,7},{6,4},{7,5},{8,10},{9,11},{10,... | collective-permute-start | bytes 43016 | tf_op jit(solution)/shard_map/ppermute | solution.py:249
  29.8 10.5 %all-to-all-done = bf16[32,16,512]{2,1,0:T(8,128)(2,1)S(1)} async-done(((bf16[32,16,512]{2,1,0:T(8,128)(2,1)}), bf16[32,16,512]{2,1,0:T(8,128)(2,1)S(1)}, u32[]{:S(2)}, u32[]{:S(2)}) %all-to-all-start) | async-done | bytes 524320 | tf_op jit(solution)/shard_map/all_to_all | solution.py:514
  41.1 16.0 %all-gather = bf16[512,512]{1,0:T(8,128)(2,1)S(1)} all-gather(bf16[128,512]{1,0:T(8,128)(2,1)S(1)} %head_values.1), channel_id=2, replica_groups=mesh['dp'=8,'tp'=4] {'tp'}, dimensions={0}, use_global_device_ids=true | all-gather | bytes 655360 | tf_op jit(solution)/shard_map/all_gather | solution.py:539
  57.0 3.1 %copy-done.2 = bf16[2048,1792]{1,0:T(8,128)(2,1)S(1)} copy-done((bf16[2048,1792]{1,0:T(8,128)(2,1)S(1)}, bf16[2048,1792]{1,0:T(8,128)(2,1)}, u32[]{:S(2)}) %copy-start.2) | copy-done | bytes 7340056
  60.1 1.1 project_out.1
  61.3 12.7 %all_to_all.15.parts_ref = bf16[8,16,1792]{2,1,0:T(8,128)(2,1)S(1)} all-to-all(bf16[8,16,1792]{2,1,0:T(8,128)(2,1)S(1)} %bitcast.13), channel_id=1, replica_groups=mesh['dp'=8,'tp'=4] {'dp'}, dimensions={0} | all-to-all | bytes 917504 | tf_op jit(solution)/shard_map/all_to_all | solution.py:514
  74.0 8.8 %all_gather.14.hidden_ref = bf16[128,1792]{1,0:T(8,128)(2,1)S(1)} all-gather(bf16[16,1792]{1,0:T(8,128)(2,1)S(1)} %hidden.1), channel_id=1, replica_groups=mesh['dp'=8,'tp'=4] {'dp'}, dimensions={0}, use_global_device_ids=true | all-gather | bytes 516096 | tf_op jit(solution)/shard_map/all_gather | solution.py:544
  82.8 3.3 %copy-done = bf16[1792,2304]{1,0:T(8,128)(2,1)S(1)} copy-done((bf16[1792,2304]{1,0:T(8,128)(2,1)S(1)}, bf16[1792,2304]{1,0:T(8,128)(2,1)}, u32[]{:S(2)}) %copy-start) | copy-done | bytes 8257560
  86.2 3.3 %copy-done.1 = bf16[1792,2304]{1,0:T(8,128)(2,1)S(1)} copy-done((bf16[1792,2304]{1,0:T(8,128)(2,1)S(1)}, bf16[1792,2304]{1,0:T(8,128)(2,1)}, u32[]{:S(2)}) %copy-start.1) | copy-done | bytes 8257560
  89.5 2.3 %gate_up.1 = (bf16[64,2432]{1,0:T(8,128)(2,1)S(1)}, bf16[64,2304]{1,0:T(8,128)(2,1)S(1)}, bf16[64,2432]{1,0:T(8,128)(2,1)S(1)}, bf16[64,2304]{1,0:T(8,128)(2,1)S...) custom-call(bf16[128,1792]{1,0:T(8,128)(2,1)S(1)} %all_gather.14.hid, ...), custom_call_target="tpu_custom_call" | custom-call | tf_op jit(solution)/shard_map/gate_up/pallas_call | solution.py:378
  91.9 1.5 collective-permute-start.4
  93.4 15.1 %collective-permute-done.4.refs_3_ = bf16[64,2304]{1,0:T(8,128)(2,1)S(1)} collective-permute-done((bf16[64,2304]{1,0:T(8,128)(2,1)S(1)}, bf16[64,2304]{1,0:T(8,128)(2,1)S(1)}, u32[]{:S(2)}, u32[]{:S(2)}) %collective-permute-start.4) | collective-permute-done | bytes 294944 | tf_op jit(solution)/shard_map/ppermute | solution.py:249
  109.3 1.8 %collective-permute-start.6 = (bf16[32,2304]{1,0:T(8,128)(2,1)S(1)}, bf16[32,2304]{1,0:T(8,128)(2,1)S(1)}, u32[]{:S(2)}, u32[]{:S(2)}) collective-permute-start(bf16[32,2304]{1,0:T(8,128)(2,1)S(1)} %get-tuple-element.51), channel_id=1, source_target_pairs={{0,1},{1,0},{2,3},{3,2},{4,5},{5,4},{6,7},{7,6},{8,9},{9,8},{10,11... | collective-permute-start | bytes 442376 | tf_op jit(solution)/shard_map/ppermute | solution.py:249
  111.4 2.3 %collective-permute-start.8 = (bf16[4,1792]{1,0:T(4,128)(2,1)S(1)}, bf16[4,1792]{1,0:T(4,128)(2,1)S(1)}, u32[]{:S(2)}, u32[]{:S(2)}) collective-permute-start(bf16[4,1792]{1,0:T(4,128)(2,1)S(1)} %get-tuple-element.54), channel_id=1, source_target_pairs={{0,2},{1,3},{2,0},{3,1},{4,6},{5,7},{6,4},{7,5},{8,10},{9,11},{10,... | collective-permute-start | bytes 43016 | tf_op jit(solution)/shard_map/ppermute | solution.py:249
  113.7 1.8 %collective-permute-start.9 = (bf16[4,1792]{1,0:T(4,128)(2,1)S(1)}, bf16[4,1792]{1,0:T(4,128)(2,1)S(1)}, u32[]{:S(2)}, u32[]{:S(2)}) collective-permute-start(bf16[4,1792]{1,0:T(4,128)(2,1)S(1)} %get-tuple-element.55), channel_id=1, source_target_pairs={{0,3},{1,2},{2,1},{3,0},{4,7},{5,6},{6,5},{7,4},{8,11},{9,10},{10,... | collective-permute-start | bytes 43016 | tf_op jit(solution)/shard_map/ppermute | solution.py:249
  116.2 1.8 %collective-permute-done.5 = bf16[32,2432]{1,0:T(8,128)(2,1)S(1)} collective-permute-done((bf16[32,2432]{1,0:T(8,128)(2,1)S(1)}, bf16[32,2432]{1,0:T(8,128)(2,1)S(1)}, u32[]{:S(2)}, u32[]{:S(2)}) %collective-permute-start.5) | collective-permute-done | bytes 155680 | tf_op jit(solution)/shard_map/ppermute | solution.py:249
  118.2 1.0 collective-permute-done.9.refs_3_
  119.2 16.3 %all_gather.15.inner_ref = bf16[128,2304]{1,0:T(8,128)(2,1)S(1)} all-gather(bf16[32,2304]{1,0:T(8,128)(2,1)S(1)} %inner.1), channel_id=1, replica_groups=mesh['dp'=8,'tp'=4] {'tp'}, dimensions={0}, use_global_device_ids=true | all-gather | bytes 737280 | tf_op jit(solution)/shard_map/all_gather | solution.py:562
  135.5 1.3 project_down.1
  136.9 16.4 %all_to_all.16.parts_ref = bf16[32,56,128]{2,1,0:T(8,128)(2,1)S(1)} all-to-all(bf16[32,56,128]{2,1,0:T(8,128)(2,1)S(1)} %project_down.1), channel_id=1, replica_groups=mesh['dp'=8,'tp'=4] {'dp','tp'}, dimensions={0} | all-to-all | bytes 917504 | tf_op jit(solution)/shard_map/all_to_all | solution.py:514
  (31 shorter events, 3.8 us)
Async XLA Ops:
  1.7 23.5 %copy-start.4 = (bf16[4,7168]{1,0:T(4,128)(2,1)S(1)}, bf16[4,7168]{1,0:T(4,128)(2,1)}, u32[]{:S(2)}) copy-start(bf16[4,7168]{1,0:T(4,128)(2,1)} %rows_ref) | copy-start | bytes 172036
  1.8 38.5 %copy-start.3 = (bf16[4,512,128]{2,1,0:T(8,128)(2,1)S(1)}, bf16[4,512,128]{2,1,0:T(8,128)(2,1)}, u32[]{:S(2)}) copy-start(bf16[4,512,128]{2,1,0:T(8,128)(2,1)} %w_ref.3) | copy-start | bytes 1572868
  13.0 69.8 %copy-start.5 = (bf16[7168]{0:T(1024)(128)(2,1)S(1)}, bf16[7168]{0:T(1024)(128)(2,1)}, u32[]{:S(2)}) copy-start(bf16[7168]{0:T(1024)(128)(2,1)} %param.16) | copy-start | bytes 43012
  13.1 27.2 %all-to-all-start = ((bf16[32,16,512]{2,1,0:T(8,128)(2,1)}), bf16[32,16,512]{2,1,0:T(8,128)(2,1)S(1)}, u32[]{:S(2)}, u32[]{:S(2)}) async-start(bf16[32,16,512]{2,1,0:T(8,128)(2,1)} %attention.1), calls=%async_computation | async-start | bytes 1048576 | tf_op jit(solution)/shard_map/all_to_all | solution.py:514
  25.3 35.9 %collective-permute-start = (bf16[4,1792]{1,0:T(4,128)(2,1)S(1)}, bf16[4,1792]{1,0:T(4,128)(2,1)S(1)}, u32[]{:S(2)}, u32[]{:S(2)}) collective-permute-start(bf16[4,1792]{1,0:T(4,128)(2,1)S(1)} %get-tuple-element.36), channel_id=1, source_target_pairs={{0,1},{1,0},{2,3},{3,2},{4,5},{5,4},{6,7},{7,6},{8,9},{9,8},{10,11... | collective-permute-start | bytes 43016 | tf_op jit(solution)/shard_map/ppermute | solution.py:249
  27.1 34.1 %collective-permute-start.1 = (bf16[4,1792]{1,0:T(4,128)(2,1)S(1)}, bf16[4,1792]{1,0:T(4,128)(2,1)S(1)}, u32[]{:S(2)}, u32[]{:S(2)}) collective-permute-start(bf16[4,1792]{1,0:T(4,128)(2,1)S(1)} %get-tuple-element.37), channel_id=1, source_target_pairs={{0,2},{1,3},{2,0},{3,1},{4,6},{5,7},{6,4},{7,5},{8,10},{9,11},{10,... | collective-permute-start | bytes 43016 | tf_op jit(solution)/shard_map/ppermute | solution.py:249
  29.6 31.7 %collective-permute-start.2 = (bf16[4,1792]{1,0:T(4,128)(2,1)S(1)}, bf16[4,1792]{1,0:T(4,128)(2,1)S(1)}, u32[]{:S(2)}, u32[]{:S(2)}) collective-permute-start(bf16[4,1792]{1,0:T(4,128)(2,1)S(1)} %get-tuple-element.38), channel_id=1, source_target_pairs={{0,3},{1,2},{2,1},{3,0},{4,7},{5,6},{6,5},{7,4},{8,11},{9,10},{10,... | collective-permute-start | bytes 43016 | tf_op jit(solution)/shard_map/ppermute | solution.py:249
  57.0 3.1 %copy-start.2 = (bf16[2048,1792]{1,0:T(8,128)(2,1)S(1)}, bf16[2048,1792]{1,0:T(8,128)(2,1)}, u32[]{:S(2)}) copy-start(bf16[2048,1792]{1,0:T(8,128)(2,1)} %w_ref.4) | copy-start | bytes 22020100
  60.1 75.4 %slice-start = ((s8[8257536]{0:T(1024)(128)(4,1)}), s8[4194304]{0:T(1024)(128)(4,1)S(1)}, s32[]{:S(2)}) async-start(s8[8257536]{0:T(1024)(128)(4,1)} %bitcast.9), calls=%async_computation.3 | async-start | bytes 8388608
  82.8 3.3 %copy-start = (bf16[1792,2304]{1,0:T(8,128)(2,1)S(1)}, bf16[1792,2304]{1,0:T(8,128)(2,1)}, u32[]{:S(2)}) copy-start(bf16[1792,2304]{1,0:T(8,128)(2,1)} %gate_ref.1) | copy-start | bytes 24772612
  86.2 3.3 %copy-start.1 = (bf16[1792,2304]{1,0:T(8,128)(2,1)S(1)}, bf16[1792,2304]{1,0:T(8,128)(2,1)}, u32[]{:S(2)}) copy-start(bf16[1792,2304]{1,0:T(8,128)(2,1)} %up_ref.1) | copy-start | bytes 24772612
  89.5 46.0 %slice-start.1 = ((s8[8257536]{0:T(1024)(128)(4,1)}), s8[4063232]{0:T(1024)(128)(4,1)S(1)}, s32[]{:S(2)}) async-start(s8[8257536]{0:T(1024)(128)(4,1)} %bitcast.9), calls=%async_computation.4 | async-start | bytes 8126464
  91.8 16.7 %collective-permute-start.3 = (bf16[64,2432]{1,0:T(8,128)(2,1)S(1)}, bf16[64,2432]{1,0:T(8,128)(2,1)S(1)}, u32[]{:S(2)}, u32[]{:S(2)}) collective-permute-start(bf16[64,2432]{1,0:T(8,128)(2,1)S(1)} %get-tuple-element.46), channel_id=1, source_target_pairs={{0,1},{1,0},{2,3},{3,2},{4,5},{5,4},{6,7},{7,6},{8,9},{9,8},{10,11... | collective-permute-start | bytes 933896 | tf_op jit(solution)/shard_map/ppermute | solution.py:249
  91.9 16.6 %collective-permute-start.4 = (bf16[64,2304]{1,0:T(8,128)(2,1)S(1)}, bf16[64,2304]{1,0:T(8,128)(2,1)S(1)}, u32[]{:S(2)}, u32[]{:S(2)}) collective-permute-start(bf16[64,2304]{1,0:T(8,128)(2,1)S(1)} %get-tuple-element.47), channel_id=1, source_target_pairs={{0,2},{1,3},{2,0},{3,1},{4,6},{5,7},{6,4},{7,5},{8,10},{9,11},{10,... | collective-permute-start | bytes 884744 | tf_op jit(solution)/shard_map/ppermute | solution.py:249
  108.7 9.3 %collective-permute-start.5 = (bf16[32,2432]{1,0:T(8,128)(2,1)S(1)}, bf16[32,2432]{1,0:T(8,128)(2,1)S(1)}, u32[]{:S(2)}, u32[]{:S(2)}) collective-permute-start(bf16[32,2432]{1,0:T(8,128)(2,1)S(1)} %get-tuple-element.50), channel_id=1, source_target_pairs={{0,2},{1,3},{2,0},{3,1},{4,6},{5,7},{6,4},{7,5},{8,10},{9,11},{10,... | collective-permute-start | bytes 466952 | tf_op jit(solution)/shard_map/ppermute | solution.py:249
  109.3 6.8 %collective-permute-start.6 = (bf16[32,2304]{1,0:T(8,128)(2,1)S(1)}, bf16[32,2304]{1,0:T(8,128)(2,1)S(1)}, u32[]{:S(2)}, u32[]{:S(2)}) collective-permute-start(bf16[32,2304]{1,0:T(8,128)(2,1)S(1)} %get-tuple-element.51), channel_id=1, source_target_pairs={{0,1},{1,0},{2,3},{3,2},{4,5},{5,4},{6,7},{7,6},{8,9},{9,8},{10,11... | collective-permute-start | bytes 442376 | tf_op jit(solution)/shard_map/ppermute | solution.py:249
  111.1 7.1 %collective-permute-start.7 = (bf16[4,1792]{1,0:T(4,128)(2,1)S(1)}, bf16[4,1792]{1,0:T(4,128)(2,1)S(1)}, u32[]{:S(2)}, u32[]{:S(2)}) collective-permute-start(bf16[4,1792]{1,0:T(4,128)(2,1)S(1)} %get-tuple-element.53), channel_id=1, source_target_pairs={{0,1},{1,0},{2,3},{3,2},{4,5},{5,4},{6,7},{7,6},{8,9},{9,8},{10,11... | collective-permute-start | bytes 43016 | tf_op jit(solution)/shard_map/ppermute | solution.py:249
  111.4 6.8 %collective-permute-start.8 = (bf16[4,1792]{1,0:T(4,128)(2,1)S(1)}, bf16[4,1792]{1,0:T(4,128)(2,1)S(1)}, u32[]{:S(2)}, u32[]{:S(2)}) collective-permute-start(bf16[4,1792]{1,0:T(4,128)(2,1)S(1)} %get-tuple-element.54), channel_id=1, source_target_pairs={{0,2},{1,3},{2,0},{3,1},{4,6},{5,7},{6,4},{7,5},{8,10},{9,11},{10,... | collective-permute-start | bytes 43016 | tf_op jit(solution)/shard_map/ppermute | solution.py:249
  113.7 5.5 %collective-permute-start.9 = (bf16[4,1792]{1,0:T(4,128)(2,1)S(1)}, bf16[4,1792]{1,0:T(4,128)(2,1)S(1)}, u32[]{:S(2)}, u32[]{:S(2)}) collective-permute-start(bf16[4,1792]{1,0:T(4,128)(2,1)S(1)} %get-tuple-element.55), channel_id=1, source_target_pairs={{0,3},{1,2},{2,1},{3,0},{4,7},{5,6},{6,5},{7,4},{8,11},{9,10},{10,... | collective-permute-start | bytes 43016 | tf_op jit(solution)/shard_map/ppermute | solution.py:249

commit v8 on v6

--- a/solution.py
+++ b/solution.py
@@ -194,54 +194,56 @@
             transcendentals=heads * tokens,
         ),
         name="attention",
-    )(lengths, queries, pltpu.with_memory_space_constraint(cache_t, pltpu.HBM))
-
-
-def head_values_kernel(latent_ref, w_ref, out_ref, values):
+    )(
+        pltpu.with_memory_space_constraint(lengths, pltpu.HBM),
+        fetched(queries),
+        pltpu.with_memory_space_constraint(cache_t, pltpu.HBM),
+    )
+
+
+def head_values_kernel(latent_ref, w_ref, residual_ref, out_ref, values, slots):
     heads, _, wide = w_ref.shape
-    requests = out_ref.shape[0]
+    per_rank, model = residual_ref.shape
+    requests = latent_ref.shape[0] // heads
     latent = latent_ref[...]
     for h in range(heads):
         values[...] = jnp.dot(latent, w_ref[h], preferred_element_type=jnp.float32)
         picked = values[pl.ds(h, requests, stride=heads), :]
-        out_ref[:, h * wide : (h + 1) * wide] = picked.astype(out_ref.dtype)
-
-
-def head_values(latent, w_uv):
+        out_ref[:requests, h * wide : (h + 1) * wide] = picked.astype(out_ref.dtype)
+    ranks = lax.axis_size("tp")
+    groups = model // ranks // 128
+    rows = (out_ref.shape[0] - requests) // ranks
+    across = out_ref.shape[1] // 128
+    slots[...] = jnp.zeros_like(slots)
+    for t in range(ranks):
+        for g in range(groups):
+            at = (t * groups + g) * 128
+            row = t * rows + (g // across) * per_rank
+            column = (g % across) * 128
+            slots[row : row + per_rank, column : column + 128] = residual_ref[
+                :, at : at + 128
+            ].astype(jnp.float32)
+    out_ref[requests:, :] = slots[...].astype(out_ref.dtype)
+
+
+def head_values(latent, w_uv, residual, slot_rows):
     heads, _, wide = w_uv.shape
     requests = latent.shape[0] // heads
     return pl.pallas_call(
         head_values_kernel,
-        out_shape=jax.ShapeDtypeStruct((requests, heads * wide), jnp.bfloat16),
-        in_specs=in_vmem(2),
-        out_specs=pl.BlockSpec(memory_space=pltpu.VMEM),
-        scratch_shapes=[pltpu.VMEM((latent.shape[0], wide), jnp.float32)],
+        out_shape=jax.ShapeDtypeStruct((requests + slot_rows, heads * wide), jnp.bfloat16),
+        in_specs=in_vmem(3),
+        out_specs=pl.BlockSpec(memory_space=pltpu.VMEM),
+        scratch_shapes=[
+            pltpu.VMEM((latent.shape[0], wide), jnp.float32),
+            pltpu.VMEM((slot_rows, heads * wide), jnp.float32),
+        ],
         compiler_params=kernel_params(12),
         name="head_values",
-    )(latent, w_uv)
-
-
-def split_kernel(rows_ref, *out_refs):
-    width = out_refs[0].shape[1]
-    me = lax.axis_index("tp")
-    for k, out_ref in enumerate(out_refs):
-        start = pl.multiple_of((me ^ k) * width, 128)
-        out_ref[...] = rows_ref[:, pl.ds(start, width)]
-
-
-def split_columns(rows, ranks):
-    shape = jax.ShapeDtypeStruct((rows.shape[0], rows.shape[1] // ranks), rows.dtype)
-    return pl.pallas_call(
-        split_kernel,
-        out_shape=[shape] * ranks,
-        in_specs=in_vmem(1),
-        out_specs=in_vmem(ranks),
-        compiler_params=kernel_params(8),
-        name="split_columns",
-    )(rows)
-
-
-def across(piece, axis, distance):
+    )(latent, w_uv, residual)
+
+
+def from_distance(piece, axis, distance):
     return lax.ppermute(piece, axis, [(k, k ^ distance) for k in range(lax.axis_size(axis))])
 
 
@@ -250,7 +252,7 @@
     requests = out_ref.shape[0]
     for k in range(steps):
         term = jnp.dot(
-            values_ref[k],
+            values_ref[k, :requests, :],
             w_ref[k * depth : (k + 1) * depth, :],
             preferred_element_type=jnp.float32,
         )
@@ -274,38 +276,47 @@
     )(values, fetched(w_o))
 
 
-def hidden_kernel(parts_ref, *refs):
-    *slices, out_ref, added = refs
-    per_rank = slices[0].shape[0]
-    me = lax.axis_index("tp")
-    for k, piece in enumerate(slices):
-        added[me ^ k] = piece[...].astype(jnp.float32)
+def hidden_kernel(parts_ref, values_ref, out_ref, slots):
+    ranks = values_ref.shape[0]
     width = out_ref.shape[1]
-    for at in range(0, width, 128):
-        at = slice(at, at + 128)
+    per_rank = out_ref.shape[0] // ranks
+    across = values_ref.shape[2] // 128
+    rows = slots.shape[1]
+    requests = values_ref.shape[1] - ranks * rows
+    start = pl.multiple_of(requests + lax.axis_index("tp") * rows, 16)
+    for s in range(ranks):
+        slots[s] = values_ref[s, pl.ds(start, rows), :].astype(jnp.float32)
+    for g in range(width // 128):
+        at = slice(g * 128, (g + 1) * 128)
+        row = (g // across) * per_rank
+        column = (g % across) * 128
+        terms = [
+            slots[s, row : row + per_rank, column : column + 128] for s in range(ranks)
+        ]
         total = parts_ref[0, :, at].astype(jnp.float32)
         for d in range(1, parts_ref.shape[0]):
             total = total + parts_ref[d, :, at].astype(jnp.float32)
-        terms = [added[s, :, at] for s in range(len(slices))]
-        out_ref[:, at] = (total + jnp.concatenate(terms, 0)).astype(out_ref.dtype)
-
-
-def make_hidden(parts, slices):
+        total = total + jnp.concatenate(terms, 0)
+        out_ref[:, at] = total.astype(out_ref.dtype)
+
+
+def make_hidden(parts, values, slot_rows):
+    ranks = values.shape[0]
     return pl.pallas_call(
         hidden_kernel,
         out_shape=jax.ShapeDtypeStruct(parts.shape[1:], jnp.bfloat16),
-        in_specs=in_vmem(1 + len(slices)),
-        out_specs=pl.BlockSpec(memory_space=pltpu.VMEM),
-        scratch_shapes=[pltpu.VMEM((len(slices),) + slices[0].shape, jnp.float32)],
+        in_specs=in_vmem(2),
+        out_specs=pl.BlockSpec(memory_space=pltpu.VMEM),
+        scratch_shapes=[pltpu.VMEM((ranks, slot_rows // ranks, values.shape[2]), jnp.float32)],
         compiler_params=kernel_params(12),
         name="hidden",
-    )(parts, *slices)
+    )(parts, values)
 
 
 def gate_up_kernel(hidden_ref, gain_ref, gate_ref, up_ref, *refs):
     ranks = lax.axis_size("tp")
-    *outs, scaled, gains, own = refs
-    gate_outs, up_outs, rows_out = outs[:-ranks][0::2], outs[:-ranks][1::2], outs[-ranks:]
+    *outs, scaled, gains = refs
+    gate_outs, up_outs = outs[0::2], outs[1::2]
     requests, width = hidden_ref.shape
     units = gate_ref.shape[1]
     share = requests // ranks
@@ -343,15 +354,6 @@
             target[:, at : at + value.shape[1]] = block
 
     store(gate_outs, units, digits)
-    per_rank = own.shape[1]
-    rows = ranks * per_rank
-    start = pl.multiple_of(lax.axis_index("dp") * rows, 16)
-    own[...] = (
-        hidden_ref[pl.ds(start, rows), :].astype(jnp.float32).reshape(ranks, per_rank, width)
-    )
-    for k, target in enumerate(rows_out):
-        target[...] = own[me ^ k].astype(target.dtype)
-
     chunk = units // 3
     for w_ref, left, targets in ((gate_ref, 0, gate_outs), (up_ref, scaled.shape[0] - 1, up_outs)):
         for at in range(0, units, chunk):
@@ -361,17 +363,15 @@
             store(targets, at, term)
 
 
-def gate_up(hidden, gain, w_gate, w_up, ranks_dp, ranks_tp, halves):
+def gate_up(hidden, gain, w_gate, w_up, halves):
     requests, width = hidden.shape
     units = w_gate.shape[1]
-    rows = requests // ranks_dp
-    per_rank = rows // ranks_tp
     shapes = [
         jax.ShapeDtypeStruct((requests // halves, columns), jnp.bfloat16)
         for _ in range(halves)
         for columns in (units + 128, units)
-    ] + [jax.ShapeDtypeStruct((per_rank, width), jnp.bfloat16)] * ranks_tp
-    outs = pl.pallas_call(
+    ]
+    return pl.pallas_call(
         gate_up_kernel,
         out_shape=shapes,
         in_specs=in_vmem(4),
@@ -379,12 +379,10 @@
         scratch_shapes=[
             pltpu.VMEM((halves, requests, width), jnp.bfloat16),
             pltpu.VMEM(gain.shape, jnp.float32),
-            pltpu.VMEM((ranks_tp, per_rank, width), jnp.float32),
         ],
         compiler_params=kernel_params(12),
         name="gate_up",
     )(hidden, gain, fetched(w_gate), fetched(w_up))
-    return outs[: 2 * halves], outs[2 * halves :]
 
 
 def halve_kernel(*refs):
@@ -444,9 +442,12 @@
     )(*parts)
 
 
-def down_kernel(inner_ref, w_ref, out_ref, total):
+def down_kernel(inner_ref, w_ref, hidden_ref, out_ref, total):
     width = w_ref.shape[1]
     total[...] = jnp.dot(inner_ref[...], w_ref[...], preferred_element_type=jnp.float32)
+    rows = hidden_ref.shape[0]
+    own = pl.ds(pl.multiple_of(lax.axis_index("dp") * rows, 16), rows)
+    total[own, :] += hidden_ref[...].astype(jnp.float32)
     groups = width // 128
     per_rank = out_ref.shape[1] // groups
     for d in range(out_ref.shape[0]):
@@ -457,7 +458,7 @@
         out_ref[d] = jnp.concatenate(pieces, 0).astype(out_ref.dtype)
 
 
-def project_down(inner, w_down, ranks):
+def project_down(inner, w_down, hidden, ranks):
     requests, units = inner.shape
     width = w_down.shape[1]
     return pl.pallas_call(
@@ -465,45 +466,43 @@
         out_shape=jax.ShapeDtypeStruct(
             (ranks, requests // ranks * (width // 128), 128), jnp.bfloat16
         ),
-        in_specs=in_vmem(2),
+        in_specs=in_vmem(3),
         out_specs=pl.BlockSpec(memory_space=pltpu.VMEM),
         scratch_shapes=[pltpu.VMEM((requests, width), jnp.float32)],
         compiler_params=kernel_params(12),
         name="project_down",
-    )(inner, fetched(w_down))
-
-
-def layer_kernel(parts_ref, *refs):
-    *slices, out_ref, total = refs
-    ranks = len(slices)
+    )(inner, fetched(w_down), hidden)
+
+
+def layer_kernel(parts_ref, out_ref, total):
     per_rank, model = out_ref.shape
-    width = model // ranks
-    groups = width // 128
-    me = lax.axis_index("tp")
+    ranks = lax.axis_size("tp")
+    groups = model // ranks // 128
     for t in range(ranks):
-        ffn = sum(
+        terms = [
             parts_ref[d, :, :].astype(jnp.float32) for d in range(t, parts_ref.shape[0], ranks)
-        )
+        ]
+        layer = sum(terms[1:], terms[0])
         for g in range(groups):
             at = (t * groups + g) * 128
-            total[:, at : at + 128] = ffn[g * per_rank : (g + 1) * per_rank, :]
-    for k, piece in enumerate(slices):
-        at = pl.ds(pl.multiple_of((me ^ k) * width, 128), width)
-        total[:, at] += piece[...].astype(jnp.float32)
+            total[:, at : at + 128] = layer[g * per_rank : (g + 1) * per_rank, :]
     out_ref[...] = total[...].astype(out_ref.dtype)
 
 
-def make_layer(parts, slices, model):
-    per_rank = slices[0].shape[0]
+def make_layer(parts, per_rank, model):
     return pl.pallas_call(
         layer_kernel,
         out_shape=jax.ShapeDtypeStruct((per_rank, model), jnp.bfloat16),
-        in_specs=in_vmem(1 + len(slices)),
+        in_specs=in_vmem(1),
         out_specs=pl.BlockSpec(memory_space=pltpu.VMEM),
         scratch_shapes=[pltpu.VMEM((per_rank, model), jnp.float32)],
         compiler_params=kernel_params(12),
         name="layer",
-    )(parts, *slices)
+    )(parts)
+
+
+def round_up(value, step):
+    return (value + step - 1) // step * step
 
 
 def swap(parts, axes):
@@ -524,40 +523,34 @@
     units = w_gate.shape[1]
     width = w_o.shape[1]
 
+    groups = width // 128
+
     query = queries.reshape(per_rank, heads_all, row_length)
-    latent = attend(lengths, query, paged_latent_cache.T, ranks)
-    latent, residual, w_o, w_gate, w_up, w_down = lax.optimization_barrier(
-        (latent, residual, w_o, w_gate, w_up, w_down)
-    )
-    added = split_columns(residual, ranks_tp)
-    added = [added[0]] + [across(added[k], "tp", k) for k in range(1, ranks_tp)]
-    latent = swap(latent, ("dp", "tp"))
-
-    values = head_values(latent.reshape(requests * heads_here, C), w_uv)
+    latent = swap(attend(lengths, query, paged_latent_cache.T, ranks), ("dp", "tp"))
+
+    across = heads_here * w_uv.shape[2] // 128
+    slot_rows = ranks_tp * round_up(per_rank * ((groups + across - 1) // across), 16)
+    values = head_values(latent.reshape(requests * heads_here, C), w_uv, residual, slot_rows)
     values = lax.all_gather(values, "tp", axis=0)
     attn = project_out(values, w_o, requests)
     attn = swap(attn.reshape(ranks_dp, requests // ranks_dp, width), "dp")
-    hidden = make_hidden(attn, added)
-    hidden = lax.all_gather(hidden, "dp", axis=0, tiled=True)
+    own_hidden = make_hidden(attn, values, slot_rows)
+    hidden = lax.all_gather(own_hidden, "dp", axis=0, tiled=True)
 
     halves = 2 if ranks_tp == 4 else 1
-    parts, rows = gate_up(
-        hidden, norm_gain.reshape(-1, 128), w_gate, w_up, ranks_dp, ranks_tp, halves
-    )
+    parts = gate_up(hidden, norm_gain.reshape(-1, 128), w_gate, w_up, halves)
     if halves == 2:
         gate_send, up_send, gate_keep, up_keep = parts
-        came = [across(gate_send, "tp", 1), across(up_send, "tp", 2)]
-        rows = [rows[0]] + [across(rows[k], "tp", k) for k in range(1, ranks_tp)]
+        came = [from_distance(gate_send, "tp", 1), from_distance(up_send, "tp", 2)]
         (gate_send, up_send), (gate_keep, up_keep) = halve([gate_keep, up_keep], came)
-        parts = [gate_keep, up_keep, across(gate_send, "tp", 2), across(up_send, "tp", 1)]
-        parts = [part[None] for part in parts]
+        came = [from_distance(gate_send, "tp", 2), from_distance(up_send, "tp", 1)]
+        parts = [part[None] for part in (gate_keep, up_keep, *came)]
     else:
-        rows = [rows[0]] + [across(rows[k], "tp", k) for k in range(1, ranks_tp)]
         parts = [swap(part.reshape(ranks_tp, -1, part.shape[1]), "tp") for part in parts]
     inner = make_inner(parts, units, model)
     inner = lax.all_gather(inner, "tp", axis=0, tiled=True)
-    ffn = swap(project_down(inner, w_down, ranks), ("dp", "tp"))
-    return make_layer(ffn, rows, model)
+    ffn = swap(project_down(inner, w_down, own_hidden, ranks), ("dp", "tp"))
+    return make_layer(ffn, per_rank, model)
 
 
 def solution(mesh):

time: 156 us -> 142 us (0.910); the launches traced: 154 us -> 144 us
  blocking collectives: 65.8 us -> 99.9 us
  waiting for transfers between devices: 34.8 us -> 18.6 us
  starting transfers between devices: 22.8 us -> 7.17 us
  local copies, waits for them, and re-layouts: 15.3 us -> 1.84 us
    all_to_all x1 -> x3, blocking collectives: 24.9 us -> 56.9 us  [swap(): return lax.all_to_all(parts, axes, split_axis=0, concat_axis=0, tiled=True)]
    ppermute x10 -> x4, waiting for transfers between devices: 33.7 us -> 18.6 us  [from_distance(): lax.ppermute(piece, axis, [(k, k ^ distance) for k in range(lax.axis_size...]
    unnamed x22 -> x20, local copies, waits for them, and re-layouts: 12.6 us -> 0.05 us
    all_to_all x2 -> x0, starting transfers between devices: 8.27 us -> none  [swap(): return lax.all_to_all(parts, axes, split_axis=0, concat_axis=0, tiled=True)]
    ppermute x10 -> x4, starting transfers between devices: 14.5 us -> 7.17 us  [from_distance(): lax.ppermute(piece, axis, [(k, k ^ distance) for k in range(lax.axis_size...]
    all_gather x1, blocking collectives: 16 us -> 18.4 us  [local(): values = lax.all_gather(values, 'tp', axis=0)]
    pallas_call x1, Pallas kernels: 7.37 us -> 9.04 us  [attend(): pl.pallas_call(attention_kernel, out_shape=jax.ShapeDtypeStruct((ranks, n...]
  transfers between devices with their start and end apart: 12 -> 4, of which waited for: 8 -> 4; matrix products, arithmetic and copies ran while one was open for 0% -> 0% of each run, Pallas kernels for 0% -> 0%
where the time goes in v8:
time: 142 us; the launch traced here: 144 us
  blocking collectives  99.9 us (70%)
  waiting for transfers between devices  18.6 us (13%)
  Pallas kernels  15.8 us (11%)
  starting transfers between devices  7.17 us (5%)
  local copies, waits for them, and re-layouts  1.84 us (1%)
    all_to_all x3, blocking collectives, swap(): return lax.all_to_all(parts, axes, split_axis=0, concat_axis=0, tiled=True)  56.9 us
    ppermute x4, waiting for transfers between devices, from_distance(): lax.ppermute(piece, axis, [(k, k ^ distance) for k in range(lax.axis_size...  18.6 us
    all_gather x1, blocking collectives, local(): values = lax.all_gather(values, 'tp', axis=0)  18.4 us
    all_gather x1, blocking collectives, local(): inner = lax.all_gather(inner, 'tp', axis=0, tiled=True)  15.8 us
    pallas_call x1, Pallas kernels, attend(): pl.pallas_call(attention_kernel, out_shape=jax.ShapeDtypeStruct((ranks, n...  9.04 us
    all_gather x1, blocking collectives, local(): hidden = lax.all_gather(own_hidden, 'dp', axis=0, tiled=True)  8.78 us
    ppermute x4, starting transfers between devices, from_distance(): lax.ppermute(piece, axis, [(k, k ^ distance) for k in range(lax.axis_size...  7.17 us
  transfers between devices with their start and end apart: 4, of which 4 were waited for; matrix products, arithmetic and copies ran while one was open for 0% of the time, Pallas kernels for 0%

profile of v8, /device:TPU:0, one launch (start us, length us, event | category | flops | bytes accessed | tf_op | source)
XLA Modules:
  0.0 143.5 jit_solution(12934500594605429876)
XLA Ops:
  0.0 1.8 %reshape.12.q_ref = bf16[4,128,576]{2,1,0:T(8,128)(2,1)S(1)} reshape(bf16[4,73728]{1,0:T(4,128)(2,1)} %param.11) | data formatting | bytes 1179648 | tf_op jit(solution)/shard_map/reshape | solution.py:528
  1.9 9.0 %attention.1 = bf16[32,16,512]{2,1,0:T(8,128)(2,1)S(1)} custom-call(s32[128]{0:T(128)} %lens_ref.1, bf16[4,128,576]{2,1,0:T(8,128)(2,1)S(1)} %reshape.12.q_ref, bf16[576,14336]{1,0:T(8,128)(2,1)} %bitcast.24), custom_call_target="tpu_custom_call" | custom-call | flops 3992977408 | bytes 16515072 | tf_op jit(solution)/shard_map/attention/pallas_call | solution.py:165
  10.9 27.2 %all_to_all.15 = bf16[32,16,512]{2,1,0:T(8,128)(2,1)S(1)} all-to-all(bf16[32,16,512]{2,1,0:T(8,128)(2,1)S(1)} %attention.1), channel_id=1, replica_groups=mesh['dp'=8,'tp'=4] {'dp','tp'}, dimensions={0} | all-to-all | bytes 1048576 | tf_op jit(solution)/shard_map/all_to_all | solution.py:509
  38.1 0.8 head_values.1
  38.9 18.4 %all-gather = bf16[768,512]{1,0:T(8,128)(2,1)S(1)} all-gather(bf16[192,512]{1,0:T(8,128)(2,1)S(1)} %head_values.1), channel_id=2, replica_groups=mesh['dp'=8,'tp'=4] {'tp'}, dimensions={0}, use_global_device_ids=true | all-gather | bytes 983040 | tf_op jit(solution)/shard_map/all_gather | solution.py:534
  57.3 1.1 project_out.1
  58.5 11.8 %all_to_all.16.parts_ref = bf16[8,16,1792]{2,1,0:T(8,128)(2,1)S(1)} all-to-all(bf16[8,16,1792]{2,1,0:T(8,128)(2,1)S(1)} %bitcast.18), channel_id=1, replica_groups=mesh['dp'=8,'tp'=4] {'dp'}, dimensions={0} | all-to-all | bytes 917504 | tf_op jit(solution)/shard_map/all_to_all | solution.py:509
  70.2 0.1 hidden.1.hidden_ref
  70.3 8.8 %all_gather.14.hidden_ref = bf16[128,1792]{1,0:T(8,128)(2,1)S(1)} all-gather(bf16[16,1792]{1,0:T(8,128)(2,1)S(1)} %hidden.1.hidden_ref), channel_id=1, replica_groups=mesh['dp'=8,'tp'=4] {'dp'}, dimensions={0}, use_global_device_ids=true | all-gather | bytes 516096 | tf_op jit(solution)/shard_map/all_gather | solution.py:538
  79.2 2.3 %gate_up.1 = (bf16[64,2432]{1,0:T(8,128)(2,1)S(1)}, bf16[64,2304]{1,0:T(8,128)(2,1)S(1)}, bf16[64,2432]{1,0:T(8,128)(2,1)S(1)}, bf16[64,2304]{1,0:T(8,128)(2,1)S(1)}) custom-call(bf16[128,1792]{1,0:T(8,128)(2,1)S(1)} %all_gather.14.hidden_ref, bf16[56,128]{1,0:T(8,128)(2,1)S(1)} %bitcast.23, bf16[1792,2304]{1,0:T(8,128)(2,1)S(1)} %bitcast.10, ...), custom_call_target="tpu_custom_call" | custom-call | tf_op jit(solution)/shard_map/gate_up/pallas_call | solution.py:374
  81.5 0.6 collective-permute-start
  82.1 2.6 %collective-permute-start.1 = (bf16[64,2304]{1,0:T(8,128)(2,1)S(1)}, bf16[64,2304]{1,0:T(8,128)(2,1)S(1)}, u32[]{:S(2)}, u32[]{:S(2)}) collective-permute-start(bf16[64,2304]{1,0:T(8,128)(2,1)S(1)} %get-tuple-element.16), channel_id=1, source_target_pairs={{0,2},{1,3},{2,0},{3,1},{4,6},{5,7},{6,4},{7,5},{8,10},{9,11},{10,... | collective-permute-start | bytes 884744 | tf_op jit(solution)/shard_map/ppermute | solution.py:247
  84.7 10.9 %collective-permute-done.1.refs_3_ = bf16[64,2304]{1,0:T(8,128)(2,1)S(1)} collective-permute-done((bf16[64,2304]{1,0:T(8,128)(2,1)S(1)}, bf16[64,2304]{1,0:T(8,128)(2,1)S(1)}, u32[]{:S(2)}, u32[]{:S(2)}) %collective-permute-start.1) | collective-permute-done | bytes 294944 | tf_op jit(solution)/shard_map/ppermute | solution.py:247
  95.6 1.9 %collective-permute-done.refs_2_ = bf16[64,2432]{1,0:T(8,128)(2,1)S(1)} collective-permute-done((bf16[64,2432]{1,0:T(8,128)(2,1)S(1)}, bf16[64,2432]{1,0:T(8,128)(2,1)S(1)}, u32[]{:S(2)}, u32[]{:S(2)}) %collective-permute-start) | collective-permute-done | bytes 311328 | tf_op jit(solution)/shard_map/ppermute | solution.py:247
  97.5 0.2 halve.1
  97.7 1.6 %collective-permute-start.2 = (bf16[32,2432]{1,0:T(8,128)(2,1)S(1)}, bf16[32,2432]{1,0:T(8,128)(2,1)S(1)}, u32[]{:S(2)}, u32[]{:S(2)}) collective-permute-start(bf16[32,2432]{1,0:T(8,128)(2,1)S(1)} %get-tuple-element.19), channel_id=1, source_target_pairs={{0,2},{1,3},{2,0},{3,1},{4,6},{5,7},{6,4},{7,5},{8,10},{9,11},{10,... | collective-permute-start | bytes 466952 | tf_op jit(solution)/shard_map/ppermute | solution.py:247
  99.3 2.3 %collective-permute-start.3 = (bf16[32,2304]{1,0:T(8,128)(2,1)S(1)}, bf16[32,2304]{1,0:T(8,128)(2,1)S(1)}, u32[]{:S(2)}, u32[]{:S(2)}) collective-permute-start(bf16[32,2304]{1,0:T(8,128)(2,1)S(1)} %get-tuple-element.20), channel_id=1, source_target_pairs={{0,1},{1,0},{2,3},{3,2},{4,5},{5,4},{6,7},{7,6},{8,9},{9,8},{10,11... | collective-permute-start | bytes 442376 | tf_op jit(solution)/shard_map/ppermute | solution.py:247
  101.6 4.5 %collective-permute-done.3 = bf16[32,2304]{1,0:T(8,128)(2,1)S(1)} collective-permute-done((bf16[32,2304]{1,0:T(8,128)(2,1)S(1)}, bf16[32,2304]{1,0:T(8,128)(2,1)S(1)}, u32[]{:S(2)}, u32[]{:S(2)}) %collective-permute-start.3) | collective-permute-done | bytes 147488 | tf_op jit(solution)/shard_map/ppermute | solution.py:247
  106.1 1.4 collective-permute-done.2
  107.4 0.2 inner.1
  107.7 15.8 %all_gather.15.inner_ref = bf16[128,2304]{1,0:T(8,128)(2,1)S(1)} all-gather(bf16[32,2304]{1,0:T(8,128)(2,1)S(1)} %inner.1), channel_id=1, replica_groups=mesh['dp'=8,'tp'=4] {'tp'}, dimensions={0}, use_global_device_ids=true | all-gather | bytes 737280 | tf_op jit(solution)/shard_map/all_gather | solution.py:551
  123.5 1.4 project_down.1
  124.9 17.9 %all_to_all.17.parts_ref = bf16[32,56,128]{2,1,0:T(8,128)(2,1)S(1)} all-to-all(bf16[32,56,128]{2,1,0:T(8,128)(2,1)S(1)} %project_down.1), channel_id=1, replica_groups=mesh['dp'=8,'tp'=4] {'dp','tp'}, dimensions={0} | all-to-all | bytes 917504 | tf_op jit(solution)/shard_map/all_to_all | solution.py:509
  142.8 0.7 layer.1
  (23 shorter events, 0.1 us)
Async XLA Ops:
  0.0 38.1 %copy-start.1 = (bf16[4,512,128]{2,1,0:T(8,128)(2,1)S(1)}, bf16[4,512,128]{2,1,0:T(8,128)(2,1)}, u32[]{:S(2)}) copy-start(bf16[4,512,128]{2,1,0:T(8,128)(2,1)} %w_ref.3) | copy-start | bytes 1572868
  0.0 38.1 %copy-start.2 = (bf16[4,7168]{1,0:T(4,128)(2,1)S(1)}, bf16[4,7168]{1,0:T(4,128)(2,1)}, u32[]{:S(2)}) copy-start(bf16[4,7168]{1,0:T(4,128)(2,1)} %residual_ref.1) | copy-start | bytes 172036
  1.8 55.5 %copy-start = (bf16[2048,1792]{1,0:T(8,128)(2,1)S(1)}, bf16[2048,1792]{1,0:T(8,128)(2,1)}, u32[]{:S(2)}) copy-start(bf16[2048,1792]{1,0:T(8,128)(2,1)} %w_ref.4) | copy-start | bytes 22020100
  1.8 77.3 %slice-start = ((s8[8257536]{0:T(1024)(128)(4,1)}), s8[4194304]{0:T(1024)(128)(4,1)S(1)}, s32[]{:S(2)}) async-start(s8[8257536]{0:T(1024)(128)(4,1)} %bitcast.9), calls=%async_computation.3 | async-start | bytes 8388608
  1.8 77.3 %slice-start.2 = ((s8[8257536]{0:T(1024)(128)(4,1)}), s8[4194304]{0:T(1024)(128)(4,1)S(1)}, s32[]{:S(2)}) async-start(s8[8257536]{0:T(1024)(128)(4,1)} %bitcast.11), calls=%async_computation.5 | async-start | bytes 8388608
  1.8 77.3 %slice-start.1 = ((s8[8257536]{0:T(1024)(128)(4,1)}), s8[4063232]{0:T(1024)(128)(4,1)S(1)}, s32[]{:S(2)}) async-start(s8[8257536]{0:T(1024)(128)(4,1)} %bitcast.9), calls=%async_computation.4 | async-start | bytes 8126464
  1.8 77.3 %slice-start.3 = ((s8[8257536]{0:T(1024)(128)(4,1)}), s8[4063232]{0:T(1024)(128)(4,1)S(1)}, s32[]{:S(2)}) async-start(s8[8257536]{0:T(1024)(128)(4,1)} %bitcast.11), calls=%async_computation.6 | async-start | bytes 8126464
  10.9 68.2 %copy-start.3 = (bf16[7168]{0:T(1024)(128)(2,1)S(1)}, bf16[7168]{0:T(1024)(128)(2,1)}, u32[]{:S(2)}) copy-start(bf16[7168]{0:T(1024)(128)(2,1)} %param.16) | copy-start | bytes 43012
  79.1 44.4 %slice-start.4 = ((s8[8257536]{0:T(1024)(128)(4,1)}), s8[4194304]{0:T(1024)(128)(4,1)S(1)}, s32[]{:S(2)}) async-start(s8[8257536]{0:T(1024)(128)(4,1)} %bitcast.13), calls=%async_computation.7 | async-start | bytes 8388608
  79.2 44.3 %slice-start.5 = ((s8[8257536]{0:T(1024)(128)(4,1)}), s8[4063232]{0:T(1024)(128)(4,1)S(1)}, s32[]{:S(2)}) async-start(s8[8257536]{0:T(1024)(128)(4,1)} %bitcast.13), calls=%async_computation.8 | async-start | bytes 8126464
  81.5 16.0 %collective-permute-start = (bf16[64,2432]{1,0:T(8,128)(2,1)S(1)}, bf16[64,2432]{1,0:T(8,128)(2,1)S(1)}, u32[]{:S(2)}, u32[]{:S(2)}) collective-permute-start(bf16[64,2432]{1,0:T(8,128)(2,1)S(1)} %get-tuple-element.15), channel_id=1, source_target_pairs={{0,1},{1,0},{2,3},{3,2},{4,5},{5,4},{6,7},{7,6},{8,9},{9,8},{10,11... | collective-permute-start | bytes 933896 | tf_op jit(solution)/shard_map/ppermute | solution.py:247
  82.1 13.5 %collective-permute-start.1 = (bf16[64,2304]{1,0:T(8,128)(2,1)S(1)}, bf16[64,2304]{1,0:T(8,128)(2,1)S(1)}, u32[]{:S(2)}, u32[]{:S(2)}) collective-permute-start(bf16[64,2304]{1,0:T(8,128)(2,1)S(1)} %get-tuple-element.16), channel_id=1, source_target_pairs={{0,2},{1,3},{2,0},{3,1},{4,6},{5,7},{6,4},{7,5},{8,10},{9,11},{10,... | collective-permute-start | bytes 884744 | tf_op jit(solution)/shard_map/ppermute | solution.py:247
  97.7 9.8 %collective-permute-start.2 = (bf16[32,2432]{1,0:T(8,128)(2,1)S(1)}, bf16[32,2432]{1,0:T(8,128)(2,1)S(1)}, u32[]{:S(2)}, u32[]{:S(2)}) collective-permute-start(bf16[32,2432]{1,0:T(8,128)(2,1)S(1)} %get-tuple-element.19), channel_id=1, source_target_pairs={{0,2},{1,3},{2,0},{3,1},{4,6},{5,7},{6,4},{7,5},{8,10},{9,11},{10,... | collective-permute-start | bytes 466952 | tf_op jit(solution)/shard_map/ppermute | solution.py:247
  99.3 6.8 %collective-permute-start.3 = (bf16[32,2304]{1,0:T(8,128)(2,1)S(1)}, bf16[32,2304]{1,0:T(8,128)(2,1)S(1)}, u32[]{:S(2)}, u32[]{:S(2)}) collective-permute-start(bf16[32,2304]{1,0:T(8,128)(2,1)S(1)} %get-tuple-element.20), channel_id=1, source_target_pairs={{0,1},{1,0},{2,3},{3,2},{4,5},{5,4},{6,7},{7,6},{8,9},{9,8},{10,11... | collective-permute-start | bytes 442376 | tf_op jit(solution)/shard_map/ppermute | solution.py:247

commit v9 on v8

--- a/solution.py
+++ b/solution.py
@@ -89,7 +89,7 @@
         end_at = jnp.where(live, hi[r], 0)
         s = jnp.dot(q_ref[r], held[i], preferred_element_type=jnp.float32)
         token = i * tile + lax.broadcasted_iota(jnp.int32, (1, tile), 1)
-        target[...] = jnp.where((token >= begin_at) & (token < end_at), s, negative)
+        target[...] = s + jnp.where((token >= begin_at) & (token < end_at), 0.0, negative)
 
     def soften(r, source, weights, keeps):
         s = source[...]
@@ -313,76 +313,109 @@
     )(parts, values)
 
 
-def gate_up_kernel(hidden_ref, gain_ref, gate_ref, up_ref, *refs):
+def scale_kernel(hidden_ref, gain_ref, gate_ref, up_ref, scaled, gate_sum, up_sum, *refs):
+    *outs, gains = refs
     ranks = lax.axis_size("tp")
-    *outs, scaled, gains = refs
-    gate_outs, up_outs = outs[0::2], outs[1::2]
+    halves = scaled.shape[0]
     requests, width = hidden_ref.shape
-    units = gate_ref.shape[1]
     share = requests // ranks
     groups = width // 128
     me = lax.axis_index("tp")
-    if len(gate_outs) == 1:
-        orders = [[0 * me + t for t in range(ranks)]] * 2
-    else:
-        orders = [[me ^ 3, me ^ 1, me ^ 2, me], [me ^ 3, me ^ 2, me ^ 1, me]]
+    places = [[3, 1, 2, 0], [3, 2, 1, 0]] if halves == 2 else [list(range(ranks))]
 
     gains[...] = gain_ref[...].astype(jnp.float32)
-    squares = []
-    for k, order in enumerate(orders[:1] if len(gate_outs) == 1 else orders):
-        square = [jnp.zeros((share, 128), jnp.float32) for _ in order]
-        for t, block in enumerate(order):
-            start = pl.multiple_of(block * share, 16)
-            for g in range(groups):
-                at = slice(g * 128, (g + 1) * 128)
-                x = hidden_ref[pl.ds(start, share), at].astype(jnp.float32)
-                square[t] = square[t] + x * x
-                gain = gains[pl.ds(me * groups + g, 1), :]
-                scaled[k, t * share : (t + 1) * share, at] = (x * gain).astype(scaled.dtype)
-        squares.append(square)
-    square = jnp.sum(jnp.concatenate(squares[0], 0), 1, keepdims=True)
+    squares = [None] * ranks
+    for k in range(ranks):
+        block = me ^ k if halves == 2 else k
+        start = block * share if halves == 1 else pl.multiple_of(block * share, 16)
+        square = jnp.zeros((share, 128), jnp.float32)
+        for g in range(groups):
+            at = slice(g * 128, (g + 1) * 128)
+            x = hidden_ref[pl.ds(start, share), at].astype(jnp.float32)
+            square = square + x * x
+            gain = gains[pl.ds(me * groups + g, 1), :]
+            value = (x * gain).astype(scaled.dtype)
+            for n, place in enumerate(places):
+                scaled[n, place[k] * share : (place[k] + 1) * share, at] = value
+        squares[places[0][k]] = square
+    square = jnp.sum(jnp.concatenate(squares, 0), 1, keepdims=True)
     top = square.astype(jnp.bfloat16).astype(jnp.float32)
     middle = (square - top).astype(jnp.bfloat16).astype(jnp.float32)
     low = square - top - middle
     lane = lax.broadcasted_iota(jnp.int32, (requests, 128), 1)
     digits = jnp.where(lane == 0, top, jnp.where(lane == 1, middle, jnp.where(lane == 2, low, 0.0)))
-
-    def store(targets, at, value):
-        rows = requests // len(targets)
-        for n, target in enumerate(targets):
-            block = value[n * rows : (n + 1) * rows].astype(target.dtype)
-            target[:, at : at + value.shape[1]] = block
-
-    store(gate_outs, units, digits)
-    chunk = units // 3
-    for w_ref, left, targets in ((gate_ref, 0, gate_outs), (up_ref, scaled.shape[0] - 1, up_outs)):
-        for at in range(0, units, chunk):
+    gates = [gate_sum, outs[0]] if halves == 2 else [gate_sum]
+    ups = [up_sum, outs[1]] if halves == 2 else [up_sum]
+    columns = up_sum.shape[1]
+    for n, target in enumerate(gates):
+        rows = target.shape[0]
+        target[:, columns:] = digits[n * rows : (n + 1) * rows].astype(target.dtype)
+    products(scaled, gate_ref, up_ref, 0, columns, gates, ups)
+
+
+def products(scaled, gate_ref, up_ref, first, columns, gates, ups):
+    for left, w_ref, targets in ((0, gate_ref, gates), (scaled.shape[0] - 1, up_ref, ups)):
+        for at in range(0, columns, 256):
+            upto = min(at + 256, columns)
             term = jnp.dot(
-                scaled[left], w_ref[:, at : at + chunk], preferred_element_type=jnp.float32
+                scaled[left],
+                w_ref[:, first + at : first + upto],
+                preferred_element_type=jnp.float32,
             )
-            store(targets, at, term)
+            for n, target in enumerate(targets):
+                rows = target.shape[0]
+                target[:, at:upto] = term[n * rows : (n + 1) * rows].astype(target.dtype)
+
+
+def second_kernel(scaled, gate_ref, up_ref, *outs):
+    columns = outs[1].shape[1]
+    first = gate_ref.shape[1] - columns
+    products(scaled, gate_ref, up_ref, first, columns, outs[0::2], outs[1::2])
 
 
 def gate_up(hidden, gain, w_gate, w_up, halves):
     requests, width = hidden.shape
     units = w_gate.shape[1]
-    shapes = [
-        jax.ShapeDtypeStruct((requests // halves, columns), jnp.bfloat16)
-        for _ in range(halves)
-        for columns in (units + 128, units)
-    ]
-    return pl.pallas_call(
-        gate_up_kernel,
-        out_shape=shapes,
+    first = units if halves == 1 else round_up(units // 2, 256)
+    w_gate, w_up = fetched(w_gate), fetched(w_up)
+
+    def shapes(columns, extra):
+        return [
+            jax.ShapeDtypeStruct((requests // halves, columns + more), jnp.bfloat16)
+            for _ in range(halves)
+            for more in (extra, 0)
+        ]
+
+    outs = [jax.ShapeDtypeStruct((halves, requests, width), jnp.bfloat16)] + shapes(first, 128)
+    scaled, *parts = pl.pallas_call(
+        scale_kernel,
+        out_shape=outs,
         in_specs=in_vmem(4),
-        out_specs=in_vmem(len(shapes)),
-        scratch_shapes=[
-            pltpu.VMEM((halves, requests, width), jnp.bfloat16),
-            pltpu.VMEM(gain.shape, jnp.float32),
-        ],
-        compiler_params=kernel_params(12),
+        out_specs=in_vmem(len(outs)),
+        scratch_shapes=[pltpu.VMEM(gain.shape, jnp.float32)],
+        compiler_params=kernel_params(12),
+        cost_estimate=pl.CostEstimate(
+            flops=4 * requests * width * first, bytes_accessed=4 * width * first, transcendentals=0
+        ),
         name="gate_up",
-    )(hidden, gain, fetched(w_gate), fetched(w_up))
+    )(hidden, gain, w_gate, w_up)
+    if halves == 1:
+        return [parts]
+    outs = shapes(units - first, 0)
+    others = pl.pallas_call(
+        second_kernel,
+        out_shape=outs,
+        in_specs=in_vmem(3),
+        out_specs=in_vmem(len(outs)),
+        compiler_params=kernel_params(12),
+        cost_estimate=pl.CostEstimate(
+            flops=4 * requests * width * (units - first),
+            bytes_accessed=4 * width * (units - first),
+            transcendentals=0,
+        ),
+        name="gate_up_rest",
+    )(scaled, w_gate, w_up)
+    return [parts, others]
 
 
 def halve_kernel(*refs):
@@ -411,29 +444,36 @@
     return outs[: len(kept)], outs[len(kept) :]
 
 
-def inner_kernel(model, *refs):
+def inner_kernel(model, counts, *refs):
     *parts, out_ref = refs
-    gates, ups = parts[0::2], parts[1::2]
-    units = out_ref.shape[1]
-
-    def total(parts, at):
-        terms = [
-            part[n, :, at].astype(jnp.float32) for part in parts for n in range(part.shape[0])
-        ]
-        return sum(terms[1:], terms[0])
-
-    square = jnp.sum(total(gates, slice(units, units + 128)), 1, keepdims=True)
-    factor = lax.rsqrt(square / model + 1e-06)
-    for at in range(0, units, 128):
-        at = slice(at, at + 128)
-        gate = total(gates, at) * factor
-        up = total(ups, at) * factor
-        out_ref[:, at] = (gate / (1.0 + jnp.exp(-gate)) * up).astype(out_ref.dtype)
-
-
-def make_inner(parts, units, model):
+    factor = None
+    at = 0
+    for count in counts:
+        gates, ups, parts = parts[0:count:2], parts[1:count:2], parts[count:]
+        columns = ups[0].shape[2]
+
+        def total(parts, at):
+            terms = [
+                part[n, :, at].astype(jnp.float32) for part in parts for n in range(part.shape[0])
+            ]
+            return sum(terms[1:], terms[0])
+
+        if factor is None:
+            square = jnp.sum(total(gates, slice(columns, columns + 128)), 1, keepdims=True)
+            factor = lax.rsqrt(square / model + 1e-06)
+        for start in range(0, columns, 128):
+            span = slice(start, start + 128)
+            gate = total(gates, span) * factor
+            up = total(ups, span) * factor
+            value = gate / (1.0 + jnp.exp(-gate)) * up
+            out_ref[:, at + start : at + start + 128] = value.astype(out_ref.dtype)
+        at += columns
+
+
+def make_inner(chunks, units, model):
+    parts = [part for chunk in chunks for part in chunk]
     return pl.pallas_call(
-        functools.partial(inner_kernel, model),
+        functools.partial(inner_kernel, model, [len(chunk) for chunk in chunks]),
         out_shape=jax.ShapeDtypeStruct((parts[0].shape[1], units), jnp.bfloat16),
         in_specs=in_vmem(len(parts)),
         out_specs=pl.BlockSpec(memory_space=pltpu.VMEM),
@@ -538,16 +578,20 @@
     hidden = lax.all_gather(own_hidden, "dp", axis=0, tiled=True)
 
     halves = 2 if ranks_tp == 4 else 1
-    parts = gate_up(hidden, norm_gain.reshape(-1, 128), w_gate, w_up, halves)
+    chunks = gate_up(hidden, norm_gain.reshape(-1, 128), w_gate, w_up, halves)
     if halves == 2:
-        gate_send, up_send, gate_keep, up_keep = parts
-        came = [from_distance(gate_send, "tp", 1), from_distance(up_send, "tp", 2)]
-        (gate_send, up_send), (gate_keep, up_keep) = halve([gate_keep, up_keep], came)
-        came = [from_distance(gate_send, "tp", 2), from_distance(up_send, "tp", 1)]
-        parts = [part[None] for part in (gate_keep, up_keep, *came)]
+        sums = []
+        for gate_send, up_send, gate_keep, up_keep in chunks:
+            came = [from_distance(gate_send, "tp", 1), from_distance(up_send, "tp", 2)]
+            (gate_send, up_send), kept = halve([gate_keep, up_keep], came)
+            came = [from_distance(gate_send, "tp", 2), from_distance(up_send, "tp", 1)]
+            sums.append([part[None] for part in (*kept, *came)])
     else:
-        parts = [swap(part.reshape(ranks_tp, -1, part.shape[1]), "tp") for part in parts]
-    inner = make_inner(parts, units, model)
+        sums = [
+            [swap(part.reshape(ranks_tp, -1, part.shape[1]), "tp") for part in chunk]
+            for chunk in chunks
+        ]
+    inner = make_inner(sums, units, model)
     inner = lax.all_gather(inner, "tp", axis=0, tiled=True)
     ffn = swap(project_down(inner, w_down, own_hidden, ranks), ("dp", "tp"))
     return make_layer(ffn, per_rank, model)

time: 142 us -> 140 us (0.986); the launches traced: 144 us -> 139 us
  waiting for transfers between devices: 18.6 us -> 12.4 us
  starting transfers between devices: 7.17 us -> 10.1 us
    ppermute x4 -> x8, waiting for transfers between devices: 18.6 us -> 12.4 us  [from_distance(): lax.ppermute(piece, axis, [(k, k ^ distance) for k in range(lax.axis_size...]
    ppermute x4 -> x8, starting transfers between devices: 7.17 us -> 10.1 us  [from_distance(): lax.ppermute(piece, axis, [(k, k ^ distance) for k in range(lax.axis_size...]
  transfers between devices with their start and end apart: 4 -> 8, of which waited for: 4 -> 5; matrix products, arithmetic and copies ran while one was open for 0% -> 0% of each run, Pallas kernels for 0% -> 1%
where the time goes in v9:
time: 140 us; the launch traced here: 139 us
  blocking collectives  100 us (71%)
  Pallas kernels  14.7 us (10%)
  waiting for transfers between devices  12.4 us (9%)
  starting transfers between devices  10.1 us (7%)
  local copies, waits for them, and re-layouts  1.84 us (1%)
    all_to_all x3, blocking collectives, swap(): return lax.all_to_all(parts, axes, split_axis=0, concat_axis=0, tiled=True)  56.9 us
    all_gather x1, blocking collectives, local(): values = lax.all_gather(values, 'tp', axis=0)  18.4 us
    all_gather x1, blocking collectives, local(): inner = lax.all_gather(inner, 'tp', axis=0, tiled=True)  15.9 us
    ppermute x8, waiting for transfers between devices, from_distance(): lax.ppermute(piece, axis, [(k, k ^ distance) for k in range(lax.axis_size...  12.4 us
    ppermute x8, starting transfers between devices, from_distance(): lax.ppermute(piece, axis, [(k, k ^ distance) for k in range(lax.axis_size...  10.1 us
    all_gather x1, blocking collectives, local(): hidden = lax.all_gather(own_hidden, 'dp', axis=0, tiled=True)  8.78 us
    pallas_call x1, Pallas kernels, attend(): pl.pallas_call(attention_kernel, out_shape=jax.ShapeDtypeStruct((ranks, n...  7.78 us
  transfers between devices with their start and end apart: 8, of which 5 were waited for; matrix products, arithmetic and copies ran while one was open for 0% of the time, Pallas kernels for 1%

profile of v9, /device:TPU:0, one launch (start us, length us, event | category | flops | bytes accessed | tf_op | source)
XLA Modules:
  0.0 139.2 jit_solution(11634594400096228209)
XLA Ops:
  0.0 1.8 %reshape.12.q_ref = bf16[4,128,576]{2,1,0:T(8,128)(2,1)S(1)} reshape(bf16[4,73728]{1,0:T(4,128)(2,1)} %param.11) | data formatting | bytes 1179648 | tf_op jit(solution)/shard_map/reshape | solution.py:568
  1.9 7.8 %attention.1 = bf16[32,16,512]{2,1,0:T(8,128)(2,1)S(1)} custom-call(s32[128]{0:T(128)} %lens_ref.1, bf16[4,128,576]{2,1,0:T(8,128)(2,1)S(1)} %reshape.12.q_ref, bf16[576,14336]{1,0:T(8,128)(2,1)} %bitcast.32), custom_call_target="tpu_custom_call" | custom-call | flops 3992977408 | bytes 16515072 | tf_op jit(solution)/shard_map/attention/pallas_call | solution.py:165
  9.7 28.5 %all_to_all.15 = bf16[32,16,512]{2,1,0:T(8,128)(2,1)S(1)} all-to-all(bf16[32,16,512]{2,1,0:T(8,128)(2,1)S(1)} %attention.1), channel_id=1, replica_groups=mesh['dp'=8,'tp'=4] {'dp','tp'}, dimensions={0} | all-to-all | bytes 1048576 | tf_op jit(solution)/shard_map/all_to_all | solution.py:549
  38.2 0.8 head_values.1
  39.0 18.4 %all-gather = bf16[768,512]{1,0:T(8,128)(2,1)S(1)} all-gather(bf16[192,512]{1,0:T(8,128)(2,1)S(1)} %head_values.1), channel_id=2, replica_groups=mesh['dp'=8,'tp'=4] {'tp'}, dimensions={0}, use_global_device_ids=true | all-gather | bytes 983040 | tf_op jit(solution)/shard_map/all_gather | solution.py:574
  57.3 1.1 project_out.1
  58.5 11.8 %all_to_all.16.parts_ref = bf16[8,16,1792]{2,1,0:T(8,128)(2,1)S(1)} all-to-all(bf16[8,16,1792]{2,1,0:T(8,128)(2,1)S(1)} %bitcast.22), channel_id=1, replica_groups=mesh['dp'=8,'tp'=4] {'dp'}, dimensions={0} | all-to-all | bytes 917504 | tf_op jit(solution)/shard_map/all_to_all | solution.py:549
  70.4 8.8 %all_gather.14.hidden_ref = bf16[128,1792]{1,0:T(8,128)(2,1)S(1)} all-gather(bf16[16,1792]{1,0:T(8,128)(2,1)S(1)} %hidden.1.hidden_ref), channel_id=1, replica_groups=mesh['dp'=8,'tp'=4] {'dp'}, dimensions={0}, use_global_device_ids=true | all-gather | bytes 516096 | tf_op jit(solution)/shard_map/all_gather | solution.py:578
  79.2 1.4 gate_up.1
  80.6 0.9 collective-permute-start.1
  81.5 2.3 %collective-permute-start = (bf16[64,1408]{1,0:T(8,128)(2,1)S(1)}, bf16[64,1408]{1,0:T(8,128)(2,1)S(1)}, u32[]{:S(2)}, u32[]{:S(2)}) collective-permute-start(bf16[64,1408]{1,0:T(8,128)(2,1)S(1)} %get-tuple-element.24), channel_id=1, source_target_pairs={{0,1},{1,0},{2,3},{3,2},{4,5},{5,4},{6,7},{7,6},{8,9},{9,8},{10,11... | collective-permute-start | bytes 540680 | tf_op jit(solution)/shard_map/ppermute | solution.py:247
  83.8 1.1 gate_up_rest.1
  85.0 1.8 %collective-permute-start.5 = (bf16[64,1024]{1,0:T(8,128)(2,1)S(1)}, bf16[64,1024]{1,0:T(8,128)(2,1)S(1)}, u32[]{:S(2)}, u32[]{:S(2)}) collective-permute-start(bf16[64,1024]{1,0:T(8,128)(2,1)S(1)} %get-tuple-element.34), channel_id=1, source_target_pairs={{0,2},{1,3},{2,0},{3,1},{4,6},{5,7},{6,4},{7,5},{8,10},{9,11},{10,... | collective-permute-start | bytes 393224 | tf_op jit(solution)/shard_map/ppermute | solution.py:247
  86.8 4.8 %collective-permute-done.1.refs_3_ = bf16[64,1280]{1,0:T(8,128)(2,1)S(1)} collective-permute-done((bf16[64,1280]{1,0:T(8,128)(2,1)S(1)}, bf16[64,1280]{1,0:T(8,128)(2,1)S(1)}, u32[]{:S(2)}, u32[]{:S(2)}) %collective-permute-start.1) | collective-permute-done | bytes 163872 | tf_op jit(solution)/shard_map/ppermute | solution.py:247
  91.6 3.9 %collective-permute-done.refs_2_ = bf16[64,1408]{1,0:T(8,128)(2,1)S(1)} collective-permute-done((bf16[64,1408]{1,0:T(8,128)(2,1)S(1)}, bf16[64,1408]{1,0:T(8,128)(2,1)S(1)}, u32[]{:S(2)}, u32[]{:S(2)}) %collective-permute-start) | collective-permute-done | bytes 180256 | tf_op jit(solution)/shard_map/ppermute | solution.py:247
  95.7 2.4 %collective-permute-start.3 = (bf16[32,1280]{1,0:T(8,128)(2,1)S(1)}, bf16[32,1280]{1,0:T(8,128)(2,1)S(1)}, u32[]{:S(2)}, u32[]{:S(2)}) collective-permute-start(bf16[32,1280]{1,0:T(8,128)(2,1)S(1)} %get-tuple-element.29), channel_id=1, source_target_pairs={{0,1},{1,0},{2,3},{3,2},{4,5},{5,4},{6,7},{7,6},{8,9},{9,8},{10,11... | collective-permute-start | bytes 245768 | tf_op jit(solution)/shard_map/ppermute | solution.py:247
  98.1 0.2 collective-permute-done.4.refs_2_
  98.4 0.8 collective-permute-start.6
  99.1 1.7 %collective-permute-start.7 = (bf16[32,1024]{1,0:T(8,128)(2,1)S(1)}, bf16[32,1024]{1,0:T(8,128)(2,1)S(1)}, u32[]{:S(2)}, u32[]{:S(2)}) collective-permute-start(bf16[32,1024]{1,0:T(8,128)(2,1)S(1)} %get-tuple-element.38), channel_id=1, source_target_pairs={{0,1},{1,0},{2,3},{3,2},{4,5},{5,4},{6,7},{7,6},{8,9},{9,8},{10,11... | collective-permute-start | bytes 196616 | tf_op jit(solution)/shard_map/ppermute | solution.py:247
  100.9 3.4 %collective-permute-done.6 = bf16[32,1024]{1,0:T(8,128)(2,1)S(1)} collective-permute-done((bf16[32,1024]{1,0:T(8,128)(2,1)S(1)}, bf16[32,1024]{1,0:T(8,128)(2,1)S(1)}, u32[]{:S(2)}, u32[]{:S(2)}) %collective-permute-start.6) | collective-permute-done | bytes 65568 | tf_op jit(solution)/shard_map/ppermute | solution.py:247
  104.5 15.9 %all_gather.15.inner_ref = bf16[128,2304]{1,0:T(8,128)(2,1)S(1)} all-gather(bf16[32,2304]{1,0:T(8,128)(2,1)S(1)} %inner.1), channel_id=1, replica_groups=mesh['dp'=8,'tp'=4] {'tp'}, dimensions={0}, use_global_device_ids=true | all-gather | bytes 737280 | tf_op jit(solution)/shard_map/all_gather | solution.py:595
  120.5 1.4 project_down.1
  121.9 16.6 %all_to_all.17.parts_ref = bf16[32,56,128]{2,1,0:T(8,128)(2,1)S(1)} all-to-all(bf16[32,56,128]{2,1,0:T(8,128)(2,1)S(1)} %project_down.1), channel_id=1, replica_groups=mesh['dp'=8,'tp'=4] {'dp','tp'}, dimensions={0} | all-to-all | bytes 917504 | tf_op jit(solution)/shard_map/all_to_all | solution.py:549
  138.5 0.7 layer.1
  (33 shorter events, 0.7 us)
Async XLA Ops:
  0.0 38.1 %copy-start.1 = (bf16[4,512,128]{2,1,0:T(8,128)(2,1)S(1)}, bf16[4,512,128]{2,1,0:T(8,128)(2,1)}, u32[]{:S(2)}) copy-start(bf16[4,512,128]{2,1,0:T(8,128)(2,1)} %w_ref.3) | copy-start | bytes 1572868
  0.0 38.1 %copy-start.2 = (bf16[4,7168]{1,0:T(4,128)(2,1)S(1)}, bf16[4,7168]{1,0:T(4,128)(2,1)}, u32[]{:S(2)}) copy-start(bf16[4,7168]{1,0:T(4,128)(2,1)} %residual_ref.1) | copy-start | bytes 172036
  1.8 55.5 %copy-start = (bf16[2048,1792]{1,0:T(8,128)(2,1)S(1)}, bf16[2048,1792]{1,0:T(8,128)(2,1)}, u32[]{:S(2)}) copy-start(bf16[2048,1792]{1,0:T(8,128)(2,1)} %w_ref.4) | copy-start | bytes 22020100
  1.8 77.3 %slice-start = ((s8[8257536]{0:T(1024)(128)(4,1)}), s8[4194304]{0:T(1024)(128)(4,1)S(1)}, s32[]{:S(2)}) async-start(s8[8257536]{0:T(1024)(128)(4,1)} %bitcast.13), calls=%async_computation.3 | async-start | bytes 8388608
  1.8 77.3 %slice-start.2 = ((s8[8257536]{0:T(1024)(128)(4,1)}), s8[4194304]{0:T(1024)(128)(4,1)S(1)}, s32[]{:S(2)}) async-start(s8[8257536]{0:T(1024)(128)(4,1)} %bitcast.15), calls=%async_computation.5 | async-start | bytes 8388608
  1.8 77.3 %slice-start.1 = ((s8[8257536]{0:T(1024)(128)(4,1)}), s8[4063232]{0:T(1024)(128)(4,1)S(1)}, s32[]{:S(2)}) async-start(s8[8257536]{0:T(1024)(128)(4,1)} %bitcast.13), calls=%async_computation.4 | async-start | bytes 8126464
  1.8 77.3 %slice-start.3 = ((s8[8257536]{0:T(1024)(128)(4,1)}), s8[4063232]{0:T(1024)(128)(4,1)S(1)}, s32[]{:S(2)}) async-start(s8[8257536]{0:T(1024)(128)(4,1)} %bitcast.15), calls=%async_computation.6 | async-start | bytes 8126464
  9.6 69.5 %copy-start.3 = (bf16[7168]{0:T(1024)(128)(2,1)S(1)}, bf16[7168]{0:T(1024)(128)(2,1)}, u32[]{:S(2)}) copy-start(bf16[7168]{0:T(1024)(128)(2,1)} %param.16) | copy-start | bytes 43012
  80.6 11.1 %collective-permute-start.1 = (bf16[64,1280]{1,0:T(8,128)(2,1)S(1)}, bf16[64,1280]{1,0:T(8,128)(2,1)S(1)}, u32[]{:S(2)}, u32[]{:S(2)}) collective-permute-start(bf16[64,1280]{1,0:T(8,128)(2,1)S(1)} %get-tuple-element.25), channel_id=1, source_target_pairs={{0,2},{1,3},{2,0},{3,1},{4,6},{5,7},{6,4},{7,5},{8,10},{9,11},{10,... | collective-permute-start | bytes 491528 | tf_op jit(solution)/shard_map/ppermute | solution.py:247
  81.5 14.0 %collective-permute-start = (bf16[64,1408]{1,0:T(8,128)(2,1)S(1)}, bf16[64,1408]{1,0:T(8,128)(2,1)S(1)}, u32[]{:S(2)}, u32[]{:S(2)}) collective-permute-start(bf16[64,1408]{1,0:T(8,128)(2,1)S(1)} %get-tuple-element.24), channel_id=1, source_target_pairs={{0,1},{1,0},{2,3},{3,2},{4,5},{5,4},{6,7},{7,6},{8,9},{9,8},{10,11... | collective-permute-start | bytes 540680 | tf_op jit(solution)/shard_map/ppermute | solution.py:247
  83.8 36.7 %slice-start.4 = ((s8[8257536]{0:T(1024)(128)(4,1)}), s8[4194304]{0:T(1024)(128)(4,1)S(1)}, s32[]{:S(2)}) async-start(s8[8257536]{0:T(1024)(128)(4,1)} %bitcast.17), calls=%async_computation.7 | async-start | bytes 8388608
  83.8 36.7 %slice-start.5 = ((s8[8257536]{0:T(1024)(128)(4,1)}), s8[4063232]{0:T(1024)(128)(4,1)S(1)}, s32[]{:S(2)}) async-start(s8[8257536]{0:T(1024)(128)(4,1)} %bitcast.17), calls=%async_computation.8 | async-start | bytes 8126464
  84.9 13.4 %collective-permute-start.4 = (bf16[64,1024]{1,0:T(8,128)(2,1)S(1)}, bf16[64,1024]{1,0:T(8,128)(2,1)S(1)}, u32[]{:S(2)}, u32[]{:S(2)}) collective-permute-start(bf16[64,1024]{1,0:T(8,128)(2,1)S(1)} %get-tuple-element.33), channel_id=1, source_target_pairs={{0,1},{1,0},{2,3},{3,2},{4,5},{5,4},{6,7},{7,6},{8,9},{9,8},{10,11... | collective-permute-start | bytes 393224 | tf_op jit(solution)/shard_map/ppermute | solution.py:247
  85.0 13.3 %collective-permute-start.5 = (bf16[64,1024]{1,0:T(8,128)(2,1)S(1)}, bf16[64,1024]{1,0:T(8,128)(2,1)S(1)}, u32[]{:S(2)}, u32[]{:S(2)}) collective-permute-start(bf16[64,1024]{1,0:T(8,128)(2,1)S(1)} %get-tuple-element.34), channel_id=1, source_target_pairs={{0,2},{1,3},{2,0},{3,1},{4,6},{5,7},{6,4},{7,5},{8,10},{9,11},{10,... | collective-permute-start | bytes 393224 | tf_op jit(solution)/shard_map/ppermute | solution.py:247
  95.6 8.7 %collective-permute-start.2 = (bf16[32,1408]{1,0:T(8,128)(2,1)S(1)}, bf16[32,1408]{1,0:T(8,128)(2,1)S(1)}, u32[]{:S(2)}, u32[]{:S(2)}) collective-permute-start(bf16[32,1408]{1,0:T(8,128)(2,1)S(1)} %get-tuple-element.28), channel_id=1, source_target_pairs={{0,2},{1,3},{2,0},{3,1},{4,6},{5,7},{6,4},{7,5},{8,10},{9,11},{10,... | collective-permute-start | bytes 270344 | tf_op jit(solution)/shard_map/ppermute | solution.py:247
  95.7 8.7 %collective-permute-start.3 = (bf16[32,1280]{1,0:T(8,128)(2,1)S(1)}, bf16[32,1280]{1,0:T(8,128)(2,1)S(1)}, u32[]{:S(2)}, u32[]{:S(2)}) collective-permute-start(bf16[32,1280]{1,0:T(8,128)(2,1)S(1)} %get-tuple-element.29), channel_id=1, source_target_pairs={{0,1},{1,0},{2,3},{3,2},{4,5},{5,4},{6,7},{7,6},{8,9},{9,8},{10,11... | collective-permute-start | bytes 245768 | tf_op jit(solution)/shard_map/ppermute | solution.py:247
  98.4 5.9 %collective-permute-start.6 = (bf16[32,1024]{1,0:T(8,128)(2,1)S(1)}, bf16[32,1024]{1,0:T(8,128)(2,1)S(1)}, u32[]{:S(2)}, u32[]{:S(2)}) collective-permute-start(bf16[32,1024]{1,0:T(8,128)(2,1)S(1)} %get-tuple-element.37), channel_id=1, source_target_pairs={{0,2},{1,3},{2,0},{3,1},{4,6},{5,7},{6,4},{7,5},{8,10},{9,11},{10,... | collective-permute-start | bytes 196616 | tf_op jit(solution)/shard_map/ppermute | solution.py:247
  99.1 5.2 %collective-permute-start.7 = (bf16[32,1024]{1,0:T(8,128)(2,1)S(1)}, bf16[32,1024]{1,0:T(8,128)(2,1)S(1)}, u32[]{:S(2)}, u32[]{:S(2)}) collective-permute-start(bf16[32,1024]{1,0:T(8,128)(2,1)S(1)} %get-tuple-element.38), channel_id=1, source_target_pairs={{0,1},{1,0},{2,3},{3,2},{4,5},{5,4},{6,7},{7,6},{8,9},{9,8},{10,11... | collective-permute-start | bytes 196616 | tf_op jit(solution)/shard_map/ppermute | solution.py:247

commit v10 on v9

--- a/solution.py
+++ b/solution.py
@@ -201,61 +201,65 @@
     )
 
 
-def head_values_kernel(latent_ref, w_ref, residual_ref, out_ref, values, slots):
+def head_values_kernel(latent_ref, w_ref, out_ref, values):
     heads, _, wide = w_ref.shape
-    per_rank, model = residual_ref.shape
-    requests = latent_ref.shape[0] // heads
+    requests = out_ref.shape[0]
     latent = latent_ref[...]
     for h in range(heads):
         values[...] = jnp.dot(latent, w_ref[h], preferred_element_type=jnp.float32)
         picked = values[pl.ds(h, requests, stride=heads), :]
-        out_ref[:requests, h * wide : (h + 1) * wide] = picked.astype(out_ref.dtype)
-    ranks = lax.axis_size("tp")
-    groups = model // ranks // 128
-    rows = (out_ref.shape[0] - requests) // ranks
-    across = out_ref.shape[1] // 128
-    slots[...] = jnp.zeros_like(slots)
-    for t in range(ranks):
-        for g in range(groups):
-            at = (t * groups + g) * 128
-            row = t * rows + (g // across) * per_rank
-            column = (g % across) * 128
-            slots[row : row + per_rank, column : column + 128] = residual_ref[
-                :, at : at + 128
-            ].astype(jnp.float32)
-    out_ref[requests:, :] = slots[...].astype(out_ref.dtype)
-
-
-def head_values(latent, w_uv, residual, slot_rows):
+        out_ref[:, h * wide : (h + 1) * wide] = picked.astype(out_ref.dtype)
+
+
+def head_values(latent, w_uv):
     heads, _, wide = w_uv.shape
     requests = latent.shape[0] // heads
     return pl.pallas_call(
         head_values_kernel,
-        out_shape=jax.ShapeDtypeStruct((requests + slot_rows, heads * wide), jnp.bfloat16),
-        in_specs=in_vmem(3),
+        out_shape=jax.ShapeDtypeStruct((requests, heads * wide), jnp.bfloat16),
+        in_specs=in_vmem(2),
         out_specs=pl.BlockSpec(memory_space=pltpu.VMEM),
-        scratch_shapes=[
-            pltpu.VMEM((latent.shape[0], wide), jnp.float32),
-            pltpu.VMEM((slot_rows, heads * wide), jnp.float32),
-        ],
+        scratch_shapes=[pltpu.VMEM((latent.shape[0], wide), jnp.float32)],
         compiler_params=kernel_params(12),
         name="head_values",
-    )(latent, w_uv, residual)
+    )(latent, w_uv)
+
+
+def split_kernel(rows_ref, *out_refs):
+    width = out_refs[0].shape[1]
+    me = lax.axis_index("tp")
+    for k, out_ref in enumerate(out_refs):
+        start = pl.multiple_of((me ^ k) * width, 128)
+        out_ref[...] = rows_ref[:, pl.ds(start, width)]
+
+
+def split_columns(rows, ranks):
+    shape = jax.ShapeDtypeStruct((rows.shape[0], rows.shape[1] // ranks), rows.dtype)
+    return pl.pallas_call(
+        split_kernel,
+        out_shape=[shape] * ranks,
+        in_specs=in_vmem(1),
+        out_specs=in_vmem(ranks),
+        compiler_params=kernel_params(8),
+        name="split_columns",
+    )(rows)
 
 
 def from_distance(piece, axis, distance):
     return lax.ppermute(piece, axis, [(k, k ^ distance) for k in range(lax.axis_size(axis))])
 
 
-def output_kernel(values_ref, w_ref, out_ref, total):
-    steps, _, depth = values_ref.shape
-    requests = out_ref.shape[0]
-    for k in range(steps):
-        term = jnp.dot(
-            values_ref[k, :requests, :],
-            w_ref[k * depth : (k + 1) * depth, :],
-            preferred_element_type=jnp.float32,
-        )
+def from_all(piece, axis):
+    return [piece] + [from_distance(piece, axis, k) for k in range(1, lax.axis_size(axis))]
+
+
+def output_kernel(*refs):
+    *values, w_ref, out_ref, total = refs
+    depth = values[0].shape[1]
+    me = lax.axis_index("tp")
+    for k, value in enumerate(values):
+        rows = pl.ds(pl.multiple_of((me ^ k) * depth, 128), depth)
+        term = jnp.dot(value[...], w_ref[rows, :], preferred_element_type=jnp.float32)
         if k == 0:
             total[...] = term
         else:
@@ -263,54 +267,46 @@
     out_ref[...] = total[...].astype(out_ref.dtype)
 
 
-def project_out(values, w_o, requests):
+def project_out(values, w_o):
+    requests = values[0].shape[0]
     width = w_o.shape[1]
     return pl.pallas_call(
         output_kernel,
         out_shape=jax.ShapeDtypeStruct((requests, width), jnp.bfloat16),
-        in_specs=in_vmem(2),
+        in_specs=in_vmem(len(values) + 1),
         out_specs=pl.BlockSpec(memory_space=pltpu.VMEM),
         scratch_shapes=[pltpu.VMEM((requests, width), jnp.float32)],
         compiler_params=kernel_params(12),
         name="project_out",
-    )(values, fetched(w_o))
-
-
-def hidden_kernel(parts_ref, values_ref, out_ref, slots):
-    ranks = values_ref.shape[0]
+    )(*values, fetched(w_o))
+
+
+def hidden_kernel(parts_ref, *refs):
+    *slices, out_ref, added = refs
+    per_rank = slices[0].shape[0]
+    me = lax.axis_index("tp")
+    for k, piece in enumerate(slices):
+        added[me ^ k] = piece[...].astype(jnp.float32)
     width = out_ref.shape[1]
-    per_rank = out_ref.shape[0] // ranks
-    across = values_ref.shape[2] // 128
-    rows = slots.shape[1]
-    requests = values_ref.shape[1] - ranks * rows
-    start = pl.multiple_of(requests + lax.axis_index("tp") * rows, 16)
-    for s in range(ranks):
-        slots[s] = values_ref[s, pl.ds(start, rows), :].astype(jnp.float32)
-    for g in range(width // 128):
-        at = slice(g * 128, (g + 1) * 128)
-        row = (g // across) * per_rank
-        column = (g % across) * 128
-        terms = [
-            slots[s, row : row + per_rank, column : column + 128] for s in range(ranks)
-        ]
+    for at in range(0, width, 128):
+        at = slice(at, at + 128)
         total = parts_ref[0, :, at].astype(jnp.float32)
         for d in range(1, parts_ref.shape[0]):
             total = total + parts_ref[d, :, at].astype(jnp.float32)
-        total = total + jnp.concatenate(terms, 0)
-        out_ref[:, at] = total.astype(out_ref.dtype)
-
-
-def make_hidden(parts, values, slot_rows):
-    ranks = values.shape[0]
+        terms = [added[s, :, at] for s in range(len(slices))]
+        out_ref[:, at] = (total + jnp.concatenate(terms, 0)).astype(out_ref.dtype)
+
+
+def make_hidden(parts, slices):
     return pl.pallas_call(
         hidden_kernel,
         out_shape=jax.ShapeDtypeStruct(parts.shape[1:], jnp.bfloat16),
-        in_specs=in_vmem(2),
+        in_specs=in_vmem(1 + len(slices)),
         out_specs=pl.BlockSpec(memory_space=pltpu.VMEM),
-        scratch_shapes=[pltpu.VMEM((ranks, slot_rows // ranks, values.shape[2]), jnp.float32)],
+        scratch_shapes=[pltpu.VMEM((len(slices),) + slices[0].shape, jnp.float32)],
         compiler_params=kernel_params(12),
         name="hidden",
-    )(parts, values)
+    )(parts, *slices)
 
 
 def scale_kernel(hidden_ref, gain_ref, gate_ref, up_ref, scaled, gate_sum, up_sum, *refs):
@@ -444,74 +440,93 @@
     return outs[: len(kept)], outs[len(kept) :]
 
 
-def inner_kernel(model, counts, *refs):
-    *parts, out_ref = refs
-    factor = None
+def inner_kernel(model, given, *refs):
+    *parts, out_ref, factor_ref = refs
+    gates, ups = parts[given::2], parts[given + 1 :: 2]
+    columns = out_ref.shape[1]
+
+    def total(parts, at):
+        terms = [
+            part[n, :, at].astype(jnp.float32) for part in parts for n in range(part.shape[0])
+        ]
+        return sum(terms[1:], terms[0])
+
+    if given:
+        factor = parts[0][...]
+    else:
+        square = jnp.sum(total(gates, slice(columns, columns + 128)), 1, keepdims=True)
+        factor = jnp.broadcast_to(lax.rsqrt(square / model + 1e-06), factor_ref.shape)
+    factor_ref[...] = factor
+    for at in range(0, columns, 128):
+        at = slice(at, at + 128)
+        gate = total(gates, at) * factor
+        up = total(ups, at) * factor
+        out_ref[:, at] = (gate / (1.0 + jnp.exp(-gate)) * up).astype(out_ref.dtype)
+
+
+def make_inner(parts, factor, model):
+    given = [] if factor is None else [factor]
+    rows, columns = parts[1].shape[1:]
+    return pl.pallas_call(
+        functools.partial(inner_kernel, model, len(given)),
+        out_shape=[
+            jax.ShapeDtypeStruct((rows, columns), jnp.bfloat16),
+            jax.ShapeDtypeStruct((rows, 128), jnp.float32),
+        ],
+        in_specs=in_vmem(len(given) + len(parts)),
+        out_specs=in_vmem(2),
+        compiler_params=kernel_params(12),
+        name="inner",
+    )(*given, *parts)
+
+
+def down_kernel(chunks, *refs):
+    *pieces, w_ref, hidden_ref, out_ref, inner, total = refs
+    width = w_ref.shape[1]
+    count = len(pieces) // chunks
+    share = total.shape[0] // count
     at = 0
-    for count in counts:
-        gates, ups, parts = parts[0:count:2], parts[1:count:2], parts[count:]
-        columns = ups[0].shape[2]
-
-        def total(parts, at):
-            terms = [
-                part[n, :, at].astype(jnp.float32) for part in parts for n in range(part.shape[0])
-            ]
-            return sum(terms[1:], terms[0])
-
-        if factor is None:
-            square = jnp.sum(total(gates, slice(columns, columns + 128)), 1, keepdims=True)
-            factor = lax.rsqrt(square / model + 1e-06)
-        for start in range(0, columns, 128):
-            span = slice(start, start + 128)
-            gate = total(gates, span) * factor
-            up = total(ups, span) * factor
-            value = gate / (1.0 + jnp.exp(-gate)) * up
-            out_ref[:, at + start : at + start + 128] = value.astype(out_ref.dtype)
+    for c in range(chunks):
+        columns = pieces[c * count].shape[1]
+        for k in range(count):
+            inner[k * share : (k + 1) * share, at : at + columns] = pieces[c * count + k][...]
         at += columns
-
-
-def make_inner(chunks, units, model):
-    parts = [part for chunk in chunks for part in chunk]
-    return pl.pallas_call(
-        functools.partial(inner_kernel, model, [len(chunk) for chunk in chunks]),
-        out_shape=jax.ShapeDtypeStruct((parts[0].shape[1], units), jnp.bfloat16),
-        in_specs=in_vmem(len(parts)),
-        out_specs=pl.BlockSpec(memory_space=pltpu.VMEM),
-        compiler_params=kernel_params(12),
-        name="inner",
-    )(*parts)
-
-
-def down_kernel(inner_ref, w_ref, hidden_ref, out_ref, total):
-    width = w_ref.shape[1]
-    total[...] = jnp.dot(inner_ref[...], w_ref[...], preferred_element_type=jnp.float32)
+    result = jnp.dot(inner[...], w_ref[...], preferred_element_type=jnp.float32)
+    me = lax.axis_index("tp")
+    for k in range(count):
+        start = pl.multiple_of((me ^ k) * share, 16) if count > 1 else 0
+        total[pl.ds(start, share), :] = result[k * share : (k + 1) * share]
     rows = hidden_ref.shape[0]
     own = pl.ds(pl.multiple_of(lax.axis_index("dp") * rows, 16), rows)
     total[own, :] += hidden_ref[...].astype(jnp.float32)
     groups = width // 128
     per_rank = out_ref.shape[1] // groups
     for d in range(out_ref.shape[0]):
-        pieces = [
+        owned = [
             total[d * per_rank : (d + 1) * per_rank, g * 128 : (g + 1) * 128]
             for g in range(groups)
         ]
-        out_ref[d] = jnp.concatenate(pieces, 0).astype(out_ref.dtype)
-
-
-def project_down(inner, w_down, hidden, ranks):
-    requests, units = inner.shape
-    width = w_down.shape[1]
-    return pl.pallas_call(
-        down_kernel,
+        out_ref[d] = jnp.concatenate(owned, 0).astype(out_ref.dtype)
+
+
+def project_down(chunks, w_down, hidden, ranks):
+    units, width = w_down.shape
+    pieces = [piece for chunk in chunks for piece in chunk]
+    requests = sum(piece.shape[0] for piece in chunks[0])
+    return pl.pallas_call(
+        functools.partial(down_kernel, len(chunks)),
         out_shape=jax.ShapeDtypeStruct(
             (ranks, requests // ranks * (width // 128), 128), jnp.bfloat16
         ),
-        in_specs=in_vmem(3),
+        in_specs=in_vmem(len(pieces) + 2),
         out_specs=pl.BlockSpec(memory_space=pltpu.VMEM),
-        scratch_shapes=[pltpu.VMEM((requests, width), jnp.float32)],
+        scratch_shapes=[
+            pltpu.VMEM((requests, units), jnp.bfloat16),
+            pltpu.VMEM((requests, width), jnp.float32),
+        ],
         compiler_params=kernel_params(12),
         name="project_down",
-    )(inner, fetched(w_down), hidden)
+    )(*pieces, fetched(w_down), hidden)
 
 
 def layer_kernel(parts_ref, out_ref, total):
@@ -563,36 +578,37 @@
     units = w_gate.shape[1]
     width = w_o.shape[1]
 
-    groups = width // 128
 
     query = queries.reshape(per_rank, heads_all, row_length)
     latent = swap(attend(lengths, query, paged_latent_cache.T, ranks), ("dp", "tp"))
 
-    across = heads_here * w_uv.shape[2] // 128
-    slot_rows = ranks_tp * round_up(per_rank * ((groups + across - 1) // across), 16)
-    values = head_values(latent.reshape(requests * heads_here, C), w_uv, residual, slot_rows)
-    values = lax.all_gather(values, "tp", axis=0)
-    attn = project_out(values, w_o, requests)
+    values = head_values(latent.reshape(requests * heads_here, C), w_uv)
+    values, residual = lax.optimization_barrier((values, residual))
+    values = from_all(values, "tp")
+    added = list(split_columns(residual, ranks_tp))
+    added = added[:1] + [from_distance(added[k], "tp", k) for k in range(1, ranks_tp)]
+    attn, added = lax.optimization_barrier((project_out(values, w_o), added))
     attn = swap(attn.reshape(ranks_dp, requests // ranks_dp, width), "dp")
-    own_hidden = make_hidden(attn, values, slot_rows)
+    own_hidden = make_hidden(attn, added)
     hidden = lax.all_gather(own_hidden, "dp", axis=0, tiled=True)
 
     halves = 2 if ranks_tp == 4 else 1
     chunks = gate_up(hidden, norm_gain.reshape(-1, 128), w_gate, w_up, halves)
-    if halves == 2:
-        sums = []
-        for gate_send, up_send, gate_keep, up_keep in chunks:
+    inner = []
+    factor = None
+    for chunk in chunks:
+        if halves == 2:
+            gate_send, up_send, gate_keep, up_keep = chunk
             came = [from_distance(gate_send, "tp", 1), from_distance(up_send, "tp", 2)]
             (gate_send, up_send), kept = halve([gate_keep, up_keep], came)
             came = [from_distance(gate_send, "tp", 2), from_distance(up_send, "tp", 1)]
-            sums.append([part[None] for part in (*kept, *came)])
-    else:
-        sums = [
-            [swap(part.reshape(ranks_tp, -1, part.shape[1]), "tp") for part in chunk]
-            for chunk in chunks
-        ]
-    inner = make_inner(sums, units, model)
-    inner = lax.all_gather(inner, "tp", axis=0, tiled=True)
+            own, factor = make_inner([part[None] for part in (*kept, *came)], factor, model)
+            far = from_distance(own, "tp", 2)
+            inner.append([own, from_distance(own, "tp", 1), far, from_distance(far, "tp", 1)])
+        else:
+            parts = [swap(part.reshape(ranks_tp, -1, part.shape[1]), "tp") for part in chunk]
+            own, factor = make_inner(parts, factor, model)
+            inner.append([lax.all_gather(own, "tp", axis=0, tiled=True)])
     ffn = swap(project_down(inner, w_down, own_hidden, ranks), ("dp", "tp"))
     return make_layer(ffn, per_rank, model)
 

time: 140 us -> 133 us (0.950); the launches traced: 139 us -> 130 us
  blocking collectives: 100 us -> 59.8 us
  starting transfers between devices: 10.1 us -> 25.9 us
  waiting for transfers between devices: 12.4 us -> 24.2 us
  local copies, waits for them, and re-layouts: 1.84 us -> 4.87 us
    all_gather x2 -> x0, blocking collectives: 34.3 us -> none  [the longest x1 18.4 us: local(): values = lax.all_gather(values, 'tp', axis=0)]
    ppermute x8 -> x20, starting transfers between devices: 10.1 us -> 25.9 us  [from_distance(): lax.ppermute(piece, axis, [(k, k ^ distance) for k in range(lax.axis_size...]
    ppermute x8 -> x20, waiting for transfers between devices: 12.4 us -> 24.2 us  [from_distance(): lax.ppermute(piece, axis, [(k, k ^ distance) for k in range(lax.axis_size...]
    all_to_all x3, blocking collectives: 56.9 us -> 51 us  [swap(): return lax.all_to_all(parts, axes, split_axis=0, concat_axis=0, tiled=True)]
    unnamed x20, local copies, waits for them, and re-layouts: 0.05 us -> 3.14 us
  transfers between devices with their start and end apart: 8 -> 20, of which waited for: 5 -> 11; matrix products, arithmetic and copies ran while one was open for 0% -> 0% of each run, Pallas kernels for 1% -> 2%
where the time goes in v10:
time: 133 us; the launch traced here: 130 us
  blocking collectives  59.8 us (45%)
  starting transfers between devices  25.9 us (19%)
  waiting for transfers between devices  24.2 us (18%)
  Pallas kernels  15.4 us (12%)
  local copies, waits for them, and re-layouts  4.87 us (4%)
    all_to_all x3, blocking collectives, swap(): return lax.all_to_all(parts, axes, split_axis=0, concat_axis=0, tiled=True)  51 us
    ppermute x20, starting transfers between devices, from_distance(): lax.ppermute(piece, axis, [(k, k ^ distance) for k in range(lax.axis_size...  25.9 us
    ppermute x20, waiting for transfers between devices, from_distance(): lax.ppermute(piece, axis, [(k, k ^ distance) for k in range(lax.axis_size...  24.2 us
    all_gather x1, blocking collectives, local(): hidden = lax.all_gather(own_hidden, 'dp', axis=0, tiled=True)  8.78 us
    pallas_call x1, Pallas kernels, attend(): pl.pallas_call(attention_kernel, out_shape=jax.ShapeDtypeStruct((ranks, n...  7.86 us
    unnamed x20, local copies, waits for them, and re-layouts  3.14 us
  transfers between devices with their start and end apart: 20, of which 11 were waited for; matrix products, arithmetic and copies ran while one was open for 0% of the time, Pallas kernels for 2%

profile of v10, /device:TPU:0, one launch (start us, length us, event | category | flops | bytes accessed | tf_op | source)
XLA Modules:
  0.0 130.4 jit_solution(429959510124989442)
XLA Ops:
  0.0 1.7 %reshape.12.q_ref = bf16[4,128,576]{2,1,0:T(8,128)(2,1)S(1)} reshape(bf16[4,73728]{1,0:T(4,128)(2,1)} %param.11) | data formatting | bytes 1179648 | tf_op jit(solution)/shard_map/reshape | solution.py:582
  1.8 7.9 %attention.1 = bf16[32,16,512]{2,1,0:T(8,128)(2,1)S(1)} custom-call(s32[128]{0:T(128)} %lens_ref.1, bf16[4,128,576]{2,1,0:T(8,128)(2,1)S(1)} %reshape.12.q_ref, bf16[576,14336]{1,0:T(8,128)(2,1)} %bitcast.29), custom_call_target="tpu_custom_call" | custom-call | flops 3992977408 | bytes 16515072 | tf_op jit(solution)/shard_map/attention/pallas_call | solution.py:165
  9.7 23.0 %all_to_all.15 = bf16[32,16,512]{2,1,0:T(8,128)(2,1)S(1)} all-to-all(bf16[32,16,512]{2,1,0:T(8,128)(2,1)S(1)} %attention.1), channel_id=1, replica_groups=mesh['dp'=8,'tp'=4] {'dp','tp'}, dimensions={0} | all-to-all | bytes 1048576 | tf_op jit(solution)/shard_map/all_to_all | solution.py:564
  33.5 2.9 %collective-permute-start.2 = (bf16[128,512]{1,0:T(8,128)(2,1)S(1)}, bf16[128,512]{1,0:T(8,128)(2,1)S(1)}, u32[]{:S(2)}, u32[]{:S(2)}) collective-permute-start(bf16[128,512]{1,0:T(8,128)(2,1)S(1)} %head_values.1.refs_0_), channel_id=1, source_target_pairs={{0,3},{1,2},{2,1},{3,0},{4,7},{5,6},{6,5},{7,4},{8,11},{9,10},{10,... | collective-permute-start | bytes 393224 | tf_op jit(solution)/shard_map/ppermute | solution.py:249
  38.0 1.7 %collective-permute-start.3 = (bf16[4,1792]{1,0:T(4,128)(2,1)S(1)}, bf16[4,1792]{1,0:T(4,128)(2,1)S(1)}, u32[]{:S(2)}, u32[]{:S(2)}) collective-permute-start(bf16[4,1792]{1,0:T(4,128)(2,1)S(1)} %get-tuple-element.39), channel_id=1, source_target_pairs={{0,1},{1,0},{2,3},{3,2},{4,5},{5,4},{6,7},{7,6},{8,9},{9,8},{10,11... | collective-permute-start | bytes 43016 | tf_op jit(solution)/shard_map/ppermute | solution.py:249
  39.7 1.7 %collective-permute-start.4 = (bf16[4,1792]{1,0:T(4,128)(2,1)S(1)}, bf16[4,1792]{1,0:T(4,128)(2,1)S(1)}, u32[]{:S(2)}, u32[]{:S(2)}) collective-permute-start(bf16[4,1792]{1,0:T(4,128)(2,1)S(1)} %get-tuple-element.40), channel_id=1, source_target_pairs={{0,2},{1,3},{2,0},{3,1},{4,6},{5,7},{6,4},{7,5},{8,10},{9,11},{10,... | collective-permute-start | bytes 43016 | tf_op jit(solution)/shard_map/ppermute | solution.py:249
  41.7 3.0 %collective-permute-start.5 = (bf16[4,1792]{1,0:T(4,128)(2,1)S(1)}, bf16[4,1792]{1,0:T(4,128)(2,1)S(1)}, u32[]{:S(2)}, u32[]{:S(2)}) collective-permute-start(bf16[4,1792]{1,0:T(4,128)(2,1)S(1)} %get-tuple-element.41), channel_id=1, source_target_pairs={{0,3},{1,2},{2,1},{3,0},{4,7},{5,6},{6,5},{7,4},{8,11},{9,10},{10,... | collective-permute-start | bytes 43016 | tf_op jit(solution)/shard_map/ppermute | solution.py:249
  44.7 5.0 %collective-permute-done.1.refs_2_ = bf16[128,512]{1,0:T(8,128)(2,1)S(1)} collective-permute-done((bf16[128,512]{1,0:T(8,128)(2,1)S(1)}, bf16[128,512]{1,0:T(8,128)(2,1)S(1)}, u32[]{:S(2)}, u32[]{:S(2)}) %collective-permute-start.1) | collective-permute-done | bytes 131104 | tf_op jit(solution)/shard_map/ppermute | solution.py:249
  49.7 3.1 %copy-done = bf16[2048,1792]{1,0:T(8,128)(2,1)S(1)} copy-done((bf16[2048,1792]{1,0:T(8,128)(2,1)S(1)}, bf16[2048,1792]{1,0:T(8,128)(2,1)}, u32[]{:S(2)}) %copy-start) | copy-done | bytes 7340056
  53.9 11.6 %all_to_all.16.parts_ref = bf16[8,16,1792]{2,1,0:T(8,128)(2,1)S(1)} all-to-all(bf16[8,16,1792]{2,1,0:T(8,128)(2,1)S(1)} %bitcast.19), channel_id=1, replica_groups=mesh['dp'=8,'tp'=4] {'dp'}, dimensions={0} | all-to-all | bytes 917504 | tf_op jit(solution)/shard_map/all_to_all | solution.py:564
  65.6 8.8 %all_gather.3.hidden_ref = bf16[128,1792]{1,0:T(8,128)(2,1)S(1)} all-gather(bf16[16,1792]{1,0:T(8,128)(2,1)S(1)} %hidden.1.refs_9_), channel_id=1, replica_groups=mesh['dp'=8,'tp'=4] {'dp'}, dimensions={0}, use_global_device_ids=true | all-gather | bytes 516096 | tf_op jit(solution)/shard_map/all_gather | solution.py:593
  75.9 2.3 %collective-permute-start.7 = (bf16[64,1280]{1,0:T(8,128)(2,1)S(1)}, bf16[64,1280]{1,0:T(8,128)(2,1)S(1)}, u32[]{:S(2)}, u32[]{:S(2)}) collective-permute-start(bf16[64,1280]{1,0:T(8,128)(2,1)S(1)} %get-tuple-element.50), channel_id=1, source_target_pairs={{0,2},{1,3},{2,0},{3,1},{4,6},{5,7},{6,4},{7,5},{8,10},{9,11},{10,... | collective-permute-start | bytes 491528 | tf_op jit(solution)/shard_map/ppermute | solution.py:249
  79.5 2.5 %collective-permute-start.14 = (bf16[64,1024]{1,0:T(8,128)(2,1)S(1)}, bf16[64,1024]{1,0:T(8,128)(2,1)S(1)}, u32[]{:S(2)}, u32[]{:S(2)}) collective-permute-start(bf16[64,1024]{1,0:T(8,128)(2,1)S(1)} %get-tuple-element.61), channel_id=1, source_target_pairs={{0,2},{1,3},{2,0},{3,1},{4,6},{5,7},{6,4},{7,5},{8,10},{9,11},{10,... | collective-permute-start | bytes 393224 | tf_op jit(solution)/shard_map/ppermute | solution.py:249
  82.0 5.5 %collective-permute-done.7.refs_3_ = bf16[64,1280]{1,0:T(8,128)(2,1)S(1)} collective-permute-done((bf16[64,1280]{1,0:T(8,128)(2,1)S(1)}, bf16[64,1280]{1,0:T(8,128)(2,1)S(1)}, u32[]{:S(2)}, u32[]{:S(2)}) %collective-permute-start.7) | collective-permute-done | bytes 163872 | tf_op jit(solution)/shard_map/ppermute | solution.py:249
  87.9 2.0 %collective-permute-start.9 = (bf16[32,1280]{1,0:T(8,128)(2,1)S(1)}, bf16[32,1280]{1,0:T(8,128)(2,1)S(1)}, u32[]{:S(2)}, u32[]{:S(2)}) collective-permute-start(bf16[32,1280]{1,0:T(8,128)(2,1)S(1)} %get-tuple-element.54), channel_id=1, source_target_pairs={{0,1},{1,0},{2,3},{3,2},{4,5},{5,4},{6,7},{7,6},{8,9},{9,8},{10,11... | collective-permute-start | bytes 245768 | tf_op jit(solution)/shard_map/ppermute | solution.py:249
  89.9 2.0 %collective-permute-done.13.refs_2_ = bf16[64,1024]{1,0:T(8,128)(2,1)S(1)} collective-permute-done((bf16[64,1024]{1,0:T(8,128)(2,1)S(1)}, bf16[64,1024]{1,0:T(8,128)(2,1)S(1)}, u32[]{:S(2)}, u32[]{:S(2)}) %collective-permute-start.13) | collective-permute-done | bytes 131104 | tf_op jit(solution)/shard_map/ppermute | solution.py:249
  91.8 3.2 %collective-permute-done.14.refs_3_ = bf16[64,1024]{1,0:T(8,128)(2,1)S(1)} collective-permute-done((bf16[64,1024]{1,0:T(8,128)(2,1)S(1)}, bf16[64,1024]{1,0:T(8,128)(2,1)S(1)}, u32[]{:S(2)}, u32[]{:S(2)}) %collective-permute-start.14) | collective-permute-done | bytes 131104 | tf_op jit(solution)/shard_map/ppermute | solution.py:249
  95.2 2.2 %collective-permute-start.16 = (bf16[32,1024]{1,0:T(8,128)(2,1)S(1)}, bf16[32,1024]{1,0:T(8,128)(2,1)S(1)}, u32[]{:S(2)}, u32[]{:S(2)}) collective-permute-start(bf16[32,1024]{1,0:T(8,128)(2,1)S(1)} %get-tuple-element.65), channel_id=1, source_target_pairs={{0,1},{1,0},{2,3},{3,2},{4,5},{5,4},{6,7},{7,6},{8,9},{9,8},{10,11... | collective-permute-start | bytes 196616 | tf_op jit(solution)/shard_map/ppermute | solution.py:249
  98.3 2.8 %collective-permute-done.15 = bf16[32,1024]{1,0:T(8,128)(2,1)S(1)} collective-permute-done((bf16[32,1024]{1,0:T(8,128)(2,1)S(1)}, bf16[32,1024]{1,0:T(8,128)(2,1)S(1)}, u32[]{:S(2)}, u32[]{:S(2)}) %collective-permute-start.15) | collective-permute-done | bytes 65568 | tf_op jit(solution)/shard_map/ppermute | solution.py:249
  105.1 2.0 %collective-permute-start.17 = (bf16[32,1024]{1,0:T(8,128)(2,1)S(1)}, bf16[32,1024]{1,0:T(8,128)(2,1)S(1)}, u32[]{:S(2)}, u32[]{:S(2)}) collective-permute-start(bf16[32,1024]{1,0:T(8,128)(2,1)S(1)} %get-tuple-element.66.refs_4_), channel_id=1, source_target_pairs={{0,1},{1,0},{2,3},{3,2},{4,5},{5,4},{6,7},{7,6},{8,9},{9,8},{10,11... | collective-permute-start | bytes 196616 | tf_op jit(solution)/shard_map/ppermute | solution.py:249
  107.9 2.5 %collective-permute-done.17.refs_5_ = bf16[32,1024]{1,0:T(8,128)(2,1)S(1)} collective-permute-done((bf16[32,1024]{1,0:T(8,128)(2,1)S(1)}, bf16[32,1024]{1,0:T(8,128)(2,1)S(1)}, u32[]{:S(2)}, u32[]{:S(2)}) %collective-permute-start.17) | collective-permute-done | bytes 65568 | tf_op jit(solution)/shard_map/ppermute | solution.py:249
  110.4 1.5 %collective-permute-done.19.refs_7_ = bf16[32,1024]{1,0:T(8,128)(2,1)S(1)} collective-permute-done((bf16[32,1024]{1,0:T(8,128)(2,1)S(1)}, bf16[32,1024]{1,0:T(8,128)(2,1)S(1)}, u32[]{:S(2)}, u32[]{:S(2)}) %collective-permute-start.19) | collective-permute-done | bytes 65568 | tf_op jit(solution)/shard_map/ppermute | solution.py:249
  111.9 1.4 %project_down.1 = bf16[32,56,128]{2,1,0:T(8,128)(2,1)S(1)} custom-call(bf16[32,1280]{1,0:T(8,128)(2,1)S(1)} %get-tuple-element.55.refs_0_, bf16[32,1280]{1,0:T(8,128)(2,1)S(1)} %collective-permute-done.10.refs_1_, bf16[32,1280]{1,0:T(8,128)(2,1)S(1)} %collective-permute-done.11.refs_2_, bf16[32,1280]{1,0:T(8,128)(2,1)S(1)} %collective-permute-done.12.refs_3_, ...), custom_call_target="tpu_custom_call" | custom-call | tf_op jit(solution)/shard_map/project_down/pallas_call | solution.py:516
  113.3 16.4 %all_to_all.17.parts_ref = bf16[32,56,128]{2,1,0:T(8,128)(2,1)S(1)} all-to-all(bf16[32,56,128]{2,1,0:T(8,128)(2,1)S(1)} %project_down.1), channel_id=1, replica_groups=mesh['dp'=8,'tp'=4] {'dp','tp'}, dimensions={0} | all-to-all | bytes 917504 | tf_op jit(solution)/shard_map/all_to_all | solution.py:564
  (57 shorter events, 13.6 us)
Async XLA Ops:
  1.7 72.7 %slice-start = ((s8[8257536]{0:T(1024)(128)(4,1)}), s8[4194304]{0:T(1024)(128)(4,1)S(1)}, s32[]{:S(2)}) async-start(s8[8257536]{0:T(1024)(128)(4,1)} %bitcast.12), calls=%async_computation.3 | async-start | bytes 8388608
  1.8 72.6 %slice-start.2 = ((s8[8257536]{0:T(1024)(128)(4,1)}), s8[4194304]{0:T(1024)(128)(4,1)S(1)}, s32[]{:S(2)}) async-start(s8[8257536]{0:T(1024)(128)(4,1)} %bitcast.14), calls=%async_computation.5 | async-start | bytes 8388608
  1.8 72.6 %slice-start.1 = ((s8[8257536]{0:T(1024)(128)(4,1)}), s8[4063232]{0:T(1024)(128)(4,1)S(1)}, s32[]{:S(2)}) async-start(s8[8257536]{0:T(1024)(128)(4,1)} %bitcast.12), calls=%async_computation.4 | async-start | bytes 8126464
  1.8 72.6 %slice-start.3 = ((s8[8257536]{0:T(1024)(128)(4,1)}), s8[4063232]{0:T(1024)(128)(4,1)S(1)}, s32[]{:S(2)}) async-start(s8[8257536]{0:T(1024)(128)(4,1)} %bitcast.14), calls=%async_computation.6 | async-start | bytes 8126464
  33.5 8.2 %collective-permute-start.2 = (bf16[128,512]{1,0:T(8,128)(2,1)S(1)}, bf16[128,512]{1,0:T(8,128)(2,1)S(1)}, u32[]{:S(2)}, u32[]{:S(2)}) collective-permute-start(bf16[128,512]{1,0:T(8,128)(2,1)S(1)} %head_values.1.refs_0_), channel_id=1, source_target_pairs={{0,3},{1,2},{2,1},{3,0},{4,7},{5,6},{6,5},{7,4},{8,11},{9,10},{10,... | collective-permute-start | bytes 393224 | tf_op jit(solution)/shard_map/ppermute | solution.py:249
  36.4 13.3 %collective-permute-start.1 = (bf16[128,512]{1,0:T(8,128)(2,1)S(1)}, bf16[128,512]{1,0:T(8,128)(2,1)S(1)}, u32[]{:S(2)}, u32[]{:S(2)}) collective-permute-start(bf16[128,512]{1,0:T(8,128)(2,1)S(1)} %head_values.1.refs_0_), channel_id=1, source_target_pairs={{0,2},{1,3},{2,0},{3,1},{4,6},{5,7},{6,4},{7,5},{8,10},{9,11},{10,... | collective-permute-start | bytes 393224 | tf_op jit(solution)/shard_map/ppermute | solution.py:249
  37.6 12.1 %collective-permute-start = (bf16[128,512]{1,0:T(8,128)(2,1)S(1)}, bf16[128,512]{1,0:T(8,128)(2,1)S(1)}, u32[]{:S(2)}, u32[]{:S(2)}) collective-permute-start(bf16[128,512]{1,0:T(8,128)(2,1)S(1)} %head_values.1.refs_0_), channel_id=1, source_target_pairs={{0,1},{1,0},{2,3},{3,2},{4,5},{5,4},{6,7},{7,6},{8,9},{9,8},{10,11... | collective-permute-start | bytes 393224 | tf_op jit(solution)/shard_map/ppermute | solution.py:249
  38.0 15.9 %collective-permute-start.3 = (bf16[4,1792]{1,0:T(4,128)(2,1)S(1)}, bf16[4,1792]{1,0:T(4,128)(2,1)S(1)}, u32[]{:S(2)}, u32[]{:S(2)}) collective-permute-start(bf16[4,1792]{1,0:T(4,128)(2,1)S(1)} %get-tuple-element.39), channel_id=1, source_target_pairs={{0,1},{1,0},{2,3},{3,2},{4,5},{5,4},{6,7},{7,6},{8,9},{9,8},{10,11... | collective-permute-start | bytes 43016 | tf_op jit(solution)/shard_map/ppermute | solution.py:249
  39.7 14.2 %collective-permute-start.4 = (bf16[4,1792]{1,0:T(4,128)(2,1)S(1)}, bf16[4,1792]{1,0:T(4,128)(2,1)S(1)}, u32[]{:S(2)}, u32[]{:S(2)}) collective-permute-start(bf16[4,1792]{1,0:T(4,128)(2,1)S(1)} %get-tuple-element.40), channel_id=1, source_target_pairs={{0,2},{1,3},{2,0},{3,1},{4,6},{5,7},{6,4},{7,5},{8,10},{9,11},{10,... | collective-permute-start | bytes 43016 | tf_op jit(solution)/shard_map/ppermute | solution.py:249
  41.7 12.2 %collective-permute-start.5 = (bf16[4,1792]{1,0:T(4,128)(2,1)S(1)}, bf16[4,1792]{1,0:T(4,128)(2,1)S(1)}, u32[]{:S(2)}, u32[]{:S(2)}) collective-permute-start(bf16[4,1792]{1,0:T(4,128)(2,1)S(1)} %get-tuple-element.41), channel_id=1, source_target_pairs={{0,3},{1,2},{2,1},{3,0},{4,7},{5,6},{6,5},{7,4},{8,11},{9,10},{10,... | collective-permute-start | bytes 43016 | tf_op jit(solution)/shard_map/ppermute | solution.py:249
  75.8 11.7 %collective-permute-start.6 = (bf16[64,1408]{1,0:T(8,128)(2,1)S(1)}, bf16[64,1408]{1,0:T(8,128)(2,1)S(1)}, u32[]{:S(2)}, u32[]{:S(2)}) collective-permute-start(bf16[64,1408]{1,0:T(8,128)(2,1)S(1)} %get-tuple-element.49), channel_id=1, source_target_pairs={{0,1},{1,0},{2,3},{3,2},{4,5},{5,4},{6,7},{7,6},{8,9},{9,8},{10,11... | collective-permute-start | bytes 540680 | tf_op jit(solution)/shard_map/ppermute | solution.py:249
  75.9 11.7 %collective-permute-start.7 = (bf16[64,1280]{1,0:T(8,128)(2,1)S(1)}, bf16[64,1280]{1,0:T(8,128)(2,1)S(1)}, u32[]{:S(2)}, u32[]{:S(2)}) collective-permute-start(bf16[64,1280]{1,0:T(8,128)(2,1)S(1)} %get-tuple-element.50), channel_id=1, source_target_pairs={{0,2},{1,3},{2,0},{3,1},{4,6},{5,7},{6,4},{7,5},{8,10},{9,11},{10,... | collective-permute-start | bytes 491528 | tf_op jit(solution)/shard_map/ppermute | solution.py:249
  79.4 12.5 %collective-permute-start.13 = (bf16[64,1024]{1,0:T(8,128)(2,1)S(1)}, bf16[64,1024]{1,0:T(8,128)(2,1)S(1)}, u32[]{:S(2)}, u32[]{:S(2)}) collective-permute-start(bf16[64,1024]{1,0:T(8,128)(2,1)S(1)} %get-tuple-element.60), channel_id=1, source_target_pairs={{0,1},{1,0},{2,3},{3,2},{4,5},{5,4},{6,7},{7,6},{8,9},{9,8},{10,11... | collective-permute-start | bytes 393224 | tf_op jit(solution)/shard_map/ppermute | solution.py:249
  79.5 15.5 %collective-permute-start.14 = (bf16[64,1024]{1,0:T(8,128)(2,1)S(1)}, bf16[64,1024]{1,0:T(8,128)(2,1)S(1)}, u32[]{:S(2)}, u32[]{:S(2)}) collective-permute-start(bf16[64,1024]{1,0:T(8,128)(2,1)S(1)} %get-tuple-element.61), channel_id=1, source_target_pairs={{0,2},{1,3},{2,0},{3,1},{4,6},{5,7},{6,4},{7,5},{8,10},{9,11},{10,... | collective-permute-start | bytes 393224 | tf_op jit(solution)/shard_map/ppermute | solution.py:249
  87.6 10.0 %collective-permute-start.8 = (bf16[32,1408]{1,0:T(8,128)(2,1)S(1)}, bf16[32,1408]{1,0:T(8,128)(2,1)S(1)}, u32[]{:S(2)}, u32[]{:S(2)}) collective-permute-start(bf16[32,1408]{1,0:T(8,128)(2,1)S(1)} %get-tuple-element.53), channel_id=1, source_target_pairs={{0,2},{1,3},{2,0},{3,1},{4,6},{5,7},{6,4},{7,5},{8,10},{9,11},{10,... | collective-permute-start | bytes 270344 | tf_op jit(solution)/shard_map/ppermute | solution.py:249
  87.9 9.4 %collective-permute-start.9 = (bf16[32,1280]{1,0:T(8,128)(2,1)S(1)}, bf16[32,1280]{1,0:T(8,128)(2,1)S(1)}, u32[]{:S(2)}, u32[]{:S(2)}) collective-permute-start(bf16[32,1280]{1,0:T(8,128)(2,1)S(1)} %get-tuple-element.54), channel_id=1, source_target_pairs={{0,1},{1,0},{2,3},{3,2},{4,5},{5,4},{6,7},{7,6},{8,9},{9,8},{10,11... | collective-permute-start | bytes 245768 | tf_op jit(solution)/shard_map/ppermute | solution.py:249
  95.1 6.0 %collective-permute-start.15 = (bf16[32,1024]{1,0:T(8,128)(2,1)S(1)}, bf16[32,1024]{1,0:T(8,128)(2,1)S(1)}, u32[]{:S(2)}, u32[]{:S(2)}) collective-permute-start(bf16[32,1024]{1,0:T(8,128)(2,1)S(1)} %get-tuple-element.64), channel_id=1, source_target_pairs={{0,2},{1,3},{2,0},{3,1},{4,6},{5,7},{6,4},{7,5},{8,10},{9,11},{10,... | collective-permute-start | bytes 196616 | tf_op jit(solution)/shard_map/ppermute | solution.py:249
  95.2 5.9 %collective-permute-start.16 = (bf16[32,1024]{1,0:T(8,128)(2,1)S(1)}, bf16[32,1024]{1,0:T(8,128)(2,1)S(1)}, u32[]{:S(2)}, u32[]{:S(2)}) collective-permute-start(bf16[32,1024]{1,0:T(8,128)(2,1)S(1)} %get-tuple-element.65), channel_id=1, source_target_pairs={{0,1},{1,0},{2,3},{3,2},{4,5},{5,4},{6,7},{7,6},{8,9},{9,8},{10,11... | collective-permute-start | bytes 196616 | tf_op jit(solution)/shard_map/ppermute | solution.py:249
  97.8 7.2 %collective-permute-start.11 = (bf16[32,1280]{1,0:T(8,128)(2,1)S(1)}, bf16[32,1280]{1,0:T(8,128)(2,1)S(1)}, u32[]{:S(2)}, u32[]{:S(2)}) collective-permute-start(bf16[32,1280]{1,0:T(8,128)(2,1)S(1)} %get-tuple-element.55.refs_0_), channel_id=1, source_target_pairs={{0,2},{1,3},{2,0},{3,1},{4,6},{5,7},{6,4},{7,5},{8,10},{9,11},{10,... | collective-permute-start | bytes 245768 | tf_op jit(solution)/shard_map/ppermute | solution.py:249
  101.7 5.9 %collective-permute-start.18 = (bf16[32,1024]{1,0:T(8,128)(2,1)S(1)}, bf16[32,1024]{1,0:T(8,128)(2,1)S(1)}, u32[]{:S(2)}, u32[]{:S(2)}) collective-permute-start(bf16[32,1024]{1,0:T(8,128)(2,1)S(1)} %get-tuple-element.66.refs_4_), channel_id=1, source_target_pairs={{0,2},{1,3},{2,0},{3,1},{4,6},{5,7},{6,4},{7,5},{8,10},{9,11},{10,... | collective-permute-start | bytes 196616 | tf_op jit(solution)/shard_map/ppermute | solution.py:249
  103.0 7.4 %collective-permute-start.10 = (bf16[32,1280]{1,0:T(8,128)(2,1)S(1)}, bf16[32,1280]{1,0:T(8,128)(2,1)S(1)}, u32[]{:S(2)}, u32[]{:S(2)}) collective-permute-start(bf16[32,1280]{1,0:T(8,128)(2,1)S(1)} %get-tuple-element.55.refs_0_), channel_id=1, source_target_pairs={{0,1},{1,0},{2,3},{3,2},{4,5},{5,4},{6,7},{7,6},{8,9},{9,8},{10,11... | collective-permute-start | bytes 245768 | tf_op jit(solution)/shard_map/ppermute | solution.py:249
  105.1 6.8 %collective-permute-start.12 = (bf16[32,1280]{1,0:T(8,128)(2,1)S(1)}, bf16[32,1280]{1,0:T(8,128)(2,1)S(1)}, u32[]{:S(2)}, u32[]{:S(2)}) collective-permute-start(bf16[32,1280]{1,0:T(8,128)(2,1)S(1)} %collective-permute-done.11.refs_2_), channel_id=1, source_target_pairs={{0,1},{1,0},{2,3},{3,2},{4,5},{5,4},{6,7},{7,6},{8,9},{9,8},{10,11... | collective-permute-start | bytes 245768 | tf_op jit(solution)/shard_map/ppermute | solution.py:249
  105.1 5.3 %collective-permute-start.17 = (bf16[32,1024]{1,0:T(8,128)(2,1)S(1)}, bf16[32,1024]{1,0:T(8,128)(2,1)S(1)}, u32[]{:S(2)}, u32[]{:S(2)}) collective-permute-start(bf16[32,1024]{1,0:T(8,128)(2,1)S(1)} %get-tuple-element.66.refs_4_), channel_id=1, source_target_pairs={{0,1},{1,0},{2,3},{3,2},{4,5},{5,4},{6,7},{7,6},{8,9},{9,8},{10,11... | collective-permute-start | bytes 196616 | tf_op jit(solution)/shard_map/ppermute | solution.py:249
  107.6 4.3 %collective-permute-start.19 = (bf16[32,1024]{1,0:T(8,128)(2,1)S(1)}, bf16[32,1024]{1,0:T(8,128)(2,1)S(1)}, u32[]{:S(2)}, u32[]{:S(2)}) collective-permute-start(bf16[32,1024]{1,0:T(8,128)(2,1)S(1)} %collective-permute-done.18.refs_6_), channel_id=1, source_target_pairs={{0,1},{1,0},{2,3},{3,2},{4,5},{5,4},{6,7},{7,6},{8,9},{9,8},{10,11... | collective-permute-start | bytes 196616 | tf_op jit(solution)/shard_map/ppermute | solution.py:249
  (6 other events, 206.0 us)

commit v11 on v10

--- a/solution.py
+++ b/solution.py
@@ -102,14 +102,14 @@
             part = part + weight[:, at : at + 128]
         mass[r] = mass[r] * keep + part
         best[r] = new
-        weights[...] = weight.astype(weights.dtype)
+        weights[...] = weight.T.astype(weights.dtype)
         keeps[...] = keep.T[:8, :]
 
     def gather(r, i, weights, keeps):
         values = lax.dot_general(
             held[i, :C, :],
             weights[...],
-            (((1,), (1,)), ((), ())),
+            (((1,), (0,)), ((), ())),
             preferred_element_type=jnp.float32,
         )
         acc[r] = acc[r] * keeps[:1, :] + values
@@ -173,8 +173,8 @@
             pltpu.VMEM((tiles, width, tile), jnp.bfloat16),
             pltpu.VMEM((heads, tile), jnp.float32),
             pltpu.VMEM((heads, tile), jnp.float32),
-            pltpu.VMEM((heads, tile), jnp.bfloat16),
-            pltpu.VMEM((heads, tile), jnp.bfloat16),
+            pltpu.VMEM((tile, heads), jnp.bfloat16),
+            pltpu.VMEM((tile, heads), jnp.bfloat16),
             pltpu.VMEM((8, heads), jnp.float32),
             pltpu.VMEM((8, heads), jnp.float32),
             pltpu.VMEM((nreq, C, heads), jnp.float32),
@@ -253,23 +253,41 @@
     return [piece] + [from_distance(piece, axis, k) for k in range(1, lax.axis_size(axis))]
 
 
+def own_output_kernel(value_ref, w_ref, out_ref):
+    depth = value_ref.shape[1]
+    rows = pl.ds(pl.multiple_of(lax.axis_index("tp") * depth, 128), depth)
+    out_ref[...] = jnp.dot(value_ref[...], w_ref[rows, :], preferred_element_type=jnp.float32)
+
+
 def output_kernel(*refs):
-    *values, w_ref, out_ref, total = refs
+    own_ref, *values, w_ref, out_ref, total = refs
     depth = values[0].shape[1]
     me = lax.axis_index("tp")
-    for k, value in enumerate(values):
+    for k, value in enumerate(values, 1):
         rows = pl.ds(pl.multiple_of((me ^ k) * depth, 128), depth)
         term = jnp.dot(value[...], w_ref[rows, :], preferred_element_type=jnp.float32)
-        if k == 0:
-            total[...] = term
+        if k == 1:
+            total[...] = own_ref[...] + term
         else:
             total[...] += term
     out_ref[...] = total[...].astype(out_ref.dtype)
 
 
 def project_out(values, w_o):
-    requests = values[0].shape[0]
+    requests, depth = values[0].shape
     width = w_o.shape[1]
+    w_o = fetched(w_o)
+    own = pl.pallas_call(
+        own_output_kernel,
+        out_shape=jax.ShapeDtypeStruct((requests, width), jnp.float32),
+        in_specs=in_vmem(2),
+        out_specs=pl.BlockSpec(memory_space=pltpu.VMEM),
+        compiler_params=kernel_params(12),
+        cost_estimate=pl.CostEstimate(
+            flops=2 * requests * depth * width, bytes_accessed=2 * depth * width, transcendentals=0
+        ),
+        name="project_own",
+    )(values[0], w_o)
     return pl.pallas_call(
         output_kernel,
         out_shape=jax.ShapeDtypeStruct((requests, width), jnp.bfloat16),
@@ -278,7 +296,7 @@
         scratch_shapes=[pltpu.VMEM((requests, width), jnp.float32)],
         compiler_params=kernel_params(12),
         name="project_out",
-    )(*values, fetched(w_o))
+    )(own, *values[1:], w_o)
 
 
 def hidden_kernel(parts_ref, *refs):
@@ -372,7 +390,7 @@
 def gate_up(hidden, gain, w_gate, w_up, halves):
     requests, width = hidden.shape
     units = w_gate.shape[1]
-    first = units if halves == 1 else round_up(units // 2, 256)
+    first = units if halves == 1 else round_up(units * 5 // 8, 256)
     w_gate, w_up = fetched(w_gate), fetched(w_up)
 
     def shapes(columns, extra):

time: 133 us -> 143 us (1.075); the launches traced: 130 us -> 142 us
  waiting for transfers between devices: 24.2 us -> 32 us
  Pallas kernels: 15.4 us -> 18 us
  blocking collectives: 59.8 us -> 62 us
    ppermute x20, waiting for transfers between devices: 24.2 us -> 32 us  [from_distance(): lax.ppermute(piece, axis, [(k, k ^ distance) for k in range(lax.axis_size...]
    pallas_call x1, Pallas kernels: 7.86 us -> 10.3 us  [attend(): pl.pallas_call(attention_kernel, out_shape=jax.ShapeDtypeStruct((ranks, n...]
    all_to_all x3, blocking collectives: 51 us -> 53.2 us  [swap(): return lax.all_to_all(parts, axes, split_axis=0, concat_axis=0, tiled=True)]
    unnamed x20 -> x24, local copies, waits for them, and re-layouts: 3.14 us -> 1.13 us
  transfers between devices with their start and end apart: 20 -> 20, of which waited for: 11 -> 12; matrix products, arithmetic and copies ran while one was open for 0% -> 0% of each run, Pallas kernels for 2% -> 2%
where the time goes in v11:
time: 143 us; the launch traced here: 142 us
  blocking collectives  62 us (43%)
  waiting for transfers between devices  32 us (22%)
  starting transfers between devices  26 us (18%)
  Pallas kernels  18 us (13%)
  local copies, waits for them, and re-layouts  3.86 us (3%)
    all_to_all x3, blocking collectives, swap(): return lax.all_to_all(parts, axes, split_axis=0, concat_axis=0, tiled=True)  53.2 us
    ppermute x20, waiting for transfers between devices, from_distance(): lax.ppermute(piece, axis, [(k, k ^ distance) for k in range(lax.axis_size...  32 us
    ppermute x20, starting transfers between devices, from_distance(): lax.ppermute(piece, axis, [(k, k ^ distance) for k in range(lax.axis_size...  26 us
    pallas_call x1, Pallas kernels, attend(): pl.pallas_call(attention_kernel, out_shape=jax.ShapeDtypeStruct((ranks, n...  10.3 us
    all_gather x1, blocking collectives, local(): hidden = lax.all_gather(own_hidden, 'dp', axis=0, tiled=True)  8.78 us
  transfers between devices with their start and end apart: 20, of which 12 were waited for; matrix products, arithmetic and copies ran while one was open for 0% of the time, Pallas kernels for 2%

profile of v11, /device:TPU:0, one launch (start us, length us, event | category | flops | bytes accessed | tf_op | source)
XLA Modules:
  0.0 142.0 jit_solution(4037491002001064070)
XLA Ops:
  0.0 2.7 %reshape.12.q_ref = bf16[4,128,576]{2,1,0:T(8,128)(2,1)} reshape(bf16[4,73728]{1,0:T(4,128)(2,1)} %param.11) | data formatting | bytes 1179648 | tf_op jit(solution)/shard_map/reshape | solution.py:600
  3.8 10.3 %attention.1 = bf16[32,16,512]{2,1,0:T(8,128)(2,1)S(1)} custom-call(s32[128]{0:T(128)} %lens_ref.1, bf16[4,128,576]{2,1,0:T(8,128)(2,1)S(1)} %copy-done, bf16[576,14336]{1,0:T(8,128)(2,1)} %bitcast.31), custom_call_target="tpu_custom_call" | custom-call | flops 3992977408 | bytes 16515072 | tf_op jit(solution)/shard_map/attention/pallas_call | solution.py:165
  14.1 25.3 %all_to_all.15 = bf16[32,16,512]{2,1,0:T(8,128)(2,1)S(1)} all-to-all(bf16[32,16,512]{2,1,0:T(8,128)(2,1)S(1)} %attention.1), channel_id=1, replica_groups=mesh['dp'=8,'tp'=4] {'dp','tp'}, dimensions={0} | all-to-all | bytes 1048576 | tf_op jit(solution)/shard_map/all_to_all | solution.py:582
  40.3 2.6 %collective-permute-start = (bf16[128,512]{1,0:T(8,128)(2,1)S(1)}, bf16[128,512]{1,0:T(8,128)(2,1)S(1)}, u32[]{:S(2)}, u32[]{:S(2)}) collective-permute-start(bf16[128,512]{1,0:T(8,128)(2,1)S(1)} %head_values.1.value_ref), channel_id=1, source_target_pairs={{0,1},{1,0},{2,3},{3,2},{4,5},{5,4},{6,7},{7,6},{8,9},{9,8},{10,11... | collective-permute-start | bytes 393224 | tf_op jit(solution)/shard_map/ppermute | solution.py:249
  43.7 1.6 %collective-permute-start.2 = (bf16[128,512]{1,0:T(8,128)(2,1)S(1)}, bf16[128,512]{1,0:T(8,128)(2,1)S(1)}, u32[]{:S(2)}, u32[]{:S(2)}) collective-permute-start(bf16[128,512]{1,0:T(8,128)(2,1)S(1)} %head_values.1.value_ref), channel_id=1, source_target_pairs={{0,3},{1,2},{2,1},{3,0},{4,7},{5,6},{6,5},{7,4},{8,11},{9,10},{10,... | collective-permute-start | bytes 393224 | tf_op jit(solution)/shard_map/ppermute | solution.py:249
  46.4 1.7 %collective-permute-start.4 = (bf16[4,1792]{1,0:T(4,128)(2,1)S(1)}, bf16[4,1792]{1,0:T(4,128)(2,1)S(1)}, u32[]{:S(2)}, u32[]{:S(2)}) collective-permute-start(bf16[4,1792]{1,0:T(4,128)(2,1)S(1)} %get-tuple-element.40), channel_id=1, source_target_pairs={{0,2},{1,3},{2,0},{3,1},{4,6},{5,7},{6,4},{7,5},{8,10},{9,11},{10,... | collective-permute-start | bytes 43016 | tf_op jit(solution)/shard_map/ppermute | solution.py:249
  50.2 5.7 %collective-permute-done.1.refs_2_ = bf16[128,512]{1,0:T(8,128)(2,1)S(1)} collective-permute-done((bf16[128,512]{1,0:T(8,128)(2,1)S(1)}, bf16[128,512]{1,0:T(8,128)(2,1)S(1)}, u32[]{:S(2)}, u32[]{:S(2)}) %collective-permute-start.1) | collective-permute-done | bytes 131104 | tf_op jit(solution)/shard_map/ppermute | solution.py:249
  57.4 11.9 %all_to_all.16.parts_ref = bf16[8,16,1792]{2,1,0:T(8,128)(2,1)S(1)} all-to-all(bf16[8,16,1792]{2,1,0:T(8,128)(2,1)S(1)} %bitcast.21), channel_id=1, replica_groups=mesh['dp'=8,'tp'=4] {'dp'}, dimensions={0} | all-to-all | bytes 917504 | tf_op jit(solution)/shard_map/all_to_all | solution.py:582
  69.4 8.8 %all_gather.3.hidden_ref = bf16[128,1792]{1,0:T(8,128)(2,1)S(1)} all-gather(bf16[16,1792]{1,0:T(8,128)(2,1)S(1)} %hidden.1.refs_9_), channel_id=1, replica_groups=mesh['dp'=8,'tp'=4] {'dp'}, dimensions={0}, use_global_device_ids=true | all-gather | bytes 516096 | tf_op jit(solution)/shard_map/all_gather | solution.py:611
  78.2 1.6 %gate_up.1 = (bf16[2,128,1792]{2,1,0:T(8,128)(2,1)S(1)}, bf16[64,1664]{1,0:T(8,128)(2,1)S(1)}, bf16[64,1536]{1,0:T(8,128)(2,1)S(1)}, bf16[64,1664]{1,0:T(8,128)(2,1)S(1)}, bf16[64,1536]{1,0:T(8,128)(2,1)S(1)}) custom-call(bf16[128,1792]{1,0:T(8,128)(2,1)S(1)} %all_gather.3.hidden_ref, bf16[56,128]{1,0:T(8,128)(2,1)S(1)} %bitcast.30, ...), custom_call_target="tpu_custom_call" | custom-call | flops 1409286144 | bytes 11010048 | tf_op jit(solution)/shard_map/gate_up/pallas_call | solution.py:404
  79.9 1.4 collective-permute-start.6
  82.3 11.0 %collective-permute-done.7.refs_3_ = bf16[64,1536]{1,0:T(8,128)(2,1)S(1)} collective-permute-done((bf16[64,1536]{1,0:T(8,128)(2,1)S(1)}, bf16[64,1536]{1,0:T(8,128)(2,1)S(1)}, u32[]{:S(2)}, u32[]{:S(2)}) %collective-permute-start.7) | collective-permute-done | bytes 196640 | tf_op jit(solution)/shard_map/ppermute | solution.py:249
  94.2 1.6 %collective-permute-start.9 = (bf16[32,1536]{1,0:T(8,128)(2,1)S(1)}, bf16[32,1536]{1,0:T(8,128)(2,1)S(1)}, u32[]{:S(2)}, u32[]{:S(2)}) collective-permute-start(bf16[32,1536]{1,0:T(8,128)(2,1)S(1)} %get-tuple-element.54), channel_id=1, source_target_pairs={{0,1},{1,0},{2,3},{3,2},{4,5},{5,4},{6,7},{7,6},{8,9},{9,8},{10,11... | collective-permute-start | bytes 294920 | tf_op jit(solution)/shard_map/ppermute | solution.py:249
  97.2 2.2 %collective-permute-start.14 = (bf16[64,768]{1,0:T(8,128)(2,1)S(1)}, bf16[64,768]{1,0:T(8,128)(2,1)S(1)}, u32[]{:S(2)}, u32[]{:S(2)}) collective-permute-start(bf16[64,768]{1,0:T(8,128)(2,1)S(1)} %get-tuple-element.61), channel_id=1, source_target_pairs={{0,2},{1,3},{2,0},{3,1},{4,6},{5,7},{6,4},{7,5},{8,10},{9,11},{10,... | collective-permute-start | bytes 294920 | tf_op jit(solution)/shard_map/ppermute | solution.py:249
  99.4 2.0 %collective-permute-done.9 = bf16[32,1536]{1,0:T(8,128)(2,1)S(1)} collective-permute-done((bf16[32,1536]{1,0:T(8,128)(2,1)S(1)}, bf16[32,1536]{1,0:T(8,128)(2,1)S(1)}, u32[]{:S(2)}, u32[]{:S(2)}) %collective-permute-start.9) | collective-permute-done | bytes 98336 | tf_op jit(solution)/shard_map/ppermute | solution.py:249
  103.5 4.6 %collective-permute-done.14.refs_3_ = bf16[64,768]{1,0:T(8,128)(2,1)S(1)} collective-permute-done((bf16[64,768]{1,0:T(8,128)(2,1)S(1)}, bf16[64,768]{1,0:T(8,128)(2,1)S(1)}, u32[]{:S(2)}, u32[]{:S(2)}) %collective-permute-start.14) | collective-permute-done | bytes 98336 | tf_op jit(solution)/shard_map/ppermute | solution.py:249
  108.2 2.6 %collective-permute-start.16 = (bf16[32,768]{1,0:T(8,128)(2,1)S(1)}, bf16[32,768]{1,0:T(8,128)(2,1)S(1)}, u32[]{:S(2)}, u32[]{:S(2)}) collective-permute-start(bf16[32,768]{1,0:T(8,128)(2,1)S(1)} %get-tuple-element.65), channel_id=1, source_target_pairs={{0,1},{1,0},{2,3},{3,2},{4,5},{5,4},{6,7},{7,6},{8,9},{9,8},{10,11... | collective-permute-start | bytes 147464 | tf_op jit(solution)/shard_map/ppermute | solution.py:249
  110.8 3.0 %collective-permute-done.15 = bf16[32,768]{1,0:T(8,128)(2,1)S(1)} collective-permute-done((bf16[32,768]{1,0:T(8,128)(2,1)S(1)}, bf16[32,768]{1,0:T(8,128)(2,1)S(1)}, u32[]{:S(2)}, u32[]{:S(2)}) %collective-permute-start.15) | collective-permute-done | bytes 49184 | tf_op jit(solution)/shard_map/ppermute | solution.py:249
  114.8 1.5 %collective-permute-start.18 = (bf16[32,768]{1,0:T(8,128)(2,1)S(1)}, bf16[32,768]{1,0:T(8,128)(2,1)S(1)}, u32[]{:S(2)}, u32[]{:S(2)}) collective-permute-start(bf16[32,768]{1,0:T(8,128)(2,1)S(1)} %get-tuple-element.66.refs_4_), channel_id=1, source_target_pairs={{0,2},{1,3},{2,0},{3,1},{4,6},{5,7},{6,4},{7,5},{8,10},{9,11},{10,... | collective-permute-start | bytes 147464 | tf_op jit(solution)/shard_map/ppermute | solution.py:249
  119.8 1.2 collective-permute-start.19
  121.0 1.4 %collective-permute-done.17.refs_5_ = bf16[32,768]{1,0:T(8,128)(2,1)S(1)} collective-permute-done((bf16[32,768]{1,0:T(8,128)(2,1)S(1)}, bf16[32,768]{1,0:T(8,128)(2,1)S(1)}, u32[]{:S(2)}, u32[]{:S(2)}) %collective-permute-start.17) | collective-permute-done | bytes 49184 | tf_op jit(solution)/shard_map/ppermute | solution.py:249
  122.5 1.4 %collective-permute-done.19.refs_7_ = bf16[32,768]{1,0:T(8,128)(2,1)S(1)} collective-permute-done((bf16[32,768]{1,0:T(8,128)(2,1)S(1)}, bf16[32,768]{1,0:T(8,128)(2,1)S(1)}, u32[]{:S(2)}, u32[]{:S(2)}) %collective-permute-start.19) | collective-permute-done | bytes 49184 | tf_op jit(solution)/shard_map/ppermute | solution.py:249
  123.9 1.4 project_down.1
  125.3 15.9 %all_to_all.17.parts_ref = bf16[32,56,128]{2,1,0:T(8,128)(2,1)S(1)} all-to-all(bf16[32,56,128]{2,1,0:T(8,128)(2,1)S(1)} %project_down.1), channel_id=1, replica_groups=mesh['dp'=8,'tp'=4] {'dp','tp'}, dimensions={0} | all-to-all | bytes 917504 | tf_op jit(solution)/shard_map/all_to_all | solution.py:582
  (63 shorter events, 18.2 us)
Async XLA Ops:
  0.0 49.8 %slice-start.4 = ((s8[7340032]{0:T(1024)(128)(4,1)}), s8[3145728]{0:T(1024)(128)(4,1)S(1)}, s32[]{:S(2)}) async-start(s8[7340032]{0:T(1024)(128)(4,1)} %bitcast.16), calls=%async_computation.7 | async-start | bytes 6291456
  3.8 41.5 %copy-start.2 = (bf16[4,7168]{1,0:T(4,128)(2,1)S(1)}, bf16[4,7168]{1,0:T(4,128)(2,1)}, u32[]{:S(2)}) copy-start(bf16[4,7168]{1,0:T(4,128)(2,1)} %rows_ref) | copy-start | bytes 172036
  3.8 46.0 %slice-start.5 = ((s8[7340032]{0:T(1024)(128)(4,1)}), s8[4194304]{0:T(1024)(128)(4,1)S(1)}, s32[]{:S(2)}) async-start(s8[7340032]{0:T(1024)(128)(4,1)} %bitcast.16), calls=%async_computation.8 | async-start | bytes 8388608
  3.8 74.4 %slice-start.2 = ((s8[8257536]{0:T(1024)(128)(4,1)}), s8[4194304]{0:T(1024)(128)(4,1)S(1)}, s32[]{:S(2)}) async-start(s8[8257536]{0:T(1024)(128)(4,1)} %bitcast.14), calls=%async_computation.5 | async-start | bytes 8388608
  40.3 8.3 %collective-permute-start = (bf16[128,512]{1,0:T(8,128)(2,1)S(1)}, bf16[128,512]{1,0:T(8,128)(2,1)S(1)}, u32[]{:S(2)}, u32[]{:S(2)}) collective-permute-start(bf16[128,512]{1,0:T(8,128)(2,1)S(1)} %head_values.1.value_ref), channel_id=1, source_target_pairs={{0,1},{1,0},{2,3},{3,2},{4,5},{5,4},{6,7},{7,6},{8,9},{9,8},{10,11... | collective-permute-start | bytes 393224 | tf_op jit(solution)/shard_map/ppermute | solution.py:249
  42.9 13.0 %collective-permute-start.1 = (bf16[128,512]{1,0:T(8,128)(2,1)S(1)}, bf16[128,512]{1,0:T(8,128)(2,1)S(1)}, u32[]{:S(2)}, u32[]{:S(2)}) collective-permute-start(bf16[128,512]{1,0:T(8,128)(2,1)S(1)} %head_values.1.value_ref), channel_id=1, source_target_pairs={{0,2},{1,3},{2,0},{3,1},{4,6},{5,7},{6,4},{7,5},{8,10},{9,11},{10,... | collective-permute-start | bytes 393224 | tf_op jit(solution)/shard_map/ppermute | solution.py:249
  43.7 12.2 %collective-permute-start.2 = (bf16[128,512]{1,0:T(8,128)(2,1)S(1)}, bf16[128,512]{1,0:T(8,128)(2,1)S(1)}, u32[]{:S(2)}, u32[]{:S(2)}) collective-permute-start(bf16[128,512]{1,0:T(8,128)(2,1)S(1)} %head_values.1.value_ref), channel_id=1, source_target_pairs={{0,3},{1,2},{2,1},{3,0},{4,7},{5,6},{6,5},{7,4},{8,11},{9,10},{10,... | collective-permute-start | bytes 393224 | tf_op jit(solution)/shard_map/ppermute | solution.py:249
  45.3 11.5 %collective-permute-start.3 = (bf16[4,1792]{1,0:T(4,128)(2,1)S(1)}, bf16[4,1792]{1,0:T(4,128)(2,1)S(1)}, u32[]{:S(2)}, u32[]{:S(2)}) collective-permute-start(bf16[4,1792]{1,0:T(4,128)(2,1)S(1)} %get-tuple-element.39), channel_id=1, source_target_pairs={{0,1},{1,0},{2,3},{3,2},{4,5},{5,4},{6,7},{7,6},{8,9},{9,8},{10,11... | collective-permute-start | bytes 43016 | tf_op jit(solution)/shard_map/ppermute | solution.py:249
  46.4 11.0 %collective-permute-start.4 = (bf16[4,1792]{1,0:T(4,128)(2,1)S(1)}, bf16[4,1792]{1,0:T(4,128)(2,1)S(1)}, u32[]{:S(2)}, u32[]{:S(2)}) collective-permute-start(bf16[4,1792]{1,0:T(4,128)(2,1)S(1)} %get-tuple-element.40), channel_id=1, source_target_pairs={{0,2},{1,3},{2,0},{3,1},{4,6},{5,7},{6,4},{7,5},{8,10},{9,11},{10,... | collective-permute-start | bytes 43016 | tf_op jit(solution)/shard_map/ppermute | solution.py:249
  48.6 8.8 %collective-permute-start.5 = (bf16[4,1792]{1,0:T(4,128)(2,1)S(1)}, bf16[4,1792]{1,0:T(4,128)(2,1)S(1)}, u32[]{:S(2)}, u32[]{:S(2)}) collective-permute-start(bf16[4,1792]{1,0:T(4,128)(2,1)S(1)} %get-tuple-element.41), channel_id=1, source_target_pairs={{0,3},{1,2},{2,1},{3,0},{4,7},{5,6},{6,5},{7,4},{8,11},{9,10},{10,... | collective-permute-start | bytes 43016 | tf_op jit(solution)/shard_map/ppermute | solution.py:249
  79.9 13.5 %collective-permute-start.6 = (bf16[64,1664]{1,0:T(8,128)(2,1)S(1)}, bf16[64,1664]{1,0:T(8,128)(2,1)S(1)}, u32[]{:S(2)}, u32[]{:S(2)}) collective-permute-start(bf16[64,1664]{1,0:T(8,128)(2,1)S(1)} %get-tuple-element.49), channel_id=1, source_target_pairs={{0,1},{1,0},{2,3},{3,2},{4,5},{5,4},{6,7},{7,6},{8,9},{9,8},{10,11... | collective-permute-start | bytes 638984 | tf_op jit(solution)/shard_map/ppermute | solution.py:249
  81.3 12.0 %collective-permute-start.7 = (bf16[64,1536]{1,0:T(8,128)(2,1)S(1)}, bf16[64,1536]{1,0:T(8,128)(2,1)S(1)}, u32[]{:S(2)}, u32[]{:S(2)}) collective-permute-start(bf16[64,1536]{1,0:T(8,128)(2,1)S(1)} %get-tuple-element.50), channel_id=1, source_target_pairs={{0,2},{1,3},{2,0},{3,1},{4,6},{5,7},{6,4},{7,5},{8,10},{9,11},{10,... | collective-permute-start | bytes 589832 | tf_op jit(solution)/shard_map/ppermute | solution.py:249
  93.4 7.9 %collective-permute-start.8 = (bf16[32,1664]{1,0:T(8,128)(2,1)S(1)}, bf16[32,1664]{1,0:T(8,128)(2,1)S(1)}, u32[]{:S(2)}, u32[]{:S(2)}) collective-permute-start(bf16[32,1664]{1,0:T(8,128)(2,1)S(1)} %get-tuple-element.53), channel_id=1, source_target_pairs={{0,2},{1,3},{2,0},{3,1},{4,6},{5,7},{6,4},{7,5},{8,10},{9,11},{10,... | collective-permute-start | bytes 319496 | tf_op jit(solution)/shard_map/ppermute | solution.py:249
  94.2 7.2 %collective-permute-start.9 = (bf16[32,1536]{1,0:T(8,128)(2,1)S(1)}, bf16[32,1536]{1,0:T(8,128)(2,1)S(1)}, u32[]{:S(2)}, u32[]{:S(2)}) collective-permute-start(bf16[32,1536]{1,0:T(8,128)(2,1)S(1)} %get-tuple-element.54), channel_id=1, source_target_pairs={{0,1},{1,0},{2,3},{3,2},{4,5},{5,4},{6,7},{7,6},{8,9},{9,8},{10,11... | collective-permute-start | bytes 294920 | tf_op jit(solution)/shard_map/ppermute | solution.py:249
  96.7 6.8 %collective-permute-start.13 = (bf16[64,768]{1,0:T(8,128)(2,1)S(1)}, bf16[64,768]{1,0:T(8,128)(2,1)S(1)}, u32[]{:S(2)}, u32[]{:S(2)}) collective-permute-start(bf16[64,768]{1,0:T(8,128)(2,1)S(1)} %get-tuple-element.60), channel_id=1, source_target_pairs={{0,1},{1,0},{2,3},{3,2},{4,5},{5,4},{6,7},{7,6},{8,9},{9,8},{10,11... | collective-permute-start | bytes 294920 | tf_op jit(solution)/shard_map/ppermute | solution.py:249
  97.2 10.9 %collective-permute-start.14 = (bf16[64,768]{1,0:T(8,128)(2,1)S(1)}, bf16[64,768]{1,0:T(8,128)(2,1)S(1)}, u32[]{:S(2)}, u32[]{:S(2)}) collective-permute-start(bf16[64,768]{1,0:T(8,128)(2,1)S(1)} %get-tuple-element.61), channel_id=1, source_target_pairs={{0,2},{1,3},{2,0},{3,1},{4,6},{5,7},{6,4},{7,5},{8,10},{9,11},{10,... | collective-permute-start | bytes 294920 | tf_op jit(solution)/shard_map/ppermute | solution.py:249
  101.5 15.6 %collective-permute-start.11 = (bf16[32,1536]{1,0:T(8,128)(2,1)S(1)}, bf16[32,1536]{1,0:T(8,128)(2,1)S(1)}, u32[]{:S(2)}, u32[]{:S(2)}) collective-permute-start(bf16[32,1536]{1,0:T(8,128)(2,1)S(1)} %get-tuple-element.55.refs_0_), channel_id=1, source_target_pairs={{0,2},{1,3},{2,0},{3,1},{4,6},{5,7},{6,4},{7,5},{8,10},{9,11},{10,... | collective-permute-start | bytes 294920 | tf_op jit(solution)/shard_map/ppermute | solution.py:249
  108.1 5.6 %collective-permute-start.15 = (bf16[32,768]{1,0:T(8,128)(2,1)S(1)}, bf16[32,768]{1,0:T(8,128)(2,1)S(1)}, u32[]{:S(2)}, u32[]{:S(2)}) collective-permute-start(bf16[32,768]{1,0:T(8,128)(2,1)S(1)} %get-tuple-element.64), channel_id=1, source_target_pairs={{0,2},{1,3},{2,0},{3,1},{4,6},{5,7},{6,4},{7,5},{8,10},{9,11},{10,... | collective-permute-start | bytes 147464 | tf_op jit(solution)/shard_map/ppermute | solution.py:249
  108.2 6.0 %collective-permute-start.16 = (bf16[32,768]{1,0:T(8,128)(2,1)S(1)}, bf16[32,768]{1,0:T(8,128)(2,1)S(1)}, u32[]{:S(2)}, u32[]{:S(2)}) collective-permute-start(bf16[32,768]{1,0:T(8,128)(2,1)S(1)} %get-tuple-element.65), channel_id=1, source_target_pairs={{0,1},{1,0},{2,3},{3,2},{4,5},{5,4},{6,7},{7,6},{8,9},{9,8},{10,11... | collective-permute-start | bytes 147464 | tf_op jit(solution)/shard_map/ppermute | solution.py:249
  114.8 5.0 %collective-permute-start.18 = (bf16[32,768]{1,0:T(8,128)(2,1)S(1)}, bf16[32,768]{1,0:T(8,128)(2,1)S(1)}, u32[]{:S(2)}, u32[]{:S(2)}) collective-permute-start(bf16[32,768]{1,0:T(8,128)(2,1)S(1)} %get-tuple-element.66.refs_4_), channel_id=1, source_target_pairs={{0,2},{1,3},{2,0},{3,1},{4,6},{5,7},{6,4},{7,5},{8,10},{9,11},{10,... | collective-permute-start | bytes 147464 | tf_op jit(solution)/shard_map/ppermute | solution.py:249
  116.3 7.6 %collective-permute-start.10 = (bf16[32,1536]{1,0:T(8,128)(2,1)S(1)}, bf16[32,1536]{1,0:T(8,128)(2,1)S(1)}, u32[]{:S(2)}, u32[]{:S(2)}) collective-permute-start(bf16[32,1536]{1,0:T(8,128)(2,1)S(1)} %get-tuple-element.55.refs_0_), channel_id=1, source_target_pairs={{0,1},{1,0},{2,3},{3,2},{4,5},{5,4},{6,7},{7,6},{8,9},{9,8},{10,11... | collective-permute-start | bytes 294920 | tf_op jit(solution)/shard_map/ppermute | solution.py:249
  117.1 6.8 %collective-permute-start.12 = (bf16[32,1536]{1,0:T(8,128)(2,1)S(1)}, bf16[32,1536]{1,0:T(8,128)(2,1)S(1)}, u32[]{:S(2)}, u32[]{:S(2)}) collective-permute-start(bf16[32,1536]{1,0:T(8,128)(2,1)S(1)} %collective-permute-done.11.refs_2_), channel_id=1, source_target_pairs={{0,1},{1,0},{2,3},{3,2},{4,5},{5,4},{6,7},{7,6},{8,9},{9,8},{10,11... | collective-permute-start | bytes 294920 | tf_op jit(solution)/shard_map/ppermute | solution.py:249
  118.3 4.2 %collective-permute-start.17 = (bf16[32,768]{1,0:T(8,128)(2,1)S(1)}, bf16[32,768]{1,0:T(8,128)(2,1)S(1)}, u32[]{:S(2)}, u32[]{:S(2)}) collective-permute-start(bf16[32,768]{1,0:T(8,128)(2,1)S(1)} %get-tuple-element.66.refs_4_), channel_id=1, source_target_pairs={{0,1},{1,0},{2,3},{3,2},{4,5},{5,4},{6,7},{7,6},{8,9},{9,8},{10,11... | collective-permute-start | bytes 147464 | tf_op jit(solution)/shard_map/ppermute | solution.py:249
  119.8 4.1 %collective-permute-start.19 = (bf16[32,768]{1,0:T(8,128)(2,1)S(1)}, bf16[32,768]{1,0:T(8,128)(2,1)S(1)}, u32[]{:S(2)}, u32[]{:S(2)}) collective-permute-start(bf16[32,768]{1,0:T(8,128)(2,1)S(1)} %collective-permute-done.18.refs_6_), channel_id=1, source_target_pairs={{0,1},{1,0},{2,3},{3,2},{4,5},{5,4},{6,7},{7,6},{8,9},{9,8},{10,11... | collective-permute-start | bytes 147464 | tf_op jit(solution)/shard_map/ppermute | solution.py:249
  (8 other events, 221.4 us)

commit v12 on v11

--- a/solution.py
+++ b/solution.py
@@ -9,7 +9,7 @@
 
 C = 512
 BLOCK_TOKENS = 64
-TILE = 1024
+TILE = 512
 
 score_scale = 192.0 ** (-0.5)
 log2_e = 1.4426950408889634
@@ -18,9 +18,12 @@
 
 def attention_kernel(
     lens_ref,
-    q_ref,
+    raw_ref,
     cache_ref,
     out_ref,
+    q_ref,
+    pairs_of_heads,
+    rows_of_heads,
     held,
     score0,
     score1,
@@ -64,6 +67,28 @@
     def _(i):
         copy(i).start()
 
+    width = q_ref.shape[2]
+    half = heads // 2
+    tail = width % 128
+    full = width // 128
+    for j in range(half):
+        for c in range(pairs_of_heads.shape[0]):
+            at = 2 * width * j + 128 * c
+            pairs_of_heads[c, pl.ds(j, nreq, stride=half), :] = raw_ref[:, at : at + 128].astype(
+                jnp.float32
+            )
+    for r in range(nreq):
+        rows = slice(r * half, (r + 1) * half)
+        for c in range(full + 1):
+            rows_of_heads[c, pl.ds(0, half, stride=2), :] = pairs_of_heads[c, rows, :]
+            ahead = min(full + c + 1, pairs_of_heads.shape[0] - 1)
+            rows_of_heads[c, pl.ds(1, half, stride=2), :] = jnp.concatenate(
+                [pairs_of_heads[full + c, rows, tail:], pairs_of_heads[ahead, rows, :tail]], 1
+            )
+        for c in range(full):
+            q_ref[r, :, c * 128 : (c + 1) * 128] = rows_of_heads[c].astype(q_ref.dtype)
+        q_ref[r, :, full * 128 :] = rows_of_heads[full, :, :tail].astype(q_ref.dtype)
+
     acc[...] = jnp.zeros_like(acc)
     best[...] = jnp.full_like(best, negative)
     mass[...] = jnp.zeros_like(mass)
@@ -158,8 +183,9 @@
 
 
 def attend(lengths, queries, cache_t, ranks):
-    nreq, heads, width = queries.shape
-    tokens = cache_t.shape[1]
+    nreq = queries.shape[0]
+    width, tokens = cache_t.shape
+    heads = queries.shape[1] // width
     tile = TILE
     tiles = tokens // tile
     return pl.pallas_call(
@@ -170,6 +196,9 @@
         + [pl.BlockSpec(memory_space=pltpu.HBM)],
         out_specs=pl.BlockSpec(memory_space=pltpu.VMEM),
         scratch_shapes=[
+            pltpu.VMEM((nreq, heads, width), jnp.bfloat16),
+            pltpu.VMEM((2 * width // 128, nreq * heads // 2, 128), jnp.float32),
+            pltpu.VMEM((width // 128 + 1, heads, 128), jnp.float32),
             pltpu.VMEM((tiles, width, tile), jnp.bfloat16),
             pltpu.VMEM((heads, tile), jnp.float32),
             pltpu.VMEM((heads, tile), jnp.float32),
@@ -187,7 +216,7 @@
             pltpu.SMEM((nreq,), jnp.int32),
             pltpu.SemaphoreType.DMA((tiles,)),
         ],
-        compiler_params=kernel_params(26),
+        compiler_params=kernel_params(28),
         cost_estimate=pl.CostEstimate(
             flops=2 * heads * tokens * (width + C),
             bytes_accessed=2 * tokens * width,
@@ -196,7 +225,7 @@
         name="attention",
     )(
         pltpu.with_memory_space_constraint(lengths, pltpu.HBM),
-        fetched(queries),
+        pltpu.with_memory_space_constraint(queries, pltpu.HBM),
         pltpu.with_memory_space_constraint(cache_t, pltpu.HBM),
     )
 
@@ -390,7 +419,7 @@
 def gate_up(hidden, gain, w_gate, w_up, halves):
     requests, width = hidden.shape
     units = w_gate.shape[1]
-    first = units if halves == 1 else round_up(units * 5 // 8, 256)
+    first = units if halves == 1 else round_up(units // 2, 256)
     w_gate, w_up = fetched(w_gate), fetched(w_up)
 
     def shapes(columns, extra):
@@ -590,15 +619,12 @@
     ranks = ranks_dp * ranks_tp
     per_rank, model = residual.shape
     requests = per_rank * ranks
-    row_length = paged_latent_cache.shape[1]
-    heads_all = queries.shape[1] // row_length
     heads_here = w_uv.shape[0]
     units = w_gate.shape[1]
     width = w_o.shape[1]
 
 
-    query = queries.reshape(per_rank, heads_all, row_length)
-    latent = swap(attend(lengths, query, paged_latent_cache.T, ranks), ("dp", "tp"))
+    latent = swap(attend(lengths, queries, paged_latent_cache.T, ranks), ("dp", "tp"))
 
     values = head_values(latent.reshape(requests * heads_here, C), w_uv)
     values, residual = lax.optimization_barrier((values, residual))
@@ -612,6 +638,10 @@
 
     halves = 2 if ranks_tp == 4 else 1
     chunks = gate_up(hidden, norm_gain.reshape(-1, 128), w_gate, w_up, halves)
+    if halves == 2:
+        first, second = chunks
+        kept, second = lax.optimization_barrier((first[2:], second))
+        chunks = [[*first[:2], *kept], second]
     inner = []
     factor = None
     for chunk in chunks:

time: 143 us -> 131 us (0.916)
  local copies, waits for them, and re-layouts: 3.86 us -> 0.04 us
  starting transfers between devices: 26 us -> 22.3 us
  waiting for transfers between devices: 32 us -> 28.5 us
  Pallas kernels: 18 us -> 15 us
  blocking collectives: 62 us -> 63.7 us
    ppermute x20, starting transfers between devices: 26 us -> 22.3 us  [from_distance(): lax.ppermute(piece, axis, [(k, k ^ distance) for k in range(lax.axis_size...]
    ppermute x20, waiting for transfers between devices: 32 us -> 28.5 us  [from_distance(): lax.ppermute(piece, axis, [(k, k ^ distance) for k in range(lax.axis_size...]
    pallas_call x1, Pallas kernels: 10.3 us -> 7.25 us  [attend(): pl.pallas_call(attention_kernel, out_shape=jax.ShapeDtypeStruct((ranks, n...]
    reshape x1 -> x0, local copies, waits for them, and re-layouts: 2.73 us -> none  [local(): query = queries.reshape(per_rank, heads_all, row_length)]
    all_to_all x3, blocking collectives: 53.2 us -> 54.9 us  [swap(): return lax.all_to_all(parts, axes, split_axis=0, concat_axis=0, tiled=True)]
  transfers between devices with their start and end apart: 20 -> 20, of which waited for: 12 -> 12; matrix products, arithmetic and copies ran while one was open for 0% -> 0% of each run, Pallas kernels for 2% -> 3%
where the time goes in v12:
time: 131 us; the launch traced here: 130 us
  blocking collectives  63.7 us (49%)
  waiting for transfers between devices  28.5 us (22%)
  starting transfers between devices  22.3 us (17%)
  Pallas kernels  15 us (11%)
    all_to_all x3, blocking collectives, swap(): return lax.all_to_all(parts, axes, split_axis=0, concat_axis=0, tiled=True)  54.9 us
    ppermute x20, waiting for transfers between devices, from_distance(): lax.ppermute(piece, axis, [(k, k ^ distance) for k in range(lax.axis_size...  28.5 us
    ppermute x20, starting transfers between devices, from_distance(): lax.ppermute(piece, axis, [(k, k ^ distance) for k in range(lax.axis_size...  22.3 us
    all_gather x1, blocking collectives, local(): hidden = lax.all_gather(own_hidden, 'dp', axis=0, tiled=True)  8.78 us
    pallas_call x1, Pallas kernels, attend(): pl.pallas_call(attention_kernel, out_shape=jax.ShapeDtypeStruct((ranks, n...  7.25 us
  transfers between devices with their start and end apart: 20, of which 12 were waited for; matrix products, arithmetic and copies ran while one was open for 0% of the time, Pallas kernels for 3%

profile of v12, /device:TPU:0, one launch (start us, length us, event | category | flops | bytes accessed | tf_op | source)
XLA Modules:
  0.0 129.7 jit_solution(11162296534896152610)
XLA Ops:
  0.0 7.3 %attention.1 = bf16[32,16,512]{2,1,0:T(8,128)(2,1)S(1)} custom-call(s32[128]{0:T(128)} %lens_ref.1, bf16[4,73728]{1,0:T(4,128)(2,1)} %raw_ref.1, bf16[576,14336]{1,0:T(8,128)(2,1)} %bitcast.29), custom_call_target="tpu_custom_call" | custom-call | flops 3992977408 | bytes 16515072 | tf_op jit(solution)/shard_map/attention/pallas_call | solution.py:191
  7.3 27.1 %all_to_all.15 = bf16[32,16,512]{2,1,0:T(8,128)(2,1)S(1)} all-to-all(bf16[32,16,512]{2,1,0:T(8,128)(2,1)S(1)} %attention.1), channel_id=1, replica_groups=mesh['dp'=8,'tp'=4] {'dp','tp'}, dimensions={0} | all-to-all | bytes 1048576 | tf_op jit(solution)/shard_map/all_to_all | solution.py:611
  35.2 2.9 %collective-permute-start.2 = (bf16[128,512]{1,0:T(8,128)(2,1)S(1)}, bf16[128,512]{1,0:T(8,128)(2,1)S(1)}, u32[]{:S(2)}, u32[]{:S(2)}) collective-permute-start(bf16[128,512]{1,0:T(8,128)(2,1)S(1)} %head_values.1.value_ref), channel_id=1, source_target_pairs={{0,3},{1,2},{2,1},{3,0},{4,7},{5,6},{6,5},{7,4},{8,11},{9,10},{10,... | collective-permute-start | bytes 393224 | tf_op jit(solution)/shard_map/ppermute | solution.py:278
  38.0 1.2 collective-permute-start.1
  39.6 1.7 %collective-permute-start.3 = (bf16[4,1792]{1,0:T(4,128)(2,1)S(1)}, bf16[4,1792]{1,0:T(4,128)(2,1)S(1)}, u32[]{:S(2)}, u32[]{:S(2)}) collective-permute-start(bf16[4,1792]{1,0:T(4,128)(2,1)S(1)} %get-tuple-element.45), channel_id=1, source_target_pairs={{0,1},{1,0},{2,3},{3,2},{4,5},{5,4},{6,7},{7,6},{8,9},{9,8},{10,11... | collective-permute-start | bytes 43016 | tf_op jit(solution)/shard_map/ppermute | solution.py:278
  41.3 1.7 %collective-permute-start.4 = (bf16[4,1792]{1,0:T(4,128)(2,1)S(1)}, bf16[4,1792]{1,0:T(4,128)(2,1)S(1)}, u32[]{:S(2)}, u32[]{:S(2)}) collective-permute-start(bf16[4,1792]{1,0:T(4,128)(2,1)S(1)} %get-tuple-element.46), channel_id=1, source_target_pairs={{0,2},{1,3},{2,0},{3,1},{4,6},{5,7},{6,4},{7,5},{8,10},{9,11},{10,... | collective-permute-start | bytes 43016 | tf_op jit(solution)/shard_map/ppermute | solution.py:278
  43.3 3.0 %collective-permute-start.5 = (bf16[4,1792]{1,0:T(4,128)(2,1)S(1)}, bf16[4,1792]{1,0:T(4,128)(2,1)S(1)}, u32[]{:S(2)}, u32[]{:S(2)}) collective-permute-start(bf16[4,1792]{1,0:T(4,128)(2,1)S(1)} %get-tuple-element.47), channel_id=1, source_target_pairs={{0,3},{1,2},{2,1},{3,0},{4,7},{5,6},{6,5},{7,4},{8,11},{9,10},{10,... | collective-permute-start | bytes 43016 | tf_op jit(solution)/shard_map/ppermute | solution.py:278
  46.7 4.6 %collective-permute-done.1.refs_2_ = bf16[128,512]{1,0:T(8,128)(2,1)S(1)} collective-permute-done((bf16[128,512]{1,0:T(8,128)(2,1)S(1)}, bf16[128,512]{1,0:T(8,128)(2,1)S(1)}, u32[]{:S(2)}, u32[]{:S(2)}) %collective-permute-start.1) | collective-permute-done | bytes 131104 | tf_op jit(solution)/shard_map/ppermute | solution.py:278
  52.3 11.6 %all_to_all.16.parts_ref = bf16[8,16,1792]{2,1,0:T(8,128)(2,1)S(1)} all-to-all(bf16[8,16,1792]{2,1,0:T(8,128)(2,1)S(1)} %bitcast.19), channel_id=1, replica_groups=mesh['dp'=8,'tp'=4] {'dp'}, dimensions={0} | all-to-all | bytes 917504 | tf_op jit(solution)/shard_map/all_to_all | solution.py:611
  63.9 8.8 %all_gather.3.hidden_ref = bf16[128,1792]{1,0:T(8,128)(2,1)S(1)} all-gather(bf16[16,1792]{1,0:T(8,128)(2,1)S(1)} %hidden.1.refs_9_), channel_id=1, replica_groups=mesh['dp'=8,'tp'=4] {'dp'}, dimensions={0}, use_global_device_ids=true | all-gather | bytes 516096 | tf_op jit(solution)/shard_map/all_gather | solution.py:637
  72.8 1.4 %gate_up.1 = (bf16[2,128,1792]{2,1,0:T(8,128)(2,1)S(1)}, bf16[64,1408]{1,0:T(8,128)(2,1)S(1)}, bf16[64,1280]{1,0:T(8,128)(2,1)S(1)}, bf16[64,1408]{1,0:T(8,128)(2,1)S(1)}, bf16[64,1280]{1,0:T(8,128)(2,1)S(1)}) custom-call(bf16[128,1792]{1,0:T(8,128)(2,1)S(1)} %all_gather.3.hidden_ref, bf16[56,128]{1,0:T(8,128)(2,1)S(1)} %bitcast.28, ...), custom_call_target="tpu_custom_call" | custom-call | flops 1174405120 | bytes 9175040 | tf_op jit(solution)/shard_map/gate_up/pallas_call | solution.py:433
  75.1 1.5 %collective-permute-start.7 = (bf16[64,1280]{1,0:T(8,128)(2,1)S(1)}, bf16[64,1280]{1,0:T(8,128)(2,1)S(1)}, u32[]{:S(2)}, u32[]{:S(2)}) collective-permute-start(bf16[64,1280]{1,0:T(8,128)(2,1)S(1)} %get-tuple-element.63), channel_id=1, source_target_pairs={{0,2},{1,3},{2,0},{3,1},{4,6},{5,7},{6,4},{7,5},{8,10},{9,11},{10,... | collective-permute-start | bytes 491528 | tf_op jit(solution)/shard_map/ppermute | solution.py:278
  76.6 1.1 gate_up_rest.1
  78.2 2.1 %collective-permute-start.14 = (bf16[64,1024]{1,0:T(8,128)(2,1)S(1)}, bf16[64,1024]{1,0:T(8,128)(2,1)S(1)}, u32[]{:S(2)}, u32[]{:S(2)}) collective-permute-start(bf16[64,1024]{1,0:T(8,128)(2,1)S(1)} %get-tuple-element.73), channel_id=1, source_target_pairs={{0,2},{1,3},{2,0},{3,1},{4,6},{5,7},{6,4},{7,5},{8,10},{9,11},{10,... | collective-permute-start | bytes 393224 | tf_op jit(solution)/shard_map/ppermute | solution.py:278
  80.4 6.3 %collective-permute-done.7.refs_3_ = bf16[64,1280]{1,0:T(8,128)(2,1)S(1)} collective-permute-done((bf16[64,1280]{1,0:T(8,128)(2,1)S(1)}, bf16[64,1280]{1,0:T(8,128)(2,1)S(1)}, u32[]{:S(2)}, u32[]{:S(2)}) %collective-permute-start.7) | collective-permute-done | bytes 163872 | tf_op jit(solution)/shard_map/ppermute | solution.py:278
  88.0 1.9 %collective-permute-done.13.refs_2_ = bf16[64,1024]{1,0:T(8,128)(2,1)S(1)} collective-permute-done((bf16[64,1024]{1,0:T(8,128)(2,1)S(1)}, bf16[64,1024]{1,0:T(8,128)(2,1)S(1)}, u32[]{:S(2)}, u32[]{:S(2)}) %collective-permute-start.13) | collective-permute-done | bytes 131104 | tf_op jit(solution)/shard_map/ppermute | solution.py:278
  89.9 4.9 %collective-permute-done.14.refs_3_ = bf16[64,1024]{1,0:T(8,128)(2,1)S(1)} collective-permute-done((bf16[64,1024]{1,0:T(8,128)(2,1)S(1)}, bf16[64,1024]{1,0:T(8,128)(2,1)S(1)}, u32[]{:S(2)}, u32[]{:S(2)}) %collective-permute-start.14) | collective-permute-done | bytes 131104 | tf_op jit(solution)/shard_map/ppermute | solution.py:278
  95.0 2.4 %collective-permute-done.8 = bf16[32,1408]{1,0:T(8,128)(2,1)S(1)} collective-permute-done((bf16[32,1408]{1,0:T(8,128)(2,1)S(1)}, bf16[32,1408]{1,0:T(8,128)(2,1)S(1)}, u32[]{:S(2)}, u32[]{:S(2)}) %collective-permute-start.8) | collective-permute-done | bytes 90144 | tf_op jit(solution)/shard_map/ppermute | solution.py:278
  98.0 2.5 %collective-permute-done.15 = bf16[32,1024]{1,0:T(8,128)(2,1)S(1)} collective-permute-done((bf16[32,1024]{1,0:T(8,128)(2,1)S(1)}, bf16[32,1024]{1,0:T(8,128)(2,1)S(1)}, u32[]{:S(2)}, u32[]{:S(2)}) %collective-permute-start.15) | collective-permute-done | bytes 65568 | tf_op jit(solution)/shard_map/ppermute | solution.py:278
  101.4 1.9 %collective-permute-start.18 = (bf16[32,1024]{1,0:T(8,128)(2,1)S(1)}, bf16[32,1024]{1,0:T(8,128)(2,1)S(1)}, u32[]{:S(2)}, u32[]{:S(2)}) collective-permute-start(bf16[32,1024]{1,0:T(8,128)(2,1)S(1)} %get-tuple-element.78.refs_4_), channel_id=1, source_target_pairs={{0,2},{1,3},{2,0},{3,1},{4,6},{5,7},{6,4},{7,5},{8,10},{9,11},{10,... | collective-permute-start | bytes 196616 | tf_op jit(solution)/shard_map/ppermute | solution.py:278
  107.4 2.7 %collective-permute-done.17.refs_5_ = bf16[32,1024]{1,0:T(8,128)(2,1)S(1)} collective-permute-done((bf16[32,1024]{1,0:T(8,128)(2,1)S(1)}, bf16[32,1024]{1,0:T(8,128)(2,1)S(1)}, u32[]{:S(2)}, u32[]{:S(2)}) %collective-permute-start.17) | collective-permute-done | bytes 65568 | tf_op jit(solution)/shard_map/ppermute | solution.py:278
  110.1 1.1 collective-permute-done.19.refs_7_
  111.2 1.4 %project_down.1 = bf16[32,56,128]{2,1,0:T(8,128)(2,1)S(1)} custom-call(bf16[32,1280]{1,0:T(8,128)(2,1)S(1)} %get-tuple-element.68.refs_0_, bf16[32,1280]{1,0:T(8,128)(2,1)S(1)} %collective-permute-done.10.refs_1_, bf16[32,1280]{1,0:T(8,128)(2,1)S(1)} %collective-permute-done.11.refs_2_, bf16[32,1280]{1,0:T(8,128)(2,1)S(1)} %collective-permute-done.12.refs_3_, ...), custom_call_target="tpu_custom_call" | custom-call | tf_op jit(solution)/shard_map/project_down/pallas_call | solution.py:563
  112.7 16.3 %all_to_all.17.parts_ref = bf16[32,56,128]{2,1,0:T(8,128)(2,1)S(1)} all-to-all(bf16[32,56,128]{2,1,0:T(8,128)(2,1)S(1)} %project_down.1), channel_id=1, replica_groups=mesh['dp'=8,'tp'=4] {'dp','tp'}, dimensions={0} | all-to-all | bytes 917504 | tf_op jit(solution)/shard_map/all_to_all | solution.py:611
  (57 shorter events, 12.2 us)
Async XLA Ops:
  0.0 39.6 %copy-start.2 = (bf16[4,7168]{1,0:T(4,128)(2,1)S(1)}, bf16[4,7168]{1,0:T(4,128)(2,1)}, u32[]{:S(2)}) copy-start(bf16[4,7168]{1,0:T(4,128)(2,1)} %rows_ref) | copy-start | bytes 172036
  0.0 46.3 %copy-start = (bf16[2048,1792]{1,0:T(8,128)(2,1)S(1)}, bf16[2048,1792]{1,0:T(8,128)(2,1)}, u32[]{:S(2)}) copy-start(bf16[2048,1792]{1,0:T(8,128)(2,1)} %refs_4_.1) | copy-start | bytes 22020100
  0.0 72.7 %slice-start.2 = ((s8[8257536]{0:T(1024)(128)(4,1)}), s8[4194304]{0:T(1024)(128)(4,1)S(1)}, s32[]{:S(2)}) async-start(s8[8257536]{0:T(1024)(128)(4,1)} %bitcast.14), calls=%async_computation.5 | async-start | bytes 8388608
  35.2 8.2 %collective-permute-start.2 = (bf16[128,512]{1,0:T(8,128)(2,1)S(1)}, bf16[128,512]{1,0:T(8,128)(2,1)S(1)}, u32[]{:S(2)}, u32[]{:S(2)}) collective-permute-start(bf16[128,512]{1,0:T(8,128)(2,1)S(1)} %head_values.1.value_ref), channel_id=1, source_target_pairs={{0,3},{1,2},{2,1},{3,0},{4,7},{5,6},{6,5},{7,4},{8,11},{9,10},{10,... | collective-permute-start | bytes 393224 | tf_op jit(solution)/shard_map/ppermute | solution.py:278
  38.0 13.3 %collective-permute-start.1 = (bf16[128,512]{1,0:T(8,128)(2,1)S(1)}, bf16[128,512]{1,0:T(8,128)(2,1)S(1)}, u32[]{:S(2)}, u32[]{:S(2)}) collective-permute-start(bf16[128,512]{1,0:T(8,128)(2,1)S(1)} %head_values.1.value_ref), channel_id=1, source_target_pairs={{0,2},{1,3},{2,0},{3,1},{4,6},{5,7},{6,4},{7,5},{8,10},{9,11},{10,... | collective-permute-start | bytes 393224 | tf_op jit(solution)/shard_map/ppermute | solution.py:278
  39.2 12.1 %collective-permute-start = (bf16[128,512]{1,0:T(8,128)(2,1)S(1)}, bf16[128,512]{1,0:T(8,128)(2,1)S(1)}, u32[]{:S(2)}, u32[]{:S(2)}) collective-permute-start(bf16[128,512]{1,0:T(8,128)(2,1)S(1)} %head_values.1.value_ref), channel_id=1, source_target_pairs={{0,1},{1,0},{2,3},{3,2},{4,5},{5,4},{6,7},{7,6},{8,9},{9,8},{10,11... | collective-permute-start | bytes 393224 | tf_op jit(solution)/shard_map/ppermute | solution.py:278
  39.6 12.6 %collective-permute-start.3 = (bf16[4,1792]{1,0:T(4,128)(2,1)S(1)}, bf16[4,1792]{1,0:T(4,128)(2,1)S(1)}, u32[]{:S(2)}, u32[]{:S(2)}) collective-permute-start(bf16[4,1792]{1,0:T(4,128)(2,1)S(1)} %get-tuple-element.45), channel_id=1, source_target_pairs={{0,1},{1,0},{2,3},{3,2},{4,5},{5,4},{6,7},{7,6},{8,9},{9,8},{10,11... | collective-permute-start | bytes 43016 | tf_op jit(solution)/shard_map/ppermute | solution.py:278
  41.3 10.9 %collective-permute-start.4 = (bf16[4,1792]{1,0:T(4,128)(2,1)S(1)}, bf16[4,1792]{1,0:T(4,128)(2,1)S(1)}, u32[]{:S(2)}, u32[]{:S(2)}) collective-permute-start(bf16[4,1792]{1,0:T(4,128)(2,1)S(1)} %get-tuple-element.46), channel_id=1, source_target_pairs={{0,2},{1,3},{2,0},{3,1},{4,6},{5,7},{6,4},{7,5},{8,10},{9,11},{10,... | collective-permute-start | bytes 43016 | tf_op jit(solution)/shard_map/ppermute | solution.py:278
  43.3 8.9 %collective-permute-start.5 = (bf16[4,1792]{1,0:T(4,128)(2,1)S(1)}, bf16[4,1792]{1,0:T(4,128)(2,1)S(1)}, u32[]{:S(2)}, u32[]{:S(2)}) collective-permute-start(bf16[4,1792]{1,0:T(4,128)(2,1)S(1)} %get-tuple-element.47), channel_id=1, source_target_pairs={{0,3},{1,2},{2,1},{3,0},{4,7},{5,6},{6,5},{7,4},{8,11},{9,10},{10,... | collective-permute-start | bytes 43016 | tf_op jit(solution)/shard_map/ppermute | solution.py:278
  72.8 38.5 %slice-start.4 = ((s8[8257536]{0:T(1024)(128)(4,1)}), s8[4194304]{0:T(1024)(128)(4,1)S(1)}, s32[]{:S(2)}) async-start(s8[8257536]{0:T(1024)(128)(4,1)} %bitcast.16), calls=%async_computation.7 | async-start | bytes 8388608
  74.2 12.5 %collective-permute-start.6 = (bf16[64,1408]{1,0:T(8,128)(2,1)S(1)}, bf16[64,1408]{1,0:T(8,128)(2,1)S(1)}, u32[]{:S(2)}, u32[]{:S(2)}) collective-permute-start(bf16[64,1408]{1,0:T(8,128)(2,1)S(1)} %get-tuple-element.62), channel_id=1, source_target_pairs={{0,1},{1,0},{2,3},{3,2},{4,5},{5,4},{6,7},{7,6},{8,9},{9,8},{10,11... | collective-permute-start | bytes 540680 | tf_op jit(solution)/shard_map/ppermute | solution.py:278
  75.1 11.6 %collective-permute-start.7 = (bf16[64,1280]{1,0:T(8,128)(2,1)S(1)}, bf16[64,1280]{1,0:T(8,128)(2,1)S(1)}, u32[]{:S(2)}, u32[]{:S(2)}) collective-permute-start(bf16[64,1280]{1,0:T(8,128)(2,1)S(1)} %get-tuple-element.63), channel_id=1, source_target_pairs={{0,2},{1,3},{2,0},{3,1},{4,6},{5,7},{6,4},{7,5},{8,10},{9,11},{10,... | collective-permute-start | bytes 491528 | tf_op jit(solution)/shard_map/ppermute | solution.py:278
  77.7 12.2 %collective-permute-start.13 = (bf16[64,1024]{1,0:T(8,128)(2,1)S(1)}, bf16[64,1024]{1,0:T(8,128)(2,1)S(1)}, u32[]{:S(2)}, u32[]{:S(2)}) collective-permute-start(bf16[64,1024]{1,0:T(8,128)(2,1)S(1)} %get-tuple-element.72), channel_id=1, source_target_pairs={{0,1},{1,0},{2,3},{3,2},{4,5},{5,4},{6,7},{7,6},{8,9},{9,8},{10,11... | collective-permute-start | bytes 393224 | tf_op jit(solution)/shard_map/ppermute | solution.py:278
  78.2 16.5 %collective-permute-start.14 = (bf16[64,1024]{1,0:T(8,128)(2,1)S(1)}, bf16[64,1024]{1,0:T(8,128)(2,1)S(1)}, u32[]{:S(2)}, u32[]{:S(2)}) collective-permute-start(bf16[64,1024]{1,0:T(8,128)(2,1)S(1)} %get-tuple-element.73), channel_id=1, source_target_pairs={{0,2},{1,3},{2,0},{3,1},{4,6},{5,7},{6,4},{7,5},{8,10},{9,11},{10,... | collective-permute-start | bytes 393224 | tf_op jit(solution)/shard_map/ppermute | solution.py:278
  86.8 10.6 %collective-permute-start.8 = (bf16[32,1408]{1,0:T(8,128)(2,1)S(1)}, bf16[32,1408]{1,0:T(8,128)(2,1)S(1)}, u32[]{:S(2)}, u32[]{:S(2)}) collective-permute-start(bf16[32,1408]{1,0:T(8,128)(2,1)S(1)} %get-tuple-element.66), channel_id=1, source_target_pairs={{0,2},{1,3},{2,0},{3,1},{4,6},{5,7},{6,4},{7,5},{8,10},{9,11},{10,... | collective-permute-start | bytes 270344 | tf_op jit(solution)/shard_map/ppermute | solution.py:278
  87.1 7.9 %collective-permute-start.9 = (bf16[32,1280]{1,0:T(8,128)(2,1)S(1)}, bf16[32,1280]{1,0:T(8,128)(2,1)S(1)}, u32[]{:S(2)}, u32[]{:S(2)}) collective-permute-start(bf16[32,1280]{1,0:T(8,128)(2,1)S(1)} %get-tuple-element.67), channel_id=1, source_target_pairs={{0,1},{1,0},{2,3},{3,2},{4,5},{5,4},{6,7},{7,6},{8,9},{9,8},{10,11... | collective-permute-start | bytes 245768 | tf_op jit(solution)/shard_map/ppermute | solution.py:278
  94.8 5.7 %collective-permute-start.15 = (bf16[32,1024]{1,0:T(8,128)(2,1)S(1)}, bf16[32,1024]{1,0:T(8,128)(2,1)S(1)}, u32[]{:S(2)}, u32[]{:S(2)}) collective-permute-start(bf16[32,1024]{1,0:T(8,128)(2,1)S(1)} %get-tuple-element.76), channel_id=1, source_target_pairs={{0,2},{1,3},{2,0},{3,1},{4,6},{5,7},{6,4},{7,5},{8,10},{9,11},{10,... | collective-permute-start | bytes 196616 | tf_op jit(solution)/shard_map/ppermute | solution.py:278
  94.9 5.9 %collective-permute-start.16 = (bf16[32,1024]{1,0:T(8,128)(2,1)S(1)}, bf16[32,1024]{1,0:T(8,128)(2,1)S(1)}, u32[]{:S(2)}, u32[]{:S(2)}) collective-permute-start(bf16[32,1024]{1,0:T(8,128)(2,1)S(1)} %get-tuple-element.77), channel_id=1, source_target_pairs={{0,1},{1,0},{2,3},{3,2},{4,5},{5,4},{6,7},{7,6},{8,9},{9,8},{10,11... | collective-permute-start | bytes 196616 | tf_op jit(solution)/shard_map/ppermute | solution.py:278
  97.5 6.9 %collective-permute-start.11 = (bf16[32,1280]{1,0:T(8,128)(2,1)S(1)}, bf16[32,1280]{1,0:T(8,128)(2,1)S(1)}, u32[]{:S(2)}, u32[]{:S(2)}) collective-permute-start(bf16[32,1280]{1,0:T(8,128)(2,1)S(1)} %get-tuple-element.68.refs_0_), channel_id=1, source_target_pairs={{0,2},{1,3},{2,0},{3,1},{4,6},{5,7},{6,4},{7,5},{8,10},{9,11},{10,... | collective-permute-start | bytes 245768 | tf_op jit(solution)/shard_map/ppermute | solution.py:278
  101.4 5.5 %collective-permute-start.18 = (bf16[32,1024]{1,0:T(8,128)(2,1)S(1)}, bf16[32,1024]{1,0:T(8,128)(2,1)S(1)}, u32[]{:S(2)}, u32[]{:S(2)}) collective-permute-start(bf16[32,1024]{1,0:T(8,128)(2,1)S(1)} %get-tuple-element.78.refs_4_), channel_id=1, source_target_pairs={{0,2},{1,3},{2,0},{3,1},{4,6},{5,7},{6,4},{7,5},{8,10},{9,11},{10,... | collective-permute-start | bytes 196616 | tf_op jit(solution)/shard_map/ppermute | solution.py:278
  103.4 6.7 %collective-permute-start.10 = (bf16[32,1280]{1,0:T(8,128)(2,1)S(1)}, bf16[32,1280]{1,0:T(8,128)(2,1)S(1)}, u32[]{:S(2)}, u32[]{:S(2)}) collective-permute-start(bf16[32,1280]{1,0:T(8,128)(2,1)S(1)} %get-tuple-element.68.refs_0_), channel_id=1, source_target_pairs={{0,1},{1,0},{2,3},{3,2},{4,5},{5,4},{6,7},{7,6},{8,9},{9,8},{10,11... | collective-permute-start | bytes 245768 | tf_op jit(solution)/shard_map/ppermute | solution.py:278
  104.4 6.8 %collective-permute-start.12 = (bf16[32,1280]{1,0:T(8,128)(2,1)S(1)}, bf16[32,1280]{1,0:T(8,128)(2,1)S(1)}, u32[]{:S(2)}, u32[]{:S(2)}) collective-permute-start(bf16[32,1280]{1,0:T(8,128)(2,1)S(1)} %collective-permute-done.11.refs_2_), channel_id=1, source_target_pairs={{0,1},{1,0},{2,3},{3,2},{4,5},{5,4},{6,7},{7,6},{8,9},{9,8},{10,11... | collective-permute-start | bytes 245768 | tf_op jit(solution)/shard_map/ppermute | solution.py:278
  105.4 4.7 %collective-permute-start.17 = (bf16[32,1024]{1,0:T(8,128)(2,1)S(1)}, bf16[32,1024]{1,0:T(8,128)(2,1)S(1)}, u32[]{:S(2)}, u32[]{:S(2)}) collective-permute-start(bf16[32,1024]{1,0:T(8,128)(2,1)S(1)} %get-tuple-element.78.refs_4_), channel_id=1, source_target_pairs={{0,1},{1,0},{2,3},{3,2},{4,5},{5,4},{6,7},{7,6},{8,9},{9,8},{10,11... | collective-permute-start | bytes 196616 | tf_op jit(solution)/shard_map/ppermute | solution.py:278
  107.0 4.3 %collective-permute-start.19 = (bf16[32,1024]{1,0:T(8,128)(2,1)S(1)}, bf16[32,1024]{1,0:T(8,128)(2,1)S(1)}, u32[]{:S(2)}, u32[]{:S(2)}) collective-permute-start(bf16[32,1024]{1,0:T(8,128)(2,1)S(1)} %collective-permute-done.18.refs_6_), channel_id=1, source_target_pairs={{0,1},{1,0},{2,3},{3,2},{4,5},{5,4},{6,7},{7,6},{8,9},{9,8},{10,11... | collective-permute-start | bytes 196616 | tf_op jit(solution)/shard_map/ppermute | solution.py:278
  (6 other events, 192.2 us)

commit v13 on v12

--- a/solution.py
+++ b/solution.py
@@ -34,7 +34,8 @@
     acc,
     done,
     best,
-    mass,
+    mass0,
+    mass1,
     lo,
     hi,
     first,
@@ -89,11 +90,9 @@
             q_ref[r, :, c * 128 : (c + 1) * 128] = rows_of_heads[c].astype(q_ref.dtype)
         q_ref[r, :, full * 128 :] = rows_of_heads[full, :, :tail].astype(q_ref.dtype)
 
-    acc[...] = jnp.zeros_like(acc)
+    for ref in (acc, mass0, mass1, keep0, keep1, weight0, weight1):
+        ref[...] = jnp.zeros_like(ref)
     best[...] = jnp.full_like(best, negative)
-    mass[...] = jnp.zeros_like(mass)
-    weight1[...] = jnp.zeros_like(weight1)
-    keep1[...] = jnp.ones_like(keep1)
 
     def advance(p, r, i):
         live = p + 1 < pairs
@@ -109,65 +108,74 @@
         def _():
             copy(i).wait()
 
-    def scores(r, i, live, target):
+    def scores(r, i, live):
         begin_at = jnp.where(live, lo[r], 0)
         end_at = jnp.where(live, hi[r], 0)
-        s = jnp.dot(q_ref[r], held[i], preferred_element_type=jnp.float32)
         token = i * tile + lax.broadcasted_iota(jnp.int32, (1, tile), 1)
-        target[...] = s + jnp.where((token >= begin_at) & (token < end_at), 0.0, negative)
-
-    def soften(r, source, weights, keeps):
-        s = source[...]
-        old = best[r]
+        bias = jnp.where((token >= begin_at) & (token < end_at), 0.0, negative)
+        return jnp.dot(q_ref[r], held[i], preferred_element_type=jnp.float32) + bias
+
+    def gather(i, weights):
+        return jnp.dot(held[i, :C, :], weights[...], preferred_element_type=jnp.float32)
+
+    def half_step(before, now, after, given, found, used, made):
+        (r0, i0), (r1, i1, live1), (r2, i2, live2) = before, now, after
+        weights0, keeps0, masses0 = used
+        weights1, keeps1, masses1 = made
+        values = gather(i0, weights0)
+        ahead = scores(r2, i2, live2)
+
+        s = given[...]
+        old = jnp.where(live1 & (i1 == first[r1]), negative, best[...])
         new = jnp.maximum(old, jnp.max(s, axis=1, keepdims=True))
         weight = jnp.exp2((s - new[:, :1]) * factor)
         keep = jnp.exp2((old - new) * factor)
         part = weight[:, :128]
         for at in range(128, tile, 128):
             part = part + weight[:, at : at + 128]
-        mass[r] = mass[r] * keep + part
-        best[r] = new
-        weights[...] = weight.T.astype(weights.dtype)
-        keeps[...] = keep.T[:8, :]
-
-    def gather(r, i, weights, keeps):
-        values = lax.dot_general(
-            held[i, :C, :],
-            weights[...],
-            (((1,), (0,)), ((), ())),
-            preferred_element_type=jnp.float32,
-        )
-        acc[r] = acc[r] * keeps[:1, :] + values
+
+        acc[...] = acc[...] * keeps0[:1, :] + values
+        found[...] = ahead
+        weights1[...] = weight.T.astype(weights1.dtype)
+        keeps1[...] = keep.T[:8, :]
+        masses1[...] = masses0[...] * keep + part
+        best[...] = new
+
+        @pl.when(r1 != r0)
+        def _():
+            close(r0, masses0)
+
+    def close(r, masses):
+        total = jnp.sum(masses[...], axis=1, keepdims=True)
+        done[r] = acc[...].T / total
 
     zero = jnp.int32(0)
     fetch(zero, zero, pairs > 0)
-    scores(zero, zero, pairs > 0, score0)
+    score0[...] = scores(zero, zero, pairs > 0)
+    stage0 = (weight0, keep0, mass0)
+    stage1 = (weight1, keep1, mass1)
 
     def step(j, carry):
-        r0, i0, r1, i1 = carry
+        r0, i0, r1, i1, live1 = carry
         p = 2 * j
         r2, i2, live2 = advance(p, r1, i1)
         r3, i3, live3 = advance(p + 1, r2, i2)
         fetch(r2, i2, live2)
+        half_step((r0, i0), (r1, i1, live1), (r2, i2, live2), score0, score1, stage1, stage0)
         fetch(r3, i3, live3)
-        gather(r0, i0, weight1, keep1)
-        scores(r2, i2, live2, score1)
-        soften(r1, score0, weight0, keep0)
-        gather(r1, i1, weight0, keep0)
-        scores(r3, i3, live3, score0)
-        soften(r2, score1, weight1, keep1)
-        return r2, i2, r3, i3
-
-    r0, i0, _, _ = lax.fori_loop(0, (pairs + 1) // 2, step, (zero, zero, zero, zero))
-    gather(r0, i0, weight1, keep1)
+        half_step((r1, i1), (r2, i2, live2), (r3, i3, live3), score1, score0, stage0, stage1)
+        return r2, i2, r3, i3, live3
+
+    r0, i0, _, _, _ = lax.fori_loop(
+        0, (pairs + 1) // 2, step, (zero, zero, zero, zero, pairs > 0)
+    )
+    acc[...] = acc[...] * keep1[:1, :] + gather(i0, weight1)
+    close(r0, mass1)
 
     share = heads // out_ref.shape[0]
-    for r in range(nreq):
-        total = jnp.sum(mass[r], axis=1, keepdims=True)
-        score0[:, :C] = acc[r].T / total
-        for d in range(out_ref.shape[0]):
-            done[d, r * share : (r + 1) * share, :] = score0[d * share : (d + 1) * share, :C]
-    out_ref[...] = done[...].astype(out_ref.dtype)
+    for d in range(out_ref.shape[0]):
+        rows = [done[r, d * share : (d + 1) * share, :] for r in range(nreq)]
+        out_ref[d] = jnp.concatenate(rows, 0).astype(out_ref.dtype)
 
 
 def kernel_params(limit):
@@ -206,10 +214,11 @@
             pltpu.VMEM((tile, heads), jnp.bfloat16),
             pltpu.VMEM((8, heads), jnp.float32),
             pltpu.VMEM((8, heads), jnp.float32),
-            pltpu.VMEM((nreq, C, heads), jnp.float32),
-            pltpu.VMEM((ranks, nreq * heads // ranks, C), jnp.float32),
-            pltpu.VMEM((nreq, heads, 128), jnp.float32),
-            pltpu.VMEM((nreq, heads, 128), jnp.float32),
+            pltpu.VMEM((C, heads), jnp.float32),
+            pltpu.VMEM((nreq, heads, C), jnp.float32),
+            pltpu.VMEM((heads, 128), jnp.float32),
+            pltpu.VMEM((heads, 128), jnp.float32),
+            pltpu.VMEM((heads, 128), jnp.float32),
             pltpu.SMEM((nreq,), jnp.int32),
             pltpu.SMEM((nreq,), jnp.int32),
             pltpu.SMEM((nreq,), jnp.int32),
@@ -279,6 +288,9 @@
 
 
 def from_all(piece, axis):
+    if lax.axis_size(axis) == 4:
+        far = from_distance(piece, axis, 2)
+        return [piece, from_distance(piece, axis, 1), far, from_distance(far, axis, 1)]
     return [piece] + [from_distance(piece, axis, k) for k in range(1, lax.axis_size(axis))]
 
 
@@ -651,8 +663,7 @@
             (gate_send, up_send), kept = halve([gate_keep, up_keep], came)
             came = [from_distance(gate_send, "tp", 2), from_distance(up_send, "tp", 1)]
             own, factor = make_inner([part[None] for part in (*kept, *came)], factor, model)
-            far = from_distance(own, "tp", 2)
-            inner.append([own, from_distance(own, "tp", 1), far, from_distance(far, "tp", 1)])
+            inner.append(from_all(own, "tp"))
         else:
             parts = [swap(part.reshape(ranks_tp, -1, part.shape[1]), "tp") for part in chunk]
             own, factor = make_inner(parts, factor, model)

time: 131 us -> 135 us (1.031)
  starting transfers between devices: 22.3 us -> 29.2 us
  waiting for transfers between devices: 28.5 us -> 21.6 us
  blocking collectives: 63.7 us -> 66.8 us
    ppermute x20, starting transfers between devices: 22.3 us -> 29.2 us  [from_distance(): lax.ppermute(piece, axis, [(k, k ^ distance) for k in range(lax.axis_size...]
    ppermute x20, waiting for transfers between devices: 28.5 us -> 21.6 us  [from_distance(): lax.ppermute(piece, axis, [(k, k ^ distance) for k in range(lax.axis_size...]
    all_to_all x3, blocking collectives: 54.9 us -> 58.1 us  [swap(): return lax.all_to_all(parts, axes, split_axis=0, concat_axis=0, tiled=True)]
  transfers between devices with their start and end apart: 20 -> 20, of which waited for: 12 -> 10; matrix products, arithmetic and copies ran while one was open for 0% -> 0% of each run, Pallas kernels for 3% -> 3%
where the time goes in v13:
time: 135 us; the launch traced here: 133 us
  blocking collectives  66.8 us (49%)
  starting transfers between devices  29.2 us (22%)
  waiting for transfers between devices  21.6 us (16%)
  Pallas kernels  15.6 us (12%)
    all_to_all x3, blocking collectives, swap(): return lax.all_to_all(parts, axes, split_axis=0, concat_axis=0, tiled=True)  58.1 us
    ppermute x20, starting transfers between devices, from_distance(): lax.ppermute(piece, axis, [(k, k ^ distance) for k in range(lax.axis_size...  29.2 us
    ppermute x20, waiting for transfers between devices, from_distance(): lax.ppermute(piece, axis, [(k, k ^ distance) for k in range(lax.axis_size...  21.6 us
    all_gather x1, blocking collectives, local(): hidden = lax.all_gather(own_hidden, 'dp', axis=0, tiled=True)  8.78 us
    pallas_call x1, Pallas kernels, attend(): pl.pallas_call(attention_kernel, out_shape=jax.ShapeDtypeStruct((ranks, n...  7.89 us
  transfers between devices with their start and end apart: 20, of which 10 were waited for; matrix products, arithmetic and copies ran while one was open for 0% of the time, Pallas kernels for 3%

profile of v13, /device:TPU:0, one launch (start us, length us, event | category | flops | bytes accessed | tf_op | source)
XLA Modules:
  0.0 133.4 jit_solution(10921458005867930546)
XLA Ops:
  0.0 7.9 %attention.1 = bf16[32,16,512]{2,1,0:T(8,128)(2,1)S(1)} custom-call(s32[128]{0:T(128)} %lens_ref.1, bf16[4,73728]{1,0:T(4,128)(2,1)} %raw_ref.1, bf16[576,14336]{1,0:T(8,128)(2,1)} %bitcast.29), custom_call_target="tpu_custom_call" | custom-call | flops 3992977408 | bytes 16515072 | tf_op jit(solution)/shard_map/attention/pallas_call | solution.py:199
  7.9 30.0 %all_to_all.15 = bf16[32,16,512]{2,1,0:T(8,128)(2,1)S(1)} all-to-all(bf16[32,16,512]{2,1,0:T(8,128)(2,1)S(1)} %attention.1), channel_id=1, replica_groups=mesh['dp'=8,'tp'=4] {'dp','tp'}, dimensions={0} | all-to-all | bytes 1048576 | tf_op jit(solution)/shard_map/all_to_all | solution.py:623
  38.7 1.9 %collective-permute-start.1 = (bf16[128,512]{1,0:T(8,128)(2,1)S(1)}, bf16[128,512]{1,0:T(8,128)(2,1)S(1)}, u32[]{:S(2)}, u32[]{:S(2)}) collective-permute-start(bf16[128,512]{1,0:T(8,128)(2,1)S(1)} %head_values.1.value_ref), channel_id=1, source_target_pairs={{0,2},{1,3},{2,0},{3,1},{4,6},{5,7},{6,4},{7,5},{8,10},{9,11},{10,... | collective-permute-start | bytes 393224 | tf_op jit(solution)/shard_map/ppermute | solution.py:287
  40.6 1.6 %collective-permute-start = (bf16[128,512]{1,0:T(8,128)(2,1)S(1)}, bf16[128,512]{1,0:T(8,128)(2,1)S(1)}, u32[]{:S(2)}, u32[]{:S(2)}) collective-permute-start(bf16[128,512]{1,0:T(8,128)(2,1)S(1)} %head_values.1.value_ref), channel_id=1, source_target_pairs={{0,1},{1,0},{2,3},{3,2},{4,5},{5,4},{6,7},{7,6},{8,9},{9,8},{10,11... | collective-permute-start | bytes 393224 | tf_op jit(solution)/shard_map/ppermute | solution.py:287
  42.1 6.5 %collective-permute-done.1.refs_2_ = bf16[128,512]{1,0:T(8,128)(2,1)S(1)} collective-permute-done((bf16[128,512]{1,0:T(8,128)(2,1)S(1)}, bf16[128,512]{1,0:T(8,128)(2,1)S(1)}, u32[]{:S(2)}, u32[]{:S(2)}) %collective-permute-start.1) | collective-permute-done | bytes 131104 | tf_op jit(solution)/shard_map/ppermute | solution.py:287
  48.7 2.1 %collective-permute-start.3 = (bf16[4,1792]{1,0:T(4,128)(2,1)S(1)}, bf16[4,1792]{1,0:T(4,128)(2,1)S(1)}, u32[]{:S(2)}, u32[]{:S(2)}) collective-permute-start(bf16[4,1792]{1,0:T(4,128)(2,1)S(1)} %get-tuple-element.45), channel_id=1, source_target_pairs={{0,1},{1,0},{2,3},{3,2},{4,5},{5,4},{6,7},{7,6},{8,9},{9,8},{10,11... | collective-permute-start | bytes 43016 | tf_op jit(solution)/shard_map/ppermute | solution.py:287
  51.2 2.0 %collective-permute-start.5 = (bf16[4,1792]{1,0:T(4,128)(2,1)S(1)}, bf16[4,1792]{1,0:T(4,128)(2,1)S(1)}, u32[]{:S(2)}, u32[]{:S(2)}) collective-permute-start(bf16[4,1792]{1,0:T(4,128)(2,1)S(1)} %get-tuple-element.47), channel_id=1, source_target_pairs={{0,3},{1,2},{2,1},{3,0},{4,7},{5,6},{6,5},{7,4},{8,11},{9,10},{10,... | collective-permute-start | bytes 43016 | tf_op jit(solution)/shard_map/ppermute | solution.py:287
  55.4 1.3 collective-permute-done.5.refs_3_
  56.7 11.5 %all_to_all.16.parts_ref = bf16[8,16,1792]{2,1,0:T(8,128)(2,1)S(1)} all-to-all(bf16[8,16,1792]{2,1,0:T(8,128)(2,1)S(1)} %bitcast.19), channel_id=1, replica_groups=mesh['dp'=8,'tp'=4] {'dp'}, dimensions={0} | all-to-all | bytes 917504 | tf_op jit(solution)/shard_map/all_to_all | solution.py:623
  68.3 8.8 %all_gather.3.hidden_ref = bf16[128,1792]{1,0:T(8,128)(2,1)S(1)} all-gather(bf16[16,1792]{1,0:T(8,128)(2,1)S(1)} %hidden.1.refs_9_), channel_id=1, replica_groups=mesh['dp'=8,'tp'=4] {'dp'}, dimensions={0}, use_global_device_ids=true | all-gather | bytes 516096 | tf_op jit(solution)/shard_map/all_gather | solution.py:649
  77.1 1.4 %gate_up.1 = (bf16[2,128,1792]{2,1,0:T(8,128)(2,1)S(1)}, bf16[64,1408]{1,0:T(8,128)(2,1)S(1)}, bf16[64,1280]{1,0:T(8,128)(2,1)S(1)}, bf16[64,1408]{1,0:T(8,128)(2,1)S(1)}, bf16[64,1280]{1,0:T(8,128)(2,1)S(1)}) custom-call(bf16[128,1792]{1,0:T(8,128)(2,1)S(1)} %all_gather.3.hidden_ref, bf16[56,128]{1,0:T(8,128)(2,1)S(1)} %bitcast.28, ...), custom_call_target="tpu_custom_call" | custom-call | flops 1174405120 | bytes 9175040 | tf_op jit(solution)/shard_map/gate_up/pallas_call | solution.py:445
  78.6 3.0 %collective-permute-start.7 = (bf16[64,1280]{1,0:T(8,128)(2,1)S(1)}, bf16[64,1280]{1,0:T(8,128)(2,1)S(1)}, u32[]{:S(2)}, u32[]{:S(2)}) collective-permute-start(bf16[64,1280]{1,0:T(8,128)(2,1)S(1)} %get-tuple-element.63), channel_id=1, source_target_pairs={{0,2},{1,3},{2,0},{3,1},{4,6},{5,7},{6,4},{7,5},{8,10},{9,11},{10,... | collective-permute-start | bytes 491528 | tf_op jit(solution)/shard_map/ppermute | solution.py:287
  83.0 1.8 %collective-permute-start.14 = (bf16[64,1024]{1,0:T(8,128)(2,1)S(1)}, bf16[64,1024]{1,0:T(8,128)(2,1)S(1)}, u32[]{:S(2)}, u32[]{:S(2)}) collective-permute-start(bf16[64,1024]{1,0:T(8,128)(2,1)S(1)} %get-tuple-element.73), channel_id=1, source_target_pairs={{0,2},{1,3},{2,0},{3,1},{4,6},{5,7},{6,4},{7,5},{8,10},{9,11},{10,... | collective-permute-start | bytes 393224 | tf_op jit(solution)/shard_map/ppermute | solution.py:287
  84.8 2.3 %collective-permute-done.7.refs_3_ = bf16[64,1280]{1,0:T(8,128)(2,1)S(1)} collective-permute-done((bf16[64,1280]{1,0:T(8,128)(2,1)S(1)}, bf16[64,1280]{1,0:T(8,128)(2,1)S(1)}, u32[]{:S(2)}, u32[]{:S(2)}) %collective-permute-start.7) | collective-permute-done | bytes 163872 | tf_op jit(solution)/shard_map/ppermute | solution.py:287
  87.1 2.8 %collective-permute-done.6.refs_2_ = bf16[64,1408]{1,0:T(8,128)(2,1)S(1)} collective-permute-done((bf16[64,1408]{1,0:T(8,128)(2,1)S(1)}, bf16[64,1408]{1,0:T(8,128)(2,1)S(1)}, u32[]{:S(2)}, u32[]{:S(2)}) %collective-permute-start.6) | collective-permute-done | bytes 180256 | tf_op jit(solution)/shard_map/ppermute | solution.py:287
  90.6 2.9 %collective-permute-start.9 = (bf16[32,1280]{1,0:T(8,128)(2,1)S(1)}, bf16[32,1280]{1,0:T(8,128)(2,1)S(1)}, u32[]{:S(2)}, u32[]{:S(2)}) collective-permute-start(bf16[32,1280]{1,0:T(8,128)(2,1)S(1)} %get-tuple-element.67), channel_id=1, source_target_pairs={{0,1},{1,0},{2,3},{3,2},{4,5},{5,4},{6,7},{7,6},{8,9},{9,8},{10,11... | collective-permute-start | bytes 245768 | tf_op jit(solution)/shard_map/ppermute | solution.py:287
  93.5 1.7 %collective-permute-done.13.refs_2_ = bf16[64,1024]{1,0:T(8,128)(2,1)S(1)} collective-permute-done((bf16[64,1024]{1,0:T(8,128)(2,1)S(1)}, bf16[64,1024]{1,0:T(8,128)(2,1)S(1)}, u32[]{:S(2)}, u32[]{:S(2)}) %collective-permute-start.13) | collective-permute-done | bytes 131104 | tf_op jit(solution)/shard_map/ppermute | solution.py:287
  96.3 4.7 %collective-permute-start.16 = (bf16[32,1024]{1,0:T(8,128)(2,1)S(1)}, bf16[32,1024]{1,0:T(8,128)(2,1)S(1)}, u32[]{:S(2)}, u32[]{:S(2)}) collective-permute-start(bf16[32,1024]{1,0:T(8,128)(2,1)S(1)} %get-tuple-element.77), channel_id=1, source_target_pairs={{0,1},{1,0},{2,3},{3,2},{4,5},{5,4},{6,7},{7,6},{8,9},{9,8},{10,11... | collective-permute-start | bytes 196616 | tf_op jit(solution)/shard_map/ppermute | solution.py:287
  101.3 2.2 %collective-permute-done.16 = bf16[32,1024]{1,0:T(8,128)(2,1)S(1)} collective-permute-done((bf16[32,1024]{1,0:T(8,128)(2,1)S(1)}, bf16[32,1024]{1,0:T(8,128)(2,1)S(1)}, u32[]{:S(2)}, u32[]{:S(2)}) %collective-permute-start.16) | collective-permute-done | bytes 65568 | tf_op jit(solution)/shard_map/ppermute | solution.py:287
  105.2 2.9 %collective-permute-start.10 = (bf16[32,1280]{1,0:T(8,128)(2,1)S(1)}, bf16[32,1280]{1,0:T(8,128)(2,1)S(1)}, u32[]{:S(2)}, u32[]{:S(2)}) collective-permute-start(bf16[32,1280]{1,0:T(8,128)(2,1)S(1)} %get-tuple-element.68.refs_0_), channel_id=1, source_target_pairs={{0,1},{1,0},{2,3},{3,2},{4,5},{5,4},{6,7},{7,6},{8,9},{9,8},{10,11... | collective-permute-start | bytes 245768 | tf_op jit(solution)/shard_map/ppermute | solution.py:287
  108.4 2.0 %collective-permute-start.17 = (bf16[32,1024]{1,0:T(8,128)(2,1)S(1)}, bf16[32,1024]{1,0:T(8,128)(2,1)S(1)}, u32[]{:S(2)}, u32[]{:S(2)}) collective-permute-start(bf16[32,1024]{1,0:T(8,128)(2,1)S(1)} %get-tuple-element.78.refs_4_), channel_id=1, source_target_pairs={{0,1},{1,0},{2,3},{3,2},{4,5},{5,4},{6,7},{7,6},{8,9},{9,8},{10,11... | collective-permute-start | bytes 196616 | tf_op jit(solution)/shard_map/ppermute | solution.py:287
  111.2 2.3 %collective-permute-done.17.refs_5_ = bf16[32,1024]{1,0:T(8,128)(2,1)S(1)} collective-permute-done((bf16[32,1024]{1,0:T(8,128)(2,1)S(1)}, bf16[32,1024]{1,0:T(8,128)(2,1)S(1)}, u32[]{:S(2)}, u32[]{:S(2)}) %collective-permute-start.17) | collective-permute-done | bytes 65568 | tf_op jit(solution)/shard_map/ppermute | solution.py:287
  114.7 1.4 %project_down.1 = bf16[32,56,128]{2,1,0:T(8,128)(2,1)S(1)} custom-call(bf16[32,1280]{1,0:T(8,128)(2,1)S(1)} %get-tuple-element.68.refs_0_, bf16[32,1280]{1,0:T(8,128)(2,1)S(1)} %collective-permute-done.10.refs_1_, bf16[32,1280]{1,0:T(8,128)(2,1)S(1)} %collective-permute-done.11.refs_2_, bf16[32,1280]{1,0:T(8,128)(2,1)S(1)} %collective-permute-done.12.refs_3_, ...), custom_call_target="tpu_custom_call" | custom-call | tf_op jit(solution)/shard_map/project_down/pallas_call | solution.py:575
  116.2 16.5 %all_to_all.17.parts_ref = bf16[32,56,128]{2,1,0:T(8,128)(2,1)S(1)} all-to-all(bf16[32,56,128]{2,1,0:T(8,128)(2,1)S(1)} %project_down.1), channel_id=1, replica_groups=mesh['dp'=8,'tp'=4] {'dp','tp'}, dimensions={0} | all-to-all | bytes 917504 | tf_op jit(solution)/shard_map/all_to_all | solution.py:623
  (57 shorter events, 11.7 us)
Async XLA Ops:
  0.0 48.7 %copy-start.2 = (bf16[4,7168]{1,0:T(4,128)(2,1)S(1)}, bf16[4,7168]{1,0:T(4,128)(2,1)}, u32[]{:S(2)}) copy-start(bf16[4,7168]{1,0:T(4,128)(2,1)} %rows_ref) | copy-start | bytes 172036
  0.0 53.2 %copy-start = (bf16[2048,1792]{1,0:T(8,128)(2,1)S(1)}, bf16[2048,1792]{1,0:T(8,128)(2,1)}, u32[]{:S(2)}) copy-start(bf16[2048,1792]{1,0:T(8,128)(2,1)} %refs_4_.1) | copy-start | bytes 22020100
  0.0 77.1 %slice-start.2 = ((s8[8257536]{0:T(1024)(128)(4,1)}), s8[4194304]{0:T(1024)(128)(4,1)S(1)}, s32[]{:S(2)}) async-start(s8[8257536]{0:T(1024)(128)(4,1)} %bitcast.14), calls=%async_computation.5 | async-start | bytes 8388608
  37.9 39.2 %slice-start.3 = ((s8[8257536]{0:T(1024)(128)(4,1)}), s8[4063232]{0:T(1024)(128)(4,1)S(1)}, s32[]{:S(2)}) async-start(s8[8257536]{0:T(1024)(128)(4,1)} %bitcast.14), calls=%async_computation.6 | async-start | bytes 8126464
  38.7 10.0 %collective-permute-start.1 = (bf16[128,512]{1,0:T(8,128)(2,1)S(1)}, bf16[128,512]{1,0:T(8,128)(2,1)S(1)}, u32[]{:S(2)}, u32[]{:S(2)}) collective-permute-start(bf16[128,512]{1,0:T(8,128)(2,1)S(1)} %head_values.1.value_ref), channel_id=1, source_target_pairs={{0,2},{1,3},{2,0},{3,1},{4,6},{5,7},{6,4},{7,5},{8,10},{9,11},{10,... | collective-permute-start | bytes 393224 | tf_op jit(solution)/shard_map/ppermute | solution.py:287
  40.6 13.1 %collective-permute-start = (bf16[128,512]{1,0:T(8,128)(2,1)S(1)}, bf16[128,512]{1,0:T(8,128)(2,1)S(1)}, u32[]{:S(2)}, u32[]{:S(2)}) collective-permute-start(bf16[128,512]{1,0:T(8,128)(2,1)S(1)} %head_values.1.value_ref), channel_id=1, source_target_pairs={{0,1},{1,0},{2,3},{3,2},{4,5},{5,4},{6,7},{7,6},{8,9},{9,8},{10,11... | collective-permute-start | bytes 393224 | tf_op jit(solution)/shard_map/ppermute | solution.py:287
  48.7 5.8 %collective-permute-start.2 = (bf16[128,512]{1,0:T(8,128)(2,1)S(1)}, bf16[128,512]{1,0:T(8,128)(2,1)S(1)}, u32[]{:S(2)}, u32[]{:S(2)}) collective-permute-start(bf16[128,512]{1,0:T(8,128)(2,1)S(1)} %collective-permute-done.1.refs_2_), channel_id=1, source_target_pairs={{0,1},{1,0},{2,3},{3,2},{4,5},{5,4},{6,7},{7,6},{8,9},{9,8},{10,11... | collective-permute-start | bytes 393224 | tf_op jit(solution)/shard_map/ppermute | solution.py:287
  48.7 6.7 %collective-permute-start.3 = (bf16[4,1792]{1,0:T(4,128)(2,1)S(1)}, bf16[4,1792]{1,0:T(4,128)(2,1)S(1)}, u32[]{:S(2)}, u32[]{:S(2)}) collective-permute-start(bf16[4,1792]{1,0:T(4,128)(2,1)S(1)} %get-tuple-element.45), channel_id=1, source_target_pairs={{0,1},{1,0},{2,3},{3,2},{4,5},{5,4},{6,7},{7,6},{8,9},{9,8},{10,11... | collective-permute-start | bytes 43016 | tf_op jit(solution)/shard_map/ppermute | solution.py:287
  50.8 4.6 %collective-permute-start.4 = (bf16[4,1792]{1,0:T(4,128)(2,1)S(1)}, bf16[4,1792]{1,0:T(4,128)(2,1)S(1)}, u32[]{:S(2)}, u32[]{:S(2)}) collective-permute-start(bf16[4,1792]{1,0:T(4,128)(2,1)S(1)} %get-tuple-element.46), channel_id=1, source_target_pairs={{0,2},{1,3},{2,0},{3,1},{4,6},{5,7},{6,4},{7,5},{8,10},{9,11},{10,... | collective-permute-start | bytes 43016 | tf_op jit(solution)/shard_map/ppermute | solution.py:287
  51.2 5.5 %collective-permute-start.5 = (bf16[4,1792]{1,0:T(4,128)(2,1)S(1)}, bf16[4,1792]{1,0:T(4,128)(2,1)S(1)}, u32[]{:S(2)}, u32[]{:S(2)}) collective-permute-start(bf16[4,1792]{1,0:T(4,128)(2,1)S(1)} %get-tuple-element.47), channel_id=1, source_target_pairs={{0,3},{1,2},{2,1},{3,0},{4,7},{5,6},{6,5},{7,4},{8,11},{9,10},{10,... | collective-permute-start | bytes 43016 | tf_op jit(solution)/shard_map/ppermute | solution.py:287
  78.5 11.3 %collective-permute-start.6 = (bf16[64,1408]{1,0:T(8,128)(2,1)S(1)}, bf16[64,1408]{1,0:T(8,128)(2,1)S(1)}, u32[]{:S(2)}, u32[]{:S(2)}) collective-permute-start(bf16[64,1408]{1,0:T(8,128)(2,1)S(1)} %get-tuple-element.62), channel_id=1, source_target_pairs={{0,1},{1,0},{2,3},{3,2},{4,5},{5,4},{6,7},{7,6},{8,9},{9,8},{10,11... | collective-permute-start | bytes 540680 | tf_op jit(solution)/shard_map/ppermute | solution.py:287
  78.6 8.4 %collective-permute-start.7 = (bf16[64,1280]{1,0:T(8,128)(2,1)S(1)}, bf16[64,1280]{1,0:T(8,128)(2,1)S(1)}, u32[]{:S(2)}, u32[]{:S(2)}) collective-permute-start(bf16[64,1280]{1,0:T(8,128)(2,1)S(1)} %get-tuple-element.63), channel_id=1, source_target_pairs={{0,2},{1,3},{2,0},{3,1},{4,6},{5,7},{6,4},{7,5},{8,10},{9,11},{10,... | collective-permute-start | bytes 491528 | tf_op jit(solution)/shard_map/ppermute | solution.py:287
  82.7 12.5 %collective-permute-start.13 = (bf16[64,1024]{1,0:T(8,128)(2,1)S(1)}, bf16[64,1024]{1,0:T(8,128)(2,1)S(1)}, u32[]{:S(2)}, u32[]{:S(2)}) collective-permute-start(bf16[64,1024]{1,0:T(8,128)(2,1)S(1)} %get-tuple-element.72), channel_id=1, source_target_pairs={{0,1},{1,0},{2,3},{3,2},{4,5},{5,4},{6,7},{7,6},{8,9},{9,8},{10,11... | collective-permute-start | bytes 393224 | tf_op jit(solution)/shard_map/ppermute | solution.py:287
  83.0 12.3 %collective-permute-start.14 = (bf16[64,1024]{1,0:T(8,128)(2,1)S(1)}, bf16[64,1024]{1,0:T(8,128)(2,1)S(1)}, u32[]{:S(2)}, u32[]{:S(2)}) collective-permute-start(bf16[64,1024]{1,0:T(8,128)(2,1)S(1)} %get-tuple-element.73), channel_id=1, source_target_pairs={{0,2},{1,3},{2,0},{3,1},{4,6},{5,7},{6,4},{7,5},{8,10},{9,11},{10,... | collective-permute-start | bytes 393224 | tf_op jit(solution)/shard_map/ppermute | solution.py:287
  89.9 11.1 %collective-permute-start.8 = (bf16[32,1408]{1,0:T(8,128)(2,1)S(1)}, bf16[32,1408]{1,0:T(8,128)(2,1)S(1)}, u32[]{:S(2)}, u32[]{:S(2)}) collective-permute-start(bf16[32,1408]{1,0:T(8,128)(2,1)S(1)} %get-tuple-element.66), channel_id=1, source_target_pairs={{0,2},{1,3},{2,0},{3,1},{4,6},{5,7},{6,4},{7,5},{8,10},{9,11},{10,... | collective-permute-start | bytes 270344 | tf_op jit(solution)/shard_map/ppermute | solution.py:287
  90.6 10.4 %collective-permute-start.9 = (bf16[32,1280]{1,0:T(8,128)(2,1)S(1)}, bf16[32,1280]{1,0:T(8,128)(2,1)S(1)}, u32[]{:S(2)}, u32[]{:S(2)}) collective-permute-start(bf16[32,1280]{1,0:T(8,128)(2,1)S(1)} %get-tuple-element.67), channel_id=1, source_target_pairs={{0,1},{1,0},{2,3},{3,2},{4,5},{5,4},{6,7},{7,6},{8,9},{9,8},{10,11... | collective-permute-start | bytes 245768 | tf_op jit(solution)/shard_map/ppermute | solution.py:287
  95.3 6.0 %collective-permute-start.15 = (bf16[32,1024]{1,0:T(8,128)(2,1)S(1)}, bf16[32,1024]{1,0:T(8,128)(2,1)S(1)}, u32[]{:S(2)}, u32[]{:S(2)}) collective-permute-start(bf16[32,1024]{1,0:T(8,128)(2,1)S(1)} %get-tuple-element.76), channel_id=1, source_target_pairs={{0,2},{1,3},{2,0},{3,1},{4,6},{5,7},{6,4},{7,5},{8,10},{9,11},{10,... | collective-permute-start | bytes 196616 | tf_op jit(solution)/shard_map/ppermute | solution.py:287
  96.3 7.2 %collective-permute-start.16 = (bf16[32,1024]{1,0:T(8,128)(2,1)S(1)}, bf16[32,1024]{1,0:T(8,128)(2,1)S(1)}, u32[]{:S(2)}, u32[]{:S(2)}) collective-permute-start(bf16[32,1024]{1,0:T(8,128)(2,1)S(1)} %get-tuple-element.77), channel_id=1, source_target_pairs={{0,1},{1,0},{2,3},{3,2},{4,5},{5,4},{6,7},{7,6},{8,9},{9,8},{10,11... | collective-permute-start | bytes 196616 | tf_op jit(solution)/shard_map/ppermute | solution.py:287
  101.2 7.2 %collective-permute-start.11 = (bf16[32,1280]{1,0:T(8,128)(2,1)S(1)}, bf16[32,1280]{1,0:T(8,128)(2,1)S(1)}, u32[]{:S(2)}, u32[]{:S(2)}) collective-permute-start(bf16[32,1280]{1,0:T(8,128)(2,1)S(1)} %get-tuple-element.68.refs_0_), channel_id=1, source_target_pairs={{0,2},{1,3},{2,0},{3,1},{4,6},{5,7},{6,4},{7,5},{8,10},{9,11},{10,... | collective-permute-start | bytes 245768 | tf_op jit(solution)/shard_map/ppermute | solution.py:287
  104.2 6.3 %collective-permute-start.18 = (bf16[32,1024]{1,0:T(8,128)(2,1)S(1)}, bf16[32,1024]{1,0:T(8,128)(2,1)S(1)}, u32[]{:S(2)}, u32[]{:S(2)}) collective-permute-start(bf16[32,1024]{1,0:T(8,128)(2,1)S(1)} %get-tuple-element.78.refs_4_), channel_id=1, source_target_pairs={{0,2},{1,3},{2,0},{3,1},{4,6},{5,7},{6,4},{7,5},{8,10},{9,11},{10,... | collective-permute-start | bytes 196616 | tf_op jit(solution)/shard_map/ppermute | solution.py:287
  105.2 8.4 %collective-permute-start.10 = (bf16[32,1280]{1,0:T(8,128)(2,1)S(1)}, bf16[32,1280]{1,0:T(8,128)(2,1)S(1)}, u32[]{:S(2)}, u32[]{:S(2)}) collective-permute-start(bf16[32,1280]{1,0:T(8,128)(2,1)S(1)} %get-tuple-element.68.refs_0_), channel_id=1, source_target_pairs={{0,1},{1,0},{2,3},{3,2},{4,5},{5,4},{6,7},{7,6},{8,9},{9,8},{10,11... | collective-permute-start | bytes 245768 | tf_op jit(solution)/shard_map/ppermute | solution.py:287
  108.4 6.3 %collective-permute-start.12 = (bf16[32,1280]{1,0:T(8,128)(2,1)S(1)}, bf16[32,1280]{1,0:T(8,128)(2,1)S(1)}, u32[]{:S(2)}, u32[]{:S(2)}) collective-permute-start(bf16[32,1280]{1,0:T(8,128)(2,1)S(1)} %collective-permute-done.11.refs_2_), channel_id=1, source_target_pairs={{0,1},{1,0},{2,3},{3,2},{4,5},{5,4},{6,7},{7,6},{8,9},{9,8},{10,11... | collective-permute-start | bytes 245768 | tf_op jit(solution)/shard_map/ppermute | solution.py:287
  108.4 5.2 %collective-permute-start.17 = (bf16[32,1024]{1,0:T(8,128)(2,1)S(1)}, bf16[32,1024]{1,0:T(8,128)(2,1)S(1)}, u32[]{:S(2)}, u32[]{:S(2)}) collective-permute-start(bf16[32,1024]{1,0:T(8,128)(2,1)S(1)} %get-tuple-element.78.refs_4_), channel_id=1, source_target_pairs={{0,1},{1,0},{2,3},{3,2},{4,5},{5,4},{6,7},{7,6},{8,9},{9,8},{10,11... | collective-permute-start | bytes 196616 | tf_op jit(solution)/shard_map/ppermute | solution.py:287
  110.4 4.3 %collective-permute-start.19 = (bf16[32,1024]{1,0:T(8,128)(2,1)S(1)}, bf16[32,1024]{1,0:T(8,128)(2,1)S(1)}, u32[]{:S(2)}, u32[]{:S(2)}) collective-permute-start(bf16[32,1024]{1,0:T(8,128)(2,1)S(1)} %collective-permute-done.18.refs_6_), channel_id=1, source_target_pairs={{0,1},{1,0},{2,3},{3,2},{4,5},{5,4},{6,7},{7,6},{8,9},{9,8},{10,11... | collective-permute-start | bytes 196616 | tf_op jit(solution)/shard_map/ppermute | solution.py:287
  (6 other events, 183.9 us)

commit v14 on v12

--- a/solution.py
+++ b/solution.py
@@ -112,7 +112,8 @@
     def scores(r, i, live, target):
         begin_at = jnp.where(live, lo[r], 0)
         end_at = jnp.where(live, hi[r], 0)
-        s = jnp.dot(q_ref[r], held[i], preferred_element_type=jnp.float32)
+        s = jnp.dot(q_ref[r, :, :C], held[i, :C, :], preferred_element_type=jnp.float32)
+        s = s + jnp.dot(q_ref[r, :, C:], held[i, C:, :], preferred_element_type=jnp.float32)
         token = i * tile + lax.broadcasted_iota(jnp.int32, (1, tile), 1)
         target[...] = s + jnp.where((token >= begin_at) & (token < end_at), 0.0, negative)
 
@@ -546,14 +547,9 @@
     rows = hidden_ref.shape[0]
     own = pl.ds(pl.multiple_of(lax.axis_index("dp") * rows, 16), rows)
     total[own, :] += hidden_ref[...].astype(jnp.float32)
-    groups = width // 128
-    per_rank = out_ref.shape[1] // groups
+    per_rank = out_ref.shape[1]
     for d in range(out_ref.shape[0]):
-        owned = [
-            total[d * per_rank : (d + 1) * per_rank, g * 128 : (g + 1) * 128]
-            for g in range(groups)
-        ]
-        out_ref[d] = jnp.concatenate(owned, 0).astype(out_ref.dtype)
+        out_ref[d] = total[d * per_rank : (d + 1) * per_rank, :].astype(out_ref.dtype)
 
 
 def project_down(chunks, w_down, hidden, ranks):
@@ -562,9 +558,7 @@
     requests = sum(piece.shape[0] for piece in chunks[0])
     return pl.pallas_call(
         functools.partial(down_kernel, len(chunks)),
-        out_shape=jax.ShapeDtypeStruct(
-            (ranks, requests // ranks * (width // 128), 128), jnp.bfloat16
-        ),
+        out_shape=jax.ShapeDtypeStruct((ranks, requests // ranks, width), jnp.bfloat16),
         in_specs=in_vmem(len(pieces) + 2),
         out_specs=pl.BlockSpec(memory_space=pltpu.VMEM),
         scratch_shapes=[
@@ -576,19 +570,13 @@
     )(*pieces, fetched(w_down), hidden)
 
 
-def layer_kernel(parts_ref, out_ref, total):
-    per_rank, model = out_ref.shape
+def layer_kernel(parts_ref, out_ref):
     ranks = lax.axis_size("tp")
-    groups = model // ranks // 128
+    width = parts_ref.shape[2]
     for t in range(ranks):
-        terms = [
-            parts_ref[d, :, :].astype(jnp.float32) for d in range(t, parts_ref.shape[0], ranks)
-        ]
+        terms = [parts_ref[d].astype(jnp.float32) for d in range(t, parts_ref.shape[0], ranks)]
         layer = sum(terms[1:], terms[0])
-        for g in range(groups):
-            at = (t * groups + g) * 128
-            total[:, at : at + 128] = layer[g * per_rank : (g + 1) * per_rank, :]
-    out_ref[...] = total[...].astype(out_ref.dtype)
+        out_ref[:, t * width : (t + 1) * width] = layer.astype(out_ref.dtype)
 
 
 def make_layer(parts, per_rank, model):
@@ -597,7 +585,6 @@
         out_shape=jax.ShapeDtypeStruct((per_rank, model), jnp.bfloat16),
         in_specs=in_vmem(1),
         out_specs=pl.BlockSpec(memory_space=pltpu.VMEM),
-        scratch_shapes=[pltpu.VMEM((per_rank, model), jnp.float32)],
         compiler_params=kernel_params(12),
         name="layer",
     )(parts)

time: 131 us -> 130 us (level)
  no operation moved by 1% of the time
where the time goes in v14:
time: 130 us; the launch traced here: 129 us
  blocking collectives  62.5 us (48%)
  waiting for transfers between devices  28.8 us (22%)
  starting transfers between devices  21.9 us (17%)
  Pallas kernels  15.6 us (12%)
    all_to_all x3, blocking collectives, swap(): return lax.all_to_all(parts, axes, split_axis=0, concat_axis=0, tiled=True)  53.8 us
    ppermute x20, waiting for transfers between devices, from_distance(): lax.ppermute(piece, axis, [(k, k ^ distance) for k in range(lax.axis_size...  28.8 us
    ppermute x20, starting transfers between devices, from_distance(): lax.ppermute(piece, axis, [(k, k ^ distance) for k in range(lax.axis_size...  21.9 us
    all_gather x1, blocking collectives, local(): hidden = lax.all_gather(own_hidden, 'dp', axis=0, tiled=True)  8.78 us
    pallas_call x1, Pallas kernels, attend(): pl.pallas_call(attention_kernel, out_shape=jax.ShapeDtypeStruct((ranks, n...  7.93 us
  transfers between devices with their start and end apart: 20, of which 12 were waited for; matrix products, arithmetic and copies ran while one was open for 0% of the time, Pallas kernels for 3%

profile of v14, /device:TPU:0, one launch (start us, length us, event | category | flops | bytes accessed | tf_op | source)
XLA Modules:
  0.0 129.1 jit_solution(12587199847417312501)
XLA Ops:
  0.0 7.9 %attention.1 = bf16[32,16,512]{2,1,0:T(8,128)(2,1)S(1)} custom-call(s32[128]{0:T(128)} %lens_ref.1, bf16[4,73728]{1,0:T(4,128)(2,1)} %raw_ref.1, bf16[576,14336]{1,0:T(8,128)(2,1)} %bitcast.29), custom_call_target="tpu_custom_call" | custom-call | flops 3992977408 | bytes 16515072 | tf_op jit(solution)/shard_map/attention/pallas_call | solution.py:192
  7.9 25.9 %all_to_all.15 = bf16[32,16,512]{2,1,0:T(8,128)(2,1)S(1)} all-to-all(bf16[32,16,512]{2,1,0:T(8,128)(2,1)S(1)} %attention.1), channel_id=1, replica_groups=mesh['dp'=8,'tp'=4] {'dp','tp'}, dimensions={0} | all-to-all | bytes 1048576 | tf_op jit(solution)/shard_map/all_to_all | solution.py:598
  34.6 2.9 %collective-permute-start.2 = (bf16[128,512]{1,0:T(8,128)(2,1)S(1)}, bf16[128,512]{1,0:T(8,128)(2,1)S(1)}, u32[]{:S(2)}, u32[]{:S(2)}) collective-permute-start(bf16[128,512]{1,0:T(8,128)(2,1)S(1)} %head_values.1.value_ref), channel_id=1, source_target_pairs={{0,3},{1,2},{2,1},{3,0},{4,7},{5,6},{6,5},{7,4},{8,11},{9,10},{10,... | collective-permute-start | bytes 393224 | tf_op jit(solution)/shard_map/ppermute | solution.py:279
  37.5 1.2 collective-permute-start.1
  39.1 1.7 %collective-permute-start.3 = (bf16[4,1792]{1,0:T(4,128)(2,1)S(1)}, bf16[4,1792]{1,0:T(4,128)(2,1)S(1)}, u32[]{:S(2)}, u32[]{:S(2)}) collective-permute-start(bf16[4,1792]{1,0:T(4,128)(2,1)S(1)} %get-tuple-element.45), channel_id=1, source_target_pairs={{0,1},{1,0},{2,3},{3,2},{4,5},{5,4},{6,7},{7,6},{8,9},{9,8},{10,11... | collective-permute-start | bytes 43016 | tf_op jit(solution)/shard_map/ppermute | solution.py:279
  40.8 1.7 %collective-permute-start.4 = (bf16[4,1792]{1,0:T(4,128)(2,1)S(1)}, bf16[4,1792]{1,0:T(4,128)(2,1)S(1)}, u32[]{:S(2)}, u32[]{:S(2)}) collective-permute-start(bf16[4,1792]{1,0:T(4,128)(2,1)S(1)} %get-tuple-element.46), channel_id=1, source_target_pairs={{0,2},{1,3},{2,0},{3,1},{4,6},{5,7},{6,4},{7,5},{8,10},{9,11},{10,... | collective-permute-start | bytes 43016 | tf_op jit(solution)/shard_map/ppermute | solution.py:279
  42.8 2.9 %collective-permute-start.5 = (bf16[4,1792]{1,0:T(4,128)(2,1)S(1)}, bf16[4,1792]{1,0:T(4,128)(2,1)S(1)}, u32[]{:S(2)}, u32[]{:S(2)}) collective-permute-start(bf16[4,1792]{1,0:T(4,128)(2,1)S(1)} %get-tuple-element.47), channel_id=1, source_target_pairs={{0,3},{1,2},{2,1},{3,0},{4,7},{5,6},{6,5},{7,4},{8,11},{9,10},{10,... | collective-permute-start | bytes 43016 | tf_op jit(solution)/shard_map/ppermute | solution.py:279
  46.2 4.6 %collective-permute-done.1.refs_2_ = bf16[128,512]{1,0:T(8,128)(2,1)S(1)} collective-permute-done((bf16[128,512]{1,0:T(8,128)(2,1)S(1)}, bf16[128,512]{1,0:T(8,128)(2,1)S(1)}, u32[]{:S(2)}, u32[]{:S(2)}) %collective-permute-start.1) | collective-permute-done | bytes 131104 | tf_op jit(solution)/shard_map/ppermute | solution.py:279
  51.8 11.6 %all_to_all.16.parts_ref = bf16[8,16,1792]{2,1,0:T(8,128)(2,1)S(1)} all-to-all(bf16[8,16,1792]{2,1,0:T(8,128)(2,1)S(1)} %bitcast.19), channel_id=1, replica_groups=mesh['dp'=8,'tp'=4] {'dp'}, dimensions={0} | all-to-all | bytes 917504 | tf_op jit(solution)/shard_map/all_to_all | solution.py:598
  63.4 8.8 %all_gather.3.hidden_ref = bf16[128,1792]{1,0:T(8,128)(2,1)S(1)} all-gather(bf16[16,1792]{1,0:T(8,128)(2,1)S(1)} %hidden.1.refs_9_), channel_id=1, replica_groups=mesh['dp'=8,'tp'=4] {'dp'}, dimensions={0}, use_global_device_ids=true | all-gather | bytes 516096 | tf_op jit(solution)/shard_map/all_gather | solution.py:624
  72.2 1.4 %gate_up.1 = (bf16[2,128,1792]{2,1,0:T(8,128)(2,1)S(1)}, bf16[64,1408]{1,0:T(8,128)(2,1)S(1)}, bf16[64,1280]{1,0:T(8,128)(2,1)S(1)}, bf16[64,1408]{1,0:T(8,128)(2,1)S(1)}, bf16[64,1280]{1,0:T(8,128)(2,1)S(1)}) custom-call(bf16[128,1792]{1,0:T(8,128)(2,1)S(1)} %all_gather.3.hidden_ref, bf16[56,128]{1,0:T(8,128)(2,1)S(1)} %bitcast.28, ...), custom_call_target="tpu_custom_call" | custom-call | flops 1174405120 | bytes 9175040 | tf_op jit(solution)/shard_map/gate_up/pallas_call | solution.py:434
  74.6 1.5 %collective-permute-start.7 = (bf16[64,1280]{1,0:T(8,128)(2,1)S(1)}, bf16[64,1280]{1,0:T(8,128)(2,1)S(1)}, u32[]{:S(2)}, u32[]{:S(2)}) collective-permute-start(bf16[64,1280]{1,0:T(8,128)(2,1)S(1)} %get-tuple-element.63), channel_id=1, source_target_pairs={{0,2},{1,3},{2,0},{3,1},{4,6},{5,7},{6,4},{7,5},{8,10},{9,11},{10,... | collective-permute-start | bytes 491528 | tf_op jit(solution)/shard_map/ppermute | solution.py:279
  77.7 2.1 %collective-permute-start.14 = (bf16[64,1024]{1,0:T(8,128)(2,1)S(1)}, bf16[64,1024]{1,0:T(8,128)(2,1)S(1)}, u32[]{:S(2)}, u32[]{:S(2)}) collective-permute-start(bf16[64,1024]{1,0:T(8,128)(2,1)S(1)} %get-tuple-element.73), channel_id=1, source_target_pairs={{0,2},{1,3},{2,0},{3,1},{4,6},{5,7},{6,4},{7,5},{8,10},{9,11},{10,... | collective-permute-start | bytes 393224 | tf_op jit(solution)/shard_map/ppermute | solution.py:279
  79.9 6.3 %collective-permute-done.7.refs_3_ = bf16[64,1280]{1,0:T(8,128)(2,1)S(1)} collective-permute-done((bf16[64,1280]{1,0:T(8,128)(2,1)S(1)}, bf16[64,1280]{1,0:T(8,128)(2,1)S(1)}, u32[]{:S(2)}, u32[]{:S(2)}) %collective-permute-start.7) | collective-permute-done | bytes 163872 | tf_op jit(solution)/shard_map/ppermute | solution.py:279
  87.5 1.9 %collective-permute-done.13.refs_2_ = bf16[64,1024]{1,0:T(8,128)(2,1)S(1)} collective-permute-done((bf16[64,1024]{1,0:T(8,128)(2,1)S(1)}, bf16[64,1024]{1,0:T(8,128)(2,1)S(1)}, u32[]{:S(2)}, u32[]{:S(2)}) %collective-permute-start.13) | collective-permute-done | bytes 131104 | tf_op jit(solution)/shard_map/ppermute | solution.py:279
  89.4 4.7 %collective-permute-done.14.refs_3_ = bf16[64,1024]{1,0:T(8,128)(2,1)S(1)} collective-permute-done((bf16[64,1024]{1,0:T(8,128)(2,1)S(1)}, bf16[64,1024]{1,0:T(8,128)(2,1)S(1)}, u32[]{:S(2)}, u32[]{:S(2)}) %collective-permute-start.14) | collective-permute-done | bytes 131104 | tf_op jit(solution)/shard_map/ppermute | solution.py:279
  94.4 2.5 %collective-permute-done.8 = bf16[32,1408]{1,0:T(8,128)(2,1)S(1)} collective-permute-done((bf16[32,1408]{1,0:T(8,128)(2,1)S(1)}, bf16[32,1408]{1,0:T(8,128)(2,1)S(1)}, u32[]{:S(2)}, u32[]{:S(2)}) %collective-permute-start.8) | collective-permute-done | bytes 90144 | tf_op jit(solution)/shard_map/ppermute | solution.py:279
  97.4 2.6 %collective-permute-done.15 = bf16[32,1024]{1,0:T(8,128)(2,1)S(1)} collective-permute-done((bf16[32,1024]{1,0:T(8,128)(2,1)S(1)}, bf16[32,1024]{1,0:T(8,128)(2,1)S(1)}, u32[]{:S(2)}, u32[]{:S(2)}) %collective-permute-start.15) | collective-permute-done | bytes 65568 | tf_op jit(solution)/shard_map/ppermute | solution.py:279
  100.8 1.8 %collective-permute-start.18 = (bf16[32,1024]{1,0:T(8,128)(2,1)S(1)}, bf16[32,1024]{1,0:T(8,128)(2,1)S(1)}, u32[]{:S(2)}, u32[]{:S(2)}) collective-permute-start(bf16[32,1024]{1,0:T(8,128)(2,1)S(1)} %get-tuple-element.78.refs_4_), channel_id=1, source_target_pairs={{0,2},{1,3},{2,0},{3,1},{4,6},{5,7},{6,4},{7,5},{8,10},{9,11},{10,... | collective-permute-start | bytes 196616 | tf_op jit(solution)/shard_map/ppermute | solution.py:279
  102.6 1.3 collective-permute-done.11.refs_2_
  104.6 1.3 collective-permute-start.17
  106.7 2.8 %collective-permute-done.17.refs_5_ = bf16[32,1024]{1,0:T(8,128)(2,1)S(1)} collective-permute-done((bf16[32,1024]{1,0:T(8,128)(2,1)S(1)}, bf16[32,1024]{1,0:T(8,128)(2,1)S(1)}, u32[]{:S(2)}, u32[]{:S(2)}) %collective-permute-start.17) | collective-permute-done | bytes 65568 | tf_op jit(solution)/shard_map/ppermute | solution.py:279
  110.6 1.4 %project_down.1 = bf16[32,4,1792]{2,1,0:T(4,128)(2,1)S(1)} custom-call(bf16[32,1280]{1,0:T(8,128)(2,1)S(1)} %get-tuple-element.68.refs_0_, bf16[32,1280]{1,0:T(8,128)(2,1)S(1)} %collective-permute-done.10.refs_1_, bf16[32,1280]{1,0:T(8,128)(2,1)S(1)} %collective-permute-done.11.refs_2_, bf16[32,1280]{1,0:T(8,128)(2,1)S(1)} %collective-permute-done.12.refs_3_, ...), custom_call_target="tpu_custom_call" | custom-call | tf_op jit(solution)/shard_map/project_down/pallas_call | solution.py:559
  112.1 16.3 %all_to_all.17.parts_ref = bf16[32,4,1792]{2,1,0:T(4,128)(2,1)S(1)} all-to-all(bf16[32,4,1792]{2,1,0:T(4,128)(2,1)S(1)} %project_down.1), channel_id=1, replica_groups=mesh['dp'=8,'tp'=4] {'dp','tp'}, dimensions={0} | all-to-all | bytes 917504 | tf_op jit(solution)/shard_map/all_to_all | solution.py:598
  (57 shorter events, 11.7 us)
Async XLA Ops:
  0.0 39.1 %copy-start.2 = (bf16[4,7168]{1,0:T(4,128)(2,1)S(1)}, bf16[4,7168]{1,0:T(4,128)(2,1)}, u32[]{:S(2)}) copy-start(bf16[4,7168]{1,0:T(4,128)(2,1)} %rows_ref) | copy-start | bytes 172036
  0.0 45.8 %copy-start = (bf16[2048,1792]{1,0:T(8,128)(2,1)S(1)}, bf16[2048,1792]{1,0:T(8,128)(2,1)}, u32[]{:S(2)}) copy-start(bf16[2048,1792]{1,0:T(8,128)(2,1)} %refs_4_.1) | copy-start | bytes 22020100
  0.0 72.2 %slice-start.2 = ((s8[8257536]{0:T(1024)(128)(4,1)}), s8[4194304]{0:T(1024)(128)(4,1)S(1)}, s32[]{:S(2)}) async-start(s8[8257536]{0:T(1024)(128)(4,1)} %bitcast.14), calls=%async_computation.5 | async-start | bytes 8388608
  34.6 8.2 %collective-permute-start.2 = (bf16[128,512]{1,0:T(8,128)(2,1)S(1)}, bf16[128,512]{1,0:T(8,128)(2,1)S(1)}, u32[]{:S(2)}, u32[]{:S(2)}) collective-permute-start(bf16[128,512]{1,0:T(8,128)(2,1)S(1)} %head_values.1.value_ref), channel_id=1, source_target_pairs={{0,3},{1,2},{2,1},{3,0},{4,7},{5,6},{6,5},{7,4},{8,11},{9,10},{10,... | collective-permute-start | bytes 393224 | tf_op jit(solution)/shard_map/ppermute | solution.py:279
  37.5 13.3 %collective-permute-start.1 = (bf16[128,512]{1,0:T(8,128)(2,1)S(1)}, bf16[128,512]{1,0:T(8,128)(2,1)S(1)}, u32[]{:S(2)}, u32[]{:S(2)}) collective-permute-start(bf16[128,512]{1,0:T(8,128)(2,1)S(1)} %head_values.1.value_ref), channel_id=1, source_target_pairs={{0,2},{1,3},{2,0},{3,1},{4,6},{5,7},{6,4},{7,5},{8,10},{9,11},{10,... | collective-permute-start | bytes 393224 | tf_op jit(solution)/shard_map/ppermute | solution.py:279
  38.7 12.1 %collective-permute-start = (bf16[128,512]{1,0:T(8,128)(2,1)S(1)}, bf16[128,512]{1,0:T(8,128)(2,1)S(1)}, u32[]{:S(2)}, u32[]{:S(2)}) collective-permute-start(bf16[128,512]{1,0:T(8,128)(2,1)S(1)} %head_values.1.value_ref), channel_id=1, source_target_pairs={{0,1},{1,0},{2,3},{3,2},{4,5},{5,4},{6,7},{7,6},{8,9},{9,8},{10,11... | collective-permute-start | bytes 393224 | tf_op jit(solution)/shard_map/ppermute | solution.py:279
  39.1 12.6 %collective-permute-start.3 = (bf16[4,1792]{1,0:T(4,128)(2,1)S(1)}, bf16[4,1792]{1,0:T(4,128)(2,1)S(1)}, u32[]{:S(2)}, u32[]{:S(2)}) collective-permute-start(bf16[4,1792]{1,0:T(4,128)(2,1)S(1)} %get-tuple-element.45), channel_id=1, source_target_pairs={{0,1},{1,0},{2,3},{3,2},{4,5},{5,4},{6,7},{7,6},{8,9},{9,8},{10,11... | collective-permute-start | bytes 43016 | tf_op jit(solution)/shard_map/ppermute | solution.py:279
  40.8 10.9 %collective-permute-start.4 = (bf16[4,1792]{1,0:T(4,128)(2,1)S(1)}, bf16[4,1792]{1,0:T(4,128)(2,1)S(1)}, u32[]{:S(2)}, u32[]{:S(2)}) collective-permute-start(bf16[4,1792]{1,0:T(4,128)(2,1)S(1)} %get-tuple-element.46), channel_id=1, source_target_pairs={{0,2},{1,3},{2,0},{3,1},{4,6},{5,7},{6,4},{7,5},{8,10},{9,11},{10,... | collective-permute-start | bytes 43016 | tf_op jit(solution)/shard_map/ppermute | solution.py:279
  42.8 8.9 %collective-permute-start.5 = (bf16[4,1792]{1,0:T(4,128)(2,1)S(1)}, bf16[4,1792]{1,0:T(4,128)(2,1)S(1)}, u32[]{:S(2)}, u32[]{:S(2)}) collective-permute-start(bf16[4,1792]{1,0:T(4,128)(2,1)S(1)} %get-tuple-element.47), channel_id=1, source_target_pairs={{0,3},{1,2},{2,1},{3,0},{4,7},{5,6},{6,5},{7,4},{8,11},{9,10},{10,... | collective-permute-start | bytes 43016 | tf_op jit(solution)/shard_map/ppermute | solution.py:279
  72.2 38.4 %slice-start.4 = ((s8[8257536]{0:T(1024)(128)(4,1)}), s8[4194304]{0:T(1024)(128)(4,1)S(1)}, s32[]{:S(2)}) async-start(s8[8257536]{0:T(1024)(128)(4,1)} %bitcast.16), calls=%async_computation.7 | async-start | bytes 8388608
  73.6 12.5 %collective-permute-start.6 = (bf16[64,1408]{1,0:T(8,128)(2,1)S(1)}, bf16[64,1408]{1,0:T(8,128)(2,1)S(1)}, u32[]{:S(2)}, u32[]{:S(2)}) collective-permute-start(bf16[64,1408]{1,0:T(8,128)(2,1)S(1)} %get-tuple-element.62), channel_id=1, source_target_pairs={{0,1},{1,0},{2,3},{3,2},{4,5},{5,4},{6,7},{7,6},{8,9},{9,8},{10,11... | collective-permute-start | bytes 540680 | tf_op jit(solution)/shard_map/ppermute | solution.py:279
  74.6 11.6 %collective-permute-start.7 = (bf16[64,1280]{1,0:T(8,128)(2,1)S(1)}, bf16[64,1280]{1,0:T(8,128)(2,1)S(1)}, u32[]{:S(2)}, u32[]{:S(2)}) collective-permute-start(bf16[64,1280]{1,0:T(8,128)(2,1)S(1)} %get-tuple-element.63), channel_id=1, source_target_pairs={{0,2},{1,3},{2,0},{3,1},{4,6},{5,7},{6,4},{7,5},{8,10},{9,11},{10,... | collective-permute-start | bytes 491528 | tf_op jit(solution)/shard_map/ppermute | solution.py:279
  77.2 12.2 %collective-permute-start.13 = (bf16[64,1024]{1,0:T(8,128)(2,1)S(1)}, bf16[64,1024]{1,0:T(8,128)(2,1)S(1)}, u32[]{:S(2)}, u32[]{:S(2)}) collective-permute-start(bf16[64,1024]{1,0:T(8,128)(2,1)S(1)} %get-tuple-element.72), channel_id=1, source_target_pairs={{0,1},{1,0},{2,3},{3,2},{4,5},{5,4},{6,7},{7,6},{8,9},{9,8},{10,11... | collective-permute-start | bytes 393224 | tf_op jit(solution)/shard_map/ppermute | solution.py:279
  77.7 16.4 %collective-permute-start.14 = (bf16[64,1024]{1,0:T(8,128)(2,1)S(1)}, bf16[64,1024]{1,0:T(8,128)(2,1)S(1)}, u32[]{:S(2)}, u32[]{:S(2)}) collective-permute-start(bf16[64,1024]{1,0:T(8,128)(2,1)S(1)} %get-tuple-element.73), channel_id=1, source_target_pairs={{0,2},{1,3},{2,0},{3,1},{4,6},{5,7},{6,4},{7,5},{8,10},{9,11},{10,... | collective-permute-start | bytes 393224 | tf_op jit(solution)/shard_map/ppermute | solution.py:279
  86.3 10.6 %collective-permute-start.8 = (bf16[32,1408]{1,0:T(8,128)(2,1)S(1)}, bf16[32,1408]{1,0:T(8,128)(2,1)S(1)}, u32[]{:S(2)}, u32[]{:S(2)}) collective-permute-start(bf16[32,1408]{1,0:T(8,128)(2,1)S(1)} %get-tuple-element.66), channel_id=1, source_target_pairs={{0,2},{1,3},{2,0},{3,1},{4,6},{5,7},{6,4},{7,5},{8,10},{9,11},{10,... | collective-permute-start | bytes 270344 | tf_op jit(solution)/shard_map/ppermute | solution.py:279
  86.5 7.8 %collective-permute-start.9 = (bf16[32,1280]{1,0:T(8,128)(2,1)S(1)}, bf16[32,1280]{1,0:T(8,128)(2,1)S(1)}, u32[]{:S(2)}, u32[]{:S(2)}) collective-permute-start(bf16[32,1280]{1,0:T(8,128)(2,1)S(1)} %get-tuple-element.67), channel_id=1, source_target_pairs={{0,1},{1,0},{2,3},{3,2},{4,5},{5,4},{6,7},{7,6},{8,9},{9,8},{10,11... | collective-permute-start | bytes 245768 | tf_op jit(solution)/shard_map/ppermute | solution.py:279
  94.2 5.9 %collective-permute-start.15 = (bf16[32,1024]{1,0:T(8,128)(2,1)S(1)}, bf16[32,1024]{1,0:T(8,128)(2,1)S(1)}, u32[]{:S(2)}, u32[]{:S(2)}) collective-permute-start(bf16[32,1024]{1,0:T(8,128)(2,1)S(1)} %get-tuple-element.76), channel_id=1, source_target_pairs={{0,2},{1,3},{2,0},{3,1},{4,6},{5,7},{6,4},{7,5},{8,10},{9,11},{10,... | collective-permute-start | bytes 196616 | tf_op jit(solution)/shard_map/ppermute | solution.py:279
  94.3 5.9 %collective-permute-start.16 = (bf16[32,1024]{1,0:T(8,128)(2,1)S(1)}, bf16[32,1024]{1,0:T(8,128)(2,1)S(1)}, u32[]{:S(2)}, u32[]{:S(2)}) collective-permute-start(bf16[32,1024]{1,0:T(8,128)(2,1)S(1)} %get-tuple-element.77), channel_id=1, source_target_pairs={{0,1},{1,0},{2,3},{3,2},{4,5},{5,4},{6,7},{7,6},{8,9},{9,8},{10,11... | collective-permute-start | bytes 196616 | tf_op jit(solution)/shard_map/ppermute | solution.py:279
  97.0 6.9 %collective-permute-start.11 = (bf16[32,1280]{1,0:T(8,128)(2,1)S(1)}, bf16[32,1280]{1,0:T(8,128)(2,1)S(1)}, u32[]{:S(2)}, u32[]{:S(2)}) collective-permute-start(bf16[32,1280]{1,0:T(8,128)(2,1)S(1)} %get-tuple-element.68.refs_0_), channel_id=1, source_target_pairs={{0,2},{1,3},{2,0},{3,1},{4,6},{5,7},{6,4},{7,5},{8,10},{9,11},{10,... | collective-permute-start | bytes 245768 | tf_op jit(solution)/shard_map/ppermute | solution.py:279
  100.8 5.6 %collective-permute-start.18 = (bf16[32,1024]{1,0:T(8,128)(2,1)S(1)}, bf16[32,1024]{1,0:T(8,128)(2,1)S(1)}, u32[]{:S(2)}, u32[]{:S(2)}) collective-permute-start(bf16[32,1024]{1,0:T(8,128)(2,1)S(1)} %get-tuple-element.78.refs_4_), channel_id=1, source_target_pairs={{0,2},{1,3},{2,0},{3,1},{4,6},{5,7},{6,4},{7,5},{8,10},{9,11},{10,... | collective-permute-start | bytes 196616 | tf_op jit(solution)/shard_map/ppermute | solution.py:279
  102.6 6.9 %collective-permute-start.10 = (bf16[32,1280]{1,0:T(8,128)(2,1)S(1)}, bf16[32,1280]{1,0:T(8,128)(2,1)S(1)}, u32[]{:S(2)}, u32[]{:S(2)}) collective-permute-start(bf16[32,1280]{1,0:T(8,128)(2,1)S(1)} %get-tuple-element.68.refs_0_), channel_id=1, source_target_pairs={{0,1},{1,0},{2,3},{3,2},{4,5},{5,4},{6,7},{7,6},{8,9},{9,8},{10,11... | collective-permute-start | bytes 245768 | tf_op jit(solution)/shard_map/ppermute | solution.py:279
  103.9 6.7 %collective-permute-start.12 = (bf16[32,1280]{1,0:T(8,128)(2,1)S(1)}, bf16[32,1280]{1,0:T(8,128)(2,1)S(1)}, u32[]{:S(2)}, u32[]{:S(2)}) collective-permute-start(bf16[32,1280]{1,0:T(8,128)(2,1)S(1)} %collective-permute-done.11.refs_2_), channel_id=1, source_target_pairs={{0,1},{1,0},{2,3},{3,2},{4,5},{5,4},{6,7},{7,6},{8,9},{9,8},{10,11... | collective-permute-start | bytes 245768 | tf_op jit(solution)/shard_map/ppermute | solution.py:279
  104.6 4.8 %collective-permute-start.17 = (bf16[32,1024]{1,0:T(8,128)(2,1)S(1)}, bf16[32,1024]{1,0:T(8,128)(2,1)S(1)}, u32[]{:S(2)}, u32[]{:S(2)}) collective-permute-start(bf16[32,1024]{1,0:T(8,128)(2,1)S(1)} %get-tuple-element.78.refs_4_), channel_id=1, source_target_pairs={{0,1},{1,0},{2,3},{3,2},{4,5},{5,4},{6,7},{7,6},{8,9},{9,8},{10,11... | collective-permute-start | bytes 196616 | tf_op jit(solution)/shard_map/ppermute | solution.py:279
  106.4 4.3 %collective-permute-start.19 = (bf16[32,1024]{1,0:T(8,128)(2,1)S(1)}, bf16[32,1024]{1,0:T(8,128)(2,1)S(1)}, u32[]{:S(2)}, u32[]{:S(2)}) collective-permute-start(bf16[32,1024]{1,0:T(8,128)(2,1)S(1)} %collective-permute-done.18.refs_6_), channel_id=1, source_target_pairs={{0,1},{1,0},{2,3},{3,2},{4,5},{5,4},{6,7},{7,6},{8,9},{9,8},{10,11... | collective-permute-start | bytes 196616 | tf_op jit(solution)/shard_map/ppermute | solution.py:279
  (6 other events, 191.6 us)

commit v15 on v13

--- a/solution.py
+++ b/solution.py
@@ -122,8 +122,8 @@
         (r0, i0), (r1, i1, live1), (r2, i2, live2) = before, now, after
         weights0, keeps0, masses0 = used
         weights1, keeps1, masses1 = made
-        values = gather(i0, weights0)
-        ahead = scores(r2, i2, live2)
+        acc[...] = acc[...] * keeps0[:1, :] + gather(i0, weights0)
+        found[...] = scores(r2, i2, live2)
 
         s = given[...]
         old = jnp.where(live1 & (i1 == first[r1]), negative, best[...])
@@ -134,8 +134,6 @@
         for at in range(128, tile, 128):
             part = part + weight[:, at : at + 128]
 
-        acc[...] = acc[...] * keeps0[:1, :] + values
-        found[...] = ahead
         weights1[...] = weight.T.astype(weights1.dtype)
         keeps1[...] = keep.T[:8, :]
         masses1[...] = masses0[...] * keep + part
@@ -640,9 +638,14 @@
 
     values = head_values(latent.reshape(requests * heads_here, C), w_uv)
     values, residual = lax.optimization_barrier((values, residual))
-    values = from_all(values, "tp")
     added = list(split_columns(residual, ranks_tp))
     added = added[:1] + [from_distance(added[k], "tp", k) for k in range(1, ranks_tp)]
+    if ranks_tp == 4:
+        far, added = lax.optimization_barrier((from_distance(values, "tp", 2), added))
+        near = from_distance(values, "tp", 1)
+        values = [values, near, far, from_distance(far, "tp", 1)]
+    else:
+        values = from_all(values, "tp")
     attn, added = lax.optimization_barrier((project_out(values, w_o), added))
     attn = swap(attn.reshape(ranks_dp, requests // ranks_dp, width), "dp")
     own_hidden = make_hidden(attn, added)

time: 135 us -> 133 us (0.985); the launches traced: 133 us -> 134 us
  starting transfers between devices: 29.2 us -> 18 us
  waiting for transfers between devices: 21.6 us -> 32.8 us
    ppermute x20, waiting for transfers between devices: 21.6 us -> 32.8 us  [from_distance(): lax.ppermute(piece, axis, [(k, k ^ distance) for k in range(lax.axis_size...]
    ppermute x20, starting transfers between devices: 29.2 us -> 18 us  [from_distance(): lax.ppermute(piece, axis, [(k, k ^ distance) for k in range(lax.axis_size...]
  transfers between devices with their start and end apart: 20 -> 20, of which waited for: 10 -> 14; matrix products, arithmetic and copies ran while one was open for 0% -> 0% of each run, Pallas kernels for 3% -> 2%
where the time goes in v15:
time: 133 us; the launch traced here: 134 us
  blocking collectives  66.5 us (50%)
  waiting for transfers between devices  32.8 us (25%)
  starting transfers between devices  18 us (14%)
  Pallas kernels  16.5 us (12%)
    all_to_all x3, blocking collectives, swap(): return lax.all_to_all(parts, axes, split_axis=0, concat_axis=0, tiled=True)  57.7 us
    ppermute x20, waiting for transfers between devices, from_distance(): lax.ppermute(piece, axis, [(k, k ^ distance) for k in range(lax.axis_size...  32.8 us
    ppermute x20, starting transfers between devices, from_distance(): lax.ppermute(piece, axis, [(k, k ^ distance) for k in range(lax.axis_size...  18 us
    all_gather x1, blocking collectives, local(): hidden = lax.all_gather(own_hidden, 'dp', axis=0, tiled=True)  8.78 us
    pallas_call x1, Pallas kernels, attend(): pl.pallas_call(attention_kernel, out_shape=jax.ShapeDtypeStruct((ranks, n...  8.75 us
  transfers between devices with their start and end apart: 20, of which 14 were waited for; matrix products, arithmetic and copies ran while one was open for 0% of the time, Pallas kernels for 2%

profile of v15, /device:TPU:0, one launch (start us, length us, event | category | flops | bytes accessed | tf_op | source)
XLA Modules:
  0.0 134.0 jit_solution(17630894778056998879)
XLA Ops:
  0.0 8.8 %attention.1 = bf16[32,16,512]{2,1,0:T(8,128)(2,1)S(1)} custom-call(s32[128]{0:T(128)} %lens_ref.1, bf16[4,73728]{1,0:T(4,128)(2,1)} %raw_ref.1, bf16[576,14336]{1,0:T(8,128)(2,1)} %bitcast.29), custom_call_target="tpu_custom_call" | custom-call | flops 3992977408 | bytes 16515072 | tf_op jit(solution)/shard_map/attention/pallas_call | solution.py:197
  8.8 30.1 %all_to_all.15 = bf16[32,16,512]{2,1,0:T(8,128)(2,1)S(1)} all-to-all(bf16[32,16,512]{2,1,0:T(8,128)(2,1)S(1)} %attention.1), channel_id=1, replica_groups=mesh['dp'=8,'tp'=4] {'dp','tp'}, dimensions={0} | all-to-all | bytes 1048576 | tf_op jit(solution)/shard_map/all_to_all | solution.py:621
  39.7 1.9 %collective-permute-start.1 = (bf16[128,512]{1,0:T(8,128)(2,1)S(1)}, bf16[128,512]{1,0:T(8,128)(2,1)S(1)}, u32[]{:S(2)}, u32[]{:S(2)}) collective-permute-start(bf16[128,512]{1,0:T(8,128)(2,1)S(1)} %head_values.1.value_ref), channel_id=1, source_target_pairs={{0,2},{1,3},{2,0},{3,1},{4,6},{5,7},{6,4},{7,5},{8,10},{9,11},{10,... | collective-permute-start | bytes 393224 | tf_op jit(solution)/shard_map/ppermute | solution.py:285
  41.6 1.6 %collective-permute-start.2 = (bf16[4,1792]{1,0:T(4,128)(2,1)S(1)}, bf16[4,1792]{1,0:T(4,128)(2,1)S(1)}, u32[]{:S(2)}, u32[]{:S(2)}) collective-permute-start(bf16[4,1792]{1,0:T(4,128)(2,1)S(1)} %get-tuple-element.50), channel_id=1, source_target_pairs={{0,1},{1,0},{2,3},{3,2},{4,5},{5,4},{6,7},{7,6},{8,9},{9,8},{10,11... | collective-permute-start | bytes 43016 | tf_op jit(solution)/shard_map/ppermute | solution.py:285
  43.2 2.1 %collective-permute-start.3 = (bf16[4,1792]{1,0:T(4,128)(2,1)S(1)}, bf16[4,1792]{1,0:T(4,128)(2,1)S(1)}, u32[]{:S(2)}, u32[]{:S(2)}) collective-permute-start(bf16[4,1792]{1,0:T(4,128)(2,1)S(1)} %get-tuple-element.51), channel_id=1, source_target_pairs={{0,2},{1,3},{2,0},{3,1},{4,6},{5,7},{6,4},{7,5},{8,10},{9,11},{10,... | collective-permute-start | bytes 43016 | tf_op jit(solution)/shard_map/ppermute | solution.py:285
  46.7 3.7 %collective-permute-done.3.refs_2_ = bf16[4,1792]{1,0:T(4,128)(2,1)S(1)} collective-permute-done((bf16[4,1792]{1,0:T(4,128)(2,1)S(1)}, bf16[4,1792]{1,0:T(4,128)(2,1)S(1)}, u32[]{:S(2)}, u32[]{:S(2)}) %collective-permute-start.3) | collective-permute-done | bytes 14368 | tf_op jit(solution)/shard_map/ppermute | solution.py:285
  51.7 1.4 %collective-permute-done.refs_1_ = bf16[128,512]{1,0:T(8,128)(2,1)S(1)} collective-permute-done((bf16[128,512]{1,0:T(8,128)(2,1)S(1)}, bf16[128,512]{1,0:T(8,128)(2,1)S(1)}, u32[]{:S(2)}, u32[]{:S(2)}) %collective-permute-start) | collective-permute-done | bytes 131104 | tf_op jit(solution)/shard_map/ppermute | solution.py:285
  53.2 2.8 %collective-permute-done.5.refs_3_ = bf16[128,512]{1,0:T(8,128)(2,1)S(1)} collective-permute-done((bf16[128,512]{1,0:T(8,128)(2,1)S(1)}, bf16[128,512]{1,0:T(8,128)(2,1)S(1)}, u32[]{:S(2)}, u32[]{:S(2)}) %collective-permute-start.5) | collective-permute-done | bytes 131104 | tf_op jit(solution)/shard_map/ppermute | solution.py:285
  56.9 11.9 %all_to_all.16.parts_ref = bf16[8,16,1792]{2,1,0:T(8,128)(2,1)S(1)} all-to-all(bf16[8,16,1792]{2,1,0:T(8,128)(2,1)S(1)} %bitcast.19), channel_id=1, replica_groups=mesh['dp'=8,'tp'=4] {'dp'}, dimensions={0} | all-to-all | bytes 917504 | tf_op jit(solution)/shard_map/all_to_all | solution.py:621
  68.9 8.8 %all_gather.3.hidden_ref = bf16[128,1792]{1,0:T(8,128)(2,1)S(1)} all-gather(bf16[16,1792]{1,0:T(8,128)(2,1)S(1)} %hidden.1.refs_9_), channel_id=1, replica_groups=mesh['dp'=8,'tp'=4] {'dp'}, dimensions={0}, use_global_device_ids=true | all-gather | bytes 516096 | tf_op jit(solution)/shard_map/all_gather | solution.py:652
  77.7 1.4 %gate_up.1 = (bf16[2,128,1792]{2,1,0:T(8,128)(2,1)S(1)}, bf16[64,1408]{1,0:T(8,128)(2,1)S(1)}, bf16[64,1280]{1,0:T(8,128)(2,1)S(1)}, bf16[64,1408]{1,0:T(8,128)(2,1)S(1)}, bf16[64,1280]{1,0:T(8,128)(2,1)S(1)}) custom-call(bf16[128,1792]{1,0:T(8,128)(2,1)S(1)} %all_gather.3.hidden_ref, bf16[56,128]{1,0:T(8,128)(2,1)S(1)} %bitcast.28, ...), custom_call_target="tpu_custom_call" | custom-call | flops 1174405120 | bytes 9175040 | tf_op jit(solution)/shard_map/gate_up/pallas_call | solution.py:443
  81.0 1.1 gate_up_rest.1
  82.7 2.6 %collective-permute-start.14 = (bf16[64,1024]{1,0:T(8,128)(2,1)S(1)}, bf16[64,1024]{1,0:T(8,128)(2,1)S(1)}, u32[]{:S(2)}, u32[]{:S(2)}) collective-permute-start(bf16[64,1024]{1,0:T(8,128)(2,1)S(1)} %get-tuple-element.83), channel_id=1, source_target_pairs={{0,2},{1,3},{2,0},{3,1},{4,6},{5,7},{6,4},{7,5},{8,10},{9,11},{10,... | collective-permute-start | bytes 393224 | tf_op jit(solution)/shard_map/ppermute | solution.py:285
  85.3 6.2 %collective-permute-done.7.refs_3_ = bf16[64,1280]{1,0:T(8,128)(2,1)S(1)} collective-permute-done((bf16[64,1280]{1,0:T(8,128)(2,1)S(1)}, bf16[64,1280]{1,0:T(8,128)(2,1)S(1)}, u32[]{:S(2)}, u32[]{:S(2)}) %collective-permute-start.7) | collective-permute-done | bytes 163872 | tf_op jit(solution)/shard_map/ppermute | solution.py:285
  92.5 2.0 %collective-permute-done.13.refs_2_ = bf16[64,1024]{1,0:T(8,128)(2,1)S(1)} collective-permute-done((bf16[64,1024]{1,0:T(8,128)(2,1)S(1)}, bf16[64,1024]{1,0:T(8,128)(2,1)S(1)}, u32[]{:S(2)}, u32[]{:S(2)}) %collective-permute-start.13) | collective-permute-done | bytes 131104 | tf_op jit(solution)/shard_map/ppermute | solution.py:285
  94.4 5.3 %collective-permute-done.14.refs_3_ = bf16[64,1024]{1,0:T(8,128)(2,1)S(1)} collective-permute-done((bf16[64,1024]{1,0:T(8,128)(2,1)S(1)}, bf16[64,1024]{1,0:T(8,128)(2,1)S(1)}, u32[]{:S(2)}, u32[]{:S(2)}) %collective-permute-start.14) | collective-permute-done | bytes 131104 | tf_op jit(solution)/shard_map/ppermute | solution.py:285
  100.0 2.0 %collective-permute-done.8 = bf16[32,1408]{1,0:T(8,128)(2,1)S(1)} collective-permute-done((bf16[32,1408]{1,0:T(8,128)(2,1)S(1)}, bf16[32,1408]{1,0:T(8,128)(2,1)S(1)}, u32[]{:S(2)}, u32[]{:S(2)}) %collective-permute-start.8) | collective-permute-done | bytes 90144 | tf_op jit(solution)/shard_map/ppermute | solution.py:285
  103.1 2.4 %collective-permute-done.15 = bf16[32,1024]{1,0:T(8,128)(2,1)S(1)} collective-permute-done((bf16[32,1024]{1,0:T(8,128)(2,1)S(1)}, bf16[32,1024]{1,0:T(8,128)(2,1)S(1)}, u32[]{:S(2)}, u32[]{:S(2)}) %collective-permute-start.15) | collective-permute-done | bytes 65568 | tf_op jit(solution)/shard_map/ppermute | solution.py:285
  106.4 1.4 %collective-permute-start.18 = (bf16[32,1024]{1,0:T(8,128)(2,1)S(1)}, bf16[32,1024]{1,0:T(8,128)(2,1)S(1)}, u32[]{:S(2)}, u32[]{:S(2)}) collective-permute-start(bf16[32,1024]{1,0:T(8,128)(2,1)S(1)} %get-tuple-element.88.refs_4_), channel_id=1, source_target_pairs={{0,2},{1,3},{2,0},{3,1},{4,6},{5,7},{6,4},{7,5},{8,10},{9,11},{10,... | collective-permute-start | bytes 196616 | tf_op jit(solution)/shard_map/ppermute | solution.py:285
  108.8 1.1 collective-permute-start.12
  111.9 2.8 %collective-permute-done.17.refs_5_ = bf16[32,1024]{1,0:T(8,128)(2,1)S(1)} collective-permute-done((bf16[32,1024]{1,0:T(8,128)(2,1)S(1)}, bf16[32,1024]{1,0:T(8,128)(2,1)S(1)}, u32[]{:S(2)}, u32[]{:S(2)}) %collective-permute-start.17) | collective-permute-done | bytes 65568 | tf_op jit(solution)/shard_map/ppermute | solution.py:285
  114.7 1.4 %collective-permute-done.19.refs_7_ = bf16[32,1024]{1,0:T(8,128)(2,1)S(1)} collective-permute-done((bf16[32,1024]{1,0:T(8,128)(2,1)S(1)}, bf16[32,1024]{1,0:T(8,128)(2,1)S(1)}, u32[]{:S(2)}, u32[]{:S(2)}) %collective-permute-start.19) | collective-permute-done | bytes 65568 | tf_op jit(solution)/shard_map/ppermute | solution.py:285
  116.2 1.4 %project_down.1 = bf16[32,56,128]{2,1,0:T(8,128)(2,1)S(1)} custom-call(bf16[32,1280]{1,0:T(8,128)(2,1)S(1)} %get-tuple-element.78.refs_0_, bf16[32,1280]{1,0:T(8,128)(2,1)S(1)} %collective-permute-done.10.refs_1_, bf16[32,1280]{1,0:T(8,128)(2,1)S(1)} %collective-permute-done.11.refs_2_, bf16[32,1280]{1,0:T(8,128)(2,1)S(1)} %collective-permute-done.12.refs_3_, ...), custom_call_target="tpu_custom_call" | custom-call | tf_op jit(solution)/shard_map/project_down/pallas_call | solution.py:573
  117.6 15.7 %all_to_all.17.parts_ref = bf16[32,56,128]{2,1,0:T(8,128)(2,1)S(1)} all-to-all(bf16[32,56,128]{2,1,0:T(8,128)(2,1)S(1)} %project_down.1), channel_id=1, replica_groups=mesh['dp'=8,'tp'=4] {'dp','tp'}, dimensions={0} | all-to-all | bytes 917504 | tf_op jit(solution)/shard_map/all_to_all | solution.py:621
  (57 shorter events, 13.8 us)
Async XLA Ops:
  0.0 38.9 %copy-start.1 = (bf16[4,512,128]{2,1,0:T(8,128)(2,1)S(1)}, bf16[4,512,128]{2,1,0:T(8,128)(2,1)}, u32[]{:S(2)}) copy-start(bf16[4,512,128]{2,1,0:T(8,128)(2,1)} %w_ref.2) | copy-start | bytes 1572868
  0.0 41.6 %copy-start.2 = (bf16[4,7168]{1,0:T(4,128)(2,1)S(1)}, bf16[4,7168]{1,0:T(4,128)(2,1)}, u32[]{:S(2)}) copy-start(bf16[4,7168]{1,0:T(4,128)(2,1)} %rows_ref) | copy-start | bytes 172036
  0.0 51.3 %copy-start = (bf16[2048,1792]{1,0:T(8,128)(2,1)S(1)}, bf16[2048,1792]{1,0:T(8,128)(2,1)}, u32[]{:S(2)}) copy-start(bf16[2048,1792]{1,0:T(8,128)(2,1)} %refs_4_.1) | copy-start | bytes 22020100
  0.0 77.6 %slice-start.2 = ((s8[8257536]{0:T(1024)(128)(4,1)}), s8[4194304]{0:T(1024)(128)(4,1)S(1)}, s32[]{:S(2)}) async-start(s8[8257536]{0:T(1024)(128)(4,1)} %bitcast.14), calls=%async_computation.5 | async-start | bytes 8388608
  39.7 11.2 %collective-permute-start.1 = (bf16[128,512]{1,0:T(8,128)(2,1)S(1)}, bf16[128,512]{1,0:T(8,128)(2,1)S(1)}, u32[]{:S(2)}, u32[]{:S(2)}) collective-permute-start(bf16[128,512]{1,0:T(8,128)(2,1)S(1)} %head_values.1.value_ref), channel_id=1, source_target_pairs={{0,2},{1,3},{2,0},{3,1},{4,6},{5,7},{6,4},{7,5},{8,10},{9,11},{10,... | collective-permute-start | bytes 393224 | tf_op jit(solution)/shard_map/ppermute | solution.py:285
  41.6 5.1 %collective-permute-start.2 = (bf16[4,1792]{1,0:T(4,128)(2,1)S(1)}, bf16[4,1792]{1,0:T(4,128)(2,1)S(1)}, u32[]{:S(2)}, u32[]{:S(2)}) collective-permute-start(bf16[4,1792]{1,0:T(4,128)(2,1)S(1)} %get-tuple-element.50), channel_id=1, source_target_pairs={{0,1},{1,0},{2,3},{3,2},{4,5},{5,4},{6,7},{7,6},{8,9},{9,8},{10,11... | collective-permute-start | bytes 43016 | tf_op jit(solution)/shard_map/ppermute | solution.py:285
  43.2 7.2 %collective-permute-start.3 = (bf16[4,1792]{1,0:T(4,128)(2,1)S(1)}, bf16[4,1792]{1,0:T(4,128)(2,1)S(1)}, u32[]{:S(2)}, u32[]{:S(2)}) collective-permute-start(bf16[4,1792]{1,0:T(4,128)(2,1)S(1)} %get-tuple-element.51), channel_id=1, source_target_pairs={{0,2},{1,3},{2,0},{3,1},{4,6},{5,7},{6,4},{7,5},{8,10},{9,11},{10,... | collective-permute-start | bytes 43016 | tf_op jit(solution)/shard_map/ppermute | solution.py:285
  45.3 5.6 %collective-permute-start.4 = (bf16[4,1792]{1,0:T(4,128)(2,1)S(1)}, bf16[4,1792]{1,0:T(4,128)(2,1)S(1)}, u32[]{:S(2)}, u32[]{:S(2)}) collective-permute-start(bf16[4,1792]{1,0:T(4,128)(2,1)S(1)} %get-tuple-element.52), channel_id=1, source_target_pairs={{0,3},{1,2},{2,1},{3,0},{4,7},{5,6},{6,5},{7,4},{8,11},{9,10},{10,... | collective-permute-start | bytes 43016 | tf_op jit(solution)/shard_map/ppermute | solution.py:285
  46.0 7.1 %collective-permute-start = (bf16[128,512]{1,0:T(8,128)(2,1)S(1)}, bf16[128,512]{1,0:T(8,128)(2,1)S(1)}, u32[]{:S(2)}, u32[]{:S(2)}) collective-permute-start(bf16[128,512]{1,0:T(8,128)(2,1)S(1)} %head_values.1.value_ref), channel_id=1, source_target_pairs={{0,1},{1,0},{2,3},{3,2},{4,5},{5,4},{6,7},{7,6},{8,9},{9,8},{10,11... | collective-permute-start | bytes 393224 | tf_op jit(solution)/shard_map/ppermute | solution.py:285
  50.9 5.1 %collective-permute-start.5 = (bf16[128,512]{1,0:T(8,128)(2,1)S(1)}, bf16[128,512]{1,0:T(8,128)(2,1)S(1)}, u32[]{:S(2)}, u32[]{:S(2)}) collective-permute-start(bf16[128,512]{1,0:T(8,128)(2,1)S(1)} %collective-permute-done.1.refs_2_), channel_id=1, source_target_pairs={{0,1},{1,0},{2,3},{3,2},{4,5},{5,4},{6,7},{7,6},{8,9},{9,8},{10,11... | collective-permute-start | bytes 393224 | tf_op jit(solution)/shard_map/ppermute | solution.py:285
  79.1 12.5 %collective-permute-start.6 = (bf16[64,1408]{1,0:T(8,128)(2,1)S(1)}, bf16[64,1408]{1,0:T(8,128)(2,1)S(1)}, u32[]{:S(2)}, u32[]{:S(2)}) collective-permute-start(bf16[64,1408]{1,0:T(8,128)(2,1)S(1)} %get-tuple-element.72), channel_id=1, source_target_pairs={{0,1},{1,0},{2,3},{3,2},{4,5},{5,4},{6,7},{7,6},{8,9},{9,8},{10,11... | collective-permute-start | bytes 540680 | tf_op jit(solution)/shard_map/ppermute | solution.py:285
  79.9 11.6 %collective-permute-start.7 = (bf16[64,1280]{1,0:T(8,128)(2,1)S(1)}, bf16[64,1280]{1,0:T(8,128)(2,1)S(1)}, u32[]{:S(2)}, u32[]{:S(2)}) collective-permute-start(bf16[64,1280]{1,0:T(8,128)(2,1)S(1)} %get-tuple-element.73), channel_id=1, source_target_pairs={{0,2},{1,3},{2,0},{3,1},{4,6},{5,7},{6,4},{7,5},{8,10},{9,11},{10,... | collective-permute-start | bytes 491528 | tf_op jit(solution)/shard_map/ppermute | solution.py:285
  82.1 12.3 %collective-permute-start.13 = (bf16[64,1024]{1,0:T(8,128)(2,1)S(1)}, bf16[64,1024]{1,0:T(8,128)(2,1)S(1)}, u32[]{:S(2)}, u32[]{:S(2)}) collective-permute-start(bf16[64,1024]{1,0:T(8,128)(2,1)S(1)} %get-tuple-element.82), channel_id=1, source_target_pairs={{0,1},{1,0},{2,3},{3,2},{4,5},{5,4},{6,7},{7,6},{8,9},{9,8},{10,11... | collective-permute-start | bytes 393224 | tf_op jit(solution)/shard_map/ppermute | solution.py:285
  82.7 17.0 %collective-permute-start.14 = (bf16[64,1024]{1,0:T(8,128)(2,1)S(1)}, bf16[64,1024]{1,0:T(8,128)(2,1)S(1)}, u32[]{:S(2)}, u32[]{:S(2)}) collective-permute-start(bf16[64,1024]{1,0:T(8,128)(2,1)S(1)} %get-tuple-element.83), channel_id=1, source_target_pairs={{0,2},{1,3},{2,0},{3,1},{4,6},{5,7},{6,4},{7,5},{8,10},{9,11},{10,... | collective-permute-start | bytes 393224 | tf_op jit(solution)/shard_map/ppermute | solution.py:285
  91.6 10.3 %collective-permute-start.8 = (bf16[32,1408]{1,0:T(8,128)(2,1)S(1)}, bf16[32,1408]{1,0:T(8,128)(2,1)S(1)}, u32[]{:S(2)}, u32[]{:S(2)}) collective-permute-start(bf16[32,1408]{1,0:T(8,128)(2,1)S(1)} %get-tuple-element.76), channel_id=1, source_target_pairs={{0,2},{1,3},{2,0},{3,1},{4,6},{5,7},{6,4},{7,5},{8,10},{9,11},{10,... | collective-permute-start | bytes 270344 | tf_op jit(solution)/shard_map/ppermute | solution.py:285
  91.9 8.1 %collective-permute-start.9 = (bf16[32,1280]{1,0:T(8,128)(2,1)S(1)}, bf16[32,1280]{1,0:T(8,128)(2,1)S(1)}, u32[]{:S(2)}, u32[]{:S(2)}) collective-permute-start(bf16[32,1280]{1,0:T(8,128)(2,1)S(1)} %get-tuple-element.77), channel_id=1, source_target_pairs={{0,1},{1,0},{2,3},{3,2},{4,5},{5,4},{6,7},{7,6},{8,9},{9,8},{10,11... | collective-permute-start | bytes 245768 | tf_op jit(solution)/shard_map/ppermute | solution.py:285
  99.8 5.6 %collective-permute-start.15 = (bf16[32,1024]{1,0:T(8,128)(2,1)S(1)}, bf16[32,1024]{1,0:T(8,128)(2,1)S(1)}, u32[]{:S(2)}, u32[]{:S(2)}) collective-permute-start(bf16[32,1024]{1,0:T(8,128)(2,1)S(1)} %get-tuple-element.86), channel_id=1, source_target_pairs={{0,2},{1,3},{2,0},{3,1},{4,6},{5,7},{6,4},{7,5},{8,10},{9,11},{10,... | collective-permute-start | bytes 196616 | tf_op jit(solution)/shard_map/ppermute | solution.py:285
  99.9 5.9 %collective-permute-start.16 = (bf16[32,1024]{1,0:T(8,128)(2,1)S(1)}, bf16[32,1024]{1,0:T(8,128)(2,1)S(1)}, u32[]{:S(2)}, u32[]{:S(2)}) collective-permute-start(bf16[32,1024]{1,0:T(8,128)(2,1)S(1)} %get-tuple-element.87), channel_id=1, source_target_pairs={{0,1},{1,0},{2,3},{3,2},{4,5},{5,4},{6,7},{7,6},{8,9},{9,8},{10,11... | collective-permute-start | bytes 196616 | tf_op jit(solution)/shard_map/ppermute | solution.py:285
  102.1 6.6 %collective-permute-start.11 = (bf16[32,1280]{1,0:T(8,128)(2,1)S(1)}, bf16[32,1280]{1,0:T(8,128)(2,1)S(1)}, u32[]{:S(2)}, u32[]{:S(2)}) collective-permute-start(bf16[32,1280]{1,0:T(8,128)(2,1)S(1)} %get-tuple-element.78.refs_0_), channel_id=1, source_target_pairs={{0,2},{1,3},{2,0},{3,1},{4,6},{5,7},{6,4},{7,5},{8,10},{9,11},{10,... | collective-permute-start | bytes 245768 | tf_op jit(solution)/shard_map/ppermute | solution.py:285
  106.4 5.4 %collective-permute-start.18 = (bf16[32,1024]{1,0:T(8,128)(2,1)S(1)}, bf16[32,1024]{1,0:T(8,128)(2,1)S(1)}, u32[]{:S(2)}, u32[]{:S(2)}) collective-permute-start(bf16[32,1024]{1,0:T(8,128)(2,1)S(1)} %get-tuple-element.88.refs_4_), channel_id=1, source_target_pairs={{0,2},{1,3},{2,0},{3,1},{4,6},{5,7},{6,4},{7,5},{8,10},{9,11},{10,... | collective-permute-start | bytes 196616 | tf_op jit(solution)/shard_map/ppermute | solution.py:285
  107.9 6.8 %collective-permute-start.10 = (bf16[32,1280]{1,0:T(8,128)(2,1)S(1)}, bf16[32,1280]{1,0:T(8,128)(2,1)S(1)}, u32[]{:S(2)}, u32[]{:S(2)}) collective-permute-start(bf16[32,1280]{1,0:T(8,128)(2,1)S(1)} %get-tuple-element.78.refs_0_), channel_id=1, source_target_pairs={{0,1},{1,0},{2,3},{3,2},{4,5},{5,4},{6,7},{7,6},{8,9},{9,8},{10,11... | collective-permute-start | bytes 245768 | tf_op jit(solution)/shard_map/ppermute | solution.py:285
  108.8 7.4 %collective-permute-start.12 = (bf16[32,1280]{1,0:T(8,128)(2,1)S(1)}, bf16[32,1280]{1,0:T(8,128)(2,1)S(1)}, u32[]{:S(2)}, u32[]{:S(2)}) collective-permute-start(bf16[32,1280]{1,0:T(8,128)(2,1)S(1)} %collective-permute-done.11.refs_2_), channel_id=1, source_target_pairs={{0,1},{1,0},{2,3},{3,2},{4,5},{5,4},{6,7},{7,6},{8,9},{9,8},{10,11... | collective-permute-start | bytes 245768 | tf_op jit(solution)/shard_map/ppermute | solution.py:285
  109.9 4.8 %collective-permute-start.17 = (bf16[32,1024]{1,0:T(8,128)(2,1)S(1)}, bf16[32,1024]{1,0:T(8,128)(2,1)S(1)}, u32[]{:S(2)}, u32[]{:S(2)}) collective-permute-start(bf16[32,1024]{1,0:T(8,128)(2,1)S(1)} %get-tuple-element.88.refs_4_), channel_id=1, source_target_pairs={{0,1},{1,0},{2,3},{3,2},{4,5},{5,4},{6,7},{7,6},{8,9},{9,8},{10,11... | collective-permute-start | bytes 196616 | tf_op jit(solution)/shard_map/ppermute | solution.py:285
  111.9 4.3 %collective-permute-start.19 = (bf16[32,1024]{1,0:T(8,128)(2,1)S(1)}, bf16[32,1024]{1,0:T(8,128)(2,1)S(1)}, u32[]{:S(2)}, u32[]{:S(2)}) collective-permute-start(bf16[32,1024]{1,0:T(8,128)(2,1)S(1)} %collective-permute-done.18.refs_6_), channel_id=1, source_target_pairs={{0,1},{1,0},{2,3},{3,2},{4,5},{5,4},{6,7},{7,6},{8,9},{9,8},{10,11... | collective-permute-start | bytes 196616 | tf_op jit(solution)/shard_map/ppermute | solution.py:285
  (6 other events, 191.9 us)

commit v16 on v14

--- a/solution.py
+++ b/solution.py
@@ -10,6 +10,7 @@
 C = 512
 BLOCK_TOKENS = 64
 TILE = 512
+UNROLL = 4
 
 score_scale = 192.0 ** (-0.5)
 log2_e = 1.4426950408889634
@@ -25,12 +26,9 @@
     pairs_of_heads,
     rows_of_heads,
     held,
-    score0,
-    score1,
-    weight0,
-    weight1,
-    keep0,
-    keep1,
+    score_bufs,
+    weight_bufs,
+    keep_bufs,
     acc,
     done,
     best,
@@ -92,8 +90,11 @@
     acc[...] = jnp.zeros_like(acc)
     best[...] = jnp.full_like(best, negative)
     mass[...] = jnp.zeros_like(mass)
-    weight1[...] = jnp.zeros_like(weight1)
-    keep1[...] = jnp.ones_like(keep1)
+    score_of = [score_bufs.at[k] for k in range(UNROLL)]
+    weight_of = [weight_bufs.at[k] for k in range(UNROLL)]
+    keep_of = [keep_bufs.at[k] for k in range(UNROLL)]
+    weight_of[-1][...] = jnp.zeros(weight_bufs.shape[1:], weight_bufs.dtype)
+    keep_of[-1][...] = jnp.ones(keep_bufs.shape[1:], keep_bufs.dtype)
 
     def advance(p, r, i):
         live = p + 1 < pairs
@@ -112,8 +113,7 @@
     def scores(r, i, live, target):
         begin_at = jnp.where(live, lo[r], 0)
         end_at = jnp.where(live, hi[r], 0)
-        s = jnp.dot(q_ref[r, :, :C], held[i, :C, :], preferred_element_type=jnp.float32)
-        s = s + jnp.dot(q_ref[r, :, C:], held[i, C:, :], preferred_element_type=jnp.float32)
+        s = jnp.dot(q_ref[r], held[i], preferred_element_type=jnp.float32)
         token = i * tile + lax.broadcasted_iota(jnp.int32, (1, tile), 1)
         target[...] = s + jnp.where((token >= begin_at) & (token < end_at), 0.0, negative)
 
@@ -142,32 +142,34 @@
 
     zero = jnp.int32(0)
     fetch(zero, zero, pairs > 0)
-    scores(zero, zero, pairs > 0, score0)
+    scores(zero, zero, pairs > 0, score_of[0])
 
     def step(j, carry):
         r0, i0, r1, i1 = carry
-        p = 2 * j
-        r2, i2, live2 = advance(p, r1, i1)
-        r3, i3, live3 = advance(p + 1, r2, i2)
-        fetch(r2, i2, live2)
-        fetch(r3, i3, live3)
-        gather(r0, i0, weight1, keep1)
-        scores(r2, i2, live2, score1)
-        soften(r1, score0, weight0, keep0)
-        gather(r1, i1, weight0, keep0)
-        scores(r3, i3, live3, score0)
-        soften(r2, score1, weight1, keep1)
-        return r2, i2, r3, i3
-
-    r0, i0, _, _ = lax.fori_loop(0, (pairs + 1) // 2, step, (zero, zero, zero, zero))
-    gather(r0, i0, weight1, keep1)
+        places = [(r1, i1, True)]
+        for k in range(UNROLL):
+            places.append(advance(UNROLL * j + k, *places[-1][:2]))
+        for place in places[1:]:
+            fetch(*place)
+        for k in range(UNROLL):
+            gather(r0, i0, weight_of[k - 1], keep_of[k - 1])
+            scores(*places[k + 1], score_of[(k + 1) % UNROLL])
+            r0, i0, _ = places[k]
+            soften(r0, score_of[k], weight_of[k], keep_of[k])
+        return (r0, i0) + places[-1][:2]
+
+    steps = (pairs + UNROLL - 1) // UNROLL
+    r0, i0, _, _ = lax.fori_loop(0, steps, step, (zero, zero, zero, zero))
+    gather(r0, i0, weight_of[-1], keep_of[-1])
 
     share = heads // out_ref.shape[0]
     for r in range(nreq):
         total = jnp.sum(mass[r], axis=1, keepdims=True)
-        score0[:, :C] = acc[r].T / total
+        score_bufs[0, :, :C] = acc[r].T / total
         for d in range(out_ref.shape[0]):
-            done[d, r * share : (r + 1) * share, :] = score0[d * share : (d + 1) * share, :C]
+            done[d, r * share : (r + 1) * share, :] = score_bufs[
+                0, d * share : (d + 1) * share, :C
+            ]
     out_ref[...] = done[...].astype(out_ref.dtype)
 
 
@@ -201,12 +203,9 @@
             pltpu.VMEM((2 * width // 128, nreq * heads // 2, 128), jnp.float32),
             pltpu.VMEM((width // 128 + 1, heads, 128), jnp.float32),
             pltpu.VMEM((tiles, width, tile), jnp.bfloat16),
-            pltpu.VMEM((heads, tile), jnp.float32),
-            pltpu.VMEM((heads, tile), jnp.float32),
-            pltpu.VMEM((tile, heads), jnp.bfloat16),
-            pltpu.VMEM((tile, heads), jnp.bfloat16),
-            pltpu.VMEM((8, heads), jnp.float32),
-            pltpu.VMEM((8, heads), jnp.float32),
+            pltpu.VMEM((UNROLL, heads, tile), jnp.float32),
+            pltpu.VMEM((UNROLL, tile, heads), jnp.bfloat16),
+            pltpu.VMEM((UNROLL, 8, heads), jnp.float32),
             pltpu.VMEM((nreq, C, heads), jnp.float32),
             pltpu.VMEM((ranks, nreq * heads // ranks, C), jnp.float32),
             pltpu.VMEM((nreq, heads, 128), jnp.float32),

time: 130 us -> 131 us (level)
  no operation moved by 1% of the time
where the time goes in v16:
time: 131 us; the launch traced here: 129 us
  blocking collectives  61.4 us (47%)
  waiting for transfers between devices  28.8 us (22%)
  starting transfers between devices  21.8 us (17%)
  Pallas kernels  16.4 us (13%)
    all_to_all x3, blocking collectives, swap(): return lax.all_to_all(parts, axes, split_axis=0, concat_axis=0, tiled=True)  52.7 us
    ppermute x20, waiting for transfers between devices, from_distance(): lax.ppermute(piece, axis, [(k, k ^ distance) for k in range(lax.axis_size...  28.8 us
    ppermute x20, starting transfers between devices, from_distance(): lax.ppermute(piece, axis, [(k, k ^ distance) for k in range(lax.axis_size...  21.8 us
    all_gather x1, blocking collectives, local(): hidden = lax.all_gather(own_hidden, 'dp', axis=0, tiled=True)  8.78 us
    pallas_call x1, Pallas kernels, attend(): pl.pallas_call(attention_kernel, out_shape=jax.ShapeDtypeStruct((ranks, n...  8.73 us
  transfers between devices with their start and end apart: 20, of which 12 were waited for; matrix products, arithmetic and copies ran while one was open for 0% of the time, Pallas kernels for 3%

profile of v16, /device:TPU:0, one launch (start us, length us, event | category | flops | bytes accessed | tf_op | source)
XLA Modules:
  0.0 128.8 jit_solution(217570264643484141)
XLA Ops:
  0.0 8.7 %attention.1 = bf16[32,16,512]{2,1,0:T(8,128)(2,1)S(1)} custom-call(s32[128]{0:T(128)} %lens_ref.1, bf16[4,73728]{1,0:T(4,128)(2,1)} %raw_ref.1, bf16[576,14336]{1,0:T(8,128)(2,1)} %bitcast.29), custom_call_target="tpu_custom_call" | custom-call | flops 3992977408 | bytes 16515072 | tf_op jit(solution)/shard_map/attention/pallas_call | solution.py:194
  8.8 24.8 %all_to_all.15 = bf16[32,16,512]{2,1,0:T(8,128)(2,1)S(1)} all-to-all(bf16[32,16,512]{2,1,0:T(8,128)(2,1)S(1)} %attention.1), channel_id=1, replica_groups=mesh['dp'=8,'tp'=4] {'dp','tp'}, dimensions={0} | all-to-all | bytes 1048576 | tf_op jit(solution)/shard_map/all_to_all | solution.py:597
  34.3 2.9 %collective-permute-start.2 = (bf16[128,512]{1,0:T(8,128)(2,1)S(1)}, bf16[128,512]{1,0:T(8,128)(2,1)S(1)}, u32[]{:S(2)}, u32[]{:S(2)}) collective-permute-start(bf16[128,512]{1,0:T(8,128)(2,1)S(1)} %head_values.1.value_ref), channel_id=1, source_target_pairs={{0,3},{1,2},{2,1},{3,0},{4,7},{5,6},{6,5},{7,4},{8,11},{9,10},{10,... | collective-permute-start | bytes 393224 | tf_op jit(solution)/shard_map/ppermute | solution.py:278
  37.2 1.2 collective-permute-start.1
  38.8 1.7 %collective-permute-start.3 = (bf16[4,1792]{1,0:T(4,128)(2,1)S(1)}, bf16[4,1792]{1,0:T(4,128)(2,1)S(1)}, u32[]{:S(2)}, u32[]{:S(2)}) collective-permute-start(bf16[4,1792]{1,0:T(4,128)(2,1)S(1)} %get-tuple-element.45), channel_id=1, source_target_pairs={{0,1},{1,0},{2,3},{3,2},{4,5},{5,4},{6,7},{7,6},{8,9},{9,8},{10,11... | collective-permute-start | bytes 43016 | tf_op jit(solution)/shard_map/ppermute | solution.py:278
  40.5 1.7 %collective-permute-start.4 = (bf16[4,1792]{1,0:T(4,128)(2,1)S(1)}, bf16[4,1792]{1,0:T(4,128)(2,1)S(1)}, u32[]{:S(2)}, u32[]{:S(2)}) collective-permute-start(bf16[4,1792]{1,0:T(4,128)(2,1)S(1)} %get-tuple-element.46), channel_id=1, source_target_pairs={{0,2},{1,3},{2,0},{3,1},{4,6},{5,7},{6,4},{7,5},{8,10},{9,11},{10,... | collective-permute-start | bytes 43016 | tf_op jit(solution)/shard_map/ppermute | solution.py:278
  42.5 3.0 %collective-permute-start.5 = (bf16[4,1792]{1,0:T(4,128)(2,1)S(1)}, bf16[4,1792]{1,0:T(4,128)(2,1)S(1)}, u32[]{:S(2)}, u32[]{:S(2)}) collective-permute-start(bf16[4,1792]{1,0:T(4,128)(2,1)S(1)} %get-tuple-element.47), channel_id=1, source_target_pairs={{0,3},{1,2},{2,1},{3,0},{4,7},{5,6},{6,5},{7,4},{8,11},{9,10},{10,... | collective-permute-start | bytes 43016 | tf_op jit(solution)/shard_map/ppermute | solution.py:278
  45.9 4.6 %collective-permute-done.1.refs_2_ = bf16[128,512]{1,0:T(8,128)(2,1)S(1)} collective-permute-done((bf16[128,512]{1,0:T(8,128)(2,1)S(1)}, bf16[128,512]{1,0:T(8,128)(2,1)S(1)}, u32[]{:S(2)}, u32[]{:S(2)}) %collective-permute-start.1) | collective-permute-done | bytes 131104 | tf_op jit(solution)/shard_map/ppermute | solution.py:278
  51.5 11.6 %all_to_all.16.parts_ref = bf16[8,16,1792]{2,1,0:T(8,128)(2,1)S(1)} all-to-all(bf16[8,16,1792]{2,1,0:T(8,128)(2,1)S(1)} %bitcast.19), channel_id=1, replica_groups=mesh['dp'=8,'tp'=4] {'dp'}, dimensions={0} | all-to-all | bytes 917504 | tf_op jit(solution)/shard_map/all_to_all | solution.py:597
  63.1 8.8 %all_gather.3.hidden_ref = bf16[128,1792]{1,0:T(8,128)(2,1)S(1)} all-gather(bf16[16,1792]{1,0:T(8,128)(2,1)S(1)} %hidden.1.refs_9_), channel_id=1, replica_groups=mesh['dp'=8,'tp'=4] {'dp'}, dimensions={0}, use_global_device_ids=true | all-gather | bytes 516096 | tf_op jit(solution)/shard_map/all_gather | solution.py:623
  72.0 1.4 %gate_up.1 = (bf16[2,128,1792]{2,1,0:T(8,128)(2,1)S(1)}, bf16[64,1408]{1,0:T(8,128)(2,1)S(1)}, bf16[64,1280]{1,0:T(8,128)(2,1)S(1)}, bf16[64,1408]{1,0:T(8,128)(2,1)S(1)}, bf16[64,1280]{1,0:T(8,128)(2,1)S(1)}) custom-call(bf16[128,1792]{1,0:T(8,128)(2,1)S(1)} %all_gather.3.hidden_ref, bf16[56,128]{1,0:T(8,128)(2,1)S(1)} %bitcast.28, ...), custom_call_target="tpu_custom_call" | custom-call | flops 1174405120 | bytes 9175040 | tf_op jit(solution)/shard_map/gate_up/pallas_call | solution.py:433
  74.3 1.5 %collective-permute-start.7 = (bf16[64,1280]{1,0:T(8,128)(2,1)S(1)}, bf16[64,1280]{1,0:T(8,128)(2,1)S(1)}, u32[]{:S(2)}, u32[]{:S(2)}) collective-permute-start(bf16[64,1280]{1,0:T(8,128)(2,1)S(1)} %get-tuple-element.63), channel_id=1, source_target_pairs={{0,2},{1,3},{2,0},{3,1},{4,6},{5,7},{6,4},{7,5},{8,10},{9,11},{10,... | collective-permute-start | bytes 491528 | tf_op jit(solution)/shard_map/ppermute | solution.py:278
  77.4 2.1 %collective-permute-start.14 = (bf16[64,1024]{1,0:T(8,128)(2,1)S(1)}, bf16[64,1024]{1,0:T(8,128)(2,1)S(1)}, u32[]{:S(2)}, u32[]{:S(2)}) collective-permute-start(bf16[64,1024]{1,0:T(8,128)(2,1)S(1)} %get-tuple-element.73), channel_id=1, source_target_pairs={{0,2},{1,3},{2,0},{3,1},{4,6},{5,7},{6,4},{7,5},{8,10},{9,11},{10,... | collective-permute-start | bytes 393224 | tf_op jit(solution)/shard_map/ppermute | solution.py:278
  79.6 6.3 %collective-permute-done.7.refs_3_ = bf16[64,1280]{1,0:T(8,128)(2,1)S(1)} collective-permute-done((bf16[64,1280]{1,0:T(8,128)(2,1)S(1)}, bf16[64,1280]{1,0:T(8,128)(2,1)S(1)}, u32[]{:S(2)}, u32[]{:S(2)}) %collective-permute-start.7) | collective-permute-done | bytes 163872 | tf_op jit(solution)/shard_map/ppermute | solution.py:278
  87.2 1.9 %collective-permute-done.13.refs_2_ = bf16[64,1024]{1,0:T(8,128)(2,1)S(1)} collective-permute-done((bf16[64,1024]{1,0:T(8,128)(2,1)S(1)}, bf16[64,1024]{1,0:T(8,128)(2,1)S(1)}, u32[]{:S(2)}, u32[]{:S(2)}) %collective-permute-start.13) | collective-permute-done | bytes 131104 | tf_op jit(solution)/shard_map/ppermute | solution.py:278
  89.1 4.7 %collective-permute-done.14.refs_3_ = bf16[64,1024]{1,0:T(8,128)(2,1)S(1)} collective-permute-done((bf16[64,1024]{1,0:T(8,128)(2,1)S(1)}, bf16[64,1024]{1,0:T(8,128)(2,1)S(1)}, u32[]{:S(2)}, u32[]{:S(2)}) %collective-permute-start.14) | collective-permute-done | bytes 131104 | tf_op jit(solution)/shard_map/ppermute | solution.py:278
  94.1 2.5 %collective-permute-done.8 = bf16[32,1408]{1,0:T(8,128)(2,1)S(1)} collective-permute-done((bf16[32,1408]{1,0:T(8,128)(2,1)S(1)}, bf16[32,1408]{1,0:T(8,128)(2,1)S(1)}, u32[]{:S(2)}, u32[]{:S(2)}) %collective-permute-start.8) | collective-permute-done | bytes 90144 | tf_op jit(solution)/shard_map/ppermute | solution.py:278
  97.1 2.6 %collective-permute-done.15 = bf16[32,1024]{1,0:T(8,128)(2,1)S(1)} collective-permute-done((bf16[32,1024]{1,0:T(8,128)(2,1)S(1)}, bf16[32,1024]{1,0:T(8,128)(2,1)S(1)}, u32[]{:S(2)}, u32[]{:S(2)}) %collective-permute-start.15) | collective-permute-done | bytes 65568 | tf_op jit(solution)/shard_map/ppermute | solution.py:278
  100.5 1.8 %collective-permute-start.18 = (bf16[32,1024]{1,0:T(8,128)(2,1)S(1)}, bf16[32,1024]{1,0:T(8,128)(2,1)S(1)}, u32[]{:S(2)}, u32[]{:S(2)}) collective-permute-start(bf16[32,1024]{1,0:T(8,128)(2,1)S(1)} %get-tuple-element.78.refs_4_), channel_id=1, source_target_pairs={{0,2},{1,3},{2,0},{3,1},{4,6},{5,7},{6,4},{7,5},{8,10},{9,11},{10,... | collective-permute-start | bytes 196616 | tf_op jit(solution)/shard_map/ppermute | solution.py:278
  102.3 1.3 %collective-permute-done.11.refs_2_ = bf16[32,1280]{1,0:T(8,128)(2,1)S(1)} collective-permute-done((bf16[32,1280]{1,0:T(8,128)(2,1)S(1)}, bf16[32,1280]{1,0:T(8,128)(2,1)S(1)}, u32[]{:S(2)}, u32[]{:S(2)}) %collective-permute-start.11) | collective-permute-done | bytes 81952 | tf_op jit(solution)/shard_map/ppermute | solution.py:278
  104.3 1.3 %collective-permute-start.17 = (bf16[32,1024]{1,0:T(8,128)(2,1)S(1)}, bf16[32,1024]{1,0:T(8,128)(2,1)S(1)}, u32[]{:S(2)}, u32[]{:S(2)}) collective-permute-start(bf16[32,1024]{1,0:T(8,128)(2,1)S(1)} %get-tuple-element.78.refs_4_), channel_id=1, source_target_pairs={{0,1},{1,0},{2,3},{3,2},{4,5},{5,4},{6,7},{7,6},{8,9},{9,8},{10,11... | collective-permute-start | bytes 196616 | tf_op jit(solution)/shard_map/ppermute | solution.py:278
  106.4 2.8 %collective-permute-done.17.refs_5_ = bf16[32,1024]{1,0:T(8,128)(2,1)S(1)} collective-permute-done((bf16[32,1024]{1,0:T(8,128)(2,1)S(1)}, bf16[32,1024]{1,0:T(8,128)(2,1)S(1)}, u32[]{:S(2)}, u32[]{:S(2)}) %collective-permute-start.17) | collective-permute-done | bytes 65568 | tf_op jit(solution)/shard_map/ppermute | solution.py:278
  110.4 1.4 %project_down.1 = bf16[32,4,1792]{2,1,0:T(4,128)(2,1)S(1)} custom-call(bf16[32,1280]{1,0:T(8,128)(2,1)S(1)} %get-tuple-element.68.refs_0_, bf16[32,1280]{1,0:T(8,128)(2,1)S(1)} %collective-permute-done.10.refs_1_, bf16[32,1280]{1,0:T(8,128)(2,1)S(1)} %collective-permute-done.11.refs_2_, bf16[32,1280]{1,0:T(8,128)(2,1)S(1)} %collective-permute-done.12.refs_3_, ...), custom_call_target="tpu_custom_call" | custom-call | tf_op jit(solution)/shard_map/project_down/pallas_call | solution.py:558
  111.8 16.3 %all_to_all.17.parts_ref = bf16[32,4,1792]{2,1,0:T(4,128)(2,1)S(1)} all-to-all(bf16[32,4,1792]{2,1,0:T(4,128)(2,1)S(1)} %project_down.1), channel_id=1, replica_groups=mesh['dp'=8,'tp'=4] {'dp','tp'}, dimensions={0} | all-to-all | bytes 917504 | tf_op jit(solution)/shard_map/all_to_all | solution.py:597
  (57 shorter events, 11.7 us)
Async XLA Ops:
  0.0 38.8 %copy-start.2 = (bf16[4,7168]{1,0:T(4,128)(2,1)S(1)}, bf16[4,7168]{1,0:T(4,128)(2,1)}, u32[]{:S(2)}) copy-start(bf16[4,7168]{1,0:T(4,128)(2,1)} %rows_ref) | copy-start | bytes 172036
  0.0 45.5 %copy-start = (bf16[2048,1792]{1,0:T(8,128)(2,1)S(1)}, bf16[2048,1792]{1,0:T(8,128)(2,1)}, u32[]{:S(2)}) copy-start(bf16[2048,1792]{1,0:T(8,128)(2,1)} %refs_4_.1) | copy-start | bytes 22020100
  0.0 71.9 %slice-start.2 = ((s8[8257536]{0:T(1024)(128)(4,1)}), s8[4194304]{0:T(1024)(128)(4,1)S(1)}, s32[]{:S(2)}) async-start(s8[8257536]{0:T(1024)(128)(4,1)} %bitcast.14), calls=%async_computation.5 | async-start | bytes 8388608
  34.3 8.2 %collective-permute-start.2 = (bf16[128,512]{1,0:T(8,128)(2,1)S(1)}, bf16[128,512]{1,0:T(8,128)(2,1)S(1)}, u32[]{:S(2)}, u32[]{:S(2)}) collective-permute-start(bf16[128,512]{1,0:T(8,128)(2,1)S(1)} %head_values.1.value_ref), channel_id=1, source_target_pairs={{0,3},{1,2},{2,1},{3,0},{4,7},{5,6},{6,5},{7,4},{8,11},{9,10},{10,... | collective-permute-start | bytes 393224 | tf_op jit(solution)/shard_map/ppermute | solution.py:278
  37.2 13.3 %collective-permute-start.1 = (bf16[128,512]{1,0:T(8,128)(2,1)S(1)}, bf16[128,512]{1,0:T(8,128)(2,1)S(1)}, u32[]{:S(2)}, u32[]{:S(2)}) collective-permute-start(bf16[128,512]{1,0:T(8,128)(2,1)S(1)} %head_values.1.value_ref), channel_id=1, source_target_pairs={{0,2},{1,3},{2,0},{3,1},{4,6},{5,7},{6,4},{7,5},{8,10},{9,11},{10,... | collective-permute-start | bytes 393224 | tf_op jit(solution)/shard_map/ppermute | solution.py:278
  38.4 12.1 %collective-permute-start = (bf16[128,512]{1,0:T(8,128)(2,1)S(1)}, bf16[128,512]{1,0:T(8,128)(2,1)S(1)}, u32[]{:S(2)}, u32[]{:S(2)}) collective-permute-start(bf16[128,512]{1,0:T(8,128)(2,1)S(1)} %head_values.1.value_ref), channel_id=1, source_target_pairs={{0,1},{1,0},{2,3},{3,2},{4,5},{5,4},{6,7},{7,6},{8,9},{9,8},{10,11... | collective-permute-start | bytes 393224 | tf_op jit(solution)/shard_map/ppermute | solution.py:278
  38.8 12.6 %collective-permute-start.3 = (bf16[4,1792]{1,0:T(4,128)(2,1)S(1)}, bf16[4,1792]{1,0:T(4,128)(2,1)S(1)}, u32[]{:S(2)}, u32[]{:S(2)}) collective-permute-start(bf16[4,1792]{1,0:T(4,128)(2,1)S(1)} %get-tuple-element.45), channel_id=1, source_target_pairs={{0,1},{1,0},{2,3},{3,2},{4,5},{5,4},{6,7},{7,6},{8,9},{9,8},{10,11... | collective-permute-start | bytes 43016 | tf_op jit(solution)/shard_map/ppermute | solution.py:278
  40.5 10.9 %collective-permute-start.4 = (bf16[4,1792]{1,0:T(4,128)(2,1)S(1)}, bf16[4,1792]{1,0:T(4,128)(2,1)S(1)}, u32[]{:S(2)}, u32[]{:S(2)}) collective-permute-start(bf16[4,1792]{1,0:T(4,128)(2,1)S(1)} %get-tuple-element.46), channel_id=1, source_target_pairs={{0,2},{1,3},{2,0},{3,1},{4,6},{5,7},{6,4},{7,5},{8,10},{9,11},{10,... | collective-permute-start | bytes 43016 | tf_op jit(solution)/shard_map/ppermute | solution.py:278
  42.5 8.9 %collective-permute-start.5 = (bf16[4,1792]{1,0:T(4,128)(2,1)S(1)}, bf16[4,1792]{1,0:T(4,128)(2,1)S(1)}, u32[]{:S(2)}, u32[]{:S(2)}) collective-permute-start(bf16[4,1792]{1,0:T(4,128)(2,1)S(1)} %get-tuple-element.47), channel_id=1, source_target_pairs={{0,3},{1,2},{2,1},{3,0},{4,7},{5,6},{6,5},{7,4},{8,11},{9,10},{10,... | collective-permute-start | bytes 43016 | tf_op jit(solution)/shard_map/ppermute | solution.py:278
  71.9 38.4 %slice-start.4 = ((s8[8257536]{0:T(1024)(128)(4,1)}), s8[4194304]{0:T(1024)(128)(4,1)S(1)}, s32[]{:S(2)}) async-start(s8[8257536]{0:T(1024)(128)(4,1)} %bitcast.16), calls=%async_computation.7 | async-start | bytes 8388608
  73.3 12.6 %collective-permute-start.6 = (bf16[64,1408]{1,0:T(8,128)(2,1)S(1)}, bf16[64,1408]{1,0:T(8,128)(2,1)S(1)}, u32[]{:S(2)}, u32[]{:S(2)}) collective-permute-start(bf16[64,1408]{1,0:T(8,128)(2,1)S(1)} %get-tuple-element.62), channel_id=1, source_target_pairs={{0,1},{1,0},{2,3},{3,2},{4,5},{5,4},{6,7},{7,6},{8,9},{9,8},{10,11... | collective-permute-start | bytes 540680 | tf_op jit(solution)/shard_map/ppermute | solution.py:278
  74.3 11.6 %collective-permute-start.7 = (bf16[64,1280]{1,0:T(8,128)(2,1)S(1)}, bf16[64,1280]{1,0:T(8,128)(2,1)S(1)}, u32[]{:S(2)}, u32[]{:S(2)}) collective-permute-start(bf16[64,1280]{1,0:T(8,128)(2,1)S(1)} %get-tuple-element.63), channel_id=1, source_target_pairs={{0,2},{1,3},{2,0},{3,1},{4,6},{5,7},{6,4},{7,5},{8,10},{9,11},{10,... | collective-permute-start | bytes 491528 | tf_op jit(solution)/shard_map/ppermute | solution.py:278
  76.9 12.2 %collective-permute-start.13 = (bf16[64,1024]{1,0:T(8,128)(2,1)S(1)}, bf16[64,1024]{1,0:T(8,128)(2,1)S(1)}, u32[]{:S(2)}, u32[]{:S(2)}) collective-permute-start(bf16[64,1024]{1,0:T(8,128)(2,1)S(1)} %get-tuple-element.72), channel_id=1, source_target_pairs={{0,1},{1,0},{2,3},{3,2},{4,5},{5,4},{6,7},{7,6},{8,9},{9,8},{10,11... | collective-permute-start | bytes 393224 | tf_op jit(solution)/shard_map/ppermute | solution.py:278
  77.4 16.4 %collective-permute-start.14 = (bf16[64,1024]{1,0:T(8,128)(2,1)S(1)}, bf16[64,1024]{1,0:T(8,128)(2,1)S(1)}, u32[]{:S(2)}, u32[]{:S(2)}) collective-permute-start(bf16[64,1024]{1,0:T(8,128)(2,1)S(1)} %get-tuple-element.73), channel_id=1, source_target_pairs={{0,2},{1,3},{2,0},{3,1},{4,6},{5,7},{6,4},{7,5},{8,10},{9,11},{10,... | collective-permute-start | bytes 393224 | tf_op jit(solution)/shard_map/ppermute | solution.py:278
  86.0 10.6 %collective-permute-start.8 = (bf16[32,1408]{1,0:T(8,128)(2,1)S(1)}, bf16[32,1408]{1,0:T(8,128)(2,1)S(1)}, u32[]{:S(2)}, u32[]{:S(2)}) collective-permute-start(bf16[32,1408]{1,0:T(8,128)(2,1)S(1)} %get-tuple-element.66), channel_id=1, source_target_pairs={{0,2},{1,3},{2,0},{3,1},{4,6},{5,7},{6,4},{7,5},{8,10},{9,11},{10,... | collective-permute-start | bytes 270344 | tf_op jit(solution)/shard_map/ppermute | solution.py:278
  86.3 7.8 %collective-permute-start.9 = (bf16[32,1280]{1,0:T(8,128)(2,1)S(1)}, bf16[32,1280]{1,0:T(8,128)(2,1)S(1)}, u32[]{:S(2)}, u32[]{:S(2)}) collective-permute-start(bf16[32,1280]{1,0:T(8,128)(2,1)S(1)} %get-tuple-element.67), channel_id=1, source_target_pairs={{0,1},{1,0},{2,3},{3,2},{4,5},{5,4},{6,7},{7,6},{8,9},{9,8},{10,11... | collective-permute-start | bytes 245768 | tf_op jit(solution)/shard_map/ppermute | solution.py:278
  93.9 5.8 %collective-permute-start.15 = (bf16[32,1024]{1,0:T(8,128)(2,1)S(1)}, bf16[32,1024]{1,0:T(8,128)(2,1)S(1)}, u32[]{:S(2)}, u32[]{:S(2)}) collective-permute-start(bf16[32,1024]{1,0:T(8,128)(2,1)S(1)} %get-tuple-element.76), channel_id=1, source_target_pairs={{0,2},{1,3},{2,0},{3,1},{4,6},{5,7},{6,4},{7,5},{8,10},{9,11},{10,... | collective-permute-start | bytes 196616 | tf_op jit(solution)/shard_map/ppermute | solution.py:278
  94.0 5.9 %collective-permute-start.16 = (bf16[32,1024]{1,0:T(8,128)(2,1)S(1)}, bf16[32,1024]{1,0:T(8,128)(2,1)S(1)}, u32[]{:S(2)}, u32[]{:S(2)}) collective-permute-start(bf16[32,1024]{1,0:T(8,128)(2,1)S(1)} %get-tuple-element.77), channel_id=1, source_target_pairs={{0,1},{1,0},{2,3},{3,2},{4,5},{5,4},{6,7},{7,6},{8,9},{9,8},{10,11... | collective-permute-start | bytes 196616 | tf_op jit(solution)/shard_map/ppermute | solution.py:278
  96.7 6.9 %collective-permute-start.11 = (bf16[32,1280]{1,0:T(8,128)(2,1)S(1)}, bf16[32,1280]{1,0:T(8,128)(2,1)S(1)}, u32[]{:S(2)}, u32[]{:S(2)}) collective-permute-start(bf16[32,1280]{1,0:T(8,128)(2,1)S(1)} %get-tuple-element.68.refs_0_), channel_id=1, source_target_pairs={{0,2},{1,3},{2,0},{3,1},{4,6},{5,7},{6,4},{7,5},{8,10},{9,11},{10,... | collective-permute-start | bytes 245768 | tf_op jit(solution)/shard_map/ppermute | solution.py:278
  100.5 5.6 %collective-permute-start.18 = (bf16[32,1024]{1,0:T(8,128)(2,1)S(1)}, bf16[32,1024]{1,0:T(8,128)(2,1)S(1)}, u32[]{:S(2)}, u32[]{:S(2)}) collective-permute-start(bf16[32,1024]{1,0:T(8,128)(2,1)S(1)} %get-tuple-element.78.refs_4_), channel_id=1, source_target_pairs={{0,2},{1,3},{2,0},{3,1},{4,6},{5,7},{6,4},{7,5},{8,10},{9,11},{10,... | collective-permute-start | bytes 196616 | tf_op jit(solution)/shard_map/ppermute | solution.py:278
  102.3 6.9 %collective-permute-start.10 = (bf16[32,1280]{1,0:T(8,128)(2,1)S(1)}, bf16[32,1280]{1,0:T(8,128)(2,1)S(1)}, u32[]{:S(2)}, u32[]{:S(2)}) collective-permute-start(bf16[32,1280]{1,0:T(8,128)(2,1)S(1)} %get-tuple-element.68.refs_0_), channel_id=1, source_target_pairs={{0,1},{1,0},{2,3},{3,2},{4,5},{5,4},{6,7},{7,6},{8,9},{9,8},{10,11... | collective-permute-start | bytes 245768 | tf_op jit(solution)/shard_map/ppermute | solution.py:278
  103.6 6.7 %collective-permute-start.12 = (bf16[32,1280]{1,0:T(8,128)(2,1)S(1)}, bf16[32,1280]{1,0:T(8,128)(2,1)S(1)}, u32[]{:S(2)}, u32[]{:S(2)}) collective-permute-start(bf16[32,1280]{1,0:T(8,128)(2,1)S(1)} %collective-permute-done.11.refs_2_), channel_id=1, source_target_pairs={{0,1},{1,0},{2,3},{3,2},{4,5},{5,4},{6,7},{7,6},{8,9},{9,8},{10,11... | collective-permute-start | bytes 245768 | tf_op jit(solution)/shard_map/ppermute | solution.py:278
  104.3 4.9 %collective-permute-start.17 = (bf16[32,1024]{1,0:T(8,128)(2,1)S(1)}, bf16[32,1024]{1,0:T(8,128)(2,1)S(1)}, u32[]{:S(2)}, u32[]{:S(2)}) collective-permute-start(bf16[32,1024]{1,0:T(8,128)(2,1)S(1)} %get-tuple-element.78.refs_4_), channel_id=1, source_target_pairs={{0,1},{1,0},{2,3},{3,2},{4,5},{5,4},{6,7},{7,6},{8,9},{9,8},{10,11... | collective-permute-start | bytes 196616 | tf_op jit(solution)/shard_map/ppermute | solution.py:278
  106.1 4.3 %collective-permute-start.19 = (bf16[32,1024]{1,0:T(8,128)(2,1)S(1)}, bf16[32,1024]{1,0:T(8,128)(2,1)S(1)}, u32[]{:S(2)}, u32[]{:S(2)}) collective-permute-start(bf16[32,1024]{1,0:T(8,128)(2,1)S(1)} %collective-permute-done.18.refs_6_), channel_id=1, source_target_pairs={{0,1},{1,0},{2,3},{3,2},{4,5},{5,4},{6,7},{7,6},{8,9},{9,8},{10,11... | collective-permute-start | bytes 196616 | tf_op jit(solution)/shard_map/ppermute | solution.py:278
  (6 other events, 191.3 us)

commit v17 on v14

--- a/solution.py
+++ b/solution.py
@@ -420,7 +420,7 @@
 def gate_up(hidden, gain, w_gate, w_up, halves):
     requests, width = hidden.shape
     units = w_gate.shape[1]
-    first = units if halves == 1 else round_up(units // 2, 256)
+    first = units if halves == 1 else round_up(units * 5 // 8, 256)
     w_gate, w_up = fetched(w_gate), fetched(w_up)
 
     def shapes(columns, extra):

time: 130 us -> 135 us (1.038)
  starting transfers between devices: 21.9 us -> 25.6 us
  Pallas kernels: 15.6 us -> 17.2 us
    ppermute x20, starting transfers between devices: 21.9 us -> 25.6 us  [from_distance(): lax.ppermute(piece, axis, [(k, k ^ distance) for k in range(lax.axis_size...]
    pallas_call x1, Pallas kernels: 7.93 us -> 9.44 us  [attend(): pl.pallas_call(attention_kernel, out_shape=jax.ShapeDtypeStruct((ranks, n...]
  transfers between devices with their start and end apart: 20 -> 20, of which waited for: 12 -> 11; matrix products, arithmetic and copies ran while one was open for 0% -> 0% of each run, Pallas kernels for 3% -> 2%
where the time goes in v17:
time: 135 us
  blocking collectives  62.4 us (46%)
  waiting for transfers between devices  29.6 us (22%)
  starting transfers between devices  25.6 us (19%)
  Pallas kernels  17.2 us (13%)
    all_to_all x3, blocking collectives, swap(): return lax.all_to_all(parts, axes, split_axis=0, concat_axis=0, tiled=True)  53.6 us
    ppermute x20, waiting for transfers between devices, from_distance(): lax.ppermute(piece, axis, [(k, k ^ distance) for k in range(lax.axis_size...  29.6 us
    ppermute x20, starting transfers between devices, from_distance(): lax.ppermute(piece, axis, [(k, k ^ distance) for k in range(lax.axis_size...  25.6 us
    pallas_call x1, Pallas kernels, attend(): pl.pallas_call(attention_kernel, out_shape=jax.ShapeDtypeStruct((ranks, n...  9.44 us
    all_gather x1, blocking collectives, local(): hidden = lax.all_gather(own_hidden, 'dp', axis=0, tiled=True)  8.78 us
  transfers between devices with their start and end apart: 20, of which 11 were waited for; matrix products, arithmetic and copies ran while one was open for 0% of the time, Pallas kernels for 2%

profile of v17, /device:TPU:0, one launch (start us, length us, event | category | flops | bytes accessed | tf_op | source)
XLA Modules:
  0.0 135.0 jit_solution(3959156525742876797)
XLA Ops:
  0.0 9.4 %attention.1 = bf16[32,16,512]{2,1,0:T(8,128)(2,1)S(1)} custom-call(s32[128]{0:T(128)} %lens_ref.1, bf16[4,73728]{1,0:T(4,128)(2,1)} %raw_ref.1, bf16[576,14336]{1,0:T(8,128)(2,1)} %bitcast.29), custom_call_target="tpu_custom_call" | custom-call | flops 3992977408 | bytes 16515072 | tf_op jit(solution)/shard_map/attention/pallas_call | solution.py:192
  9.5 26.2 %all_to_all.15 = bf16[32,16,512]{2,1,0:T(8,128)(2,1)S(1)} all-to-all(bf16[32,16,512]{2,1,0:T(8,128)(2,1)S(1)} %attention.1), channel_id=1, replica_groups=mesh['dp'=8,'tp'=4] {'dp','tp'}, dimensions={0} | all-to-all | bytes 1048576 | tf_op jit(solution)/shard_map/all_to_all | solution.py:598
  36.5 2.9 %collective-permute-start.2 = (bf16[128,512]{1,0:T(8,128)(2,1)S(1)}, bf16[128,512]{1,0:T(8,128)(2,1)S(1)}, u32[]{:S(2)}, u32[]{:S(2)}) collective-permute-start(bf16[128,512]{1,0:T(8,128)(2,1)S(1)} %head_values.1.value_ref), channel_id=1, source_target_pairs={{0,3},{1,2},{2,1},{3,0},{4,7},{5,6},{6,5},{7,4},{8,11},{9,10},{10,... | collective-permute-start | bytes 393224 | tf_op jit(solution)/shard_map/ppermute | solution.py:279
  41.0 1.7 %collective-permute-start.3 = (bf16[4,1792]{1,0:T(4,128)(2,1)S(1)}, bf16[4,1792]{1,0:T(4,128)(2,1)S(1)}, u32[]{:S(2)}, u32[]{:S(2)}) collective-permute-start(bf16[4,1792]{1,0:T(4,128)(2,1)S(1)} %get-tuple-element.45), channel_id=1, source_target_pairs={{0,1},{1,0},{2,3},{3,2},{4,5},{5,4},{6,7},{7,6},{8,9},{9,8},{10,11... | collective-permute-start | bytes 43016 | tf_op jit(solution)/shard_map/ppermute | solution.py:279
  42.7 1.7 %collective-permute-start.4 = (bf16[4,1792]{1,0:T(4,128)(2,1)S(1)}, bf16[4,1792]{1,0:T(4,128)(2,1)S(1)}, u32[]{:S(2)}, u32[]{:S(2)}) collective-permute-start(bf16[4,1792]{1,0:T(4,128)(2,1)S(1)} %get-tuple-element.46), channel_id=1, source_target_pairs={{0,2},{1,3},{2,0},{3,1},{4,6},{5,7},{6,4},{7,5},{8,10},{9,11},{10,... | collective-permute-start | bytes 43016 | tf_op jit(solution)/shard_map/ppermute | solution.py:279
  44.7 3.0 %collective-permute-start.5 = (bf16[4,1792]{1,0:T(4,128)(2,1)S(1)}, bf16[4,1792]{1,0:T(4,128)(2,1)S(1)}, u32[]{:S(2)}, u32[]{:S(2)}) collective-permute-start(bf16[4,1792]{1,0:T(4,128)(2,1)S(1)} %get-tuple-element.47), channel_id=1, source_target_pairs={{0,3},{1,2},{2,1},{3,0},{4,7},{5,6},{6,5},{7,4},{8,11},{9,10},{10,... | collective-permute-start | bytes 43016 | tf_op jit(solution)/shard_map/ppermute | solution.py:279
  48.1 4.6 %collective-permute-done.1.refs_2_ = bf16[128,512]{1,0:T(8,128)(2,1)S(1)} collective-permute-done((bf16[128,512]{1,0:T(8,128)(2,1)S(1)}, bf16[128,512]{1,0:T(8,128)(2,1)S(1)}, u32[]{:S(2)}, u32[]{:S(2)}) %collective-permute-start.1) | collective-permute-done | bytes 131104 | tf_op jit(solution)/shard_map/ppermute | solution.py:279
  53.6 11.6 %all_to_all.16.parts_ref = bf16[8,16,1792]{2,1,0:T(8,128)(2,1)S(1)} all-to-all(bf16[8,16,1792]{2,1,0:T(8,128)(2,1)S(1)} %bitcast.19), channel_id=1, replica_groups=mesh['dp'=8,'tp'=4] {'dp'}, dimensions={0} | all-to-all | bytes 917504 | tf_op jit(solution)/shard_map/all_to_all | solution.py:598
  65.3 8.8 %all_gather.3.hidden_ref = bf16[128,1792]{1,0:T(8,128)(2,1)S(1)} all-gather(bf16[16,1792]{1,0:T(8,128)(2,1)S(1)} %hidden.1.refs_9_), channel_id=1, replica_groups=mesh['dp'=8,'tp'=4] {'dp'}, dimensions={0}, use_global_device_ids=true | all-gather | bytes 516096 | tf_op jit(solution)/shard_map/all_gather | solution.py:624
  74.1 1.6 %gate_up.1 = (bf16[2,128,1792]{2,1,0:T(8,128)(2,1)S(1)}, bf16[64,1664]{1,0:T(8,128)(2,1)S(1)}, bf16[64,1536]{1,0:T(8,128)(2,1)S(1)}, bf16[64,1664]{1,0:T(8,128)(2,1)S(1)}, bf16[64,1536]{1,0:T(8,128)(2,1)S(1)}) custom-call(bf16[128,1792]{1,0:T(8,128)(2,1)S(1)} %all_gather.3.hidden_ref, bf16[56,128]{1,0:T(8,128)(2,1)S(1)} %bitcast.28, ...), custom_call_target="tpu_custom_call" | custom-call | flops 1409286144 | bytes 11010048 | tf_op jit(solution)/shard_map/gate_up/pallas_call | solution.py:434
  76.7 1.5 %collective-permute-start.7 = (bf16[64,1536]{1,0:T(8,128)(2,1)S(1)}, bf16[64,1536]{1,0:T(8,128)(2,1)S(1)}, u32[]{:S(2)}, u32[]{:S(2)}) collective-permute-start(bf16[64,1536]{1,0:T(8,128)(2,1)S(1)} %get-tuple-element.63), channel_id=1, source_target_pairs={{0,2},{1,3},{2,0},{3,1},{4,6},{5,7},{6,4},{7,5},{8,10},{9,11},{10,... | collective-permute-start | bytes 589832 | tf_op jit(solution)/shard_map/ppermute | solution.py:279
  79.0 9.7 %collective-permute-done.7.refs_3_ = bf16[64,1536]{1,0:T(8,128)(2,1)S(1)} collective-permute-done((bf16[64,1536]{1,0:T(8,128)(2,1)S(1)}, bf16[64,1536]{1,0:T(8,128)(2,1)S(1)}, u32[]{:S(2)}, u32[]{:S(2)}) %collective-permute-start.7) | collective-permute-done | bytes 196640 | tf_op jit(solution)/shard_map/ppermute | solution.py:279
  90.1 1.5 %collective-permute-start.13 = (bf16[64,768]{1,0:T(8,128)(2,1)S(1)}, bf16[64,768]{1,0:T(8,128)(2,1)S(1)}, u32[]{:S(2)}, u32[]{:S(2)}) collective-permute-start(bf16[64,768]{1,0:T(8,128)(2,1)S(1)} %get-tuple-element.72), channel_id=1, source_target_pairs={{0,1},{1,0},{2,3},{3,2},{4,5},{5,4},{6,7},{7,6},{8,9},{9,8},{10,11... | collective-permute-start | bytes 294920 | tf_op jit(solution)/shard_map/ppermute | solution.py:279
  91.5 2.3 %collective-permute-start.14 = (bf16[64,768]{1,0:T(8,128)(2,1)S(1)}, bf16[64,768]{1,0:T(8,128)(2,1)S(1)}, u32[]{:S(2)}, u32[]{:S(2)}) collective-permute-start(bf16[64,768]{1,0:T(8,128)(2,1)S(1)} %get-tuple-element.73), channel_id=1, source_target_pairs={{0,2},{1,3},{2,0},{3,1},{4,6},{5,7},{6,4},{7,5},{8,10},{9,11},{10,... | collective-permute-start | bytes 294920 | tf_op jit(solution)/shard_map/ppermute | solution.py:279
  93.9 2.8 %collective-permute-done.9 = bf16[32,1536]{1,0:T(8,128)(2,1)S(1)} collective-permute-done((bf16[32,1536]{1,0:T(8,128)(2,1)S(1)}, bf16[32,1536]{1,0:T(8,128)(2,1)S(1)}, u32[]{:S(2)}, u32[]{:S(2)}) %collective-permute-start.9) | collective-permute-done | bytes 98336 | tf_op jit(solution)/shard_map/ppermute | solution.py:279
  96.9 1.6 %collective-permute-start.11 = (bf16[32,1536]{1,0:T(8,128)(2,1)S(1)}, bf16[32,1536]{1,0:T(8,128)(2,1)S(1)}, u32[]{:S(2)}, u32[]{:S(2)}) collective-permute-start(bf16[32,1536]{1,0:T(8,128)(2,1)S(1)} %get-tuple-element.68.refs_0_), channel_id=1, source_target_pairs={{0,2},{1,3},{2,0},{3,1},{4,6},{5,7},{6,4},{7,5},{8,10},{9,11},{10,... | collective-permute-start | bytes 294920 | tf_op jit(solution)/shard_map/ppermute | solution.py:279
  98.8 2.7 %collective-permute-done.14.refs_3_ = bf16[64,768]{1,0:T(8,128)(2,1)S(1)} collective-permute-done((bf16[64,768]{1,0:T(8,128)(2,1)S(1)}, bf16[64,768]{1,0:T(8,128)(2,1)S(1)}, u32[]{:S(2)}, u32[]{:S(2)}) %collective-permute-start.14) | collective-permute-done | bytes 98336 | tf_op jit(solution)/shard_map/ppermute | solution.py:279
  102.7 4.1 %collective-permute-done.15 = bf16[32,768]{1,0:T(8,128)(2,1)S(1)} collective-permute-done((bf16[32,768]{1,0:T(8,128)(2,1)S(1)}, bf16[32,768]{1,0:T(8,128)(2,1)S(1)}, u32[]{:S(2)}, u32[]{:S(2)}) %collective-permute-start.15) | collective-permute-done | bytes 49184 | tf_op jit(solution)/shard_map/ppermute | solution.py:279
  107.7 1.9 %collective-permute-start.18 = (bf16[32,768]{1,0:T(8,128)(2,1)S(1)}, bf16[32,768]{1,0:T(8,128)(2,1)S(1)}, u32[]{:S(2)}, u32[]{:S(2)}) collective-permute-start(bf16[32,768]{1,0:T(8,128)(2,1)S(1)} %get-tuple-element.78.refs_4_), channel_id=1, source_target_pairs={{0,2},{1,3},{2,0},{3,1},{4,6},{5,7},{6,4},{7,5},{8,10},{9,11},{10,... | collective-permute-start | bytes 147464 | tf_op jit(solution)/shard_map/ppermute | solution.py:279
  109.6 2.0 %collective-permute-start.12 = (bf16[32,1536]{1,0:T(8,128)(2,1)S(1)}, bf16[32,1536]{1,0:T(8,128)(2,1)S(1)}, u32[]{:S(2)}, u32[]{:S(2)}) collective-permute-start(bf16[32,1536]{1,0:T(8,128)(2,1)S(1)} %collective-permute-done.11.refs_2_), channel_id=1, source_target_pairs={{0,1},{1,0},{2,3},{3,2},{4,5},{5,4},{6,7},{7,6},{8,9},{9,8},{10,11... | collective-permute-start | bytes 294920 | tf_op jit(solution)/shard_map/ppermute | solution.py:279
  111.6 1.3 collective-permute-done.18.refs_6_
  113.6 2.1 %collective-permute-done.17.refs_5_ = bf16[32,768]{1,0:T(8,128)(2,1)S(1)} collective-permute-done((bf16[32,768]{1,0:T(8,128)(2,1)S(1)}, bf16[32,768]{1,0:T(8,128)(2,1)S(1)}, u32[]{:S(2)}, u32[]{:S(2)}) %collective-permute-start.17) | collective-permute-done | bytes 49184 | tf_op jit(solution)/shard_map/ppermute | solution.py:279
  117.1 1.4 %project_down.1 = bf16[32,4,1792]{2,1,0:T(4,128)(2,1)S(1)} custom-call(bf16[32,1536]{1,0:T(8,128)(2,1)S(1)} %get-tuple-element.68.refs_0_, bf16[32,1536]{1,0:T(8,128)(2,1)S(1)} %collective-permute-done.10.refs_1_, bf16[32,1536]{1,0:T(8,128)(2,1)S(1)} %collective-permute-done.11.refs_2_, bf16[32,1536]{1,0:T(8,128)(2,1)S(1)} %collective-permute-done.12.refs_3_, ...), custom_call_target="tpu_custom_call" | custom-call | tf_op jit(solution)/shard_map/project_down/pallas_call | solution.py:559
  118.5 15.8 %all_to_all.17.parts_ref = bf16[32,4,1792]{2,1,0:T(4,128)(2,1)S(1)} all-to-all(bf16[32,4,1792]{2,1,0:T(4,128)(2,1)S(1)} %project_down.1), channel_id=1, replica_groups=mesh['dp'=8,'tp'=4] {'dp','tp'}, dimensions={0} | all-to-all | bytes 917504 | tf_op jit(solution)/shard_map/all_to_all | solution.py:598
  (57 shorter events, 12.5 us)
Async XLA Ops:
  0.0 41.0 %copy-start.2 = (bf16[4,7168]{1,0:T(4,128)(2,1)S(1)}, bf16[4,7168]{1,0:T(4,128)(2,1)}, u32[]{:S(2)}) copy-start(bf16[4,7168]{1,0:T(4,128)(2,1)} %rows_ref) | copy-start | bytes 172036
  0.0 47.7 %copy-start = (bf16[2048,1792]{1,0:T(8,128)(2,1)S(1)}, bf16[2048,1792]{1,0:T(8,128)(2,1)}, u32[]{:S(2)}) copy-start(bf16[2048,1792]{1,0:T(8,128)(2,1)} %refs_4_.1) | copy-start | bytes 22020100
  0.0 74.1 %slice-start.2 = ((s8[8257536]{0:T(1024)(128)(4,1)}), s8[4194304]{0:T(1024)(128)(4,1)S(1)}, s32[]{:S(2)}) async-start(s8[8257536]{0:T(1024)(128)(4,1)} %bitcast.14), calls=%async_computation.5 | async-start | bytes 8388608
  36.5 8.2 %collective-permute-start.2 = (bf16[128,512]{1,0:T(8,128)(2,1)S(1)}, bf16[128,512]{1,0:T(8,128)(2,1)S(1)}, u32[]{:S(2)}, u32[]{:S(2)}) collective-permute-start(bf16[128,512]{1,0:T(8,128)(2,1)S(1)} %head_values.1.value_ref), channel_id=1, source_target_pairs={{0,3},{1,2},{2,1},{3,0},{4,7},{5,6},{6,5},{7,4},{8,11},{9,10},{10,... | collective-permute-start | bytes 393224 | tf_op jit(solution)/shard_map/ppermute | solution.py:279
  39.4 13.3 %collective-permute-start.1 = (bf16[128,512]{1,0:T(8,128)(2,1)S(1)}, bf16[128,512]{1,0:T(8,128)(2,1)S(1)}, u32[]{:S(2)}, u32[]{:S(2)}) collective-permute-start(bf16[128,512]{1,0:T(8,128)(2,1)S(1)} %head_values.1.value_ref), channel_id=1, source_target_pairs={{0,2},{1,3},{2,0},{3,1},{4,6},{5,7},{6,4},{7,5},{8,10},{9,11},{10,... | collective-permute-start | bytes 393224 | tf_op jit(solution)/shard_map/ppermute | solution.py:279
  40.6 12.1 %collective-permute-start = (bf16[128,512]{1,0:T(8,128)(2,1)S(1)}, bf16[128,512]{1,0:T(8,128)(2,1)S(1)}, u32[]{:S(2)}, u32[]{:S(2)}) collective-permute-start(bf16[128,512]{1,0:T(8,128)(2,1)S(1)} %head_values.1.value_ref), channel_id=1, source_target_pairs={{0,1},{1,0},{2,3},{3,2},{4,5},{5,4},{6,7},{7,6},{8,9},{9,8},{10,11... | collective-permute-start | bytes 393224 | tf_op jit(solution)/shard_map/ppermute | solution.py:279
  41.0 12.6 %collective-permute-start.3 = (bf16[4,1792]{1,0:T(4,128)(2,1)S(1)}, bf16[4,1792]{1,0:T(4,128)(2,1)S(1)}, u32[]{:S(2)}, u32[]{:S(2)}) collective-permute-start(bf16[4,1792]{1,0:T(4,128)(2,1)S(1)} %get-tuple-element.45), channel_id=1, source_target_pairs={{0,1},{1,0},{2,3},{3,2},{4,5},{5,4},{6,7},{7,6},{8,9},{9,8},{10,11... | collective-permute-start | bytes 43016 | tf_op jit(solution)/shard_map/ppermute | solution.py:279
  42.7 10.9 %collective-permute-start.4 = (bf16[4,1792]{1,0:T(4,128)(2,1)S(1)}, bf16[4,1792]{1,0:T(4,128)(2,1)S(1)}, u32[]{:S(2)}, u32[]{:S(2)}) collective-permute-start(bf16[4,1792]{1,0:T(4,128)(2,1)S(1)} %get-tuple-element.46), channel_id=1, source_target_pairs={{0,2},{1,3},{2,0},{3,1},{4,6},{5,7},{6,4},{7,5},{8,10},{9,11},{10,... | collective-permute-start | bytes 43016 | tf_op jit(solution)/shard_map/ppermute | solution.py:279
  44.7 8.9 %collective-permute-start.5 = (bf16[4,1792]{1,0:T(4,128)(2,1)S(1)}, bf16[4,1792]{1,0:T(4,128)(2,1)S(1)}, u32[]{:S(2)}, u32[]{:S(2)}) collective-permute-start(bf16[4,1792]{1,0:T(4,128)(2,1)S(1)} %get-tuple-element.47), channel_id=1, source_target_pairs={{0,3},{1,2},{2,1},{3,0},{4,7},{5,6},{6,5},{7,4},{8,11},{9,10},{10,... | collective-permute-start | bytes 43016 | tf_op jit(solution)/shard_map/ppermute | solution.py:279
  74.1 42.9 %slice-start.4 = ((s8[8257536]{0:T(1024)(128)(4,1)}), s8[4194304]{0:T(1024)(128)(4,1)S(1)}, s32[]{:S(2)}) async-start(s8[8257536]{0:T(1024)(128)(4,1)} %bitcast.16), calls=%async_computation.7 | async-start | bytes 8388608
  75.7 13.0 %collective-permute-start.6 = (bf16[64,1664]{1,0:T(8,128)(2,1)S(1)}, bf16[64,1664]{1,0:T(8,128)(2,1)S(1)}, u32[]{:S(2)}, u32[]{:S(2)}) collective-permute-start(bf16[64,1664]{1,0:T(8,128)(2,1)S(1)} %get-tuple-element.62), channel_id=1, source_target_pairs={{0,1},{1,0},{2,3},{3,2},{4,5},{5,4},{6,7},{7,6},{8,9},{9,8},{10,11... | collective-permute-start | bytes 638984 | tf_op jit(solution)/shard_map/ppermute | solution.py:279
  76.7 12.0 %collective-permute-start.7 = (bf16[64,1536]{1,0:T(8,128)(2,1)S(1)}, bf16[64,1536]{1,0:T(8,128)(2,1)S(1)}, u32[]{:S(2)}, u32[]{:S(2)}) collective-permute-start(bf16[64,1536]{1,0:T(8,128)(2,1)S(1)} %get-tuple-element.63), channel_id=1, source_target_pairs={{0,2},{1,3},{2,0},{3,1},{4,6},{5,7},{6,4},{7,5},{8,10},{9,11},{10,... | collective-permute-start | bytes 589832 | tf_op jit(solution)/shard_map/ppermute | solution.py:279
  88.8 7.9 %collective-permute-start.8 = (bf16[32,1664]{1,0:T(8,128)(2,1)S(1)}, bf16[32,1664]{1,0:T(8,128)(2,1)S(1)}, u32[]{:S(2)}, u32[]{:S(2)}) collective-permute-start(bf16[32,1664]{1,0:T(8,128)(2,1)S(1)} %get-tuple-element.66), channel_id=1, source_target_pairs={{0,2},{1,3},{2,0},{3,1},{4,6},{5,7},{6,4},{7,5},{8,10},{9,11},{10,... | collective-permute-start | bytes 319496 | tf_op jit(solution)/shard_map/ppermute | solution.py:279
  89.5 7.2 %collective-permute-start.9 = (bf16[32,1536]{1,0:T(8,128)(2,1)S(1)}, bf16[32,1536]{1,0:T(8,128)(2,1)S(1)}, u32[]{:S(2)}, u32[]{:S(2)}) collective-permute-start(bf16[32,1536]{1,0:T(8,128)(2,1)S(1)} %get-tuple-element.67), channel_id=1, source_target_pairs={{0,1},{1,0},{2,3},{3,2},{4,5},{5,4},{6,7},{7,6},{8,9},{9,8},{10,11... | collective-permute-start | bytes 294920 | tf_op jit(solution)/shard_map/ppermute | solution.py:279
  90.1 8.8 %collective-permute-start.13 = (bf16[64,768]{1,0:T(8,128)(2,1)S(1)}, bf16[64,768]{1,0:T(8,128)(2,1)S(1)}, u32[]{:S(2)}, u32[]{:S(2)}) collective-permute-start(bf16[64,768]{1,0:T(8,128)(2,1)S(1)} %get-tuple-element.72), channel_id=1, source_target_pairs={{0,1},{1,0},{2,3},{3,2},{4,5},{5,4},{6,7},{7,6},{8,9},{9,8},{10,11... | collective-permute-start | bytes 294920 | tf_op jit(solution)/shard_map/ppermute | solution.py:279
  91.5 10.0 %collective-permute-start.14 = (bf16[64,768]{1,0:T(8,128)(2,1)S(1)}, bf16[64,768]{1,0:T(8,128)(2,1)S(1)}, u32[]{:S(2)}, u32[]{:S(2)}) collective-permute-start(bf16[64,768]{1,0:T(8,128)(2,1)S(1)} %get-tuple-element.73), channel_id=1, source_target_pairs={{0,2},{1,3},{2,0},{3,1},{4,6},{5,7},{6,4},{7,5},{8,10},{9,11},{10,... | collective-permute-start | bytes 294920 | tf_op jit(solution)/shard_map/ppermute | solution.py:279
  96.9 12.7 %collective-permute-start.11 = (bf16[32,1536]{1,0:T(8,128)(2,1)S(1)}, bf16[32,1536]{1,0:T(8,128)(2,1)S(1)}, u32[]{:S(2)}, u32[]{:S(2)}) collective-permute-start(bf16[32,1536]{1,0:T(8,128)(2,1)S(1)} %get-tuple-element.68.refs_0_), channel_id=1, source_target_pairs={{0,2},{1,3},{2,0},{3,1},{4,6},{5,7},{6,4},{7,5},{8,10},{9,11},{10,... | collective-permute-start | bytes 294920 | tf_op jit(solution)/shard_map/ppermute | solution.py:279
  101.6 5.2 %collective-permute-start.15 = (bf16[32,768]{1,0:T(8,128)(2,1)S(1)}, bf16[32,768]{1,0:T(8,128)(2,1)S(1)}, u32[]{:S(2)}, u32[]{:S(2)}) collective-permute-start(bf16[32,768]{1,0:T(8,128)(2,1)S(1)} %get-tuple-element.76), channel_id=1, source_target_pairs={{0,2},{1,3},{2,0},{3,1},{4,6},{5,7},{6,4},{7,5},{8,10},{9,11},{10,... | collective-permute-start | bytes 147464 | tf_op jit(solution)/shard_map/ppermute | solution.py:279
  102.4 4.6 %collective-permute-start.16 = (bf16[32,768]{1,0:T(8,128)(2,1)S(1)}, bf16[32,768]{1,0:T(8,128)(2,1)S(1)}, u32[]{:S(2)}, u32[]{:S(2)}) collective-permute-start(bf16[32,768]{1,0:T(8,128)(2,1)S(1)} %get-tuple-element.77), channel_id=1, source_target_pairs={{0,1},{1,0},{2,3},{3,2},{4,5},{5,4},{6,7},{7,6},{8,9},{9,8},{10,11... | collective-permute-start | bytes 147464 | tf_op jit(solution)/shard_map/ppermute | solution.py:279
  107.7 5.3 %collective-permute-start.18 = (bf16[32,768]{1,0:T(8,128)(2,1)S(1)}, bf16[32,768]{1,0:T(8,128)(2,1)S(1)}, u32[]{:S(2)}, u32[]{:S(2)}) collective-permute-start(bf16[32,768]{1,0:T(8,128)(2,1)S(1)} %get-tuple-element.78.refs_4_), channel_id=1, source_target_pairs={{0,2},{1,3},{2,0},{3,1},{4,6},{5,7},{6,4},{7,5},{8,10},{9,11},{10,... | collective-permute-start | bytes 147464 | tf_op jit(solution)/shard_map/ppermute | solution.py:279
  109.6 7.5 %collective-permute-start.10 = (bf16[32,1536]{1,0:T(8,128)(2,1)S(1)}, bf16[32,1536]{1,0:T(8,128)(2,1)S(1)}, u32[]{:S(2)}, u32[]{:S(2)}) collective-permute-start(bf16[32,1536]{1,0:T(8,128)(2,1)S(1)} %get-tuple-element.68.refs_0_), channel_id=1, source_target_pairs={{0,1},{1,0},{2,3},{3,2},{4,5},{5,4},{6,7},{7,6},{8,9},{9,8},{10,11... | collective-permute-start | bytes 294920 | tf_op jit(solution)/shard_map/ppermute | solution.py:279
  109.6 7.5 %collective-permute-start.12 = (bf16[32,1536]{1,0:T(8,128)(2,1)S(1)}, bf16[32,1536]{1,0:T(8,128)(2,1)S(1)}, u32[]{:S(2)}, u32[]{:S(2)}) collective-permute-start(bf16[32,1536]{1,0:T(8,128)(2,1)S(1)} %collective-permute-done.11.refs_2_), channel_id=1, source_target_pairs={{0,1},{1,0},{2,3},{3,2},{4,5},{5,4},{6,7},{7,6},{8,9},{9,8},{10,11... | collective-permute-start | bytes 294920 | tf_op jit(solution)/shard_map/ppermute | solution.py:279
  111.6 4.2 %collective-permute-start.17 = (bf16[32,768]{1,0:T(8,128)(2,1)S(1)}, bf16[32,768]{1,0:T(8,128)(2,1)S(1)}, u32[]{:S(2)}, u32[]{:S(2)}) collective-permute-start(bf16[32,768]{1,0:T(8,128)(2,1)S(1)} %get-tuple-element.78.refs_4_), channel_id=1, source_target_pairs={{0,1},{1,0},{2,3},{3,2},{4,5},{5,4},{6,7},{7,6},{8,9},{9,8},{10,11... | collective-permute-start | bytes 147464 | tf_op jit(solution)/shard_map/ppermute | solution.py:279
  112.9 4.1 %collective-permute-start.19 = (bf16[32,768]{1,0:T(8,128)(2,1)S(1)}, bf16[32,768]{1,0:T(8,128)(2,1)S(1)}, u32[]{:S(2)}, u32[]{:S(2)}) collective-permute-start(bf16[32,768]{1,0:T(8,128)(2,1)S(1)} %collective-permute-done.18.refs_6_), channel_id=1, source_target_pairs={{0,1},{1,0},{2,3},{3,2},{4,5},{5,4},{6,7},{7,6},{8,9},{9,8},{10,11... | collective-permute-start | bytes 147464 | tf_op jit(solution)/shard_map/ppermute | solution.py:279
  (6 other events, 197.8 us)

commit v18 on v14

--- a/solution.py
+++ b/solution.py
@@ -489,7 +489,7 @@
 
 
 def inner_kernel(model, given, *refs):
-    *parts, out_ref, factor_ref = refs
+    *parts, out_ref = refs if given else refs[:-1]
     gates, ups = parts[given::2], parts[given + 1 :: 2]
     columns = out_ref.shape[1]
 
@@ -503,8 +503,8 @@
         factor = parts[0][...]
     else:
         square = jnp.sum(total(gates, slice(columns, columns + 128)), 1, keepdims=True)
-        factor = jnp.broadcast_to(lax.rsqrt(square / model + 1e-06), factor_ref.shape)
-    factor_ref[...] = factor
+        factor = jnp.broadcast_to(lax.rsqrt(square / model + 1e-06), refs[-1].shape)
+        refs[-1][...] = factor
     for at in range(0, columns, 128):
         at = slice(at, at + 128)
         gate = total(gates, at) * factor
@@ -515,17 +515,19 @@
 def make_inner(parts, factor, model):
     given = [] if factor is None else [factor]
     rows, columns = parts[1].shape[1:]
-    return pl.pallas_call(
+    shapes = [
+        jax.ShapeDtypeStruct((rows, columns), jnp.bfloat16),
+        jax.ShapeDtypeStruct((rows, 128), jnp.float32),
+    ][: 2 - len(given)]
+    outs = pl.pallas_call(
         functools.partial(inner_kernel, model, len(given)),
-        out_shape=[
-            jax.ShapeDtypeStruct((rows, columns), jnp.bfloat16),
-            jax.ShapeDtypeStruct((rows, 128), jnp.float32),
-        ],
+        out_shape=shapes,
         in_specs=in_vmem(len(given) + len(parts)),
-        out_specs=in_vmem(2),
+        out_specs=in_vmem(len(shapes)),
         compiler_params=kernel_params(12),
         name="inner",
     )(*given, *parts)
+    return [*outs, *given]
 
 
 def down_kernel(chunks, *refs):

time: 130 us -> 132 us (1.015)
  blocking collectives: 62.5 us -> 64.8 us
    all_to_all x3, blocking collectives: 53.8 us -> 56 us  [swap(): return lax.all_to_all(parts, axes, split_axis=0, concat_axis=0, tiled=True)]
  transfers between devices with their start and end apart: 20 -> 20, of which waited for: 12 -> 11; matrix products, arithmetic and copies ran while one was open for 0% -> 0% of each run, Pallas kernels for 3% -> 2%
where the time goes in v18:
time: 132 us; the launch traced here: 131 us
  blocking collectives  64.8 us (49%)
  waiting for transfers between devices  29.7 us (22%)
  starting transfers between devices  21.2 us (16%)
  Pallas kernels  15.2 us (12%)
    all_to_all x3, blocking collectives, swap(): return lax.all_to_all(parts, axes, split_axis=0, concat_axis=0, tiled=True)  56 us
    ppermute x20, waiting for transfers between devices, from_distance(): lax.ppermute(piece, axis, [(k, k ^ distance) for k in range(lax.axis_size...  29.7 us
    ppermute x20, starting transfers between devices, from_distance(): lax.ppermute(piece, axis, [(k, k ^ distance) for k in range(lax.axis_size...  21.2 us
    all_gather x1, blocking collectives, local(): hidden = lax.all_gather(own_hidden, 'dp', axis=0, tiled=True)  8.78 us
    pallas_call x1, Pallas kernels, attend(): pl.pallas_call(attention_kernel, out_shape=jax.ShapeDtypeStruct((ranks, n...  8.02 us
  transfers between devices with their start and end apart: 20, of which 11 were waited for; matrix products, arithmetic and copies ran while one was open for 0% of the time, Pallas kernels for 2%

profile of v18, /device:TPU:0, one launch (start us, length us, event | category | flops | bytes accessed | tf_op | source)
XLA Modules:
  0.0 131.1 jit_solution(10323677768267297232)
XLA Ops:
  0.0 8.0 %attention.1 = bf16[32,16,512]{2,1,0:T(8,128)(2,1)S(1)} custom-call(s32[128]{0:T(128)} %lens_ref.1, bf16[4,73728]{1,0:T(4,128)(2,1)} %raw_ref.1, bf16[576,14336]{1,0:T(8,128)(2,1)} %bitcast.29), custom_call_target="tpu_custom_call" | custom-call | flops 3992977408 | bytes 16515072 | tf_op jit(solution)/shard_map/attention/pallas_call | solution.py:192
  8.0 28.7 %all_to_all.15 = bf16[32,16,512]{2,1,0:T(8,128)(2,1)S(1)} all-to-all(bf16[32,16,512]{2,1,0:T(8,128)(2,1)S(1)} %attention.1), channel_id=1, replica_groups=mesh['dp'=8,'tp'=4] {'dp','tp'}, dimensions={0} | all-to-all | bytes 1048576 | tf_op jit(solution)/shard_map/all_to_all | solution.py:600
  37.6 2.9 %collective-permute-start.2 = (bf16[128,512]{1,0:T(8,128)(2,1)S(1)}, bf16[128,512]{1,0:T(8,128)(2,1)S(1)}, u32[]{:S(2)}, u32[]{:S(2)}) collective-permute-start(bf16[128,512]{1,0:T(8,128)(2,1)S(1)} %head_values.1.value_ref), channel_id=1, source_target_pairs={{0,3},{1,2},{2,1},{3,0},{4,7},{5,6},{6,5},{7,4},{8,11},{9,10},{10,... | collective-permute-start | bytes 393224 | tf_op jit(solution)/shard_map/ppermute | solution.py:279
  42.1 1.7 %collective-permute-start.3 = (bf16[4,1792]{1,0:T(4,128)(2,1)S(1)}, bf16[4,1792]{1,0:T(4,128)(2,1)S(1)}, u32[]{:S(2)}, u32[]{:S(2)}) collective-permute-start(bf16[4,1792]{1,0:T(4,128)(2,1)S(1)} %get-tuple-element.44), channel_id=1, source_target_pairs={{0,1},{1,0},{2,3},{3,2},{4,5},{5,4},{6,7},{7,6},{8,9},{9,8},{10,11... | collective-permute-start | bytes 43016 | tf_op jit(solution)/shard_map/ppermute | solution.py:279
  43.8 1.7 %collective-permute-start.4 = (bf16[4,1792]{1,0:T(4,128)(2,1)S(1)}, bf16[4,1792]{1,0:T(4,128)(2,1)S(1)}, u32[]{:S(2)}, u32[]{:S(2)}) collective-permute-start(bf16[4,1792]{1,0:T(4,128)(2,1)S(1)} %get-tuple-element.45), channel_id=1, source_target_pairs={{0,2},{1,3},{2,0},{3,1},{4,6},{5,7},{6,4},{7,5},{8,10},{9,11},{10,... | collective-permute-start | bytes 43016 | tf_op jit(solution)/shard_map/ppermute | solution.py:279
  45.8 3.0 %collective-permute-start.5 = (bf16[4,1792]{1,0:T(4,128)(2,1)S(1)}, bf16[4,1792]{1,0:T(4,128)(2,1)S(1)}, u32[]{:S(2)}, u32[]{:S(2)}) collective-permute-start(bf16[4,1792]{1,0:T(4,128)(2,1)S(1)} %get-tuple-element.46), channel_id=1, source_target_pairs={{0,3},{1,2},{2,1},{3,0},{4,7},{5,6},{6,5},{7,4},{8,11},{9,10},{10,... | collective-permute-start | bytes 43016 | tf_op jit(solution)/shard_map/ppermute | solution.py:279
  49.2 4.6 %collective-permute-done.1.refs_2_ = bf16[128,512]{1,0:T(8,128)(2,1)S(1)} collective-permute-done((bf16[128,512]{1,0:T(8,128)(2,1)S(1)}, bf16[128,512]{1,0:T(8,128)(2,1)S(1)}, u32[]{:S(2)}, u32[]{:S(2)}) %collective-permute-start.1) | collective-permute-done | bytes 131104 | tf_op jit(solution)/shard_map/ppermute | solution.py:279
  54.7 11.6 %all_to_all.16.parts_ref = bf16[8,16,1792]{2,1,0:T(8,128)(2,1)S(1)} all-to-all(bf16[8,16,1792]{2,1,0:T(8,128)(2,1)S(1)} %bitcast.19), channel_id=1, replica_groups=mesh['dp'=8,'tp'=4] {'dp'}, dimensions={0} | all-to-all | bytes 917504 | tf_op jit(solution)/shard_map/all_to_all | solution.py:600
  66.4 8.8 %all_gather.3.hidden_ref = bf16[128,1792]{1,0:T(8,128)(2,1)S(1)} all-gather(bf16[16,1792]{1,0:T(8,128)(2,1)S(1)} %hidden.1.refs_9_), channel_id=1, replica_groups=mesh['dp'=8,'tp'=4] {'dp'}, dimensions={0}, use_global_device_ids=true | all-gather | bytes 516096 | tf_op jit(solution)/shard_map/all_gather | solution.py:626
  75.2 1.4 %gate_up.1 = (bf16[2,128,1792]{2,1,0:T(8,128)(2,1)S(1)}, bf16[64,1408]{1,0:T(8,128)(2,1)S(1)}, bf16[64,1280]{1,0:T(8,128)(2,1)S(1)}, bf16[64,1408]{1,0:T(8,128)(2,1)S(1)}, bf16[64,1280]{1,0:T(8,128)(2,1)S(1)}) custom-call(bf16[128,1792]{1,0:T(8,128)(2,1)S(1)} %all_gather.3.hidden_ref, bf16[56,128]{1,0:T(8,128)(2,1)S(1)} %bitcast.28, ...), custom_call_target="tpu_custom_call" | custom-call | flops 1174405120 | bytes 9175040 | tf_op jit(solution)/shard_map/gate_up/pallas_call | solution.py:434
  77.5 1.5 %collective-permute-start.7 = (bf16[64,1280]{1,0:T(8,128)(2,1)S(1)}, bf16[64,1280]{1,0:T(8,128)(2,1)S(1)}, u32[]{:S(2)}, u32[]{:S(2)}) collective-permute-start(bf16[64,1280]{1,0:T(8,128)(2,1)S(1)} %get-tuple-element.62), channel_id=1, source_target_pairs={{0,2},{1,3},{2,0},{3,1},{4,6},{5,7},{6,4},{7,5},{8,10},{9,11},{10,... | collective-permute-start | bytes 491528 | tf_op jit(solution)/shard_map/ppermute | solution.py:279
  80.7 2.1 %collective-permute-start.14 = (bf16[64,1024]{1,0:T(8,128)(2,1)S(1)}, bf16[64,1024]{1,0:T(8,128)(2,1)S(1)}, u32[]{:S(2)}, u32[]{:S(2)}) collective-permute-start(bf16[64,1024]{1,0:T(8,128)(2,1)S(1)} %get-tuple-element.72), channel_id=1, source_target_pairs={{0,2},{1,3},{2,0},{3,1},{4,6},{5,7},{6,4},{7,5},{8,10},{9,11},{10,... | collective-permute-start | bytes 393224 | tf_op jit(solution)/shard_map/ppermute | solution.py:279
  82.8 6.3 %collective-permute-done.7.refs_3_ = bf16[64,1280]{1,0:T(8,128)(2,1)S(1)} collective-permute-done((bf16[64,1280]{1,0:T(8,128)(2,1)S(1)}, bf16[64,1280]{1,0:T(8,128)(2,1)S(1)}, u32[]{:S(2)}, u32[]{:S(2)}) %collective-permute-start.7) | collective-permute-done | bytes 163872 | tf_op jit(solution)/shard_map/ppermute | solution.py:279
  90.4 1.9 %collective-permute-done.13.refs_2_ = bf16[64,1024]{1,0:T(8,128)(2,1)S(1)} collective-permute-done((bf16[64,1024]{1,0:T(8,128)(2,1)S(1)}, bf16[64,1024]{1,0:T(8,128)(2,1)S(1)}, u32[]{:S(2)}, u32[]{:S(2)}) %collective-permute-start.13) | collective-permute-done | bytes 131104 | tf_op jit(solution)/shard_map/ppermute | solution.py:279
  92.3 4.8 %collective-permute-done.14.refs_3_ = bf16[64,1024]{1,0:T(8,128)(2,1)S(1)} collective-permute-done((bf16[64,1024]{1,0:T(8,128)(2,1)S(1)}, bf16[64,1024]{1,0:T(8,128)(2,1)S(1)}, u32[]{:S(2)}, u32[]{:S(2)}) %collective-permute-start.14) | collective-permute-done | bytes 131104 | tf_op jit(solution)/shard_map/ppermute | solution.py:279
  97.3 2.5 %collective-permute-done.8 = bf16[32,1408]{1,0:T(8,128)(2,1)S(1)} collective-permute-done((bf16[32,1408]{1,0:T(8,128)(2,1)S(1)}, bf16[32,1408]{1,0:T(8,128)(2,1)S(1)}, u32[]{:S(2)}, u32[]{:S(2)}) %collective-permute-start.8) | collective-permute-done | bytes 90144 | tf_op jit(solution)/shard_map/ppermute | solution.py:279
  100.4 3.0 %collective-permute-done.15 = bf16[32,1024]{1,0:T(8,128)(2,1)S(1)} collective-permute-done((bf16[32,1024]{1,0:T(8,128)(2,1)S(1)}, bf16[32,1024]{1,0:T(8,128)(2,1)S(1)}, u32[]{:S(2)}, u32[]{:S(2)}) %collective-permute-start.15) | collective-permute-done | bytes 65568 | tf_op jit(solution)/shard_map/ppermute | solution.py:279
  103.5 1.4 %collective-permute-start.18 = (bf16[32,1024]{1,0:T(8,128)(2,1)S(1)}, bf16[32,1024]{1,0:T(8,128)(2,1)S(1)}, u32[]{:S(2)}, u32[]{:S(2)}) collective-permute-start(bf16[32,1024]{1,0:T(8,128)(2,1)S(1)} %inner.3.refs_4_), channel_id=1, source_target_pairs={{0,2},{1,3},{2,0},{3,1},{4,6},{5,7},{6,4},{7,5},{8,10},{9,11},{10,... | collective-permute-start | bytes 196616 | tf_op jit(solution)/shard_map/ppermute | solution.py:279
  104.9 1.3 collective-permute-done.11.refs_2_
  106.9 1.3 collective-permute-start.17
  109.0 2.9 %collective-permute-done.17.refs_5_ = bf16[32,1024]{1,0:T(8,128)(2,1)S(1)} collective-permute-done((bf16[32,1024]{1,0:T(8,128)(2,1)S(1)}, bf16[32,1024]{1,0:T(8,128)(2,1)S(1)}, u32[]{:S(2)}, u32[]{:S(2)}) %collective-permute-start.17) | collective-permute-done | bytes 65568 | tf_op jit(solution)/shard_map/ppermute | solution.py:279
  111.9 1.4 %collective-permute-done.19.refs_7_ = bf16[32,1024]{1,0:T(8,128)(2,1)S(1)} collective-permute-done((bf16[32,1024]{1,0:T(8,128)(2,1)S(1)}, bf16[32,1024]{1,0:T(8,128)(2,1)S(1)}, u32[]{:S(2)}, u32[]{:S(2)}) %collective-permute-start.19) | collective-permute-done | bytes 65568 | tf_op jit(solution)/shard_map/ppermute | solution.py:279
  113.3 1.4 %project_down.1 = bf16[32,4,1792]{2,1,0:T(4,128)(2,1)S(1)} custom-call(bf16[32,1280]{1,0:T(8,128)(2,1)S(1)} %get-tuple-element.67.refs_0_, bf16[32,1280]{1,0:T(8,128)(2,1)S(1)} %collective-permute-done.10.refs_1_, bf16[32,1280]{1,0:T(8,128)(2,1)S(1)} %collective-permute-done.11.refs_2_, bf16[32,1280]{1,0:T(8,128)(2,1)S(1)} %collective-permute-done.12.refs_3_, ...), custom_call_target="tpu_custom_call" | custom-call | tf_op jit(solution)/shard_map/project_down/pallas_call | solution.py:561
  114.7 15.7 %all_to_all.17.parts_ref = bf16[32,4,1792]{2,1,0:T(4,128)(2,1)S(1)} all-to-all(bf16[32,4,1792]{2,1,0:T(4,128)(2,1)S(1)} %project_down.1), channel_id=1, replica_groups=mesh['dp'=8,'tp'=4] {'dp','tp'}, dimensions={0} | all-to-all | bytes 917504 | tf_op jit(solution)/shard_map/all_to_all | solution.py:600
  (57 shorter events, 11.2 us)
Async XLA Ops:
  0.0 42.0 %copy-start.2 = (bf16[4,7168]{1,0:T(4,128)(2,1)S(1)}, bf16[4,7168]{1,0:T(4,128)(2,1)}, u32[]{:S(2)}) copy-start(bf16[4,7168]{1,0:T(4,128)(2,1)} %rows_ref) | copy-start | bytes 172036
  0.0 48.7 %copy-start = (bf16[2048,1792]{1,0:T(8,128)(2,1)S(1)}, bf16[2048,1792]{1,0:T(8,128)(2,1)}, u32[]{:S(2)}) copy-start(bf16[2048,1792]{1,0:T(8,128)(2,1)} %refs_4_.1) | copy-start | bytes 22020100
  0.0 75.1 %slice-start.2 = ((s8[8257536]{0:T(1024)(128)(4,1)}), s8[4194304]{0:T(1024)(128)(4,1)S(1)}, s32[]{:S(2)}) async-start(s8[8257536]{0:T(1024)(128)(4,1)} %bitcast.14), calls=%async_computation.5 | async-start | bytes 8388608
  36.8 38.4 %slice-start.3 = ((s8[8257536]{0:T(1024)(128)(4,1)}), s8[4063232]{0:T(1024)(128)(4,1)S(1)}, s32[]{:S(2)}) async-start(s8[8257536]{0:T(1024)(128)(4,1)} %bitcast.14), calls=%async_computation.6 | async-start | bytes 8126464
  37.6 8.2 %collective-permute-start.2 = (bf16[128,512]{1,0:T(8,128)(2,1)S(1)}, bf16[128,512]{1,0:T(8,128)(2,1)S(1)}, u32[]{:S(2)}, u32[]{:S(2)}) collective-permute-start(bf16[128,512]{1,0:T(8,128)(2,1)S(1)} %head_values.1.value_ref), channel_id=1, source_target_pairs={{0,3},{1,2},{2,1},{3,0},{4,7},{5,6},{6,5},{7,4},{8,11},{9,10},{10,... | collective-permute-start | bytes 393224 | tf_op jit(solution)/shard_map/ppermute | solution.py:279
  40.5 13.3 %collective-permute-start.1 = (bf16[128,512]{1,0:T(8,128)(2,1)S(1)}, bf16[128,512]{1,0:T(8,128)(2,1)S(1)}, u32[]{:S(2)}, u32[]{:S(2)}) collective-permute-start(bf16[128,512]{1,0:T(8,128)(2,1)S(1)} %head_values.1.value_ref), channel_id=1, source_target_pairs={{0,2},{1,3},{2,0},{3,1},{4,6},{5,7},{6,4},{7,5},{8,10},{9,11},{10,... | collective-permute-start | bytes 393224 | tf_op jit(solution)/shard_map/ppermute | solution.py:279
  41.7 12.1 %collective-permute-start = (bf16[128,512]{1,0:T(8,128)(2,1)S(1)}, bf16[128,512]{1,0:T(8,128)(2,1)S(1)}, u32[]{:S(2)}, u32[]{:S(2)}) collective-permute-start(bf16[128,512]{1,0:T(8,128)(2,1)S(1)} %head_values.1.value_ref), channel_id=1, source_target_pairs={{0,1},{1,0},{2,3},{3,2},{4,5},{5,4},{6,7},{7,6},{8,9},{9,8},{10,11... | collective-permute-start | bytes 393224 | tf_op jit(solution)/shard_map/ppermute | solution.py:279
  42.1 12.6 %collective-permute-start.3 = (bf16[4,1792]{1,0:T(4,128)(2,1)S(1)}, bf16[4,1792]{1,0:T(4,128)(2,1)S(1)}, u32[]{:S(2)}, u32[]{:S(2)}) collective-permute-start(bf16[4,1792]{1,0:T(4,128)(2,1)S(1)} %get-tuple-element.44), channel_id=1, source_target_pairs={{0,1},{1,0},{2,3},{3,2},{4,5},{5,4},{6,7},{7,6},{8,9},{9,8},{10,11... | collective-permute-start | bytes 43016 | tf_op jit(solution)/shard_map/ppermute | solution.py:279
  43.8 10.9 %collective-permute-start.4 = (bf16[4,1792]{1,0:T(4,128)(2,1)S(1)}, bf16[4,1792]{1,0:T(4,128)(2,1)S(1)}, u32[]{:S(2)}, u32[]{:S(2)}) collective-permute-start(bf16[4,1792]{1,0:T(4,128)(2,1)S(1)} %get-tuple-element.45), channel_id=1, source_target_pairs={{0,2},{1,3},{2,0},{3,1},{4,6},{5,7},{6,4},{7,5},{8,10},{9,11},{10,... | collective-permute-start | bytes 43016 | tf_op jit(solution)/shard_map/ppermute | solution.py:279
  45.8 8.9 %collective-permute-start.5 = (bf16[4,1792]{1,0:T(4,128)(2,1)S(1)}, bf16[4,1792]{1,0:T(4,128)(2,1)S(1)}, u32[]{:S(2)}, u32[]{:S(2)}) collective-permute-start(bf16[4,1792]{1,0:T(4,128)(2,1)S(1)} %get-tuple-element.46), channel_id=1, source_target_pairs={{0,3},{1,2},{2,1},{3,0},{4,7},{5,6},{6,5},{7,4},{8,11},{9,10},{10,... | collective-permute-start | bytes 43016 | tf_op jit(solution)/shard_map/ppermute | solution.py:279
  76.6 12.5 %collective-permute-start.6 = (bf16[64,1408]{1,0:T(8,128)(2,1)S(1)}, bf16[64,1408]{1,0:T(8,128)(2,1)S(1)}, u32[]{:S(2)}, u32[]{:S(2)}) collective-permute-start(bf16[64,1408]{1,0:T(8,128)(2,1)S(1)} %get-tuple-element.61), channel_id=1, source_target_pairs={{0,1},{1,0},{2,3},{3,2},{4,5},{5,4},{6,7},{7,6},{8,9},{9,8},{10,11... | collective-permute-start | bytes 540680 | tf_op jit(solution)/shard_map/ppermute | solution.py:279
  77.5 11.6 %collective-permute-start.7 = (bf16[64,1280]{1,0:T(8,128)(2,1)S(1)}, bf16[64,1280]{1,0:T(8,128)(2,1)S(1)}, u32[]{:S(2)}, u32[]{:S(2)}) collective-permute-start(bf16[64,1280]{1,0:T(8,128)(2,1)S(1)} %get-tuple-element.62), channel_id=1, source_target_pairs={{0,2},{1,3},{2,0},{3,1},{4,6},{5,7},{6,4},{7,5},{8,10},{9,11},{10,... | collective-permute-start | bytes 491528 | tf_op jit(solution)/shard_map/ppermute | solution.py:279
  80.1 12.2 %collective-permute-start.13 = (bf16[64,1024]{1,0:T(8,128)(2,1)S(1)}, bf16[64,1024]{1,0:T(8,128)(2,1)S(1)}, u32[]{:S(2)}, u32[]{:S(2)}) collective-permute-start(bf16[64,1024]{1,0:T(8,128)(2,1)S(1)} %get-tuple-element.71), channel_id=1, source_target_pairs={{0,1},{1,0},{2,3},{3,2},{4,5},{5,4},{6,7},{7,6},{8,9},{9,8},{10,11... | collective-permute-start | bytes 393224 | tf_op jit(solution)/shard_map/ppermute | solution.py:279
  80.7 16.4 %collective-permute-start.14 = (bf16[64,1024]{1,0:T(8,128)(2,1)S(1)}, bf16[64,1024]{1,0:T(8,128)(2,1)S(1)}, u32[]{:S(2)}, u32[]{:S(2)}) collective-permute-start(bf16[64,1024]{1,0:T(8,128)(2,1)S(1)} %get-tuple-element.72), channel_id=1, source_target_pairs={{0,2},{1,3},{2,0},{3,1},{4,6},{5,7},{6,4},{7,5},{8,10},{9,11},{10,... | collective-permute-start | bytes 393224 | tf_op jit(solution)/shard_map/ppermute | solution.py:279
  89.2 10.6 %collective-permute-start.8 = (bf16[32,1408]{1,0:T(8,128)(2,1)S(1)}, bf16[32,1408]{1,0:T(8,128)(2,1)S(1)}, u32[]{:S(2)}, u32[]{:S(2)}) collective-permute-start(bf16[32,1408]{1,0:T(8,128)(2,1)S(1)} %get-tuple-element.65), channel_id=1, source_target_pairs={{0,2},{1,3},{2,0},{3,1},{4,6},{5,7},{6,4},{7,5},{8,10},{9,11},{10,... | collective-permute-start | bytes 270344 | tf_op jit(solution)/shard_map/ppermute | solution.py:279
  89.5 7.8 %collective-permute-start.9 = (bf16[32,1280]{1,0:T(8,128)(2,1)S(1)}, bf16[32,1280]{1,0:T(8,128)(2,1)S(1)}, u32[]{:S(2)}, u32[]{:S(2)}) collective-permute-start(bf16[32,1280]{1,0:T(8,128)(2,1)S(1)} %get-tuple-element.66), channel_id=1, source_target_pairs={{0,1},{1,0},{2,3},{3,2},{4,5},{5,4},{6,7},{7,6},{8,9},{9,8},{10,11... | collective-permute-start | bytes 245768 | tf_op jit(solution)/shard_map/ppermute | solution.py:279
  97.1 6.3 %collective-permute-start.15 = (bf16[32,1024]{1,0:T(8,128)(2,1)S(1)}, bf16[32,1024]{1,0:T(8,128)(2,1)S(1)}, u32[]{:S(2)}, u32[]{:S(2)}) collective-permute-start(bf16[32,1024]{1,0:T(8,128)(2,1)S(1)} %get-tuple-element.75), channel_id=1, source_target_pairs={{0,2},{1,3},{2,0},{3,1},{4,6},{5,7},{6,4},{7,5},{8,10},{9,11},{10,... | collective-permute-start | bytes 196616 | tf_op jit(solution)/shard_map/ppermute | solution.py:279
  97.2 6.2 %collective-permute-start.16 = (bf16[32,1024]{1,0:T(8,128)(2,1)S(1)}, bf16[32,1024]{1,0:T(8,128)(2,1)S(1)}, u32[]{:S(2)}, u32[]{:S(2)}) collective-permute-start(bf16[32,1024]{1,0:T(8,128)(2,1)S(1)} %get-tuple-element.76), channel_id=1, source_target_pairs={{0,1},{1,0},{2,3},{3,2},{4,5},{5,4},{6,7},{7,6},{8,9},{9,8},{10,11... | collective-permute-start | bytes 196616 | tf_op jit(solution)/shard_map/ppermute | solution.py:279
  99.9 6.2 %collective-permute-start.11 = (bf16[32,1280]{1,0:T(8,128)(2,1)S(1)}, bf16[32,1280]{1,0:T(8,128)(2,1)S(1)}, u32[]{:S(2)}, u32[]{:S(2)}) collective-permute-start(bf16[32,1280]{1,0:T(8,128)(2,1)S(1)} %get-tuple-element.67.refs_0_), channel_id=1, source_target_pairs={{0,2},{1,3},{2,0},{3,1},{4,6},{5,7},{6,4},{7,5},{8,10},{9,11},{10,... | collective-permute-start | bytes 245768 | tf_op jit(solution)/shard_map/ppermute | solution.py:279
  103.5 5.5 %collective-permute-start.18 = (bf16[32,1024]{1,0:T(8,128)(2,1)S(1)}, bf16[32,1024]{1,0:T(8,128)(2,1)S(1)}, u32[]{:S(2)}, u32[]{:S(2)}) collective-permute-start(bf16[32,1024]{1,0:T(8,128)(2,1)S(1)} %inner.3.refs_4_), channel_id=1, source_target_pairs={{0,2},{1,3},{2,0},{3,1},{4,6},{5,7},{6,4},{7,5},{8,10},{9,11},{10,... | collective-permute-start | bytes 196616 | tf_op jit(solution)/shard_map/ppermute | solution.py:279
  104.9 7.0 %collective-permute-start.10 = (bf16[32,1280]{1,0:T(8,128)(2,1)S(1)}, bf16[32,1280]{1,0:T(8,128)(2,1)S(1)}, u32[]{:S(2)}, u32[]{:S(2)}) collective-permute-start(bf16[32,1280]{1,0:T(8,128)(2,1)S(1)} %get-tuple-element.67.refs_0_), channel_id=1, source_target_pairs={{0,1},{1,0},{2,3},{3,2},{4,5},{5,4},{6,7},{7,6},{8,9},{9,8},{10,11... | collective-permute-start | bytes 245768 | tf_op jit(solution)/shard_map/ppermute | solution.py:279
  106.2 7.1 %collective-permute-start.12 = (bf16[32,1280]{1,0:T(8,128)(2,1)S(1)}, bf16[32,1280]{1,0:T(8,128)(2,1)S(1)}, u32[]{:S(2)}, u32[]{:S(2)}) collective-permute-start(bf16[32,1280]{1,0:T(8,128)(2,1)S(1)} %collective-permute-done.11.refs_2_), channel_id=1, source_target_pairs={{0,1},{1,0},{2,3},{3,2},{4,5},{5,4},{6,7},{7,6},{8,9},{9,8},{10,11... | collective-permute-start | bytes 245768 | tf_op jit(solution)/shard_map/ppermute | solution.py:279
  106.9 4.9 %collective-permute-start.17 = (bf16[32,1024]{1,0:T(8,128)(2,1)S(1)}, bf16[32,1024]{1,0:T(8,128)(2,1)S(1)}, u32[]{:S(2)}, u32[]{:S(2)}) collective-permute-start(bf16[32,1024]{1,0:T(8,128)(2,1)S(1)} %inner.3.refs_4_), channel_id=1, source_target_pairs={{0,1},{1,0},{2,3},{3,2},{4,5},{5,4},{6,7},{7,6},{8,9},{9,8},{10,11... | collective-permute-start | bytes 196616 | tf_op jit(solution)/shard_map/ppermute | solution.py:279
  109.0 4.3 %collective-permute-start.19 = (bf16[32,1024]{1,0:T(8,128)(2,1)S(1)}, bf16[32,1024]{1,0:T(8,128)(2,1)S(1)}, u32[]{:S(2)}, u32[]{:S(2)}) collective-permute-start(bf16[32,1024]{1,0:T(8,128)(2,1)S(1)} %collective-permute-done.18.refs_6_), channel_id=1, source_target_pairs={{0,1},{1,0},{2,3},{3,2},{4,5},{5,4},{6,7},{7,6},{8,9},{9,8},{10,11... | collective-permute-start | bytes 196616 | tf_op jit(solution)/shard_map/ppermute | solution.py:279
  (6 other events, 193.9 us)
